TPU v7x, 128 devices: a whole 4x4x4 slice. The times are simulated.
128 devices in a mesh: seq: 32 (over x, y, core), fsdp: 4 (over z).
Axes of the slice: x: 4, y: 4, z: 4, core: 2. Of those that a mesh axis runs over, the one named last changes fastest.
Arguments:
- tokens: bfloat16 [4, 4096, 1536], P('fsdp', 'seq'), may hold values from -6 to 6
- cotangent: bfloat16 [4, 4096, 1536], P('fsdp', 'seq'), may hold values from -6 to 6
- lengths: int32 [4], P('fsdp'), may hold values from 1024 to 4096, as said below
- routes: int32 [4, 4096, 6], P('fsdp', 'seq'), may hold values from 0 to 7, all different within a row; in each aligned block of 128 rows (0 to 127, 128 to 255, ..., all dimensions but the last counted through in order) at most 112 rows name the same one
- norm_gain: float32 [1536], replicated, may hold values from 0.5 to 1.5
- w_in: bfloat16 [1536, 6448], P('fsdp'), may hold values from -0.15625 to 0.15625
- conv_weight: float32 [4, 3328], replicated, may hold values from -3 to 3
- conv_bias: float32 [3328], replicated, may hold values from -0.5 to 0.5
- a_log: float32 [48], replicated
- dt_bias: float32 [48], replicated, may hold values from -1 to 1
- skip_scale: float32 [48], replicated, may hold values from 0.5 to 1.5
- gated_gain: float32 [3072], replicated, may hold values from 0.5 to 1.5
- w_out: bfloat16 [3072, 1536], P('fsdp'), may hold values from -0.109375 to 0.109375
- post_gain: float32 [1536], replicated, may hold values from 0.5 to 1.5
- w_router: bfloat16 [1536, 8], P('fsdp'), may hold values from -0.078125 to 0.078125
- shared_in: bfloat16 [1536, 2048], P('fsdp'), may hold values from -0.15625 to 0.15625
- shared_out: bfloat16 [1024, 1536], P('fsdp'), may hold values from -0.1875 to 0.1875
- expert_in: bfloat16 [8, 1536, 1024], P('fsdp'), may hold values from -0.15625 to 0.15625
- expert_out: bfloat16 [8, 512, 1536], P('fsdp'), may hold values from -0.25 to 0.25
Outputs:
- block_out: bfloat16 [4, 4096, 1536], P('fsdp', 'seq')
- grad_tokens: float32 [4, 4096, 1536], P('fsdp', 'seq')
- grad_norm_gain: float32 [1536], P(('seq', 'fsdp'))
- grad_w_in: float32 [1536, 6448], P(('seq', 'fsdp'))
- grad_conv_weight: float32 [4, 3328], P(None, ('seq', 'fsdp'))
- grad_conv_bias: float32 [3328], P(('seq', 'fsdp'))
- grad_a_log: float32 [48], replicated
- grad_dt_bias: float32 [48], replicated
- grad_skip_scale: float32 [48], replicated
- grad_gated_gain: float32 [3072], P(('seq', 'fsdp'))
- grad_w_out: float32 [3072, 1536], P(('seq', 'fsdp'))
- grad_post_gain: float32 [1536], P(('seq', 'fsdp'))
- grad_w_router: float32 [1536, 8], P(('seq', 'fsdp'))
- grad_shared_in: float32 [1536, 2048], P(('seq', 'fsdp'))
- grad_shared_out: float32 [1024, 1536], P(('seq', 'fsdp'))
- grad_expert_in: float32 [8, 1536, 1024], P('fsdp', 'seq')
- grad_expert_out: float32 [8, 512, 1536], P('fsdp', 'seq')
Inputs may be any that keep to these rules, and one draw needn't show every extreme that they name: `lengths`: one entry, drawn from the seed, equals 4096. `routes`: each row names 6 different experts. In each aligned block of 128 rows (the slots of one sequence on one device) no expert is named by more than 112 rows, and some block reaches 112.
All inputs are finite; a program needn't handle non-finite values.
Results may differ from a plain program's by a relative error of at most 0.015.
Values may be sent and summed in bfloat16 or wider, within the bound.
A program may use at most 512 MiB of HBM per device.

v0:
```python
from functools import partial
import functools

import jax
import jax.numpy as jnp
from jax import lax
from jax.sharding import Mesh
from jax.sharding import PartitionSpec as P

MOST = 112
SEQ = ("seq_0", "seq_1", "seq_2")
SEQ_FSDP = ("seq_0", "seq_1", "seq_2", "fsdp")


NORM_EPS = 1e-05
PRECISE = lax.Precision.HIGHEST


def side_by_side(arrays, axis, dim, along):
    both = jnp.concatenate(arrays, axis=along)
    out, at, finished = (lax.all_gather(both, axis, axis=dim, tiled=True), 0, [])
    for a in arrays:
        finished.append(lax.slice_in_dim(out, at, at + a.shape[along], axis=along))
        at += a.shape[along]
    return tuple(finished)


def from_behind(block, axis, distance):
    devices = range(lax.axis_size(axis))
    route = [(i - distance, i) for i in devices if i - distance in devices]
    return lax.ppermute(block, axis, route)


def neutral_like(array, identity):
    return jax.tree.map(
        lambda part, zero: jnp.zeros_like(part) + jnp.asarray(zero, part.dtype), array, identity
    )


def carried_in(array, axes, combine, identity, reverse):
    before = start = neutral_like(array, identity)
    subtotal = array
    for axis in reversed(axes):
        length, position = (lax.axis_size(axis), lax.axis_index(axis))
        pieces = jax.tree.map(lambda part: lax.all_gather(part, axis), subtotal)
        inside, subtotal = (start, start)
        for k in reversed(range(length)) if reverse else range(length):
            passed = k > position if reverse else k < position
            subtotal = combine(subtotal, jax.tree.map(lambda part: part[k], pieces))
            inside = jax.tree.map(lambda new, old: jnp.where(passed, new, old), subtotal, inside)
        before = combine(inside, before)
    return before


def in_blocks(array, dim, length):
    shape = array.shape
    tiles = array.reshape(*shape[:dim], length, shape[dim] // length, *shape[dim + 1 :])
    return jnp.moveaxis(tiles, dim, 0)


def sum_packed(arrays, axis, dims):
    length = lax.axis_size(axis)
    tiles = [in_blocks(a, dim, length) for a, dim in zip(arrays, dims)]
    lines = jnp.concatenate([b.reshape(length, -1) for b in tiles], axis=1)
    rows = max(16, -(-lines.shape[1] // 1024) * 8)
    lines = jnp.pad(lines, ((0, 0), (0, rows * 128 - lines.shape[1]))).reshape(-1, 128)
    flat, at, finished = (lax.psum_scatter(lines, axis, tiled=True).reshape(-1), 0, [])
    for b in tiles:
        part = b[0]
        finished.append(flat[at : at + part.size].reshape(part.shape))
        at += part.size
    return tuple(finished)


def one_axis_at_a_time(array, axes):
    return functools.reduce(lax.psum, axes, array)


def scaled_rows(values, gain_vector):
    return values * lax.rsqrt(jnp.mean(values * values, -1, keepdims=True) + NORM_EPS) * gain_vector


def causal_conv(extended, conv_weight, conv_bias):
    tap_count = conv_weight.shape[0]
    length = extended.shape[0] - tap_count + 1
    summed = conv_bias[None, :]
    for offset in range(tap_count):
        summed = summed + conv_weight[offset][None, :] * extended[offset : offset + length]
    return jax.nn.silu(summed)


def scan_inputs(extended, dt_raw, conv_weight, conv_bias, a_log, dt_bias, inner_width):
    mixed = causal_conv(extended, conv_weight, conv_bias)
    length = mixed.shape[0]
    head_count = a_log.shape[0]
    state_width = (mixed.shape[1] - inner_width) // 2
    values = mixed[:, :inner_width].reshape(length, head_count, inner_width // head_count)
    in_map = mixed[:, inner_width : inner_width + state_width]
    out_map = mixed[:, inner_width + state_width :]
    step_size = jax.nn.softplus(dt_raw + dt_bias)
    log_decay = -jnp.exp(a_log) * step_size
    return (values, in_map, out_map, step_size, log_decay)


def block_scan(carried, values, in_map, out_map, step_size, log_decay):
    length = values.shape[0]
    running = jnp.cumsum(log_decay, 0)
    positions = jnp.arange(length)
    is_lower = (positions[:, None] >= positions[None, :])[:, :, None]
    decays = jnp.where(
        is_lower, jnp.exp(jnp.minimum(running[:, None, :] - running[None, :, :], 0.0)), 0.0
    )
    kernel = jnp.dot(out_map, in_map.T, precision=PRECISE)
    weights = kernel[:, :, None] * decays * step_size[None, :, :]
    result = jnp.einsum("tsh,shp->thp", weights, values, precision=PRECISE)
    result = result + jnp.exp(running)[:, :, None] * jnp.einsum(
        "tn,hpn->thp", out_map, carried, precision=PRECISE
    )
    last_sum = running[-1]
    scaled = jnp.exp(last_sum[None, :] - running) * step_size
    leaving = jnp.einsum("sh,shp,sn->hpn", scaled, values, in_map, precision=PRECISE)
    return (jnp.exp(last_sum), leaving, result)


def mixer_rows(
    extended,
    gate_raw,
    dt_raw,
    conv_weight,
    conv_bias,
    a_log,
    dt_bias,
    skip_scale,
    gated_gain,
    carried,
):
    inner_width = gated_gain.shape[0]
    values, in_map, out_map, step_size, log_decay = scan_inputs(
        extended, dt_raw, conv_weight, conv_bias, a_log, dt_bias, inner_width
    )
    unused_total, unused_state, result = block_scan(
        carried, values, in_map, out_map, step_size, log_decay
    )
    result = result + skip_scale[None, :, None] * values
    gated_rows = result.reshape(values.shape[0], inner_width) * jax.nn.silu(gate_raw)
    return scaled_rows(gated_rows, gated_gain)


def state_rows(extended, dt_raw, conv_weight, conv_bias, a_log, dt_bias, inner_width):
    values, in_map, out_map, step_size, log_decay = scan_inputs(
        extended, dt_raw, conv_weight, conv_bias, a_log, dt_bias, inner_width
    )
    carried = jnp.zeros((values.shape[1], values.shape[2], in_map.shape[1]), jnp.float32)
    decay_total, leaving, unused = block_scan(
        carried, values, in_map, out_map, step_size, log_decay
    )
    return (decay_total, leaving)


def link_states(earlier, later):
    return (earlier[0] * later[0], later[0][:, :, None, None] * earlier[1] + later[1])


def glu_back(acts_pair, hidden_back):
    half_width = acts_pair.shape[-1] // 2
    gate_part = acts_pair[..., :half_width]
    up_part = acts_pair[..., half_width:]
    sigmoid_gate = jax.nn.sigmoid(gate_part)
    gate_grad = hidden_back * up_part * sigmoid_gate * (1.0 + gate_part * (1.0 - sigmoid_gate))
    up_grad = hidden_back * gate_part * sigmoid_gate
    return jnp.concatenate([gate_grad, up_grad], -1).astype(jnp.bfloat16)


def expert_forward(buffer_rows, owned_in, owned_out):
    hidden_width = owned_out.shape[1]
    expert_acts = jnp.einsum(
        "serd,edf->serf", buffer_rows, owned_in, preferred_element_type=jnp.float32
    )
    expert_hidden = (
        jax.nn.silu(expert_acts[..., :hidden_width]) * expert_acts[..., hidden_width:]
    ).astype(jnp.bfloat16)
    expert_output = jnp.einsum(
        "serf,efd->serd", expert_hidden, owned_out, preferred_element_type=jnp.float32
    ).astype(jnp.bfloat16)
    return (expert_acts, expert_hidden, expert_output)


def select_rows(slot_table, where_rows):
    return jnp.take(slot_table, where_rows, axis=0)


def local(
    tokens,
    cotangent,
    lengths,
    routes,
    norm_gain,
    w_in,
    conv_weight,
    conv_bias,
    a_log,
    dt_bias,
    skip_scale,
    gated_gain,
    w_out,
    post_gain,
    w_router,
    shared_in,
    shared_out,
    expert_in,
    expert_out,
):
    seq_count = lax.axis_size(SEQ)
    full_in, full_out, full_router, full_shared_in, full_shared_out = (
        lax.all_gather(w_in, "fsdp", axis=0, tiled=True),
        lax.all_gather(w_out, "fsdp", axis=0, tiled=True),
        *side_by_side((w_router, shared_in), "fsdp", 0, 1),
        lax.all_gather(shared_out, "fsdp", axis=0, tiled=True),
    )
    owned_in, owned_out = (expert_in, expert_out)
    seq_rows, slot_count, model_width = tokens.shape
    inner_width = gated_gain.shape[0]
    conv_width = conv_bias.shape[0]
    tap_count = conv_weight.shape[0]
    expert_count = w_router.shape[1]
    route_count = routes.shape[2]
    capacity = MOST
    hidden_width = owned_out.shape[1]
    residual = tokens.astype(jnp.float32)
    positions = lax.axis_index(SEQ) * slot_count + jnp.arange(slot_count)
    valid_int = (positions[None, :] < lengths[:, None]).astype(jnp.int32)
    valid_rows = valid_int.astype(jnp.float32)
    first_norm = scaled_rows(residual, norm_gain).astype(jnp.bfloat16)
    projected = jnp.einsum("std,dk->stk", first_norm, full_in, preferred_element_type=jnp.float32)
    gate_raw = projected[:, :, :inner_width]
    conv_in = projected[:, :, inner_width : inner_width + conv_width]
    dt_raw = projected[:, :, inner_width + conv_width :]
    rim_rows = from_behind(conv_in[:, slot_count - tap_count + 1 :, :], SEQ, 1)
    extended = jnp.concatenate([rim_rows, conv_in], 1)
    state_fn = jax.vmap(
        partial(state_rows, inner_width=inner_width), in_axes=(0, 0, None, None, None, None)
    )
    (decay_total, leaving), state_pull = jax.vjp(
        state_fn, extended, dt_raw, conv_weight, conv_bias, a_log, dt_bias
    )
    identity = (jnp.ones_like(decay_total), jnp.zeros_like(leaving))
    carried = carried_in((decay_total, leaving), SEQ, link_states, identity, False)[1]
    mixer_fn = jax.vmap(mixer_rows, in_axes=(0, 0, 0, None, None, None, None, None, None, 0))
    normed, mixer_pull = jax.vjp(
        mixer_fn,
        extended,
        gate_raw,
        dt_raw,
        conv_weight,
        conv_bias,
        a_log,
        dt_bias,
        skip_scale,
        gated_gain,
        carried,
    )
    normed_low = normed.astype(jnp.bfloat16)
    middle = residual + jnp.einsum(
        "stk,kd->std", normed_low, full_out, preferred_element_type=jnp.float32
    )
    second_norm = scaled_rows(middle, post_gain).astype(jnp.bfloat16)
    logits = jnp.einsum("std,de->ste", second_norm, full_router, preferred_element_type=jnp.float32)
    gate_values = jax.nn.softmax(jnp.take_along_axis(logits, routes, 2), -1)
    route_hits = routes[:, :, :, None] == jnp.arange(expert_count)[None, None, None, :]
    hit_float = route_hits.astype(jnp.float32)
    chosen = jnp.sum(route_hits.astype(jnp.int32), 2) * valid_int[:, :, None]
    ranks = jnp.cumsum(chosen, 1) - chosen
    rank_at = jnp.sum(route_hits.astype(jnp.int32) * ranks[:, :, None, :], 3)
    slot_index = jnp.minimum(routes * capacity + rank_at, expert_count * capacity - 1)
    gate_dense = jnp.sum(gate_values[..., None] * hit_float, 2)
    ranks_by_expert = jnp.swapaxes(ranks, 1, 2)
    chosen_by_expert = jnp.swapaxes(chosen, 1, 2)
    dispatch_mask = (
        ranks_by_expert[:, :, None, :] == jnp.arange(capacity)[None, None, :, None]
    ) & (chosen_by_expert[:, :, None, :] > 0)
    dispatch = dispatch_mask.astype(jnp.bfloat16)
    dispatch_float = dispatch_mask.astype(jnp.float32)
    slot_gate = jnp.einsum("sert,ste->ser", dispatch_float, gate_dense, precision=PRECISE)
    buffer_rows = jnp.einsum(
        "sert,std->serd", dispatch, second_norm, preferred_element_type=jnp.float32
    ).astype(jnp.bfloat16)
    arrived = lax.all_to_all(buffer_rows, "fsdp", split_axis=1, concat_axis=0, tiled=True)
    expert_acts, expert_hidden, expert_output = expert_forward(arrived, owned_in, owned_out)
    returned = lax.all_to_all(expert_output, "fsdp", split_axis=0, concat_axis=1, tiled=True)
    slot_table = returned.reshape(seq_rows, expert_count * capacity, model_width)
    picked = jax.vmap(select_rows)(
        slot_table, slot_index.reshape(seq_rows, slot_count * route_count)
    )
    picked = picked.reshape(seq_rows, slot_count, route_count, model_width)
    expert_sum = jnp.sum(gate_values[..., None] * picked, 2)
    shared_acts = jnp.einsum(
        "std,df->stf", second_norm, full_shared_in, preferred_element_type=jnp.float32
    )
    shared_width = full_shared_out.shape[0]
    shared_hidden = (
        jax.nn.silu(shared_acts[..., :shared_width]) * shared_acts[..., shared_width:]
    ).astype(jnp.bfloat16)
    shared_sum = jnp.einsum(
        "sth,hd->std", shared_hidden, full_shared_out, preferred_element_type=jnp.float32
    )
    block_out = (valid_rows[:, :, None] * (middle + expert_sum + shared_sum)).astype(jnp.bfloat16)
    upstream = cotangent.astype(jnp.float32) * valid_rows[:, :, None]
    upstream_low = upstream.astype(jnp.bfloat16)
    shared_back = jnp.einsum(
        "std,hd->sth", upstream_low, full_shared_out, preferred_element_type=jnp.float32
    )
    grad_shared_out = jnp.einsum(
        "sth,std->hd", shared_hidden, upstream_low, preferred_element_type=jnp.float32
    )
    shared_act_grad = glu_back(shared_acts, shared_back)
    grad_shared_in = jnp.einsum(
        "std,stf->df", second_norm, shared_act_grad, preferred_element_type=jnp.float32
    )
    second_back = jnp.einsum(
        "stf,df->std", shared_act_grad, full_shared_in, preferred_element_type=jnp.float32
    )
    slot_upstream = jnp.einsum(
        "sert,std->serd", dispatch, upstream_low, preferred_element_type=jnp.float32
    )
    slot_grads = (slot_gate[..., None] * slot_upstream).astype(jnp.bfloat16)
    gate_grads = jnp.sum(upstream[:, :, None, :] * picked, 3)
    slot_arrived = lax.all_to_all(slot_grads, "fsdp", split_axis=1, concat_axis=0, tiled=True)
    hidden_back = jnp.einsum(
        "serd,efd->serf", slot_arrived, owned_out, preferred_element_type=jnp.float32
    )
    expert_act_grad = glu_back(expert_acts, hidden_back)
    buffer_back = jnp.einsum(
        "serf,edf->serd", expert_act_grad, owned_in, preferred_element_type=jnp.float32
    )
    lead_count, group_count, slot_depth = arrived.shape[:3]
    split_rows = arrived.reshape(
        lead_count, group_count, slot_depth, seq_count, model_width // seq_count
    )
    grad_in_blocks = jnp.einsum(
        "serid,serf->iedf", split_rows, expert_act_grad, preferred_element_type=jnp.float32
    )
    grad_in_blocks = grad_in_blocks.reshape(
        seq_count * group_count, model_width // seq_count, owned_in.shape[2]
    )
    split_hidden = expert_hidden.reshape(
        lead_count, group_count, slot_depth, seq_count, hidden_width // seq_count
    )
    grad_out_blocks = jnp.einsum(
        "serig,serd->iegd", split_hidden, slot_arrived, preferred_element_type=jnp.float32
    )
    grad_out_blocks = grad_out_blocks.reshape(
        seq_count * group_count, hidden_width // seq_count, model_width
    )
    returned_back = lax.all_to_all(
        buffer_back.astype(jnp.bfloat16), "fsdp", split_axis=0, concat_axis=1, tiled=True
    ).astype(buffer_back.dtype)
    grad_expert_in, grad_expert_out = tuple(
        (
            part.astype(jnp.float32)
            for part in sum_packed(
                (grad_in_blocks.astype(jnp.bfloat16), grad_out_blocks.astype(jnp.bfloat16)),
                SEQ,
                (0, 0),
            )
        )
    )
    second_back = second_back + jnp.einsum(
        "sert,serd->std", dispatch_float, returned_back, precision=PRECISE
    )
    pick_grads = gate_values * (gate_grads - jnp.sum(gate_values * gate_grads, -1, keepdims=True))
    logit_grads = jnp.sum(pick_grads[..., None] * hit_float, 2).astype(jnp.bfloat16)
    grad_router = jnp.einsum(
        "std,ste->de", second_norm, logit_grads, preferred_element_type=jnp.float32
    )
    second_back = second_back + jnp.einsum(
        "ste,de->std", logit_grads, full_router, preferred_element_type=jnp.float32
    )
    unused_second, second_pull = jax.vjp(scaled_rows, middle, post_gain)
    middle_back, grad_post_gain = second_pull(second_back)
    middle_back = middle_back + upstream
    mix_low = middle_back.astype(jnp.bfloat16)
    grad_w_out = jnp.einsum("stk,std->kd", normed_low, mix_low, preferred_element_type=jnp.float32)
    normed_back = jnp.einsum("std,kd->stk", mix_low, full_out, preferred_element_type=jnp.float32)
    (
        ext_mixer,
        gate_back,
        dt_mixer,
        conv_w_mixer,
        conv_b_mixer,
        decay_mixer,
        bias_mixer,
        grad_skip_scale,
        grad_gated_gain,
        incoming_back,
    ) = mixer_pull(normed_back)
    leaving_back = carried_in((decay_total, incoming_back), SEQ, link_states, identity, True)[1]
    decay_back = jnp.sum(leaving_back * carried, (2, 3))
    ext_state, dt_state, conv_w_state, conv_b_state, decay_state, bias_state = state_pull(
        (decay_back, leaving_back)
    )
    ext_back = ext_mixer + ext_state
    rim_back = from_behind(ext_back[:, : tap_count - 1, :].astype(jnp.bfloat16), SEQ, -1).astype(
        jnp.float32
    )
    conv_back = ext_back[:, tap_count - 1 :, :] + jnp.pad(
        rim_back, ((0, 0), (slot_count - tap_count + 1, 0), (0, 0))
    )
    proj_back = jnp.concatenate([gate_back, conv_back, dt_mixer + dt_state], -1).astype(
        jnp.bfloat16
    )
    grad_w_in = jnp.einsum("std,stk->dk", first_norm, proj_back, preferred_element_type=jnp.float32)
    first_back = jnp.einsum("stk,dk->std", proj_back, full_in, preferred_element_type=jnp.float32)
    unused_first, first_pull = jax.vjp(scaled_rows, residual, norm_gain)
    input_back, grad_norm_gain = first_pull(first_back)
    grad_tokens = middle_back + input_back
    grad_a_log, grad_dt_bias, grad_skip_total = (
        one_axis_at_a_time(decay_mixer + decay_state, SEQ_FSDP),
        one_axis_at_a_time(bias_mixer + bias_state, SEQ_FSDP),
        one_axis_at_a_time(grad_skip_scale, SEQ_FSDP),
    )
    (
        norm_gain_part,
        w_in_part,
        conv_w_part,
        conv_b_part,
        gated_part,
        w_out_part,
        post_part,
        router_part,
        shared_in_part,
        shared_out_part,
    ) = sum_packed(
        (
            grad_norm_gain,
            grad_w_in,
            conv_w_mixer + conv_w_state,
            conv_b_mixer + conv_b_state,
            grad_gated_gain,
            grad_w_out,
            grad_post_gain,
            grad_router,
            grad_shared_in,
            grad_shared_out,
        ),
        SEQ_FSDP,
        (0, 0, 1, 0, 0, 0, 0, 0, 0, 0),
    )
    return (
        block_out,
        grad_tokens,
        norm_gain_part,
        w_in_part,
        conv_w_part,
        conv_b_part,
        grad_a_log,
        grad_dt_bias,
        grad_skip_total,
        gated_part,
        w_out_part,
        post_part,
        router_part,
        shared_in_part,
        shared_out_part,
        grad_expert_in,
        grad_expert_out,
    )


def solution(mesh):
    split = Mesh(
        mesh.devices.reshape(4, 4, 2, mesh.shape["fsdp"]), ("seq_0", "seq_1", "seq_2", "fsdp")
    )
    placed = (
        P("fsdp", SEQ, None),
        P("fsdp", SEQ, None),
        P("fsdp"),
        P("fsdp", SEQ, None),
        P(),
        P("fsdp", None),
        P(),
        P(),
        P(),
        P(),
        P(),
        P(),
        P("fsdp", None),
        P(),
        P("fsdp", None),
        P("fsdp", None),
        P("fsdp", None),
        P("fsdp", None, None),
        P("fsdp", None, None),
    )
    return jax.shard_map(
        local,
        mesh=split,
        in_specs=placed,
        out_specs=(
            P("fsdp", SEQ, None),
            P("fsdp", SEQ, None),
            P(SEQ_FSDP),
            P(SEQ_FSDP, None),
            P(None, SEQ_FSDP),
            P(SEQ_FSDP),
            P(),
            P(),
            P(),
            P(SEQ_FSDP),
            P(SEQ_FSDP, None),
            P(SEQ_FSDP),
            P(SEQ_FSDP, None),
            P(SEQ_FSDP, None),
            P(SEQ_FSDP, None),
            P("fsdp", SEQ, None),
            P("fsdp", SEQ, None),
        ),
        check_vma=False,
    )
```

profile of v0, /device:TPU:0, one launch (start us, length us, event | category | flops | bytes accessed | tf_op | source)
XLA Modules:
  0.0 2341.2 jit_solution(9338898459767476628)
XLA Ops:
  11.0 181.5 %all-gather.13.cloned.1.call-done = bf16[1536,6448]{0,1:T(8,128)(2,1)} async-done(((bf16[384,6448]{0,1:T(8,128)(2,1)}), bf16[1536,6448]{0,1:T(8,128)(2,1)}) %all-gather.13.cloned.1.call-update) | async-done | bytes 19808272 | tf_op jit(solution)/shard_map/all_gather | solution.py:215
  252.1 66.6 %all-gather.15.cloned.1.call-done = f32[4,1,48,64,128]{4,3,2,1,0:T(8,128)} async-done(((f32[1,1,48,64,128]{4,3,2,1,0:T(8,128)}), f32[4,1,48,64,128]{4,3,2,1,0:T(8,128)}) %all-gather.15.cloned.1.call-update) | async-done | bytes 6291472 | tf_op jit(solution)/shard_map/all_gather | solution.py:45
  359.1 30.6 %all-gather.17.cloned.1.call-done = f32[4,1,48,64,128]{4,3,2,1,0:T(8,128)} async-done(((f32[1,1,48,64,128]{4,3,2,1,0:T(8,128)}), f32[4,1,48,64,128]{4,3,2,1,0:T(8,128)}) %all-gather.17.cloned.1.call-update) | async-done | bytes 6291472 | tf_op jit(solution)/shard_map/all_gather | solution.py:45
  416.1 67.9 %all-gather.19.cloned.1.call-done = bf16[3072,1536]{1,0:T(8,128)(2,1)} async-done(((bf16[768,1536]{1,0:T(8,128)(2,1)}), bf16[3072,1536]{1,0:T(8,128)(2,1)}) %all-gather.19.cloned.1.call-update) | async-done | bytes 9437200 | tf_op jit(solution)/shard_map/all_gather | solution.py:216
  499.3 62.8 %all-to-all-done = bf16[1,8,112,1536]{3,2,0,1:T(8,128)(2,1)} async-done(((bf16[1,8,112,1536]{3,2,0,1:T(8,128)(2,1)}), bf16[1,8,112,1536]{3,2,0,1:T(8,128)(2,1)}, u32[]{:S(2)}, u32[]{:S(2)}) %all-to-all-start) | async-done | bytes 2752544 | tf_op jit(solution)/shard_map/all_to_all | solution.py:287
  596.2 18.4 all-to-all-done.1
  614.6 12.5 gather_fusion.1
  647.3 41.3 %all-to-all-done.2 = bf16[1,8,112,1536]{3,2,0,1:T(8,128)(2,1)} async-done(((bf16[1,8,112,1536]{3,2,0,1:T(8,128)(2,1)}), bf16[1,8,112,1536]{3,2,0,1:T(8,128)(2,1)}, u32[]{:S(2)}, u32[]{:S(2)}) %all-to-all-start.2) | async-done | bytes 2752544 | tf_op jit(solution)/shard_map/all_to_all | solution.py:327
  722.0 13.7 all-to-all-done.3
  762.6 27.6 %all-gather.31.cloned.1.call-done = f32[96,64,128]{2,1,0:T(8,128)} async-done(((f32[48,64,128]{2,1,0:T(8,128)}), f32[96,64,128]{2,1,0:T(8,128)}) %all-gather.31.cloned.1.call-update) | async-done | bytes 3145744 | tf_op jit(solution)/shard_map/all_gather | solution.py:45
  835.7 25.1 %all-gather.25.cloned.1.call-done = f32[4,1,48,64,128]{4,3,2,1,0:T(8,128)} async-done(((f32[1,1,48,64,128]{4,3,2,1,0:T(8,128)}), f32[4,1,48,64,128]{4,3,2,1,0:T(8,128)}) %all-gather.25.cloned.1.call-update) | async-done | bytes 6291472 | tf_op jit(solution)/shard_map/all_gather | solution.py:45
  891.0 14.1 reshape_reshape.20
  948.2 20.4 reshape_reshape.18
  993.3 12.3 fusion.72
  1038.2 15.8 fusion.141
  1054.1 39.5 %reshape_reshape.17 = f32[128,77376]{1,0:T(8,128)} reshape(f32[1536,6448]{1,0:T(8,128)} %fusion.141) | data formatting | bytes 79233024 | tf_op jit(solution)/shard_map/reshape;reshape | solution.py:64
  1095.1 112.0 %dynamic-update-slice.1 = f32[128,151378]{1,0:T(8,128)} dynamic-update-slice(f32[128,151378]{1,0:T(8,128)} %dynamic-update-slice, f32[128,77376]{1,0:T(8,128)} %reshape_reshape.17, s32[]{} %constant.207, s32[]{} %constant.208) | dynamic-update-slice | bytes 79233024
  1212.2 56.3 %dynamic-update-slice.5 = f32[128,151378]{1,0:T(8,128)} dynamic-update-slice(f32[128,151378]{1,0:T(8,128)} %dynamic-update-slice.4, f32[128,36864]{1,0:T(8,128)} %reshape_reshape.18, s32[]{} %constant.207, s32[]{} %constant.212) | dynamic-update-slice | bytes 37748740
  1271.9 45.2 %dynamic-update-slice.8 = f32[128,151378]{1,0:T(8,128)} dynamic-update-slice(f32[128,151378]{1,0:T(8,128)} %dynamic-update-slice.7, f32[128,24576]{1,0:T(8,128)} %reshape_reshape.20, s32[]{} %constant.207, s32[]{} %constant.215) | dynamic-update-slice | bytes 25165828
  1317.1 22.9 dynamic-update-slice.9
  1340.0 50.8 %pad.101 = f32[128,151552]{1,0:T(8,128)} pad(f32[128,151378]{1,0:T(8,128)} %dynamic-update-slice.9, f32[]{:T(128)} %constant.101.clone.1), padding=0_0x0_174 | pad | bytes 155100160 | tf_op jit(solution)/shard_map/jit(_pad)/pad | solution.py:66
  1390.8 84.5 %reshape.2044 = f32[151552,128]{1,0:T(8,128)} reshape(f32[128,151552]{1,0:T(8,128)} %pad.101) | data formatting | bytes 155189248 | tf_op jit(solution)/shard_map/reshape | solution.py:66
  1489.7 12.0 all-reduce.26
  1527.5 787.7 %reduce-scatter.3.cloned.1.call-done = f32[1184,128]{1,0:T(8,128)} async-done(((f32[151552,128]{1,0:T(8,128)}), f32[1184,128]{1,0:T(8,128)}) %reduce-scatter.3.cloned.1.call-update) | async-done | bytes 606224 | tf_op jit(solution)/shard_map/reduce_scatter | solution.py:67
  (588 shorter events, 502.4 us)
Async XLA Ops:
  7.2 563.7 %copy-start = (bf16[2,512,1536]{2,1,0:T(8,128)(2,1)S(1)}, bf16[2,512,1536]{2,1,0:T(8,128)(2,1)}, u32[]{:S(2)}) copy-start(bf16[2,512,1536]{2,1,0:T(8,128)(2,1)} %param.38) | copy-start | bytes 9437188
  7.2 185.3 %all-gather.13.cloned.1.call-start = ((), (), s32[]{:S(2)}) async-start(), calls=%async_computation.6 | async-start | bytes 24760320 | tf_op jit(solution)/shard_map/all_gather | solution.py:215
  7.3 185.2 %copy-start.55 = (f32[1536]{0:T(1024)S(1)}, f32[1536]{0:T(1024)}, u32[]{:S(2)}) copy-start(f32[1536]{0:T(1024)} %param.24) | copy-start | bytes 18436
  7.9 240.1 %all-gather.29.cloned.1.call-start = ((), (), s32[]{:S(2)}) async-start(), calls=%async_computation.16 | async-start | bytes 4718592 | tf_op jit(solution)/shard_map/all_gather | solution.py:45
  10.5 192.8 %copy-start.88 = (f32[128]{0:T(128)}, f32[128]{0:T(128)S(1)}, u32[]{:S(2)}) copy-start(f32[128]{0:T(128)S(1)} %fusion.221) | copy-start | bytes 1540
  11.0 195.4 %copy-start.122 = (f32[48]{0:T(128)S(1)}, f32[48]{0:T(128)}, u32[]{:S(2)}) copy-start(f32[48]{0:T(128)} %param.29) | copy-start | bytes 580
  204.0 12.3 collective-permute-start
  232.6 86.1 %all-gather.15.cloned.1.call-start = ((), (), s32[]{:S(2)}) async-start(), calls=%async_computation.7 | async-start | bytes 7864320 | tf_op jit(solution)/shard_map/all_gather | solution.py:45
  251.4 138.3 %all-gather.17.cloned.1.call-start = ((), (), s32[]{:S(2)}) async-start(), calls=%async_computation.8 | async-start | bytes 7864320 | tf_op jit(solution)/shard_map/all_gather | solution.py:45
  323.3 160.7 %all-gather.19.cloned.1.call-start = ((), (), s32[]{:S(2)}) async-start(), calls=%async_computation.9 | async-start | bytes 11796480 | tf_op jit(solution)/shard_map/all_gather | solution.py:216
  323.8 264.2 %all-gather.21.cloned.1.call-start = ((), (), s32[]{:S(2)}) async-start(), calls=%async_computation.10 | async-start | bytes 8355840 | tf_op jit(solution)/shard_map/all_gather | solution.py:21
  338.1 152.7 %copy-start.67 = (s32[8,128]{1,0:T(8,128)}, s32[8,128]{1,0:T(8,128)S(1)}, u32[]{:S(2)}) copy-start(s32[8,128]{1,0:T(8,128)S(1)} %copy.430) | copy-start | bytes 12292
  493.2 69.0 %all-to-all-start = ((bf16[1,8,112,1536]{3,2,0,1:T(8,128)(2,1)}), bf16[1,8,112,1536]{3,2,0,1:T(8,128)(2,1)}, u32[]{:S(2)}, u32[]{:S(2)}) async-start(bf16[1,8,112,1536]{3,2,0,1:T(8,128)(2,1)} %fusion.28), calls=%async_computation | async-start | bytes 5505024 | tf_op jit(solution)/shard_map/all_to_all | solution.py:287
  574.2 40.3 %all-to-all-start.1 = ((bf16[4,2,112,1536]{3,2,1,0:T(8,128)(2,1)}), bf16[4,2,112,1536]{3,2,1,0:T(8,128)(2,1)}, u32[]{:S(2)}, u32[]{:S(2)}) async-start(bf16[4,2,112,1536]{3,2,1,0:T(8,128)(2,1)} %copy.434), calls=%async_computation.1 | async-start | bytes 5505024 | tf_op jit(solution)/shard_map/all_to_all | solution.py:289
  641.9 46.6 %all-to-all-start.2 = ((bf16[1,8,112,1536]{3,2,0,1:T(8,128)(2,1)}), bf16[1,8,112,1536]{3,2,0,1:T(8,128)(2,1)}, u32[]{:S(2)}, u32[]{:S(2)}) async-start(bf16[1,8,112,1536]{3,2,0,1:T(8,128)(2,1)} %fusion.35), calls=%async_computation.2 | async-start | bytes 5505024 | tf_op jit(solution)/shard_map/all_to_all | solution.py:327
  646.5 71.2 %all-gather.23.cloned.1.call-start = ((), (), s32[]{:S(2)}) async-start(), calls=%async_computation.11 | async-start | bytes 3932160 | tf_op jit(solution)/shard_map/all_gather | solution.py:218
  703.1 32.6 %all-to-all-start.3 = ((bf16[4,2,112,1536]{3,2,1,0:T(8,128)(2,1)}), bf16[4,2,112,1536]{3,2,1,0:T(8,128)(2,1)S(1)}, u32[]{:S(2)}, u32[]{:S(2)}) async-start(bf16[4,2,112,1536]{3,2,1,0:T(8,128)(2,1)} %copy.438), calls=%async_computation.3 | async-start | bytes 5505024 | tf_op jit(solution)/shard_map/all_to_all | solution.py:354
  706.9 83.3 %all-gather.31.cloned.1.call-start = ((), (), s32[]{:S(2)}) async-start(), calls=%async_computation.17 | async-start | bytes 4718592 | tf_op jit(solution)/shard_map/all_gather | solution.py:45
  762.2 98.7 %all-gather.25.cloned.1.call-start = ((), (), s32[]{:S(2)}) async-start(), calls=%async_computation.12 | async-start | bytes 7864320 | tf_op jit(solution)/shard_map/all_gather | solution.py:45
  793.6 182.8 %all-gather.27.cloned.1.call-start = ((), (), s32[]{:S(2)}) async-start(), calls=%async_computation.13 | async-start | bytes 7864320 | tf_op jit(solution)/shard_map/all_gather | solution.py:45
  865.3 620.7 %reduce-scatter.5.cloned.1.call-start = ((), (), s32[]{:S(2)}) async-start(), calls=%async_computation.15 | async-start | bytes 9732096 | tf_op jit(solution)/shard_map/reduce_scatter | solution.py:67
  886.3 1428.8 %reduce-scatter.3.cloned.1.call-start = ((), (), s32[]{:S(2)}) async-start(), calls=%async_computation.14 | async-start | bytes 78200832 | tf_op jit(solution)/shard_map/reduce_scatter | solution.py:67
  1022.4 3.8 collective-permute-start.1
  1524.8 809.4 %copy-start.1 = (bf16[2,512,1536]{2,1,0:T(8,128)(2,1)S(1)}, bf16[2,512,1536]{2,1,0:T(8,128)(2,1)}, u32[]{:S(2)}) copy-start(bf16[2,512,1536]{2,1,0:T(8,128)(2,1)} %param.38) | copy-start | bytes 9437188
  (161 other events, 1824.3 us)
Sparse Core Ops, SparseCore 0:
  9.7 182.7 all-gather.12
  232.7 15.3 all-gather.28
  251.6 67.0 all-gather.14
  323.4 66.3 all-gather.16
  391.2 92.7 all-gather.18
  485.5 102.3 all-gather.20
  649.0 56.2 all-gather.22
  762.3 27.8 all-gather.30
  793.7 67.0 all-gather.24
  865.4 66.2 all-gather.26
  935.5 95.9 reduce-scatter.4
  1475.5 839.5 reduce-scatter.2
where the time goes:
time: 2360 us; the launch traced here: 2340 us
  waiting for transfers between devices  1330 us (56%)
  local copies, waits for them, and re-layouts  609 us (26%)
  matrix products  170 us (7%)
  other arithmetic  127 us (5%)
  blocking collectives  67 us (3%)
    reduce_scatter x2, waiting for transfers between devices, sum_packed(): lax.psum_scatter(lines, axis, tiled=True).reshape(-1)  788 us
    unnamed x350, local copies, waits for them, and re-layouts  249 us
    all_gather x1, waiting for transfers between devices, local(): lax.all_gather(w_in, 'fsdp', axis=0, tiled=True)  182 us
    all_gather x6, waiting for transfers between devices, carried_in(): pieces = jax.tree.map(lambda part: lax.all_gather(part, axis), subtotal)  152 us
    reshape x2, local copies, waits for them, and re-layouts, sum_packed(): jnp.pad(lines, ((0, 0), (0, rows * 128 - lines.shape[1]))).reshape(-1, 128)  94.5 us
    another operation x5, local copies, waits for them, and re-layouts, sum_packed(): lines = jnp.concatenate([b.reshape(length, -1) for b in tiles], axis=1)  82.3 us
    all_gather x1, waiting for transfers between devices, local(): lax.all_gather(w_out, 'fsdp', axis=0, tiled=True)  67.9 us
    all_to_all x1, waiting for transfers between devices, local(): lax.all_to_all(buffer_rows, 'fsdp', split_axis=1, concat_axis=0, tiled=True)  62.8 us
  transfers between devices with their start and end apart: 18, of which 12 were waited for; matrix products, arithmetic and copies ran while one was open for 33% of the time, Pallas kernels for 0%

commit v1 on v0

v1 whole, which is shorter than its diff:
```python
import functools

import jax
import jax.numpy as jnp
from jax import lax
from jax.experimental import pallas as pl
from jax.experimental.pallas import tpu as pltpu
from jax.sharding import Mesh
from jax.sharding import PartitionSpec as P

SEQ = ("x", "y", "c")
ALL = ("x", "y", "c", "z")
NORM_EPS = 1e-05
PRECISE = lax.Precision.HIGHEST


def scaled_rows(values, gain_vector):
    return values * lax.rsqrt(jnp.mean(values * values, -1, keepdims=True) + NORM_EPS) * gain_vector


def causal_conv(extended, conv_weight, conv_bias):
    tap_count = conv_weight.shape[0]
    length = extended.shape[0] - tap_count + 1
    summed = conv_bias[None, :]
    for offset in range(tap_count):
        summed = summed + conv_weight[offset][None, :] * extended[offset : offset + length]
    return jax.nn.silu(summed)


def scan_inputs(extended, dt_raw, conv_weight, conv_bias, a_log, dt_bias, inner_width):
    mixed = causal_conv(extended, conv_weight, conv_bias)
    length = mixed.shape[0]
    head_count = a_log.shape[0]
    state_width = (mixed.shape[1] - inner_width) // 2
    values = mixed[:, :inner_width].reshape(length, head_count, inner_width // head_count)
    in_map = mixed[:, inner_width : inner_width + state_width]
    out_map = mixed[:, inner_width + state_width :]
    step_size = jax.nn.softplus(dt_raw + dt_bias)
    log_decay = -jnp.exp(a_log) * step_size
    return (values, in_map, out_map, step_size, log_decay)


def block_scan(carried, values, in_map, out_map, step_size, log_decay):
    length = values.shape[0]
    running = jnp.cumsum(log_decay, 0)
    positions = jnp.arange(length)
    is_lower = (positions[:, None] >= positions[None, :])[:, :, None]
    decays = jnp.where(
        is_lower, jnp.exp(jnp.minimum(running[:, None, :] - running[None, :, :], 0.0)), 0.0
    )
    kernel = jnp.dot(out_map, in_map.T, precision=PRECISE)
    weights = kernel[:, :, None] * decays * step_size[None, :, :]
    result = jnp.einsum("tsh,shp->thp", weights, values, precision=PRECISE)
    result = result + jnp.exp(running)[:, :, None] * jnp.einsum(
        "tn,hpn->thp", out_map, carried, precision=PRECISE
    )
    last_sum = running[-1]
    scaled = jnp.exp(last_sum[None, :] - running) * step_size
    leaving = jnp.einsum("sh,shp,sn->hpn", scaled, values, in_map, precision=PRECISE)
    return (jnp.exp(last_sum), leaving, result)


def mixer_rows(
    extended,
    gate_raw,
    dt_raw,
    conv_weight,
    conv_bias,
    a_log,
    dt_bias,
    skip_scale,
    gated_gain,
    carried,
):
    inner_width = gated_gain.shape[0]
    values, in_map, out_map, step_size, log_decay = scan_inputs(
        extended, dt_raw, conv_weight, conv_bias, a_log, dt_bias, inner_width
    )
    unused_total, unused_state, result = block_scan(
        carried, values, in_map, out_map, step_size, log_decay
    )
    result = result + skip_scale[None, :, None] * values
    gated_rows = result.reshape(values.shape[0], inner_width) * jax.nn.silu(gate_raw)
    return scaled_rows(gated_rows, gated_gain)


def state_rows(extended, dt_raw, conv_weight, conv_bias, a_log, dt_bias, inner_width):
    values, in_map, out_map, step_size, log_decay = scan_inputs(
        extended, dt_raw, conv_weight, conv_bias, a_log, dt_bias, inner_width
    )
    carried = jnp.zeros((values.shape[1], values.shape[2], in_map.shape[1]), jnp.float32)
    decay_total, leaving, unused = block_scan(
        carried, values, in_map, out_map, step_size, log_decay
    )
    return (decay_total, leaving)


def glu_back(acts_pair, hidden_back):
    half_width = acts_pair.shape[-1] // 2
    gate_part = acts_pair[..., :half_width]
    up_part = acts_pair[..., half_width:]
    sigmoid_gate = jax.nn.sigmoid(gate_part)
    gate_grad = hidden_back * up_part * sigmoid_gate * (1.0 + gate_part * (1.0 - sigmoid_gate))
    up_grad = hidden_back * gate_part * sigmoid_gate
    return jnp.concatenate([gate_grad, up_grad], -1).astype(jnp.bfloat16)


MESH_ID = pl.DeviceIdType.MESH
RS_ORDERS = (("x", "y", "z"), ("y", "z", "x"), ("z", "x", "y"))
RS_STEPS = 9
RS_COLS = 512


def ring(axis, offset):
    size = lax.axis_size(axis)
    return lax.rem(lax.axis_index(axis) + offset + size, size)


def greet(targets):
    barrier = pltpu.get_barrier_semaphore()
    for target in targets:
        pl.semaphore_signal(barrier, inc=1, device_id=target, device_id_type=MESH_ID)
    pl.semaphore_wait(barrier, len(targets))


def remote(src, dst, send_sem, recv_sem, target):
    return pltpu.make_async_remote_copy(
        src_ref=src,
        dst_ref=dst,
        send_sem=send_sem,
        recv_sem=recv_sem,
        device_id=target,
        device_id_type=MESH_ID,
    )


def dot32(left, right):
    return jnp.dot(left, right, preferred_element_type=jnp.float32)


def grad_sum_kernel(
    a_ref, b_ref, out_ref,
    core_out, core_in, near, far, second_in, third_out, third_in, lines,
    core_ss, core_rs, near_ss, near_rs, far_ss, far_rs, second_ss, second_rs, third_ss, third_rs,
):
    me_core = lax.axis_index("c")
    other = 1 - me_core
    half = core_out.shape[2]
    block = half // 4
    edge = block // 2
    small = block // 4
    unit = out_ref.shape[0]
    kept = small // 4
    lines[...] = jnp.zeros_like(lines)
    greet(
        [{"c": other}]
        + [{axis: ring(axis, o)} for axis in ("x", "y", "z") for o in (1, 2, 3)]
    )

    def left_of(part, k):
        if part == 0:
            return 0
        if part == 1:
            return 1 + jnp.minimum(k // 4, 1)
        return 3 + k // 3

    def core_copy(part, k):
        slot = part * RS_STEPS + k
        return remote(
            core_out.at[lax.rem(k, 2), part], core_in.at[slot],
            core_ss.at[slot], core_rs.at[slot], {"c": other},
        )

    def near_copies(part, k):
        slot = part * RS_STEPS + k
        axis = RS_ORDERS[part][0]
        after, before, across = ring(axis, 1), ring(axis, -1), ring(axis, 2)
        plan = ((before, 0, before), (after, edge, after), (across, 0, after), (across, edge, before))
        return [
            remote(
                core_in.at[slot, pl.ds(which * block + offset, edge)], near.at[slot, n],
                near_ss.at[slot, n], near_rs.at[slot, n], {axis: target},
            )
            for n, (which, offset, target) in enumerate(plan)
        ]

    def far_copies(part, k):
        slot = part * RS_STEPS + k
        axis = RS_ORDERS[part][0]
        return [
            remote(
                near.at[slot, 2 + n], far.at[slot, n],
                far_ss.at[slot, n], far_rs.at[slot, n], {axis: ring(axis, o)},
            )
            for n, o in enumerate((1, -1))
        ]

    def second_copies(part, k):
        slot = part * RS_STEPS + k
        axis = RS_ORDERS[part][1]
        copies = []
        for o in (1, 2, 3):
            target = ring(axis, o)
            copies.append(
                remote(
                    near.at[slot, target // 2, pl.ds(lax.rem(target, 2) * small, small)],
                    second_in.at[slot, o - 1],
                    second_ss.at[slot, o - 1], second_rs.at[slot, o - 1], {axis: target},
                )
            )
        return copies

    def third_copies(part, k):
        slot = part * RS_STEPS + k
        axis = RS_ORDERS[part][2]
        return [
            remote(
                third_out.at[slot, ring(axis, o)], third_in.at[slot, o - 1],
                third_ss.at[slot, o - 1], third_rs.at[slot, o - 1], {axis: ring(axis, o)},
            )
            for o in (1, 2, 3)
        ]

    def stage_product(part, k):
        slot = part * RS_STEPS + k

        @pl.when(k >= 2)
        def _():
            core_copy(part, k - 2).wait_send()

        def rows_at(j, carry):
            rows = pl.ds(pl.multiple_of(j * block, block), block)
            left = a_ref[left_of(part, k), pl.ds(pl.multiple_of(other * half + j * block, block), block), :]
            for col in range(0, RS_COLS, 256):
                core_out[lax.rem(k, 2), part, rows, col : col + 256] = dot32(
                    left, b_ref[:, pl.ds(pl.multiple_of(slot * RS_COLS + col, 256), 256)]
                ).astype(jnp.bfloat16)
            return carry

        lax.fori_loop(0, 4, rows_at, 0)
        core_copy(part, k).start()

    def stage_near(part, k):
        slot = part * RS_STEPS + k
        core_copy(part, k).wait_recv()

        def rows_at(j, carry):
            rows = pl.ds(pl.multiple_of(j * block, block), block)
            left = a_ref[left_of(part, k), pl.ds(pl.multiple_of(me_core * half + j * block, block), block), :]
            for col in range(0, RS_COLS, 256):
                mine = dot32(left, b_ref[:, pl.ds(pl.multiple_of(slot * RS_COLS + col, 256), 256)])
                theirs = core_in[slot, rows, col : col + 256].astype(jnp.float32)
                core_in[slot, rows, col : col + 256] = (mine + theirs).astype(jnp.bfloat16)
            return carry

        lax.fori_loop(0, 4, rows_at, 0)
        for copy in near_copies(part, k):
            copy.start()

    def load(ref, *where):
        return ref[where].astype(jnp.float32)

    def stage_far(part, k):
        slot = part * RS_STEPS + k
        axis = RS_ORDERS[part][0]
        copies = near_copies(part, k)
        for n, (which, offset) in enumerate(((ring(axis, 1), 0), (ring(axis, -1), edge))):
            copies[2 + n].wait_recv()
            rows = pl.ds(pl.multiple_of(which * block + offset, edge), edge)
            near[slot, 2 + n] = (load(near, slot, 2 + n) + load(core_in, slot, rows)).astype(jnp.bfloat16)
        for copy in far_copies(part, k):
            copy.start()

    def stage_second(part, k):
        slot = part * RS_STEPS + k
        me = lax.axis_index(RS_ORDERS[part][0])
        copies, far_in = near_copies(part, k), far_copies(part, k)
        for n in range(2):
            copies[n].wait_recv()
            far_in[n].wait_recv()
            rows = pl.ds(pl.multiple_of(me * block + n * edge, edge), edge)
            near[slot, n] = (
                load(near, slot, n) + load(far, slot, n) + load(core_in, slot, rows)
            ).astype(jnp.bfloat16)
        for copy in second_copies(part, k):
            copy.start()

    def stage_third(part, k):
        slot = part * RS_STEPS + k
        me = lax.axis_index(RS_ORDERS[part][1])
        for copy in second_copies(part, k):
            copy.wait_recv()
        rows = pl.ds(pl.multiple_of(lax.rem(me, 2) * small, small), small)
        lines[part, :small] = load(near, slot, me // 2, rows) + (
            load(second_in, slot, 0) + load(second_in, slot, 1) + load(second_in, slot, 2)
        )
        for j in range(4):
            third_out[slot, j] = lines[part, kept * j : kept * j + unit].astype(jnp.bfloat16)
        for copy in third_copies(part, k):
            copy.start()

    def stage_last(part, k):
        slot = part * RS_STEPS + k
        for copy in third_copies(part, k):
            copy.wait_recv()
        me = lax.axis_index(RS_ORDERS[part][2])
        out_ref[:, pl.ds(pl.multiple_of(slot * RS_COLS, RS_COLS), RS_COLS)] = load(
            third_out, slot, me
        ) + (load(third_in, slot, 0) + load(third_in, slot, 1) + load(third_in, slot, 2))

    stages = (stage_product, stage_near, stage_far, stage_second, stage_third, stage_last)

    def step(t, carry):
        for lag, stage in enumerate(stages):
            k = t - lag

            @pl.when((k >= 0) & (k < RS_STEPS))
            def _():
                for part in range(3):
                    stage(part, k)

        return carry

    lax.fori_loop(0, RS_STEPS + len(stages) - 1, step, 0)

    def finish(k, carry):
        for part in range(3):
            @pl.when(k >= RS_STEPS - 2)
            def _():
                core_copy(part, k).wait_send()

            for copies in (near_copies, far_copies, second_copies, third_copies):
                for copy in copies(part, k):
                    copy.wait_send()
        return carry

    lax.fori_loop(0, RS_STEPS, finish, 0)


def grad_sum(lefts, rights):
    cols, slots, depth = RS_COLS, rights.shape[1] // RS_COLS, rights.shape[0]
    rows = lefts.shape[1]
    half = rows // 2
    block = half // 4
    low = jnp.bfloat16
    sems = lambda *shape: pltpu.SemaphoreType.DMA(shape)
    return pl.pallas_call(
        grad_sum_kernel,
        out_shape=jax.ShapeDtypeStruct((16, slots * cols), jnp.float32),
        in_specs=[pl.BlockSpec(memory_space=pltpu.VMEM)] * 2,
        out_specs=pl.BlockSpec(memory_space=pltpu.VMEM),
        scratch_shapes=[
            pltpu.VMEM((2, 3, half, cols), low),
            pltpu.VMEM((slots, half, cols), low),
            pltpu.VMEM((slots, 4, block // 2, cols), low),
            pltpu.VMEM((slots, 2, block // 2, cols), low),
            pltpu.VMEM((slots, 3, block // 4, cols), low),
            pltpu.VMEM((slots, 4, 16, cols), low),
            pltpu.VMEM((slots, 3, 16, cols), low),
            pltpu.VMEM((3, block // 4 + 8, cols), jnp.float32),
            sems(slots), sems(slots), sems(slots, 4), sems(slots, 4), sems(slots, 2), sems(slots, 2),
            sems(slots, 3), sems(slots, 3), sems(slots, 3), sems(slots, 3),
        ],
        compiler_params=pltpu.CompilerParams(
            collective_id=0, has_side_effects=True, vmem_limit_bytes=58 * 2**20
        ),
        cost_estimate=pl.CostEstimate(flops=2 * slots * rows * depth * cols, bytes_accessed=8 * 2**20, transcendentals=0),
        name="grad_sum",
    )(lefts, rights)


def plane_spot(position):
    return {"x": position // 8, "y": lax.rem(position // 2, 4), "c": lax.rem(position, 2)}


def state_exchange(reverse, state_ref, totals_ref, out_ref, decays_ref, got, back, ss, rs, ts, tr, bs, br):
    spots = 32
    me = lax.axis_index("x") * 8 + lax.axis_index("y") * 2 + lax.axis_index("c")
    heads = got.shape[1]
    barrier = pltpu.get_barrier_semaphore()

    def spot(o):
        return lax.rem(me + o, spots)

    def share(ref, position):
        return ref.at[pl.ds(heads * (position // 2), heads), lax.rem(position, 2)]

    def knock(o, carry):
        pl.semaphore_signal(barrier, inc=1, device_id=plane_spot(spot(o)), device_id_type=MESH_ID)
        return carry

    lax.fori_loop(1, spots, knock, 0)
    pl.semaphore_wait(barrier, spots - 1)

    def out_copy(o):
        target = spot(o)
        return remote(share(state_ref, target), got.at[me], ss.at[o], rs.at[o], plane_spot(target))

    def total_copy(o):
        return remote(totals_ref, decays_ref.at[me], ts.at[o], tr.at[o], plane_spot(spot(o)))

    def back_copy(o):
        target = spot(o)
        return remote(back.at[target], share(out_ref, me), bs.at[o], br.at[o], plane_spot(target))

    def send(o, carry):
        if not reverse:
            total_copy(o).start()
        out_copy(o).start()
        return carry

    lax.fori_loop(1, spots, send, 0)
    mine = pl.ds(heads * (me // 2), heads)
    got[me] = state_ref[mine, lax.rem(me, 2)]
    if not reverse:
        decays_ref[me] = totals_ref[...]

    def arrive(o, carry):
        if not reverse:
            total_copy(o).wait_recv()
        out_copy(o).wait_recv()
        return carry

    lax.fori_loop(1, spots, arrive, 0)
    source = totals_ref if reverse else decays_ref
    lanes = lax.broadcasted_iota(jnp.int32, (8, 128), 1) - heads * (me // 2)

    def advance(step, carried):
        p = spots - 1 - step if reverse else step
        logs = source[p]
        new = []
        for h in range(heads):
            back[p, h] = carried[h].astype(back.dtype)
            decay = jnp.exp(jnp.sum(jnp.where(lanes == h, logs, 0.0), 1, keepdims=True))[:1]
            new.append(carried[h] * decay + got[p, h].astype(jnp.float32))
        return tuple(new)

    zero = jnp.zeros(got.shape[2:], jnp.float32)
    lax.fori_loop(0, spots, advance, (zero,) * heads)

    def send_back(o, carry):
        back_copy(o).start()
        return carry

    lax.fori_loop(1, spots, send_back, 0)
    out_ref[mine, lax.rem(me, 2)] = back[me]

    def finish(o, carry):
        back_copy(o).wait_recv()
        back_copy(o).wait_send()
        out_copy(o).wait_send()
        if not reverse:
            total_copy(o).wait_send()
        return carry

    lax.fori_loop(1, spots, finish, 0)


def scan_forward_kernel(state_ref, totals_ref, out_ref, decays_ref, *scratch):
    state_exchange(False, state_ref, totals_ref, out_ref, decays_ref, *scratch)


def scan_backward_kernel(state_ref, decays_ref, out_ref, *scratch):
    state_exchange(True, state_ref, decays_ref, out_ref, None, *scratch)


def carried_states(state, logs, reverse):
    heads, size, width = state.shape
    share = (heads // 16, size // 2, width)
    state = state.astype(jnp.bfloat16).reshape(heads, 2, size // 2, width)
    sem = pltpu.SemaphoreType.DMA((32,))
    out_shape = jax.ShapeDtypeStruct(state.shape, jnp.bfloat16)
    space = pl.BlockSpec(memory_space=pltpu.VMEM)
    kept = jax.ShapeDtypeStruct((32, 8, 128), jnp.float32)
    result = pl.pallas_call(
        scan_backward_kernel if reverse else scan_forward_kernel,
        out_shape=out_shape if reverse else (out_shape, kept),
        in_specs=[space] * 2,
        out_specs=space if reverse else (space, space),
        scratch_shapes=[pltpu.VMEM((32, *share), jnp.bfloat16)] * 2 + [sem] * 6,
        compiler_params=pltpu.CompilerParams(
            collective_id=2 if reverse else 1, has_side_effects=True, vmem_limit_bytes=32 * 2**20
        ),
        name="scan_backward" if reverse else "scan_forward",
    )(state, logs)
    if reverse:
        return result.reshape(heads, size, width)
    return result[0].reshape(heads, size, width), result[1]


Z_ALL = [{"z": 1}, {"z": 2}, {"z": 3}]


def z_gather_kernel(count, *refs):
    ins, outs, (ss, rs) = refs[:count], refs[count : 2 * count], refs[2 * count :]
    me = lax.axis_index("z")
    greet([{"z": ring("z", o)} for o in (1, 2, 3)])
    copies = []
    for n in range(count):
        for o in (1, 3, 2):
            copies.append(
                remote(ins[n], outs[n].at[me], ss.at[n, o], rs.at[n, o], {"z": ring("z", o)})
            )
            copies[-1].start()
    for n in range(count):
        outs[n][me] = ins[n][...]
    for copy in copies:
        copy.wait()


def z_gather(arrays, cid, name):
    count = len(arrays)
    space = pl.BlockSpec(memory_space=pltpu.VMEM)
    sem = pltpu.SemaphoreType.DMA((count, 4))
    return pl.pallas_call(
        functools.partial(z_gather_kernel, count),
        out_shape=tuple(jax.ShapeDtypeStruct((4, *a.shape), a.dtype) for a in arrays),
        in_specs=[space] * count,
        out_specs=(space,) * count,
        scratch_shapes=[sem, sem],
        compiler_params=pltpu.CompilerParams(
            collective_id=cid, has_side_effects=True, vmem_limit_bytes=32 * 2**20
        ),
        name=name,
    )(*arrays)


def z_sum_kernel(back_ref, part_ref, picks_ref, back_sum, part_sum, picks_all, got, ss, rs):
    me = lax.axis_index("z")
    greet([{"z": ring("z", o)} for o in (1, 2, 3)])
    copies = []
    for n, ref in enumerate((back_ref, part_ref)):
        for o in (1, 3, 2):
            copies.append(
                remote(ref.at[ring("z", o)], got.at[n, o - 1], ss.at[n, o], rs.at[n, o], {"z": ring("z", o)})
            )
            copies[-1].start()
    for o in (1, 3, 2):
        copies.append(
            remote(picks_ref.at[ring("z", o)], picks_all.at[me], ss.at[2, o], rs.at[2, o], {"z": ring("z", o)})
        )
        copies[-1].start()
    picks_all[me] = picks_ref[me]
    for copy in copies:
        copy.wait()
    for n, (ref, out) in enumerate(((back_ref, back_sum), (part_ref, part_sum))):
        def rows_at(j, carry, ref=ref, out=out, n=n):
            rows = pl.ds(pl.multiple_of(j * 32, 32), 32)
            total = ref[me, rows].astype(jnp.float32)
            for o in range(3):
                total = total + got[n, o, rows].astype(jnp.float32)
            out[rows] = total
            return carry

        lax.fori_loop(0, out.shape[0] // 32, rows_at, 0)


def z_sum(back, part, picks):
    space = pl.BlockSpec(memory_space=pltpu.VMEM)
    sem = pltpu.SemaphoreType.DMA((3, 4))
    total = jax.ShapeDtypeStruct(back.shape[1:], jnp.float32)
    return pl.pallas_call(
        z_sum_kernel,
        out_shape=(total, total, jax.ShapeDtypeStruct(picks.shape, picks.dtype)),
        in_specs=[space] * 3,
        out_specs=(space,) * 3,
        scratch_shapes=[pltpu.VMEM((2, 3, *back.shape[1:]), back.dtype), sem, sem],
        compiler_params=pltpu.CompilerParams(
            collective_id=4, has_side_effects=True, vmem_limit_bytes=32 * 2**20
        ),
        name="z_sum",
    )(back, part, picks)


def from_behind(block, axis, distance):
    devices = range(lax.axis_size(axis))
    route = [(i - distance, i) for i in devices if i - distance in devices]
    return lax.ppermute(block, axis, route)


def side_by_side(arrays, axis, dim, along):
    both = jnp.concatenate(arrays, axis=along)
    out, at, finished = (lax.all_gather(both, axis, axis=dim, tiled=True), 0, [])
    for a in arrays:
        finished.append(lax.slice_in_dim(out, at, at + a.shape[along], axis=along))
        at += a.shape[along]
    return tuple(finished)


def owner_rows(values, order, per_owner):
    depth, columns = values.shape
    grid = values.T.reshape(4, 4, 2, 4, per_owner, depth)
    place = {"x": 0, "y": 1, "c": 2, "z": 3}
    return jnp.transpose(grid, [place[a] for a in ("c", *order)] + [4, 5])


def left_rows(values, order, per_owner=12):
    grid = owner_rows(values, order, per_owner)
    if per_owner == 24:
        return [grid[..., :12, :].reshape(1536, -1), grid[..., 12:, :].reshape(1536, -1)]
    grid = jnp.pad(grid, ((0, 0),) * 4 + ((0, 12 - per_owner), (0, 0)))
    return [grid.reshape(1536, -1)]


def local(
    tokens,
    cotangent,
    lengths,
    routes,
    norm_gain,
    w_in,
    conv_weight,
    conv_bias,
    a_log,
    dt_bias,
    skip_scale,
    gated_gain,
    w_out,
    post_gain,
    w_router,
    shared_in,
    shared_out,
    expert_in,
    expert_out,
):
    low = jnp.bfloat16
    full_in, full_out, full_router, full_shared_in, full_shared_out = (
        lax.all_gather(w_in, "z", axis=0, tiled=True),
        lax.all_gather(w_out, "z", axis=0, tiled=True),
        *side_by_side((w_router, shared_in), "z", 0, 1),
        lax.all_gather(shared_out, "z", axis=0, tiled=True),
    )
    tokens, cotangent, routes = tokens[0], cotangent[0], routes[0]
    slot_count, model_width = tokens.shape
    inner_width = gated_gain.shape[0]
    conv_width = conv_bias.shape[0]
    head_count = a_log.shape[0]
    tap_count = conv_weight.shape[0]
    expert_count = w_router.shape[1]
    residual = tokens.astype(jnp.float32)
    positions = lax.axis_index(SEQ) * slot_count + jnp.arange(slot_count)
    valid = positions < lengths[0]
    upstream_low = jnp.where(valid[:, None], cotangent, jnp.zeros_like(cotangent))
    upstream = upstream_low.astype(jnp.float32)
    (all_upstream,) = z_gather((upstream_low,), 3, "gather_upstream")

    first_norm = scaled_rows(residual, norm_gain).astype(low)
    projected = dot32(first_norm, full_in)
    gate_raw = projected[:, :inner_width]
    conv_in = projected[:, inner_width : inner_width + conv_width]
    dt_raw = projected[:, inner_width + conv_width :]
    rim_rows = from_behind(conv_in[slot_count - tap_count + 1 :, :], SEQ, 1)
    extended = jnp.concatenate([rim_rows, conv_in], 0)
    state_fn = functools.partial(state_rows, inner_width=inner_width)
    (decay_total, leaving), state_pull = jax.vjp(
        state_fn, extended, dt_raw, conv_weight, conv_bias, a_log, dt_bias
    )
    log_total = jnp.sum(-jnp.exp(a_log) * jax.nn.softplus(dt_raw + dt_bias), 0)
    totals = jnp.broadcast_to(jnp.pad(log_total, (0, 128 - head_count))[None], (8, 128))
    carried, decays = carried_states(leaving, totals, False)
    carried = carried.astype(jnp.float32)
    normed, mixer_pull = jax.vjp(
        mixer_rows,
        extended,
        gate_raw,
        dt_raw,
        conv_weight,
        conv_bias,
        a_log,
        dt_bias,
        skip_scale,
        gated_gain,
        carried,
    )
    normed_low = normed.astype(low)
    middle = residual + dot32(normed_low, full_out)
    second_norm = scaled_rows(middle, post_gain).astype(low)
    logits = dot32(second_norm, full_router)
    gate_values = jax.nn.softmax(jnp.take_along_axis(logits, routes, 1), -1)
    hits = (routes[:, :, None] == jnp.arange(expert_count)[None, None, :]).astype(jnp.float32)
    gate_dense = jnp.sum(gate_values[..., None] * hits, 1)

    all_rows, all_gates = z_gather((second_norm, gate_dense.T), 5, "gather_rows")
    rows = all_rows.reshape(-1, model_width)
    back_rows = all_upstream.reshape(-1, model_width)
    owned = expert_in.shape[0]
    first_owned = lax.axis_index("z") * owned
    gates = lax.dynamic_slice_in_dim(all_gates, first_owned, owned, 1)
    gates = jnp.swapaxes(gates, 0, 1).reshape(owned, -1)
    hidden_width = expert_out.shape[1]
    acts = jnp.einsum("td,edf->etf", rows, expert_in, preferred_element_type=jnp.float32)
    hidden = (jax.nn.silu(acts[..., :hidden_width]) * acts[..., hidden_width:]).astype(low)
    output = jnp.einsum("etf,efd->etd", hidden, expert_out, preferred_element_type=jnp.float32)
    output = output.astype(low).astype(jnp.float32)
    part = jnp.sum(gates[..., None] * output, 0).astype(low)
    back_wide = back_rows.astype(jnp.float32)
    picks = jnp.sum(output * back_wide[None], -1)
    out_grad = (gates[..., None] * back_wide[None]).astype(low)
    hidden_back = jnp.einsum("etd,efd->etf", out_grad, expert_out, preferred_element_type=jnp.float32)
    act_grad = glu_back(acts, hidden_back)
    back = jnp.einsum("etf,edf->td", act_grad, expert_in, preferred_element_type=jnp.float32).astype(low)
    picks = jnp.swapaxes(picks.reshape(owned, 4, slot_count), 0, 1)
    picks = jnp.pad(picks, ((0, 0), (0, 8 - owned), (0, 0)))
    back_sum, expert_sum, all_picks = z_sum(
        back.reshape(4, slot_count, model_width), part.reshape(4, slot_count, model_width), picks
    )
    grad_expert_in = jnp.einsum("td,etf->edf", rows, act_grad, preferred_element_type=jnp.float32)
    grad_expert_out = jnp.einsum("etf,etd->efd", hidden, out_grad, preferred_element_type=jnp.float32)
    grad_expert_in = lax.psum_scatter(
        grad_expert_in.astype(low), SEQ, scatter_dimension=1, tiled=True
    ).astype(jnp.float32)
    grad_expert_out = lax.psum_scatter(
        grad_expert_out.astype(low), SEQ, scatter_dimension=1, tiled=True
    ).astype(jnp.float32)

    shared_width = full_shared_out.shape[0]
    shared_acts = dot32(second_norm, full_shared_in)
    shared_hidden = (
        jax.nn.silu(shared_acts[:, :shared_width]) * shared_acts[:, shared_width:]
    ).astype(low)
    shared_sum = dot32(shared_hidden, full_shared_out)
    block_out = jnp.where(valid[:, None], middle + expert_sum + shared_sum, 0.0).astype(low)
    shared_back = jnp.einsum("td,hd->th", upstream_low, full_shared_out, preferred_element_type=jnp.float32)
    shared_act_grad = glu_back(shared_acts, shared_back)
    second_back = jnp.einsum("tf,df->td", shared_act_grad, full_shared_in, preferred_element_type=jnp.float32)
    gate_grads = all_picks[:, :owned].reshape(expert_count, slot_count).T
    pick_grads = gate_dense * (gate_grads - jnp.sum(gate_dense * gate_grads, -1, keepdims=True))
    logit_grads = pick_grads.astype(low)
    second_back = second_back + back_sum + jnp.einsum(
        "te,de->td", logit_grads, full_router, preferred_element_type=jnp.float32
    )
    unused_second, second_pull = jax.vjp(scaled_rows, middle, post_gain)
    middle_back, grad_post_gain = second_pull(second_back)
    middle_back = middle_back + upstream
    mix_low = middle_back.astype(low)
    normed_back = jnp.einsum("td,kd->tk", mix_low, full_out, preferred_element_type=jnp.float32)
    (
        ext_mixer,
        gate_back,
        dt_mixer,
        conv_w_mixer,
        conv_b_mixer,
        decay_mixer,
        bias_mixer,
        grad_skip_scale,
        grad_gated_gain,
        incoming_back,
    ) = mixer_pull(normed_back)
    leaving_back = carried_states(incoming_back, decays, True).astype(jnp.float32)
    decay_back = jnp.sum(leaving_back * carried, (1, 2))
    ext_state, dt_state, conv_w_state, conv_b_state, decay_state, bias_state = state_pull(
        (decay_back, leaving_back)
    )
    ext_back = ext_mixer + ext_state
    rim_back = from_behind(ext_back[: tap_count - 1, :].astype(low), SEQ, -1).astype(jnp.float32)
    conv_back = ext_back[tap_count - 1 :, :] + jnp.pad(
        rim_back, ((slot_count - tap_count + 1, 0), (0, 0))
    )
    proj_back = jnp.concatenate([gate_back, conv_back, dt_mixer + dt_state], -1).astype(low)
    first_back = jnp.einsum("tk,dk->td", proj_back, full_in, preferred_element_type=jnp.float32)
    unused_first, first_pull = jax.vjp(scaled_rows, residual, norm_gain)
    input_back, grad_norm_gain = first_pull(first_back)
    grad_tokens = middle_back + input_back

    first, second, third = RS_ORDERS
    lefts = jnp.stack(
        left_rows(first_norm, first)
        + left_rows(first_norm, second)
        + left_rows(second_norm, second)
        + left_rows(normed_low, third, 24)
        + left_rows(shared_hidden, third, 8)
    )
    width_in = proj_back.shape[1]
    zeros = lambda columns: jnp.zeros((slot_count, columns), low)
    rights = jnp.concatenate(
        [
            proj_back,
            zeros(13 * RS_COLS - width_in),
            shared_act_grad,
            logit_grads,
            zeros(RS_COLS - expert_count),
            mix_low,
            mix_low,
            upstream_low,
        ],
        1,
    )
    summed = grad_sum(lefts, rights)
    at = 13 * RS_COLS
    w_in_part = summed[:12, :width_in]
    shared_in_part = summed[:12, at : at + 2 * shared_width]
    at = at + 4 * RS_COLS
    router_part = summed[:12, at : at + expert_count]
    at = at + RS_COLS
    w_out_part = jnp.concatenate(
        [summed[:12, at : at + model_width], summed[:12, at + model_width : at + 2 * model_width]], 0
    )
    at = at + 2 * model_width
    shared_out_part = summed[:8, at : at + model_width]

    smalls = [
        grad_norm_gain,
        (conv_w_mixer + conv_w_state).reshape(-1),
        conv_b_mixer + conv_b_state,
        grad_gated_gain,
        grad_post_gain,
        decay_mixer + decay_state,
        bias_mixer + bias_state,
        grad_skip_scale,
    ]
    sizes = [s.shape[0] for s in smalls]
    packed = jnp.concatenate(smalls)
    packed = lax.psum(jnp.pad(packed, (0, -packed.shape[0] % 1024)).reshape(-1, 128), ALL).reshape(-1)
    pieces, at = [], 0
    for size in sizes:
        pieces.append(packed[at : at + size])
        at += size
    owner = lax.axis_index(ALL)

    def owned_part(values):
        size = values.shape[-1] // 128
        return lax.dynamic_slice_in_dim(values, owner * size, size, values.ndim - 1)

    return (
        block_out[None],
        grad_tokens[None],
        owned_part(pieces[0]),
        w_in_part,
        owned_part(pieces[1].reshape(tap_count, conv_width)),
        owned_part(pieces[2]),
        pieces[5],
        pieces[6],
        pieces[7],
        owned_part(pieces[3]),
        w_out_part,
        owned_part(pieces[4]),
        router_part,
        shared_in_part,
        shared_out_part,
        grad_expert_in,
        grad_expert_out,
    )


def solution(mesh):
    split = Mesh(mesh.devices.reshape(4, 4, 2, 4), ALL)
    placed = (
        P("z", SEQ, None),
        P("z", SEQ, None),
        P("z"),
        P("z", SEQ, None),
        P(),
        P("z", None),
        P(),
        P(),
        P(),
        P(),
        P(),
        P(),
        P("z", None),
        P(),
        P("z", None),
        P("z", None),
        P("z", None),
        P("z", None, None),
        P("z", None, None),
    )
    return jax.shard_map(
        local,
        mesh=split,
        in_specs=placed,
        out_specs=(
            P("z", SEQ, None),
            P("z", SEQ, None),
            P(ALL),
            P(ALL, None),
            P(None, ALL),
            P(ALL),
            P(),
            P(),
            P(),
            P(ALL),
            P(ALL, None),
            P(ALL),
            P(ALL, None),
            P(ALL, None),
            P(ALL, None),
            P("z", SEQ, None),
            P("z", SEQ, None),
        ),
        check_vma=False,
    )
```

time: 2360 us -> 1000 us (0.42)
  waiting for transfers between devices: 1330 us -> 355 us
  local copies, waits for them, and re-layouts: 609 us -> 126 us
  Pallas kernels: 0 us -> 296 us
  blocking collectives: 67 us -> 0 us
  other arithmetic: 127 us -> 63.7 us
  matrix products: 170 us -> 127 us
    reduce_scatter x2 -> x1, waiting for transfers between devices: 788 us -> 82.1 us  [local(): lax.psum_scatter(grad_expert_out.astype(low), SEQ, scatter_dimension=1, t...]
    pallas_call x0 -> x6, Pallas kernels: none -> 296 us  [the longest x1 115 us: grad_sum(): pl.pallas_call(grad_sum_kernel, out_shape=jax.ShapeDtypeStruct((16, slots...]
    all_gather x9 -> x3, waiting for transfers between devices: 402 us -> 144 us  [the longest x1 144 us: local(): lax.all_gather(w_in, 'z', axis=0, tiled=True)]
    unnamed x350 -> x227, local copies, waits for them, and re-layouts: 249 us -> 14.2 us
    all_to_all x4 -> x0, waiting for transfers between devices: 136 us -> none  [the longest x1 62.8 us: local(): lax.all_to_all(buffer_rows, 'fsdp', split_axis=1, concat_axis=0, tiled=True)]
    reshape x16 -> x14, local copies, waits for them, and re-layouts: 105 us -> 9.3 us  [the longest x8 5.82 us: causal_conv(): conv_weight[offset][None, :] * extended[offset:offset + length]]
    another operation x7 -> x8, local copies, waits for them, and re-layouts: 84.7 us -> 7.69 us  [the longest x7 6.17 us: local(): jnp.stack(left_rows(first_norm, first) + left_rows(first_norm, second) +...]
    unnamed x12 -> x8, waiting for transfers between devices: 2.02 us -> 74.4 us
  transfers between devices with their start and end apart: 18 -> 9, of which waited for: 12 -> 4; matrix products, arithmetic and copies ran while one was open for 33% -> 21% of each run, Pallas kernels for 0% -> 26%
where the time goes in v1:
time: 1000 us; the launch traced here: 990 us
  waiting for transfers between devices  355 us (36%)
  Pallas kernels  296 us (30%)
  matrix products  127 us (13%)
  local copies, waits for them, and re-layouts  126 us (13%)
  other arithmetic  63.7 us (6%)
  between operations  17.2 us (2%)
    all_gather x1, waiting for transfers between devices, local(): lax.all_gather(w_in, 'z', axis=0, tiled=True)  144 us
    pallas_call x1, Pallas kernels, grad_sum(): pl.pallas_call(grad_sum_kernel, out_shape=jax.ShapeDtypeStruct((16, slots...  115 us
    reduce_scatter x1, waiting for transfers between devices, local(): lax.psum_scatter(grad_expert_out.astype(low), SEQ, scatter_dimension=1, t...  82.1 us
    unnamed x8, waiting for transfers between devices  74.4 us
    pallas_call x2, Pallas kernels, carried_states(): pl.pallas_call(scan_backward_kernel if reverse else scan_forward_kernel,...  73.7 us
    pallas_call x2, Pallas kernels, z_gather(): pl.pallas_call(functools.partial(z_gather_kernel, count), out_shape=tuple...  70.3 us
    all_gather x1, waiting for transfers between devices, side_by_side(): lax.all_gather(both, axis, axis=dim, tiled=True)  55 us
    pallas_call x1, Pallas kernels, z_sum(): pl.pallas_call(z_sum_kernel, out_shape=(total, total, jax.ShapeDtypeStruc...  37 us
  transfers between devices with their start and end apart: 9, of which 4 were waited for; matrix products, arithmetic and copies ran while one was open for 21% of the time, Pallas kernels for 26%

profile of v1, /device:TPU:0, one launch (start us, length us, event | category | flops | bytes accessed | tf_op | source)
XLA Modules:
  0.0 989.6 jit_solution(12187008998498518187)
XLA Ops:
  21.3 35.1 %gather_upstream.1 = bf16[4,128,1536]{2,1,0:T(8,128)(2,1)S(1)} custom-call(bf16[128,1536]{1,0:T(8,128)(2,1)S(1)} %bitcast_select_fusion.refs_0_), custom_call_target="tpu_custom_call" | custom-call | tf_op jit(solution)/shard_map/gather_upstream/pallas_call | solution.py:515
  59.2 144.0 %all-gather.5.cloned.1.call-done = bf16[1536,6448]{0,1:T(8,128)(2,1)} async-done(((bf16[384,6448]{0,1:T(8,128)(2,1)}), bf16[1536,6448]{0,1:T(8,128)(2,1)}) %all-gather.5.cloned.1.call-update) | async-done | bytes 19808272 | tf_op jit(solution)/shard_map/all_gather | solution.py:628
  203.2 10.7 %fusion.103 = f32[128,6448]{1,0:T(8,128)S(1)} fusion(bf16[1536,6448]{0,1:T(8,128)(2,1)} %all-gather.5.cloned.1.call-done, bf16[1,128,1536]{2,1,0:T(8,128)(2,1)S(1)} %copy-done.24, f32[1536]{0:T(1024)S(1)} %copy-done.72, f32[128]{0:T(128)S(1)} %fusion.130), kind=kOutput, calls=%fused_computation.174 | convolution fusion | flops 2536243200 | bytes 23509504 | tf_op jit(solution)/shard_map/dot_general | solution.py:138
  236.6 5.9 fusion.64
  251.1 38.7 %scan_forward.1 = (bf16[48,2,32,128]{3,2,1,0:T(8,128)(2,1)S(1)}, f32[32,8,128]{2,1,0:T(8,128)S(1)}) custom-call(bf16[48,2,32,128]{3,2,1,0:T(8,128)(2,1)S(1)} %bitcast.185, f32[8,128]{1,0:T(8,128)S(1)} %broadcast_in_dim.55.totals_ref), custom_call_target="tpu_custom_call" | custom-call | tf_op jit(solution)/shard_map/scan_forward/pallas_call | solution.py:475
  291.6 7.6 fusion.46
  306.8 6.6 multiply_reduce_fusion.17
  314.6 55.0 %all-gather.9.cloned.1.call-done = bf16[1536,2056]{1,0:T(8,128)(2,1)} async-done(((bf16[384,2056]{1,0:T(8,128)(2,1)}), bf16[1536,2056]{1,0:T(8,128)(2,1)}) %all-gather.9.cloned.1.call-update) | async-done | bytes 6316048 | tf_op jit(solution)/shard_map/all_gather | solution.py:583
  377.3 35.2 %gather_rows.1 = (bf16[4,128,1536]{2,1,0:T(8,128)(2,1)S(1)}, f32[4,8,128]{2,1,0:T(8,128)S(1)}) custom-call(bf16[128,1536]{1,0:T(8,128)(2,1)S(1)} %multiply_convert_fusion.9.refs_0_, f32[8,128]{1,0:T(8,128)S(1)} %bitcast.189), custom_call_target="tpu_custom_call" | custom-call | tf_op jit(solution)/shard_map/gather_rows/pallas_call | solution.py:515
  412.6 6.2 convolution_bitcast_fusion.1
  428.2 37.0 %z_sum.1 = (f32[128,1536]{1,0:T(8,128)S(1)}, f32[128,1536]{1,0:T(8,128)S(1)}, f32[4,8,128]{2,1,0:T(8,128)S(1)}) custom-call(bf16[4,128,1536]{2,1,0:T(8,128)(2,1)S(1)} %bitcast.188, bf16[4,128,1536]{2,1,0:T(8,128)(2,1)S(1)} %bitcast.187, f32[4,8,128]{2,1,0:T(8,128)S(1)} %pad.90.picks_ref), custom_call_target="tpu_custom_call" | custom-call | tf_op jit(solution)/shard_map/z_sum/pallas_call | solution.py:562
  466.4 6.2 fusion.4
  477.4 5.6 fusion.29
  486.5 6.9 fusion.152
  506.6 9.8 fusion.97
  521.2 35.1 %scan_backward.1 = bf16[48,2,32,128]{3,2,1,0:T(8,128)(2,1)S(1)} custom-call(bf16[48,2,32,128]{3,2,1,0:T(8,128)(2,1)S(1)} %bitcast.186, f32[32,8,128]{2,1,0:T(8,128)S(1)} %copy-done.7), custom_call_target="tpu_custom_call" | custom-call | tf_op jit(solution)/shard_map/scan_backward/pallas_call | solution.py:475
  580.1 6.1 multiply_reduce_fusion.6
  621.0 11.4 %fusion.83 = (f32[1536]{0:T(1024)}, f32[128]{0:T(128)}, f32[128,1536]{1,0:T(8,128)}) fusion(bf16[1,128,1536]{2,1,0:T(8,128)(2,1)S(1)} %copy-done.25, f32[128]{0:T(128)} %copy-done.87, f32[1536]{0:T(1024)} %param.24, bf16[1536,6448]{0,1:T(8,128)(2,1)} %all-gather.5.cloned.1.call-done, bf16[128,48]{1,0:T(8,128)(2,1)S(1)} %copy-done.64, ...), kind=kOutput, calls=%fused_computation.139 | convolution fusion | flops 2541783552 | bytes 22651904 | tf_op jit(solution)/shard_map/tk,dk->td/dot_general | solution.py:760
  635.6 7.1 convert_bitcast_fusion
  642.7 16.4 %copy.241 = bf16[2,1536,1024]{2,0,1:T(2,128)(2,1)} copy(bf16[2,1536,1024]{1,2,0:T(8,128)(2,1)} %convert_bitcast_fusion) | data formatting | bytes 12582912 | tf_op jit(solution)/shard_map/convert_element_type | solution.py:710
  672.5 5.8 fusion.8
  694.5 114.6 %grad_sum.1 = f32[16,13824]{1,0:T(8,128)} custom-call(bf16[6,1536,128]{2,1,0:T(8,128)(2,1)} %copy-done.71, bf16[128,13824]{1,0:T(8,128)(2,1)} %concatenate.34.b_ref), custom_call_target="tpu_custom_call" | custom-call | flops 5435817984 | bytes 8388608 | tf_op jit(solution)/shard_map/grad_sum/pallas_call | solution.py:347
  824.5 72.4 %all-reduce.33.cloned.1.call-done = bf16[2,1536,1024]{2,0,1:T(2,128)(2,1)} async-done(((bf16[2,1536,1024]{2,0,1:T(2,128)(2,1)}), bf16[2,1536,1024]{2,0,1:T(2,128)(2,1)}) %all-reduce.33.cloned.1.call-update) | async-done | bytes 6291472
  898.8 82.1 %reduce-scatter.2.cloned.1.call-done = bf16[2,16,1536]{2,1,0:T(8,128)(2,1)} async-done(((bf16[2,512,1536]{2,1,0:T(8,128)(2,1)}), bf16[2,16,1536]{2,1,0:T(8,128)(2,1)}) %reduce-scatter.2.cloned.1.call-update) | async-done | bytes 98320 | tf_op jit(solution)/shard_map/reduce_scatter | solution.py:712
  (406 shorter events, 211.0 us)
Async XLA Ops:
  7.2 411.6 %copy-start = (bf16[2,512,1536]{2,1,0:T(8,128)(2,1)S(1)}, bf16[2,512,1536]{2,1,0:T(8,128)(2,1)}, u32[]{:S(2)}) copy-start(bf16[2,512,1536]{2,1,0:T(8,128)(2,1)} %param.38) | copy-start | bytes 9437188
  7.2 196.0 %all-gather.5.cloned.1.call-start = ((), (), s32[]{:S(2)}) async-start(), calls=%async_computation.1 | async-start | bytes 24760320 | tf_op jit(solution)/shard_map/all_gather | solution.py:628
  7.9 298.8 %all-gather.7.cloned.1.call-start = ((), (), s32[]{:S(2)}) async-start(), calls=%async_computation.2 | async-start | bytes 11796480 | tf_op jit(solution)/shard_map/all_gather | solution.py:629
  8.7 360.8 %all-gather.9.cloned.1.call-start = ((), (), s32[]{:S(2)}) async-start(), calls=%async_computation.3 | async-start | bytes 8355840 | tf_op jit(solution)/shard_map/all_gather | solution.py:583
  12.3 460.3 %all-gather.11.cloned.1.call-start = ((), (), s32[]{:S(2)}) async-start(), calls=%async_computation.4 | async-start | bytes 3932160 | tf_op jit(solution)/shard_map/all_gather | solution.py:631
  12.9 804.2 %all-reduce.31.cloned.1.call-start = ((), (), s32[]{:S(2)}) async-start(), calls=%async_computation.5 | async-start | bytes 188416 | tf_op jit(solution)/shard_map/psum | solution.py:813
  14.3 42.1 %copy-start.94 = (f32[128]{0:T(128)}, f32[128]{0:T(128)S(1)}, u32[]{:S(2)}) copy-start(f32[128]{0:T(128)S(1)} %fusion.87) | copy-start | bytes 1540
  14.3 188.9 %copy-start.87 = (f32[128]{0:T(128)}, f32[128]{0:T(128)S(1)}, u32[]{:S(2)}) copy-start(f32[128]{0:T(128)S(1)} %fusion.130) | copy-start | bytes 1540
  57.2 146.0 %copy-start.72 = (f32[1536]{0:T(1024)S(1)}, f32[1536]{0:T(1024)}, u32[]{:S(2)}) copy-start(f32[1536]{0:T(1024)} %param.24) | copy-start | bytes 18436
  218.7 18.0 %collective-permute-start = (f32[3,3328]{1,0:T(4,128)}, f32[3,3328]{1,0:T(4,128)}, u32[]{:S(2)}, u32[]{:S(2)}) collective-permute-start(f32[3,3328]{1,0:T(4,128)} %slice.194), channel_id=1, source_target_pairs={{0,4},{4,8},{8,12},{12,16},{16,20},{20,24},{24,28},{28,32},{32,36}... | collective-permute-start | bytes 119816 | tf_op jit(solution)/shard_map/ppermute | solution.py:578
  251.0 40.5 %copy-start.16 = (f32[128,3072]{0,1:T(8,128)S(1)}, f32[128,3072]{0,1:T(8,128)}, u32[]{:S(2)}) copy-start(f32[128,3072]{0,1:T(8,128)} %copy.201) | copy-start | bytes 4718596
  251.0 40.5 %copy-start.56 = (f32[128,48]{0,1:T(8,128)S(1)}, f32[128,48]{0,1:T(8,128)}, u32[]{:S(2)}) copy-start(f32[128,48]{0,1:T(8,128)} %copy.206) | copy-start | bytes 73732
  251.0 40.5 %copy-start.69 = (f32[128,128]{1,0:T(8,128)S(1)}, f32[128,128]{1,0:T(8,128)}, u32[]{:S(2)}) copy-start(f32[128,128]{1,0:T(8,128)} %fusion.117) | copy-start | bytes 196612
  251.0 40.5 %copy-start.74 = (f32[128,48]{0,1:T(8,128)S(1)}, f32[128,48]{0,1:T(8,128)}, u32[]{:S(2)}) copy-start(f32[128,48]{0,1:T(8,128)} %copy.203) | copy-start | bytes 73732
  251.0 40.5 %copy-start.76 = (f32[128,48]{0,1:T(8,128)S(1)}, f32[128,48]{0,1:T(8,128)}, u32[]{:S(2)}) copy-start(f32[128,48]{0,1:T(8,128)} %copy.205) | copy-start | bytes 73732
  251.1 40.5 %copy-start.78 = (pred[128,128]{1,0:T(8,128)(4,1)S(1)}, pred[128,128]{1,0:T(8,128)(4,1)}, u32[]{:S(2)}) copy-start(pred[128,128]{1,0:T(8,128)(4,1)} %iota_compare_fusion) | copy-start | bytes 49156
  251.1 40.5 %copy-start.100 = (f32[48]{0:T(128)S(1)}, f32[48]{0:T(128)}, u32[]{:S(2)}) copy-start(f32[48]{0:T(128)} %param.30) | copy-start | bytes 580
  428.2 37.2 %copy-start.55 = (f32[128,8]{1,0:T(8,128)S(1)}, f32[128,8]{1,0:T(8,128)}, u32[]{:S(2)}) copy-start(f32[128,8]{1,0:T(8,128)} %copy.217) | copy-start | bytes 12292
  516.5 55.2 %copy-start.54 = (f32[128,128]{1,0:T(8,128)}, f32[128,128]{1,0:T(8,128)S(1)}, u32[]{:S(2)}) copy-start(f32[128,128]{1,0:T(8,128)S(1)} %get-tuple-element.131) | copy-start | bytes 196612
  521.2 35.1 %copy-start.47 = (f32[128,48]{0,1:T(8,128)S(1)}, f32[128,48]{0,1:T(8,128)}, u32[]{:S(2)}) copy-start(f32[128,48]{0,1:T(8,128)} %copy.207) | copy-start | bytes 73732
  589.2 30.1 %collective-permute-start.1 = (bf16[3,3328]{1,0:T(4,128)(2,1)}, bf16[3,3328]{1,0:T(4,128)(2,1)}, u32[]{:S(2)}, u32[]{:S(2)}) collective-permute-start(bf16[3,3328]{1,0:T(4,128)(2,1)} %slice.336), channel_id=1, source_target_pairs={{4,0},{8,4},{12,8},{16,12},{20,16},{24,20},{28,24},{32,28},{36,32}... | collective-permute-start | bytes 59912 | tf_op jit(solution)/shard_map/ppermute | solution.py:578
  635.5 261.4 %all-reduce.33.cloned.1.call-start = ((), (), s32[]{:S(2)}) async-start(), calls=%async_computation.7 | async-start | bytes 12582912
  659.1 321.9 %reduce-scatter.2.cloned.1.call-start = ((), (), s32[]{:S(2)}) async-start(), calls=%async_computation.6 | async-start | bytes 3244032 | tf_op jit(solution)/shard_map/reduce_scatter | solution.py:712
  809.1 173.4 %copy-start.1 = (bf16[2,512,1536]{2,1,0:T(8,128)(2,1)S(1)}, bf16[2,512,1536]{2,1,0:T(8,128)(2,1)}, u32[]{:S(2)}) copy-start(bf16[2,512,1536]{2,1,0:T(8,128)(2,1)} %param.38) | copy-start | bytes 9437188
  (93 other events, 411.6 us)
Sparse Core Ops, SparseCore 0:
  9.7 193.4 all-gather.4
  204.8 92.7 all-gather.6
  299.3 70.1 all-gather.8
  371.0 53.0 all-gather.10
  635.6 140.8 all-reduce.30
  780.2 116.6 all-reduce.32
  901.0 79.9 reduce-scatter.1

commit v2 on v1

v2 whole, which is shorter than its diff:
```python
import functools

import jax
import jax.numpy as jnp
from jax import lax
from jax.experimental import pallas as pl
from jax.experimental.pallas import tpu as pltpu
from jax.sharding import Mesh
from jax.sharding import PartitionSpec as P

SEQ = ("x", "y", "c")
ALL = ("x", "y", "c", "z")
NORM_EPS = 1e-05
HEADS = 48
INNER = 3072
CONV = 3328


def scaled_rows(values, gain_vector):
    return values * lax.rsqrt(jnp.mean(values * values, -1, keepdims=True) + NORM_EPS) * gain_vector


def glu_back(acts_pair, hidden_back):
    half_width = acts_pair.shape[-1] // 2
    gate_part = acts_pair[..., :half_width]
    up_part = acts_pair[..., half_width:]
    sigmoid_gate = jax.nn.sigmoid(gate_part)
    gate_grad = hidden_back * up_part * sigmoid_gate * (1.0 + gate_part * (1.0 - sigmoid_gate))
    up_grad = hidden_back * gate_part * sigmoid_gate
    return jnp.concatenate([gate_grad, up_grad], -1).astype(jnp.bfloat16)


MESH_ID = pl.DeviceIdType.MESH
RS_ORDERS = (("x", "y", "z"), ("y", "z", "x"), ("z", "x", "y"))
RS_STEPS = 9
RS_COLS = 512


def ring(axis, offset):
    size = lax.axis_size(axis)
    return lax.rem(lax.axis_index(axis) + offset + size, size)


def greet(targets):
    barrier = pltpu.get_barrier_semaphore()
    for target in targets:
        pl.semaphore_signal(barrier, inc=1, device_id=target, device_id_type=MESH_ID)
    pl.semaphore_wait(barrier, len(targets))


def remote(src, dst, send_sem, recv_sem, target):
    return pltpu.make_async_remote_copy(
        src_ref=src,
        dst_ref=dst,
        send_sem=send_sem,
        recv_sem=recv_sem,
        device_id=target,
        device_id_type=MESH_ID,
    )


def dot32(left, right):
    return jnp.dot(left, right, preferred_element_type=jnp.float32)


def grad_sum_kernel(
    a_ref, b_ref, taps_ref, gain_ref, norm_ref, post_ref, heads_ref, router_ref, out_ref, small_ref,
    core_out, core_in, near, far, second_in, third_out, third_in, lines,
    core_ss, core_rs, near_ss, near_rs, far_ss, far_rs, second_ss, second_rs, third_ss, third_rs,
    pack, pack_in, pack_work, pack_others, pack_ss, pack_rs,
):
    me_core = lax.axis_index("c")
    other = 1 - me_core
    half = core_out.shape[2]
    block = half // 4
    edge = block // 2
    small = block // 4
    unit = out_ref.shape[0]
    kept = small // 4
    lines[...] = jnp.zeros_like(lines)
    greet(
        [{"c": other}]
        + [{axis: ring(axis, o)} for axis in ("x", "y", "z") for o in (1, 2, 3)]
    )

    taps_width, wide = taps_ref.shape[1], pack.shape[1] // 2
    pack[:, :taps_width] = taps_ref[...]
    pack[5:6, : gain_ref.shape[1]] = gain_ref[0:1]
    pack[6:7, : norm_ref.shape[1]] = norm_ref[...]
    pack[6:7, norm_ref.shape[1] : 2 * norm_ref.shape[1]] = post_ref[...]
    for i in range(3):
        pack[7:8, TILE * i : TILE * (i + 1)] = heads_ref[i : i + 1]
    pack[:, taps_width:] = router_ref[...]

    def pack_half(ref, which):
        return ref.at[:, pl.ds(pl.multiple_of(which * wide, 128), wide)]

    def pack_core(last):
        if last:
            return remote(pack_work.at[3], pack_half(small_ref, me_core), pack_ss.at[4, 0], pack_rs.at[4, 0], {"c": other})
        return remote(pack_half(pack, other), pack_in, pack_ss.at[0, 0], pack_rs.at[0, 0], {"c": other})

    def pack_copies(s):
        axis = ("x", "y", "z")[s - 1]
        return [
            remote(pack_work.at[s - 1], pack_others.at[s - 1, o - 1], pack_ss.at[s, o], pack_rs.at[s, o], {axis: ring(axis, o)})
            for o in (1, 2, 3)
        ]

    def pack_step(s):
        if s == 0:
            pack_core(False).start()
        if s == 1:
            pack_core(False).wait_recv()
            pack_work[0] = pack[:, pl.ds(pl.multiple_of(me_core * wide, 128), wide)] + pack_in[...]
        if s in (2, 3, 4):
            for copy in pack_copies(s - 1):
                copy.wait_recv()
            pack_work[s - 1] = pack_work[s - 2] + (
                pack_others[s - 2, 0] + pack_others[s - 2, 1] + pack_others[s - 2, 2]
            )
        if s in (1, 2, 3):
            for copy in pack_copies(s):
                copy.start()
        if s == 4:
            pack_core(True).start()
            small_ref[:, pl.ds(pl.multiple_of(me_core * wide, 128), wide)] = pack_work[3]
        if s == 5:
            pack_core(True).wait_recv()
            pack_core(True).wait_send()
            pack_core(False).wait_send()
            for n in (1, 2, 3):
                for copy in pack_copies(n):
                    copy.wait_send()

    def left_of(part, k):
        if part == 0:
            return 0
        if part == 1:
            return 1 + k // 4
        return 4 + k // 3

    def core_copy(part, k):
        slot = part * RS_STEPS + k
        return remote(
            core_out.at[lax.rem(k, 2), part], core_in.at[slot],
            core_ss.at[slot], core_rs.at[slot], {"c": other},
        )

    def near_copies(part, k):
        slot = part * RS_STEPS + k
        axis = RS_ORDERS[part][0]
        after, before, across = ring(axis, 1), ring(axis, -1), ring(axis, 2)
        plan = ((before, 0, before), (after, edge, after), (across, 0, after), (across, edge, before))
        return [
            remote(
                core_in.at[slot, pl.ds(which * block + offset, edge)], near.at[slot, n],
                near_ss.at[slot, n], near_rs.at[slot, n], {axis: target},
            )
            for n, (which, offset, target) in enumerate(plan)
        ]

    def far_copies(part, k):
        slot = part * RS_STEPS + k
        axis = RS_ORDERS[part][0]
        return [
            remote(
                near.at[slot, 2 + n], far.at[slot, n],
                far_ss.at[slot, n], far_rs.at[slot, n], {axis: ring(axis, o)},
            )
            for n, o in enumerate((1, -1))
        ]

    def second_copies(part, k):
        slot = part * RS_STEPS + k
        axis = RS_ORDERS[part][1]
        copies = []
        for o in (1, 2, 3):
            target = ring(axis, o)
            copies.append(
                remote(
                    near.at[slot, target // 2, pl.ds(lax.rem(target, 2) * small, small)],
                    second_in.at[slot, o - 1],
                    second_ss.at[slot, o - 1], second_rs.at[slot, o - 1], {axis: target},
                )
            )
        return copies

    def third_copies(part, k):
        slot = part * RS_STEPS + k
        axis = RS_ORDERS[part][2]
        return [
            remote(
                third_out.at[slot, ring(axis, o)], third_in.at[slot, o - 1],
                third_ss.at[slot, o - 1], third_rs.at[slot, o - 1], {axis: ring(axis, o)},
            )
            for o in (1, 2, 3)
        ]

    def stage_product(part, k):
        slot = part * RS_STEPS + k

        @pl.when(k >= 2)
        def _():
            core_copy(part, k - 2).wait_send()

        left = a_ref[left_of(part, k), pl.ds(pl.multiple_of(other * half, half), half), :]
        for col in range(0, RS_COLS, 256):
            core_out[lax.rem(k, 2), part, :, col : col + 256] = dot32(
                left, b_ref[:, pl.ds(pl.multiple_of(slot * RS_COLS + col, 256), 256)]
            ).astype(jnp.bfloat16)
        core_copy(part, k).start()

    def stage_near(part, k):
        slot = part * RS_STEPS + k
        core_copy(part, k).wait_recv()

        left = a_ref[left_of(part, k), pl.ds(pl.multiple_of(me_core * half, half), half), :]
        for col in range(0, RS_COLS, 256):
            mine = dot32(left, b_ref[:, pl.ds(pl.multiple_of(slot * RS_COLS + col, 256), 256)])
            theirs = core_in[slot, :, col : col + 256].astype(jnp.float32)
            core_in[slot, :, col : col + 256] = (mine + theirs).astype(jnp.bfloat16)
        for copy in near_copies(part, k):
            copy.start()

    def load(ref, *where):
        return ref[where].astype(jnp.float32)

    def stage_far(part, k):
        slot = part * RS_STEPS + k
        axis = RS_ORDERS[part][0]
        copies = near_copies(part, k)
        for n, (which, offset) in enumerate(((ring(axis, 1), 0), (ring(axis, -1), edge))):
            copies[2 + n].wait_recv()
            rows = pl.ds(pl.multiple_of(which * block + offset, edge), edge)
            near[slot, 2 + n] = (load(near, slot, 2 + n) + load(core_in, slot, rows)).astype(jnp.bfloat16)
        for copy in far_copies(part, k):
            copy.start()

    def stage_second(part, k):
        slot = part * RS_STEPS + k
        me = lax.axis_index(RS_ORDERS[part][0])
        copies, far_in = near_copies(part, k), far_copies(part, k)
        for n in range(2):
            copies[n].wait_recv()
            far_in[n].wait_recv()
            rows = pl.ds(pl.multiple_of(me * block + n * edge, edge), edge)
            near[slot, n] = (
                load(near, slot, n) + load(far, slot, n) + load(core_in, slot, rows)
            ).astype(jnp.bfloat16)
        for copy in second_copies(part, k):
            copy.start()

    def stage_third(part, k):
        slot = part * RS_STEPS + k
        me = lax.axis_index(RS_ORDERS[part][1])
        for copy in second_copies(part, k):
            copy.wait_recv()
        rows = pl.ds(pl.multiple_of(lax.rem(me, 2) * small, small), small)
        lines[part, :small] = load(near, slot, me // 2, rows) + (
            load(second_in, slot, 0) + load(second_in, slot, 1) + load(second_in, slot, 2)
        )
        for j in range(4):
            third_out[slot, j] = lines[part, kept * j : kept * j + unit].astype(jnp.bfloat16)
        for copy in third_copies(part, k):
            copy.start()

    def stage_last(part, k):
        slot = part * RS_STEPS + k
        for copy in third_copies(part, k):
            copy.wait_recv()
        me = lax.axis_index(RS_ORDERS[part][2])
        out_ref[:, pl.ds(pl.multiple_of(slot * RS_COLS, RS_COLS), RS_COLS)] = load(
            third_out, slot, me
        ) + (load(third_in, slot, 0) + load(third_in, slot, 1) + load(third_in, slot, 2))

    stages = (stage_product, stage_near, stage_far, stage_second, stage_third, stage_last)

    def step(t, carry):
        for s in range(6):
            @pl.when(t == s)
            def _():
                pack_step(s)

        for lag, stage in enumerate(stages):
            k = t - lag

            @pl.when((k >= 0) & (k < RS_STEPS))
            def _():
                for part in range(3):
                    stage(part, k)

        return carry

    lax.fori_loop(0, RS_STEPS + len(stages) - 1, step, 0)

    def finish(k, carry):
        for part in range(3):
            @pl.when(k >= RS_STEPS - 2)
            def _():
                core_copy(part, k).wait_send()

            for copies in (near_copies, far_copies, second_copies, third_copies):
                for copy in copies(part, k):
                    copy.wait_send()
        return carry

    lax.fori_loop(0, RS_STEPS, finish, 0)


def grad_sum(lefts, rights, taps, gain, norm, post, heads, router):
    cols, slots, depth = RS_COLS, rights.shape[1] // RS_COLS, rights.shape[0]
    rows = lefts.shape[1]
    half = rows // 2
    block = half // 4
    low = jnp.bfloat16
    wide = taps.shape[1] + router.shape[1]
    space = pl.BlockSpec(memory_space=pltpu.VMEM)
    sems = lambda *shape: pltpu.SemaphoreType.DMA(shape)
    return pl.pallas_call(
        grad_sum_kernel,
        out_shape=(
            jax.ShapeDtypeStruct((16, slots * cols), jnp.float32),
            jax.ShapeDtypeStruct((8, wide), jnp.float32),
        ),
        in_specs=[space] * 8,
        out_specs=(space, space),
        scratch_shapes=[
            pltpu.VMEM((2, 3, half, cols), low),
            pltpu.VMEM((slots, half, cols), low),
            pltpu.VMEM((slots, 4, block // 2, cols), low),
            pltpu.VMEM((slots, 2, block // 2, cols), low),
            pltpu.VMEM((slots, 3, block // 4, cols), low),
            pltpu.VMEM((slots, 4, 16, cols), low),
            pltpu.VMEM((slots, 3, 16, cols), low),
            pltpu.VMEM((3, block // 4 + 8, cols), jnp.float32),
            sems(slots), sems(slots), sems(slots, 4), sems(slots, 4), sems(slots, 2), sems(slots, 2),
            sems(slots, 3), sems(slots, 3), sems(slots, 3), sems(slots, 3),
            pltpu.VMEM((8, wide), jnp.float32),
            pltpu.VMEM((8, wide // 2), jnp.float32),
            pltpu.VMEM((4, 8, wide // 2), jnp.float32),
            pltpu.VMEM((3, 3, 8, wide // 2), jnp.float32),
            sems(5, 4), sems(5, 4),
        ],
        compiler_params=pltpu.CompilerParams(
            collective_id=0, has_side_effects=True, vmem_limit_bytes=61 * 2**20
        ),
        cost_estimate=pl.CostEstimate(flops=2 * slots * rows * depth * cols, bytes_accessed=8 * 2**20, transcendentals=0),
        name="grad_sum",
    )(lefts, rights, taps, gain, norm, post, heads, router)


def plane_spot(position):
    return {"x": position // 8, "y": lax.rem(position // 2, 4), "c": lax.rem(position, 2)}


def state_exchange(
    reverse, state_ref, totals_ref, rows_ref, out_ref, decays_ref, all_rows, rows_sum, got, back, ss, rs, ts, tr, bs, br
):
    spots = 32
    me = lax.axis_index("x") * 8 + lax.axis_index("y") * 2 + lax.axis_index("c")
    heads = got.shape[1]
    barrier = pltpu.get_barrier_semaphore()

    def spot(o):
        return lax.rem(me + o, spots)

    def share(ref, position):
        return ref.at[pl.ds(heads * (position // 2), heads), lax.rem(position, 2)]

    def knock(o, carry):
        pl.semaphore_signal(barrier, inc=1, device_id=plane_spot(spot(o)), device_id_type=MESH_ID)
        return carry

    lax.fori_loop(1, spots, knock, 0)
    sides = (1, 3, 2)
    for o in sides:
        pl.semaphore_signal(barrier, inc=1, device_id={"z": ring("z", o)}, device_id_type=MESH_ID)
    pl.semaphore_wait(barrier, spots - 1 + len(sides))
    me_z = lax.axis_index("z")
    row_copies = []
    for o in sides:
        source = rows_ref.at[ring("z", o)] if reverse else rows_ref
        target = all_rows.at[o - 1] if reverse else all_rows.at[me_z]
        row_copies.append(remote(source, target, ts.at[o + 32], tr.at[o + 32], {"z": ring("z", o)}))

    def out_copy(o):
        target = spot(o)
        return remote(share(state_ref, target), got.at[me], ss.at[o], rs.at[o], plane_spot(target))

    def total_copy(o):
        return remote(totals_ref, decays_ref.at[me], ts.at[o], tr.at[o], plane_spot(spot(o)))

    def back_copy(o):
        target = spot(o)
        return remote(back.at[target], share(out_ref, me), bs.at[o], br.at[o], plane_spot(target))

    def send(o, carry):
        if not reverse:
            total_copy(o).start()
        out_copy(o).start()
        return carry

    lax.fori_loop(1, spots, send, 0)
    for copy in row_copies:
        copy.start()
    if not reverse:
        all_rows[me_z] = rows_ref[...]
    mine = pl.ds(heads * (me // 2), heads)
    got[me] = state_ref[mine, lax.rem(me, 2)]
    if not reverse:
        decays_ref[me] = totals_ref[...]

    def arrive(o, carry):
        if not reverse:
            total_copy(o).wait_recv()
        out_copy(o).wait_recv()
        return carry

    lax.fori_loop(1, spots, arrive, 0)
    source = totals_ref if reverse else decays_ref
    lanes = lax.broadcasted_iota(jnp.int32, (8, 128), 1) - heads * (me // 2)

    def advance(step, carried):
        p = spots - 1 - step if reverse else step
        logs = source[p]
        new = []
        for h in range(heads):
            back[p, h] = carried[h].astype(back.dtype)
            decay = jnp.exp(jnp.sum(jnp.where(lanes == h, logs, 0.0), 1, keepdims=True))[:1]
            new.append(carried[h] * decay + got[p, h].astype(jnp.float32))
        return tuple(new)

    zero = jnp.zeros(got.shape[2:], jnp.float32)
    lax.fori_loop(0, spots, advance, (zero,) * heads)

    def send_back(o, carry):
        back_copy(o).start()
        return carry

    lax.fori_loop(1, spots, send_back, 0)
    out_ref[mine, lax.rem(me, 2)] = back[me]

    def finish(o, carry):
        back_copy(o).wait_recv()
        back_copy(o).wait_send()
        out_copy(o).wait_send()
        if not reverse:
            total_copy(o).wait_send()
        return carry

    lax.fori_loop(1, spots, finish, 0)
    for copy in row_copies:
        copy.wait()
    if reverse:
        add_parts(rows_ref, me_z, all_rows, rows_sum)


def scan_forward_kernel(state_ref, totals_ref, rows_ref, out_ref, decays_ref, all_rows, *scratch):
    state_exchange(False, state_ref, totals_ref, rows_ref, out_ref, decays_ref, all_rows, None, *scratch)


def scan_backward_kernel(state_ref, decays_ref, parts_ref, out_ref, rows_sum, got_parts, *scratch):
    state_exchange(True, state_ref, decays_ref, parts_ref, out_ref, None, got_parts, rows_sum, *scratch)


def carried_states(state, logs, rows):
    reverse = rows.ndim == 3
    heads, size, width = state.shape
    share = (heads // 16, size // 2, width)
    state = state.astype(jnp.bfloat16).reshape(heads, 2, size // 2, width)
    sem = pltpu.SemaphoreType.DMA((32,))
    out_shape = jax.ShapeDtypeStruct(state.shape, jnp.bfloat16)
    space = pl.BlockSpec(memory_space=pltpu.VMEM)
    kept = jax.ShapeDtypeStruct((32, 8, 128), jnp.float32)
    args = (state, logs, rows)
    if reverse:
        outs = [out_shape, jax.ShapeDtypeStruct(rows.shape[1:], jnp.float32)]
        extra = [pltpu.VMEM((3, *rows.shape[1:]), rows.dtype)]
    else:
        outs = [out_shape, kept, jax.ShapeDtypeStruct((4, *rows.shape), rows.dtype)]
        extra = []
    result = pl.pallas_call(
        scan_backward_kernel if reverse else scan_forward_kernel,
        out_shape=tuple(outs),
        in_specs=[space] * len(args),
        out_specs=(space,) * len(outs),
        scratch_shapes=extra
        + [pltpu.VMEM((32, *share), jnp.bfloat16)] * 2
        + [sem] * 2
        + [pltpu.SemaphoreType.DMA((36,))] * 2
        + [sem] * 2,
        compiler_params=pltpu.CompilerParams(
            collective_id=2 if reverse else 1, has_side_effects=True, vmem_limit_bytes=32 * 2**20
        ),
        name="scan_backward" if reverse else "scan_forward",
    )(*args)
    return (result[0].reshape(heads, size, width), *result[1:])


def z_gather_kernel(count, *refs):
    ins, outs, (ss, rs) = refs[:count], refs[count : 2 * count], refs[2 * count :]
    me = lax.axis_index("z")
    greet([{"z": ring("z", o)} for o in (1, 2, 3)])
    copies = []
    for n in range(count):
        for o in (1, 3, 2):
            copies.append(
                remote(ins[n], outs[n].at[me], ss.at[n, o], rs.at[n, o], {"z": ring("z", o)})
            )
            copies[-1].start()
    for n in range(count):
        outs[n][me] = ins[n][...]
    for copy in copies:
        copy.wait()


def z_gather(arrays, cid, name):
    count = len(arrays)
    space = pl.BlockSpec(memory_space=pltpu.VMEM)
    sem = pltpu.SemaphoreType.DMA((count, 4))
    return pl.pallas_call(
        functools.partial(z_gather_kernel, count),
        out_shape=tuple(jax.ShapeDtypeStruct((4, *a.shape), a.dtype) for a in arrays),
        in_specs=[space] * count,
        out_specs=(space,) * count,
        scratch_shapes=[sem, sem],
        compiler_params=pltpu.CompilerParams(
            collective_id=cid, has_side_effects=True, vmem_limit_bytes=32 * 2**20
        ),
        name=name,
    )(*arrays)


EXPERT_ORDERS = (("x", "y"), ("y", "x"))
EXPERT_STEPS = 6
EXPERT_COLS = 256


def add_parts(ref, me, got, out):
    def rows_at(j, carry):
        rows = pl.ds(pl.multiple_of(j * 32, 32), 32)
        total = ref[me, rows].astype(jnp.float32)
        for o in range(3):
            total = total + got[o, rows].astype(jnp.float32)
        out[rows] = total
        return carry

    lax.fori_loop(0, out.shape[0] // 32, rows_at, 0)


def expert_sum_kernel(
    rows_ref, acts_ref, hidden_ref, grads_ref, back_ref, picks_ref,
    out_ref, back_sum, picks_all,
    core_out, core_in, near, far, second_in, got,
    core_ss, core_rs, near_ss, near_rs, far_ss, far_rs, second_ss, second_rs, zs, zr,
):
    me_core = lax.axis_index("c")
    me_z = lax.axis_index("z")
    other = 1 - me_core
    half = core_out.shape[2]
    block = half // 4
    edge = block // 2
    small = block // 4
    third = small // 3
    cols = EXPERT_COLS
    greet(
        [{"c": other}]
        + [{axis: ring(axis, o)} for axis in ("x", "y", "z") for o in (1, 2, 3)]
    )

    sums = []
    for n, ref in enumerate((back_ref,)):
        for o in (1, 3, 2):
            sums.append(
                remote(ref.at[ring("z", o)], got.at[n, o - 1], zs.at[n, o], zr.at[n, o], {"z": ring("z", o)})
            )
    for o in (1, 3, 2):
        sums.append(
            remote(picks_ref.at[ring("z", o)], picks_all.at[me_z], zs.at[2, o], zr.at[2, o], {"z": ring("z", o)})
        )
    for copy in sums:
        copy.start()
    picks_all[me_z] = picks_ref[me_z]

    def core_copy(part, k):
        slot = part * EXPERT_STEPS + k
        return remote(
            core_out.at[lax.rem(k, 2), part], core_in.at[slot],
            core_ss.at[slot], core_rs.at[slot], {"c": other},
        )

    def near_copies(part, k):
        slot = part * EXPERT_STEPS + k
        axis = EXPERT_ORDERS[part][0]
        after, before, across = ring(axis, 1), ring(axis, -1), ring(axis, 2)
        plan = ((before, 0, before), (after, edge, after), (across, 0, after), (across, edge, before))
        return [
            remote(
                core_in.at[slot, pl.ds(which * block + offset, edge)], near.at[slot, n],
                near_ss.at[slot, n], near_rs.at[slot, n], {axis: target},
            )
            for n, (which, offset, target) in enumerate(plan)
        ]

    def far_copies(part, k):
        slot = part * EXPERT_STEPS + k
        axis = EXPERT_ORDERS[part][0]
        return [
            remote(
                near.at[slot, 2 + n], far.at[slot, n],
                far_ss.at[slot, n], far_rs.at[slot, n], {axis: ring(axis, o)},
            )
            for n, o in enumerate((1, -1))
        ]

    def second_copies(part, k):
        slot = part * EXPERT_STEPS + k
        axis = EXPERT_ORDERS[part][1]
        copies = []
        for o in (1, 2, 3):
            target = ring(axis, o)
            copies.append(
                remote(
                    near.at[slot, target // 2, pl.ds(lax.rem(target, 2) * small, small)],
                    second_in.at[slot, o - 1],
                    second_ss.at[slot, o - 1], second_rs.at[slot, o - 1], {axis: target},
                )
            )
        return copies

    def load(ref, *where):
        return ref[where].astype(jnp.float32)

    def products(part, k, which_half, store):
        @pl.when(k < 4)
        def _():
            right = acts_ref[part, :, pl.ds(pl.multiple_of(k * cols, cols), cols)]

            at = pl.multiple_of(which_half * half, half)
            store(0, half, dot32(rows_ref[part, pl.ds(at, half), :], right))

        @pl.when(k >= 4)
        def _():
            at = pl.multiple_of(which_half * (half // 3), half // 3)
            left = hidden_ref[part, pl.ds(at, half // 3), :]
            for t in range(3):
                right = grads_ref[part, :, pl.ds(pl.multiple_of(t * 2 * cols + (k - 4) * cols, cols), cols)]
                product = dot32(left, right)
                for i in range(16):
                    store(i * small + t * third, third, product[i * third : (i + 1) * third])

    def stage_product(part, k):
        @pl.when(k >= 2)
        def _():
            core_copy(part, k - 2).wait_send()

        def store(at, size, value):
            core_out[lax.rem(k, 2), part, pl.ds(at, size), :] = value.astype(jnp.bfloat16)

        products(part, k, other, store)
        core_copy(part, k).start()

    def stage_near(part, k):
        slot = part * EXPERT_STEPS + k
        core_copy(part, k).wait_recv()

        def store(at, size, value):
            rows = pl.ds(at, size)
            core_in[slot, rows, :] = (value + load(core_in, slot, rows)).astype(jnp.bfloat16)

        products(part, k, me_core, store)
        for copy in near_copies(part, k):
            copy.start()

    def stage_far(part, k):
        slot = part * EXPERT_STEPS + k
        axis = EXPERT_ORDERS[part][0]
        copies = near_copies(part, k)
        for n, (which, offset) in enumerate(((ring(axis, 1), 0), (ring(axis, -1), edge))):
            copies[2 + n].wait_recv()
            rows = pl.ds(pl.multiple_of(which * block + offset, edge), edge)
            near[slot, 2 + n] = (load(near, slot, 2 + n) + load(core_in, slot, rows)).astype(jnp.bfloat16)
        for copy in far_copies(part, k):
            copy.start()

    def stage_second(part, k):
        slot = part * EXPERT_STEPS + k
        me = lax.axis_index(EXPERT_ORDERS[part][0])
        copies, far_in = near_copies(part, k), far_copies(part, k)
        for n in range(2):
            copies[n].wait_recv()
            far_in[n].wait_recv()
            rows = pl.ds(pl.multiple_of(me * block + n * edge, edge), edge)
            near[slot, n] = (
                load(near, slot, n) + load(far, slot, n) + load(core_in, slot, rows)
            ).astype(jnp.bfloat16)
        for copy in second_copies(part, k):
            copy.start()

    def stage_last(part, k):
        slot = part * EXPERT_STEPS + k
        me = lax.axis_index(EXPERT_ORDERS[part][1])
        for copy in second_copies(part, k):
            copy.wait_recv()
        rows = pl.ds(pl.multiple_of(lax.rem(me, 2) * small, small), small)
        out_ref[part, :, pl.ds(pl.multiple_of(k * cols, cols), cols)] = load(near, slot, me // 2, rows) + (
            load(second_in, slot, 0) + load(second_in, slot, 1) + load(second_in, slot, 2)
        )

    stages = (stage_product, stage_near, stage_far, stage_second, stage_last)

    def step(t, carry):
        for lag, stage in enumerate(stages):
            k = t - lag

            @pl.when((k >= 0) & (k < EXPERT_STEPS))
            def _():
                for part in range(2):
                    stage(part, k)

        return carry

    lax.fori_loop(0, EXPERT_STEPS + len(stages) - 1, step, 0)

    for copy in sums:
        copy.wait()
    add_parts(back_ref, me_z, got.at[0], back_sum)

    def finish(k, carry):
        for part in range(2):
            @pl.when(k >= EXPERT_STEPS - 2)
            def _():
                core_copy(part, k).wait_send()

            for copies in (near_copies, far_copies, second_copies):
                for copy in copies(part, k):
                    copy.wait_send()
        return carry

    lax.fori_loop(0, EXPERT_STEPS, finish, 0)


def expert_sum(rows, acts, hidden, grads, back, picks):
    slots, cols, half = 2 * EXPERT_STEPS, EXPERT_COLS, rows.shape[1] // 2
    block = half // 4
    low = jnp.bfloat16
    sems = lambda *shape: pltpu.SemaphoreType.DMA(shape)
    space = pl.BlockSpec(memory_space=pltpu.VMEM)
    total = jax.ShapeDtypeStruct(back.shape[1:], jnp.float32)
    return pl.pallas_call(
        expert_sum_kernel,
        out_shape=(
            jax.ShapeDtypeStruct((2, block // 4, EXPERT_STEPS * cols), jnp.float32),
            total,
            jax.ShapeDtypeStruct(picks.shape, picks.dtype),
        ),
        in_specs=[space] * 6,
        out_specs=(space,) * 3,
        scratch_shapes=[
            pltpu.VMEM((2, 2, half, cols), low),
            pltpu.VMEM((slots, half, cols), low),
            pltpu.VMEM((slots, 4, block // 2, cols), low),
            pltpu.VMEM((slots, 2, block // 2, cols), low),
            pltpu.VMEM((slots, 3, block // 4, cols), low),
            pltpu.VMEM((1, 3, *back.shape[1:]), low),
            sems(slots), sems(slots), sems(slots, 4), sems(slots, 4), sems(slots, 2), sems(slots, 2),
            sems(slots, 3), sems(slots, 3), sems(3, 4), sems(3, 4),
        ],
        compiler_params=pltpu.CompilerParams(
            collective_id=4, has_side_effects=True, vmem_limit_bytes=52 * 2**20
        ),
        name="expert_sum",
    )(rows, acts, hidden, grads, back, picks)


def gather_kernel(count, *refs):
    shards, plain_in = refs[:count], refs[count : count + 1]
    fulls, plain_out = refs[count + 1 : 2 * count + 1], refs[2 * count + 1 : 2 * count + 2]
    load_sem, own_sem, unit_ss, unit_rs, deep_ss, deep_rs, first_ss, first_rs, second_ss, second_rs, core_ss, core_rs, row_ss, row_rs, *staged = refs[2 * count + 2 :]
    x, y, c, z = (lax.axis_index(a) for a in ALL)
    first_at = (1 - c) * x + c * y
    second_at = c * x + (1 - c) * y

    def along_first(o):
        return {"x": lax.rem(x + (1 - c) * o, 4), "y": lax.rem(y + c * o, 4)}

    def along_second(o):
        return {"x": lax.rem(x + c * o, 4), "y": lax.rem(y + (1 - c) * o, 4)}

    greet(
        [{"c": 1 - c}]
        + [{axis: ring(axis, o)} for axis in ("x", "y", "z") for o in (1, 2, 3)]
    )

    by_rows = (0, 1)

    def sizes(n):
        if n == 0:
            total = fulls[0].shape[1]
            spread = total * 16 // 25
            return total // 2, spread // 2, spread // 32
        total = shards[n].shape[0]
        spread = total if total % 384 else total * 2 // 3
        if n in by_rows:
            return total // 2, spread // 2, spread // 32
        return total, spread, spread // 16

    def place(n, deep, offset):
        total, spread, unit = sizes(n)
        if n in by_rows:
            return (2 * spread + c * (total - spread) if deep else c * spread) + offset
        return (spread if deep else 0) + offset

    def window(n, shard, deep, offset, length):
        rows, width = shards[n].shape
        at = place(n, deep, offset)
        if n == 0:
            return fulls[0].at[shard, pl.ds(pl.multiple_of(at, 16), length)]
        rows = pl.ds(pl.multiple_of(at + shard * rows, 16), length)
        if n in by_rows:
            return fulls[n].at[rows]
        return fulls[n].at[rows, pl.ds(pl.multiple_of(c * (width // 2), 128), width // 2)]

    def own_window(n, deep, offset, length):
        width = shards[n].shape[1]
        rows = pl.ds(pl.multiple_of(place(n, deep, offset), 16), length)
        if n in by_rows:
            return shards[n].at[rows]
        return shards[n].at[rows, pl.ds(pl.multiple_of(c * (width // 2), 128), width // 2)]

    def own_rows(n):
        return fulls[0].shape[1] if n == 0 else shards[n].shape[0]

    def own_load(n):
        return pltpu.make_async_copy(shards[n].at[pl.ds(0, own_rows(n))], staged[n], load_sem.at[n])

    def own_copy(n):
        if n == 0:
            return pltpu.make_async_copy(staged[0], fulls[0].at[z], own_sem.at[0])
        total = shards[n].shape[0]
        return pltpu.make_async_copy(
            staged[n], fulls[n].at[pl.ds(pl.multiple_of(z * total, 16), total)], own_sem.at[n]
        )

    def came_from(o):
        return lax.rem(z - o + 4, 4)

    def unit_copy(n, o):
        unit = sizes(n)[2]
        at = (second_at * 4 + first_at) * unit
        return remote(
            own_window(n, False, at, unit), window(n, z, False, at, unit), unit_ss.at[n, o], unit_rs.at[n, o], {"z": ring("z", o)}
        )

    def deep_copy(n, o):
        total, spread, unit = sizes(n)
        return remote(
            own_window(n, True, 0, total - spread), window(n, z, True, 0, total - spread),
            deep_ss.at[n, o], deep_rs.at[n, o], {"z": ring("z", o)},
        )

    def deep_forward(n, o):
        total, spread, unit = sizes(n)
        edge = (total - spread) // 2
        block = window(n, came_from(o), True, 0 if o == 1 else edge, edge)
        return remote(block, block, deep_ss.at[n, 3 + o], deep_rs.at[n, 3 + o], {"z": ring("z", o)})

    def first_copy(n, o, step):
        unit = sizes(n)[2]
        block = window(n, came_from(o), False, (second_at * 4 + first_at) * unit, unit)
        return remote(block, block, first_ss.at[n, o, step], first_rs.at[n, o, step], along_first(step))

    def second_copy(n, o, step):
        unit = sizes(n)[2]
        block = window(n, came_from(o), False, second_at * 4 * unit, 4 * unit)
        return remote(block, block, second_ss.at[n, o, step], second_rs.at[n, o, step], along_second(step))

    def second_forward(n, o, step):
        unit = sizes(n)[2]
        source = lax.rem(second_at + 4 - step, 4)
        at = source * 4 * unit + (0 if step == 1 else 2 * unit)
        block = window(n, came_from(o), False, at, 2 * unit)
        return remote(block, block, second_ss.at[n, o, 4 + step], second_rs.at[n, o, 4 + step], along_second(step))

    def core_copies(n, o):
        total, spread, unit = sizes(n)
        shard = came_from(o)
        blocks = [window(n, shard, False, 0, spread)]
        if spread < total:
            blocks.append(window(n, shard, True, 0, total - spread))
        return [
            remote(block, block, core_ss.at[n, o, i], core_rs.at[n, o, i], {"c": 1 - c})
            for i, block in enumerate(blocks)
        ]

    def plain_copy(i, o):
        return remote(plain_in[i], plain_out[i].at[z], row_ss.at[i, o], row_rs.at[i, o], {"z": ring("z", o)})

    arrays = range(count)
    deep = [n for n in arrays if sizes(n)[0] > sizes(n)[1]]
    sides, offsets = (1, 3), (1, 3, 2)
    for n in arrays:
        for o in offsets:
            unit_copy(n, o).start()
    for n in deep:
        for o in sides:
            deep_copy(n, o).start()
    for i in range(1):
        for o in offsets:
            plain_copy(i, o).start()
    for n in arrays:
        own_load(n).start()
    own_plain = [pltpu.make_async_copy(plain_in[i], plain_out[i].at[z], own_sem.at[count + i]) for i in range(1)]
    for copy in own_plain:
        copy.start()
    for n in arrays:
        for o in offsets:
            unit_copy(n, o).wait_recv()
            for step in offsets:
                first_copy(n, o, step).start()
    for n in arrays:
        own_load(n).wait()
        own_copy(n).start()
    for n in arrays:
        for o in offsets:
            for step in offsets:
                first_copy(n, o, step).wait_recv()
            for step in sides:
                second_copy(n, o, step).start()
    for n in arrays:
        if n in deep:
            for o in sides:
                deep_copy(n, o).wait_recv()
                deep_forward(n, o).start()
                core_copies(n, o)[1].start()
        for o in offsets:
            for step in sides:
                second_copy(n, o, step).wait_recv()
                second_forward(n, o, step).start()
    for n in arrays:
        for o in offsets:
            for step in sides:
                second_forward(n, o, step).wait_recv()
            core_copies(n, o)[0].start()
        if n in deep:
            for o in sides:
                deep_forward(n, o).wait_recv()
            core_copies(n, 2)[1].start()
    for i in range(1):
        for o in offsets:
            plain_copy(i, o).wait()
        own_plain[i].wait()
    for n in arrays:
        own_copy(n).wait()
        for o in offsets:
            for copy in core_copies(n, o):
                copy.wait()
            unit_copy(n, o).wait_send()
            for step in offsets:
                first_copy(n, o, step).wait_send()
            for step in sides:
                second_copy(n, o, step).wait_send()
                second_forward(n, o, step).wait_send()
        if n in deep:
            for o in sides:
                deep_copy(n, o).wait_send()
                deep_forward(n, o).wait_send()


def gather_weights(shards, plain, main_rows):
    count = len(shards)
    space = pl.BlockSpec(memory_space=pl.ANY)
    sem = lambda *shape: pltpu.SemaphoreType.DMA(shape)
    fulls = [(4, main_rows, shards[0].shape[1])] + [(4 * s.shape[0], s.shape[1]) for s in shards[1:]]
    return pl.pallas_call(
        functools.partial(gather_kernel, count),
        out_shape=tuple(jax.ShapeDtypeStruct(f, jnp.bfloat16) for f in fulls)
        + tuple(jax.ShapeDtypeStruct((4, *p.shape), p.dtype) for p in plain),
        in_specs=[space] * (count + 1),
        out_specs=(space,) * (count + 1),
        scratch_shapes=[
            sem(count),
            sem(count + 1),
            sem(count, 4), sem(count, 4), sem(count, 8), sem(count, 8),
            sem(count, 4, 4), sem(count, 4, 4), sem(count, 4, 8), sem(count, 4, 8),
            sem(count, 4, 2), sem(count, 4, 2), sem(1, 4), sem(1, 4),
            pltpu.VMEM((main_rows, shards[0].shape[1]), jnp.bfloat16),
        ]
        + [pltpu.VMEM(s.shape, s.dtype) for s in shards[1:]],
        compiler_params=pltpu.CompilerParams(
            collective_id=6, has_side_effects=True, vmem_limit_bytes=60 * 2**20
        ),
        name="gather_weights",
    )(*shards, *plain)


TILE = 128
HIGH = lax.Precision.HIGHEST


def tile_at(j):
    return pl.ds(pl.multiple_of(j * TILE, TILE), TILE)


def dot_nt(left, right):
    return lax.dot_general(left, right, (((1,), (1,)), ((), ())), preferred_element_type=jnp.float32)


def short(values):
    return values.astype(jnp.bfloat16)


def lane_ids():
    return lax.broadcasted_iota(jnp.int32, (TILE, TILE), 1)


def row_ids():
    return lax.broadcasted_iota(jnp.int32, (TILE, TILE), 0)


def head_steps(tail_ref, heads_ref):
    raw = tail_ref[...] + heads_ref[1:2]
    used = lane_ids() < HEADS
    small = jnp.exp(-jnp.abs(raw))
    tail = jnp.where(small < 1e-3, small * (1.0 - small * (0.5 - small / 3.0)), jnp.log(1.0 + small))
    soft = jnp.maximum(raw, 0.0) + tail
    step = jnp.where(used, soft, 0.0)
    return raw, step, jnp.where(used, -jnp.exp(heads_ref[0:1]) * step, 0.0)


def head_columns(values, pair):
    moved = pltpu.roll(values, lax.rem(TILE - 2 * pair, TILE), 1)
    return moved[:, 0:1], moved[:, 1:2]


def both_heads(columns):
    return jnp.where(lane_ids() < TILE // 2, columns[0], columns[1])


def taps_of(ext, cw_ref, lanes):
    summed = cw_ref[4:5, lanes]
    for k in range(4):
        summed = summed + cw_ref[k : k + 1, lanes] * ext[5 + k : 5 + k + TILE]
    return summed


def fill_ext(ext, halo_ref, proj_ref, j):
    ext[0:8] = halo_ref[:, tile_at(j)]
    ext[8 : 8 + TILE] = proj_ref[:, pl.ds(pl.multiple_of(INNER + j * TILE, TILE), TILE)]


def mixer_in_kernel(proj_ref, tail_ref, halo_ref, cw_ref, heads_ref, mixed_ref, state_ref, totals_ref, run_ref, step_ref, ext):
    unused_raw, step, log_decay = head_steps(tail_ref, heads_ref)
    lower = (row_ids() >= lane_ids()).astype(jnp.float32)
    run = jnp.dot(lower, log_decay, precision=HIGH, preferred_element_type=jnp.float32)
    run_ref[...] = run
    step_ref[...] = step
    last = run[TILE - 1 : TILE]
    totals_ref[...] = jnp.broadcast_to(last, totals_ref.shape)
    weight = jnp.exp(last - run) * step

    def conv(j, carry):
        fill_ext(ext, halo_ref, proj_ref, j)
        u = taps_of(ext, cw_ref, tile_at(j))
        mixed_ref[:, tile_at(j)] = u * jax.nn.sigmoid(u)
        return carry

    lax.fori_loop(0, CONV // TILE, conv, 0)
    in_map = short(mixed_ref[:, INNER : INNER + TILE])

    def state(p, carry):
        scaled = mixed_ref[:, tile_at(p)] * both_heads(head_columns(weight, p))
        state_ref[p] = short(dot32(short(scaled.T), in_map))
        return carry

    lax.fori_loop(0, HEADS // 2, state, 0, unroll=2)


def decays_of(column, row, lower):
    return jnp.where(lower, jnp.exp(jnp.minimum(column - row, 0.0)), 0.0)


def mixer_out_kernel(proj_ref, mixed_ref, run_ref, step_ref, carried_ref, wide_ref, normed_ref, scanned_ref, gated, rows, ):
    run = run_ref[...]
    rows[0] = run.T
    rows[1] = step_ref[...].T
    lower = row_ids() >= lane_ids()
    in_map = mixed_ref[:, INNER : INNER + TILE]
    out_map = mixed_ref[:, INNER + TILE : INNER + 2 * TILE]
    kernel = lax.dot_general(out_map, in_map, (((1,), (1,)), ((), ())), precision=HIGH, preferred_element_type=jnp.float32)
    out_low = short(out_map)

    def pair(p, squares):
        values = mixed_ref[:, tile_at(p)]
        values_low = short(values)
        columns = head_columns(run, p)
        parts = []
        for h in range(2):
            decays = decays_of(columns[h], rows[0, pl.ds(2 * p + h, 1)], lower)
            weights = kernel * decays * rows[1, pl.ds(2 * p + h, 1)]
            parts.append(dot32(short(weights), values_low))
        result = jnp.where(lane_ids() < TILE // 2, parts[0], parts[1])
        result = result + jnp.exp(both_heads(columns)) * dot_nt(out_low, carried_ref[p])
        result = result + wide_ref[0:1, tile_at(p)] * values
        scanned_ref[:, tile_at(p)] = result
        gate = proj_ref[:, tile_at(p)]
        g = result * (gate * jax.nn.sigmoid(gate))
        gated[:, tile_at(p)] = g
        return squares + g * g

    squares = lax.fori_loop(0, HEADS // 2, pair, jnp.zeros((TILE, TILE), jnp.float32), unroll=2)
    scale = lax.rsqrt(jnp.sum(squares, 1, keepdims=True) / INNER + NORM_EPS)

    def norm(p, carry):
        normed_ref[:, tile_at(p)] = short(gated[:, tile_at(p)] * scale * wide_ref[1:2, tile_at(p)])
        return carry

    lax.fori_loop(0, HEADS // 2, norm, 0, unroll=2)


def gate_back_kernel(proj_ref, mixed_ref, scanned_ref, back_ref, run_ref, wide_ref, result_ref, gate_ref, gain_ref, state_ref, gated):
    run = run_ref[...]
    out_map = short(mixed_ref[:, INNER + TILE : INNER + 2 * TILE])

    def first(p, sums):
        gate = proj_ref[:, tile_at(p)]
        g = scanned_ref[:, tile_at(p)] * (gate * jax.nn.sigmoid(gate))
        gated[:, tile_at(p)] = g
        back = back_ref[:, tile_at(p)] * wide_ref[1:2, tile_at(p)]
        return sums[0] + g * g, sums[1] + g * back

    zero = jnp.zeros((TILE, TILE), jnp.float32)
    squares, products = lax.fori_loop(0, HEADS // 2, first, (zero, zero), unroll=2)
    scale = lax.rsqrt(jnp.sum(squares, 1, keepdims=True) / INNER + NORM_EPS)
    shift = jnp.sum(products, 1, keepdims=True) * scale * scale * scale / INNER

    def second(p, carry):
        lanes = tile_at(p)
        gate = proj_ref[:, lanes]
        sig = jax.nn.sigmoid(gate)
        g = gated[:, lanes]
        back = back_ref[:, lanes]
        gain_ref[:, lanes] = jnp.broadcast_to(jnp.sum(back * g * scale, 0, keepdims=True), (8, TILE))
        g_back = back * wide_ref[1:2, lanes] * scale - g * shift
        result_back = g_back * (gate * sig)
        result_ref[:, lanes] = result_back
        gate_ref[:, lanes] = short(g_back * scanned_ref[:, lanes] * sig * (1.0 + gate * (1.0 - sig)))
        moved = result_back * jnp.exp(both_heads(head_columns(run, p)))
        state_ref[p] = short(dot32(short(moved.T), out_map))
        return carry

    lax.fori_loop(0, HEADS // 2, second, 0, unroll=2)


def mixer_back_kernel(
    proj_ref, tail_ref, halo_ref, cw_ref, heads_ref, mixed_ref, run_ref, step_ref, wide_ref,
    carried_ref, result_ref, leaving_ref,
    conv_ref, rim_ref, taps_ref, step_back_ref, heads_back_ref,
    rows, column_sums, row_sums, kernel_back, maps_back, mixed_back, ext, padded,
):
    run, step = run_ref[...], step_ref[...]
    rows[0] = run.T
    rows[1] = step.T
    lanes_id, rows_id = lane_ids(), row_ids()
    lower = rows_id >= lanes_id
    left_half = lanes_id < TILE // 2
    half_line = lax.broadcasted_iota(jnp.int32, (1, TILE), 1) // (TILE // 2)
    in_map = mixed_ref[:, INNER : INNER + TILE]
    out_map = mixed_ref[:, INNER + TILE : INNER + 2 * TILE]
    kernel = lax.dot_general(out_map, in_map, (((1,), (1,)), ((), ())), precision=HIGH, preferred_element_type=jnp.float32)
    in_low, out_low = short(in_map), short(out_map)
    last = run[TILE - 1 : TILE]
    fade = jnp.exp(last - run)
    weight = fade * step
    column_sums[...] = jnp.zeros_like(column_sums)
    row_sums[...] = jnp.zeros_like(row_sums)
    kernel_back[...] = jnp.zeros_like(kernel_back)
    maps_back[...] = jnp.zeros_like(maps_back)

    def pair(p, carry):
        lanes = tile_at(p)
        values, back = mixed_ref[:, lanes], result_ref[:, lanes]
        values_low, back_low = short(values), short(back)
        columns = head_columns(run, p)
        which = 2 * p + (rows_id >= TILE // 2).astype(jnp.int32)
        spread = (lanes_id == which).astype(jnp.bfloat16)
        parts = []
        for h in range(2):
            at = pl.ds(2 * p + h, 1)
            decays = decays_of(columns[h], rows[0, at], lower)
            plain = kernel * decays
            steps = rows[1, at]
            weights = plain * steps
            mine = jnp.where(left_half, back, 0.0) if h == 0 else jnp.where(left_half, 0.0, back)
            weights_back = dot_nt(short(mine), values_low)
            kernel_back[...] += weights_back * (decays * steps)
            loose = weights_back * plain
            pulled = short(loose * steps)
            column_sums[0] += dot32(pulled, (lanes_id == 2 * p + h).astype(jnp.bfloat16))
            row_sums[0, at] = jnp.sum(pulled.astype(jnp.float32), 0, keepdims=True)
            row_sums[1, at] = jnp.sum(loose, 0, keepdims=True)
            parts.append(dot32(short(weights.T), back_low))
        values_back = jnp.where(left_half, parts[0], parts[1]) + wide_ref[0:1, lanes] * back
        carried, leaving = carried_ref[p], leaving_ref[p]
        moved = back * jnp.exp(both_heads(columns))
        moved_low = short(moved)
        seen = dot_nt(out_low, carried)
        column_sums[0] += dot32(short(moved * seen), spread)
        maps_back[1] += dot32(moved_low, carried)
        weight_pair = both_heads(head_columns(weight, p))
        pulled_state = dot_nt(in_low, leaving)
        values_back = values_back + weight_pair * pulled_state
        maps_back[0] += dot32(short(values * weight_pair), leaving)
        column_sums[1] += dot32(short(values * pulled_state), spread)
        mixed_back[:, lanes] = values_back
        skip_part = jnp.sum(back * values, 0, keepdims=True)
        kept = jnp.sum(carried.astype(jnp.float32) * leaving.astype(jnp.float32), 1, keepdims=True)
        for h in range(2):
            half = slice(h * TILE // 2, (h + 1) * TILE // 2)
            row_sums[2, pl.ds(2 * p + h, 1)] = jnp.broadcast_to(
                jnp.sum(jnp.where(half_line == h, skip_part, 0.0), 1, keepdims=True), (1, TILE)
            )
            row_sums[3, pl.ds(2 * p + h, 1)] = jnp.broadcast_to(
                jnp.sum(kept[half], 0, keepdims=True), (1, TILE)
            )
        return carry

    lax.fori_loop(0, HEADS // 2, pair, 0)

    used = lanes_id < HEADS
    loose_columns = row_sums[1].T
    weight_back = column_sums[1]
    run_back = column_sums[0] - row_sums[0].T - weight * weight_back
    skip_back, decay_back = row_sums[2].T, row_sums[3].T
    last_back = jnp.sum(weight * weight_back, 0, keepdims=True) + jnp.exp(last) * decay_back[0:1]
    run_back = run_back + jnp.where(rows_id == TILE - 1, last_back, 0.0)
    upper = (lanes_id >= rows_id).astype(jnp.float32)
    log_back = jnp.dot(upper, run_back, precision=HIGH, preferred_element_type=jnp.float32)
    raw, unused_step, log_decay = head_steps(tail_ref, heads_ref)
    rate = jnp.exp(heads_ref[0:1])
    step_back = loose_columns + fade * weight_back - rate * log_back
    raw_back = jnp.where(used, step_back * jax.nn.sigmoid(raw), 0.0)
    step_back_ref[...] = raw_back
    rate_back = jnp.sum(jnp.where(used, log_back * log_decay, 0.0), 0, keepdims=True)
    bias_back = jnp.sum(raw_back, 0, keepdims=True)
    at_row = lax.broadcasted_iota(jnp.int32, (8, TILE), 0)
    heads_back_ref[...] = jnp.where(
        at_row == 0, rate_back, jnp.where(at_row == 1, bias_back, jnp.where(at_row == 2, skip_back[0:1], 0.0))
    )
    both = kernel_back[...]
    mixed_back[:, INNER : INNER + TILE] = maps_back[0] + dot32(short(both.T), out_low)
    mixed_back[:, INNER + TILE : INNER + 2 * TILE] = maps_back[1] + dot32(short(both), in_low)
    padded[0:8] = jnp.zeros((8, TILE), jnp.float32)
    padded[8 + TILE : 16 + TILE] = jnp.zeros((8, TILE), jnp.float32)

    def conv(j, carry):
        lanes = tile_at(j)
        fill_ext(ext, halo_ref, proj_ref, j)
        u = taps_of(ext, cw_ref, lanes)
        sig = jax.nn.sigmoid(u)
        back = mixed_back[:, lanes] * sig * (1.0 + u * (1.0 - sig))
        padded[8 : 8 + TILE] = back
        taps_ref[4:5, lanes] = jnp.sum(back, 0, keepdims=True)
        total = jnp.zeros((TILE, TILE), jnp.float32)
        rim = jnp.zeros((8, TILE), jnp.float32)
        for k in range(4):
            tap = cw_ref[k : k + 1, lanes]
            taps_ref[k : k + 1, lanes] = jnp.sum(back * ext[5 + k : 5 + k + TILE], 0, keepdims=True)
            total = total + tap * padded[11 - k : 11 - k + TILE]
            rim = rim + tap * padded[3 - k : 11 - k]
        conv_ref[:, lanes] = total
        rim_ref[:, lanes] = rim
        return carry

    lax.fori_loop(0, CONV // TILE, conv, 0)


def tile_call(kernel, outs, scratch, name, *args):
    space = pl.BlockSpec(memory_space=pltpu.VMEM)
    return pl.pallas_call(
        kernel,
        out_shape=tuple(jax.ShapeDtypeStruct(s, d) for s, d in outs),
        in_specs=[space] * len(args),
        out_specs=(space,) * len(outs),
        scratch_shapes=[pltpu.VMEM(s, jnp.float32) for s in scratch],
        compiler_params=pltpu.CompilerParams(vmem_limit_bytes=40 * 2**20),
        name=name,
    )(*args)


PROJ_BLOCK = 640


def project_kernel(tokens_ref, gain_ref, *refs):
    *mains, tail_ref, norm_ref, proj_ref, tail_out, kept = refs
    width = mains[0].shape[2]

    def product(weights):
        total = dot32(weights[0], kept[:width])
        for i in range(1, len(weights)):
            total = total + dot32(weights[i], kept[i * width : (i + 1) * width])
        return total.T

    @pl.when(pl.program_id(0) == 0)
    def _():
        values = tokens_ref[...].astype(jnp.float32)
        scale = lax.rsqrt(jnp.mean(values * values, 1, keepdims=True) + NORM_EPS)
        normed = values * scale * gain_ref[...]
        norm_ref[...] = short(normed)
        kept[...] = short(normed.T)
        tail_out[...] = product([tail_ref[i] for i in range(len(mains))])

    proj_ref[...] = product([m[0] for m in mains])


def project(tokens, gain, main, tail):
    parts, rows, width = main.shape
    slots, model = tokens.shape
    whole = lambda shape: pl.BlockSpec(shape, lambda j: (0,) * len(shape))
    return pl.pallas_call(
        project_kernel,
        grid=(rows // PROJ_BLOCK,),
        out_shape=(
            jax.ShapeDtypeStruct((slots, model), jnp.bfloat16),
            jax.ShapeDtypeStruct((slots, rows), jnp.float32),
            jax.ShapeDtypeStruct((slots, tail.shape[1]), jnp.float32),
        ),
        in_specs=[
            whole((slots, model)),
            whole((1, model)),
            *[pl.BlockSpec((1, PROJ_BLOCK, width), lambda j, i=i: (i, j, 0)) for i in range(parts)],
            whole(tail.shape),
        ],
        out_specs=(
            whole((slots, model)),
            pl.BlockSpec((slots, PROJ_BLOCK), lambda j: (0, j)),
            whole((slots, tail.shape[1])),
        ),
        scratch_shapes=[pltpu.VMEM((model, slots), jnp.bfloat16)],
        compiler_params=pltpu.CompilerParams(vmem_limit_bytes=56 * 2**20),
        name="project",
    )(tokens, gain, *[main] * parts, tail)


def project_back_kernel(back_ref, tail_back_ref, *refs):
    *mains, tail_ref, tokens_ref, gain_ref, middle_ref, tokens_back_ref, gain_back_ref, total = refs
    parts, width = len(mains), mains[0].shape[2]
    step = pl.program_id(0)

    @pl.when(step == 0)
    def _():
        for i in range(parts):
            total[:, i * width : (i + 1) * width] = dot32(tail_back_ref[...], tail_ref[i])

    for i in range(parts):
        total[:, i * width : (i + 1) * width] += dot32(back_ref[...], mains[i][0])

    @pl.when(step == pl.num_programs(0) - 1)
    def _():
        values = tokens_ref[...].astype(jnp.float32)
        scale = lax.rsqrt(jnp.mean(values * values, 1, keepdims=True) + NORM_EPS)
        back = total[...]
        gain_back_ref[...] = jnp.sum(back * values * scale, 0, keepdims=True)
        spread = back * gain_ref[...]
        shift = jnp.mean(spread * values, 1, keepdims=True) * scale * scale * scale
        tokens_back_ref[...] = middle_ref[...] + spread * scale - values * shift


def project_back(back, tail_back, main, tail, tokens, gain, middle_back):
    parts, rows, width = main.shape
    slots, model = tokens.shape
    whole = lambda shape: pl.BlockSpec(shape, lambda j: (0,) * len(shape))
    return pl.pallas_call(
        project_back_kernel,
        grid=(rows // PROJ_BLOCK,),
        out_shape=(
            jax.ShapeDtypeStruct((slots, model), jnp.float32),
            jax.ShapeDtypeStruct((1, model), jnp.float32),
        ),
        in_specs=[
            pl.BlockSpec((slots, PROJ_BLOCK), lambda j: (0, j)),
            whole(tail_back.shape),
            *[pl.BlockSpec((1, PROJ_BLOCK, width), lambda j, i=i: (i, j, 0)) for i in range(parts)],
            whole(tail.shape),
            whole((slots, model)),
            whole((1, model)),
            whole((slots, model)),
        ],
        out_specs=(whole((slots, model)), whole((1, model))),
        scratch_shapes=[pltpu.VMEM((slots, model), jnp.float32)],
        compiler_params=pltpu.CompilerParams(vmem_limit_bytes=56 * 2**20),
        name="project_back",
    )(back, tail_back, *[main] * parts, tail, tokens, gain, middle_back)


def from_behind(block, axis, distance):
    devices = range(lax.axis_size(axis))
    route = [(i - distance, i) for i in devices if i - distance in devices]
    return lax.ppermute(block, axis, route)


def owner_rows(values, order, per_owner):
    depth, columns = values.shape
    grid = values.T.reshape(4, 4, 2, 4, per_owner, depth)
    place = {"x": 0, "y": 1, "c": 2, "z": 3}
    return jnp.transpose(grid, [place[a] for a in ("c", *order)] + [4, 5])


def plane_rows(values, order):
    depth, columns = values.shape
    grid = values.T.reshape(4, 4, 2, columns // 32, depth)
    place = {"x": 0, "y": 1, "c": 2}
    return jnp.transpose(grid, [place[a] for a in ("c", *order)] + [3, 4]).reshape(columns, depth)


def left_rows(values, order, per_owner=12):
    grid = owner_rows(values, order, per_owner)
    if per_owner == 24:
        return [grid[..., :12, :].reshape(1536, -1), grid[..., 12:, :].reshape(1536, -1)]
    grid = jnp.pad(grid, ((0, 0),) * 4 + ((0, 12 - per_owner), (0, 0)))
    return [grid.reshape(1536, -1)]


def local(
    tokens,
    cotangent,
    lengths,
    routes,
    norm_gain,
    w_in,
    conv_weight,
    conv_bias,
    a_log,
    dt_bias,
    skip_scale,
    gated_gain,
    w_out,
    post_gain,
    w_router,
    shared_in,
    shared_out,
    expert_in,
    expert_out,
):
    low = jnp.bfloat16
    tokens, cotangent, routes = tokens[0], cotangent[0], routes[0]
    slot_count, model_width = tokens.shape
    inner_width = gated_gain.shape[0]
    conv_width = conv_bias.shape[0]
    head_count = a_log.shape[0]
    tap_count = conv_weight.shape[0]
    expert_count = w_router.shape[1]
    residual = tokens.astype(jnp.float32)
    positions = lax.axis_index(SEQ) * slot_count + jnp.arange(slot_count)
    valid = positions < lengths[0]
    upstream_low = jnp.where(valid[:, None], cotangent, jnp.zeros_like(cotangent))
    upstream = upstream_low.astype(jnp.float32)
    main_rows = inner_width + conv_width
    turned = w_in.T
    tail_shard = jnp.concatenate(
        [
            turned[main_rows:],
            w_router.T,
            jnp.zeros((TILE - head_count - expert_count, turned.shape[1]), low),
        ],
        0,
    )
    full_in, full_out, full_shared_in, full_shared_out, tails = gather_weights(
        [turned, w_out, shared_in, shared_out], [tail_shard], main_rows
    )
    full_router = jnp.swapaxes(tails[:, head_count : head_count + expert_count], 0, 1)
    full_router = full_router.reshape(expert_count, model_width)

    first_norm, projected, tail_values = project(tokens, norm_gain[None], full_in, tails)
    halo = from_behind(projected[slot_count - 8 :, inner_width:], SEQ, 1)
    taps = jnp.concatenate([conv_weight, conv_bias[None], jnp.zeros((3, conv_width), jnp.float32)], 0)
    heads = jnp.pad(jnp.stack([a_log, dt_bias]), ((0, 6), (0, TILE - head_count)))
    wide = jnp.stack([jnp.repeat(skip_scale, inner_width // head_count), gated_gain])
    square, pairs = (TILE, TILE), (head_count // 2, TILE, TILE)
    mixed, leaving, totals, running, steps = tile_call(
        mixer_in_kernel,
        [((TILE, conv_width), jnp.float32), (pairs, low), ((8, TILE), jnp.float32), (square, jnp.float32), (square, jnp.float32)],
        [(TILE + 8, TILE)],
        "mixer_in",
        projected, tail_values, halo, taps, heads,
    )
    states = (head_count, inner_width // head_count, TILE)
    carried, decays, all_upstream = carried_states(leaving.reshape(states), totals, upstream_low)
    carried = carried.reshape(pairs)
    normed_low, scanned = tile_call(
        mixer_out_kernel,
        [((TILE, inner_width), low), ((TILE, inner_width), jnp.float32)],
        [(TILE, inner_width), (2, *square)],
        "mixer_out",
        projected, mixed, running, steps, carried, wide,
    )
    middle = residual + dot32(normed_low, full_out)
    second_norm = scaled_rows(middle, post_gain).astype(low)
    logits = dot_nt(second_norm, full_router)
    chosen = jnp.any(routes[:, :, None] == jnp.arange(expert_count)[None, None, :], 1)
    masked = jnp.where(chosen, logits, -jnp.inf)
    powers = jnp.exp(masked - jnp.max(masked, -1, keepdims=True))
    gate_dense = powers / jnp.sum(powers, -1, keepdims=True)

    all_rows, all_gates = z_gather((second_norm, gate_dense.T), 5, "gather_rows")
    rows = all_rows.reshape(-1, model_width)
    back_rows = all_upstream.reshape(-1, model_width)
    owned = expert_in.shape[0]
    first_owned = lax.axis_index("z") * owned
    gates = lax.dynamic_slice_in_dim(all_gates, first_owned, owned, 1)
    gates = jnp.swapaxes(gates, 0, 1).reshape(owned, -1)
    hidden_width = expert_out.shape[1]
    acts = jnp.einsum("td,edf->etf", rows, expert_in, preferred_element_type=jnp.float32)
    hidden = (jax.nn.silu(acts[..., :hidden_width]) * acts[..., hidden_width:]).astype(low)
    output = jnp.einsum("etf,efd->etd", hidden, expert_out, preferred_element_type=jnp.float32)
    output = output.astype(low).astype(jnp.float32)
    part = jnp.sum(gates[..., None] * output, 0).astype(low)
    back_wide = back_rows.astype(jnp.float32)
    picks = jnp.sum(output * back_wide[None], -1)
    out_grad = (gates[..., None] * back_wide[None]).astype(low)
    hidden_back = jnp.einsum("etd,efd->etf", out_grad, expert_out, preferred_element_type=jnp.float32)
    act_grad = glu_back(acts, hidden_back)
    back = jnp.einsum("etf,edf->td", act_grad, expert_in, preferred_element_type=jnp.float32).astype(low)
    picks = jnp.swapaxes(picks.reshape(owned, 4, slot_count), 0, 1)
    picks = jnp.pad(picks, ((0, 0), (0, 8 - owned), (0, 0)))
    expert_parts, back_sum, all_picks = expert_sum(
        jnp.stack([plane_rows(rows, order) for order in EXPERT_ORDERS]),
        act_grad,
        jnp.stack([plane_rows(hidden[e], EXPERT_ORDERS[e]) for e in range(owned)]),
        out_grad,
        back.reshape(4, slot_count, model_width),
        picks,
    )
    act_width = act_grad.shape[2]
    grad_expert_in = expert_parts[:, :, :act_width]
    grad_expert_out = expert_parts[:, :, act_width:].reshape(owned, 3, -1, model_width // 3)
    grad_expert_out = jnp.swapaxes(grad_expert_out, 1, 2).reshape(owned, -1, model_width)

    shared_width = full_shared_out.shape[0]
    shared_acts = dot32(second_norm, full_shared_in)
    shared_hidden = (
        jax.nn.silu(shared_acts[:, :shared_width]) * shared_acts[:, shared_width:]
    ).astype(low)
    shared_sum = dot32(shared_hidden, full_shared_out)
    shared_back = jnp.einsum("td,hd->th", upstream_low, full_shared_out, preferred_element_type=jnp.float32)
    shared_act_grad = glu_back(shared_acts, shared_back)
    second_back = jnp.einsum("tf,df->td", shared_act_grad, full_shared_in, preferred_element_type=jnp.float32)
    gate_grads = all_picks[:, :owned].reshape(expert_count, slot_count).T
    pick_grads = gate_dense * (gate_grads - jnp.sum(gate_dense * gate_grads, -1, keepdims=True))
    logit_grads = pick_grads.astype(low)
    second_back = second_back + back_sum + jnp.einsum(
        "te,ed->td", logit_grads, full_router, preferred_element_type=jnp.float32
    )
    unused_second, second_pull = jax.vjp(scaled_rows, middle, post_gain)
    middle_back, grad_post_gain = second_pull(second_back)
    middle_back = middle_back + upstream
    mix_low = middle_back.astype(low)
    normed_back = jnp.einsum("td,kd->tk", mix_low, full_out, preferred_element_type=jnp.float32)
    result_back, gate_back, gain_back, incoming_back = tile_call(
        gate_back_kernel,
        [((TILE, inner_width), jnp.float32), ((TILE, inner_width), low), ((8, inner_width), jnp.float32), (pairs, low)],
        [(TILE, inner_width)],
        "gate_back",
        projected, mixed, scanned, normed_back, running, wide,
    )
    leaving_back, expert_total = carried_states(
        incoming_back.reshape(states), decays, part.reshape(4, slot_count, model_width)
    )
    leaving_back = leaving_back.reshape(pairs)
    block_out = jnp.where(valid[:, None], middle + expert_total + shared_sum, 0.0).astype(low)
    conv_part, rim_part, taps_back, steps_back, heads_back = tile_call(
        mixer_back_kernel,
        [
            ((TILE, conv_width), jnp.float32), ((8, conv_width), jnp.float32), ((8, conv_width), jnp.float32),
            (square, jnp.float32), ((8, TILE), jnp.float32),
        ],
        [
            (2, *square), (2, *square), (4, *square), square, (2, *square),
            (TILE, conv_width), (TILE + 8, TILE), (TILE + 16, TILE),
        ],
        "mixer_back",
        projected, tail_values, halo, taps, heads, mixed, running, steps, wide, carried, result_back, leaving_back,
    )
    rim_back = from_behind(rim_part.astype(low), SEQ, -1).astype(jnp.float32)
    conv_back = conv_part + jnp.pad(rim_back, ((slot_count - 8, 0), (0, 0)))
    proj_back = jnp.concatenate([gate_back, conv_back.astype(low)], 1)
    tail_back = steps_back.astype(low)
    grad_tokens, grad_norm_gain = project_back(
        proj_back, tail_back, full_in, tails, tokens, norm_gain[None], middle_back
    )

    first, second, third = RS_ORDERS
    lefts = jnp.stack(
        left_rows(first_norm, first)
        + left_rows(first_norm, second)
        + left_rows(second_norm, second) * 2
        + left_rows(normed_low, third, 24)
        + left_rows(shared_hidden, third, 8)
    )
    zeros = lambda columns: jnp.zeros((slot_count, columns), low)
    rights = jnp.concatenate(
        [
            proj_back,
            tail_back,
            zeros(13 * RS_COLS - main_rows - TILE),
            shared_act_grad,
            zeros(RS_COLS),
            mix_low,
            mix_low,
            upstream_low,
        ],
        1,
    )
    router_back = jnp.einsum("te,td->ed", logit_grads, second_norm, preferred_element_type=jnp.float32)
    summed, small = grad_sum(
        lefts, rights, taps_back, gain_back, grad_norm_gain, grad_post_gain[None], heads_back, router_back
    )
    at = 13 * RS_COLS
    w_in_part = summed[:12, : w_in.shape[1]]
    shared_in_part = summed[:12, at : at + 2 * shared_width]
    at = at + 5 * RS_COLS
    w_out_part = jnp.concatenate(
        [summed[:12, at : at + model_width], summed[:12, at + model_width : at + 2 * model_width]], 0
    )
    at = at + 2 * model_width
    shared_out_part = summed[:8, at : at + model_width]
    owner = lax.axis_index(ALL)

    def owned_part(values):
        size = values.shape[-1] // 128
        return lax.dynamic_slice_in_dim(values, owner * size, size, values.ndim - 1)

    return (
        block_out[None],
        grad_tokens[None],
        owned_part(small[6, :model_width]),
        w_in_part,
        owned_part(small[:4, :conv_width]),
        owned_part(small[4, :conv_width]),
        small[7, :head_count],
        small[7, TILE : TILE + head_count],
        small[7, 2 * TILE : 2 * TILE + head_count],
        owned_part(small[5, :inner_width]),
        w_out_part,
        owned_part(small[6, model_width : 2 * model_width]),
        owned_part(small[:, conv_width:]).T,
        shared_in_part,
        shared_out_part,
        grad_expert_in,
        grad_expert_out,
    )


def solution(mesh):
    split = Mesh(mesh.devices.reshape(4, 4, 2, 4), ALL)
    placed = (
        P("z", SEQ, None),
        P("z", SEQ, None),
        P("z"),
        P("z", SEQ, None),
        P(),
        P("z", None),
        P(),
        P(),
        P(),
        P(),
        P(),
        P(),
        P("z", None),
        P(),
        P("z", None),
        P("z", None),
        P("z", None),
        P("z", None, None),
        P("z", None, None),
    )
    return jax.shard_map(
        local,
        mesh=split,
        in_specs=placed,
        out_specs=(
            P("z", SEQ, None),
            P("z", SEQ, None),
            P(ALL),
            P(ALL, None),
            P(None, ALL),
            P(ALL),
            P(),
            P(),
            P(),
            P(ALL),
            P(ALL, None),
            P(ALL),
            P(ALL, None),
            P(ALL, None),
            P(ALL, None),
            P("z", SEQ, None),
            P("z", SEQ, None),
        ),
        check_vma=False,
    )
```

time: 1000 us -> 532 us (0.53)
  waiting for transfers between devices: 355 us -> 0.01 us
  Pallas kernels: 296 us -> 398 us
  matrix products: 127 us -> 33.5 us
  local copies, waits for them, and re-layouts: 126 us -> 69.1 us
  other arithmetic: 63.7 us -> 19.1 us
  between operations: 17.2 us -> 3.07 us
    all_gather x4 -> x0, waiting for transfers between devices: 199 us -> none  [the longest x1 144 us: local(): lax.all_gather(w_in, 'z', axis=0, tiled=True)]
    pallas_call x2 -> x9, Pallas kernels: 152 us -> 306 us  [the longest x1 114 us: grad_sum(): pl.pallas_call(grad_sum_kernel, out_shape=(jax.ShapeDtypeStruct((16, slot...]
    reduce_scatter x1 -> x0, waiting for transfers between devices: 82.1 us -> none  [local(): lax.psum_scatter(grad_expert_out.astype(low), SEQ, scatter_dimension=1, t...]
    unnamed x8 -> x0, waiting for transfers between devices: 74.4 us -> none
    dot_general x16 -> x3, matrix products: 66.8 us -> 2 us  [the longest x1 1.01 us: local(): jnp.einsum('te,ed->td', logit_grads, full_router, preferred_element_type=...]
    pallas_call x2 -> x1, Pallas kernels: 70.3 us -> 21.9 us  [z_gather(): pl.pallas_call(functools.partial(z_gather_kernel, count), out_shape=tuple...]
    reduce_sum x13 -> x1, other arithmetic: 24.1 us -> 0.02 us  [local(): gate_dense = powers / jnp.sum(powers, -1, keepdims=True)]
    dot_general x5 -> x3, matrix products: 28.2 us -> 5.9 us  [dot32(): return jnp.dot(left, right, preferred_element_type=jnp.float32)]
  transfers between devices with their start and end apart: 9 -> 2, of which waited for: 4 -> 0; matrix products, arithmetic and copies ran while one was open for 21% -> 7% of each run, Pallas kernels for 26% -> 0%
where the time goes in v2:
time: 532 us; the launch traced here: 526 us
  Pallas kernels  398 us (75%)
  local copies, waits for them, and re-layouts  69.1 us (13%)
  matrix products  33.5 us (6%)
  other arithmetic  19.1 us (4%)
    pallas_call x1, Pallas kernels, grad_sum(): pl.pallas_call(grad_sum_kernel, out_shape=(jax.ShapeDtypeStruct((16, slot...  114 us
    pallas_call x1, Pallas kernels, gather_weights(): pl.pallas_call(functools.partial(gather_kernel, count), out_shape=tuple((...  82.4 us
    pallas_call x2, Pallas kernels, carried_states(): pl.pallas_call(scan_backward_kernel if reverse else scan_forward_kernel,...  70.2 us
    pallas_call x1, Pallas kernels, expert_sum(): pl.pallas_call(expert_sum_kernel, out_shape=(jax.ShapeDtypeStruct((2, blo...  46.1 us
    pallas_call x4, Pallas kernels, tile_call(): pl.pallas_call(kernel, out_shape=tuple((jax.ShapeDtypeStruct(s, d) for s,...  34.4 us
    pallas_call x1, Pallas kernels, z_gather(): pl.pallas_call(functools.partial(z_gather_kernel, count), out_shape=tuple...  21.9 us
    unnamed x193, local copies, waits for them, and re-layouts  18.8 us
    pallas_call x1, Pallas kernels, project(): pl.pallas_call(project_kernel, grid=(rows // PROJ_BLOCK,), out_shape=(jax...  14.8 us
  transfers between devices with their start and end apart: 2, of which 0 were waited for; matrix products, arithmetic and copies ran while one was open for 7% of the time, Pallas kernels for 0%

profile of v2, /device:TPU:0, one launch (start us, length us, event | category | flops | bytes accessed | tf_op | source)
XLA Modules:
  0.0 526.1 jit_solution(11240349618125152619)
XLA Ops:
  4.2 82.4 %gather_weights.1 = (bf16[4,6400,384]{2,1,0:T(8,128)(2,1)}, bf16[3072,1536]{1,0:T(8,128)(2,1)}, bf16[1536,2048]{1,0:T(8,128)(2,1)}, bf16[1024,1536]{1,0:T(8,128)(2,1)}, bf16[4,128,384]{2,1,0:T(8,128)(2,1)}) custom-call(bf16[6448,384]{1,0:T(8,128)(2,1)} %bitcast.152, bf16[768,1536]{1,0:T(8,128)(2,1)} %refs_1_.1, bf16[384,2048]{1,0:T(8,128)(2,1)} %refs_2_.1, ...), custom_call_target="tpu_custom_call" | custom-call | tf_op jit(solution)/shard_map/gather_weights/pallas_call | solution.py:976
  86.7 14.8 %project.1 = (bf16[128,1536]{1,0:T(8,128)(2,1)}, f32[128,6400]{1,0:T(8,128)}, f32[128,128]{1,0:T(8,128)}) custom-call(bf16[128,1536]{1,0:T(8,128)(2,1)} %bitcast.156, f32[1,1536]{1,0:T(1,128)} %broadcast_in_dim.70.gain_ref.refs_6_, bf16[4,6400,384]{2,1,0:T(8,128)(2,1)} %get-tuple-element.55.refs_0_.refs_1_.refs_2_.refs_3_, ...), custom_call_target="tpu_custom_call" | custom-call | tf_op jit(solution)/shard_map/project/pallas_call | solution.py:1321
  103.0 2.0 collective-permute-start
  127.3 6.7 %mixer_in.1 = (f32[128,3328]{1,0:T(8,128)S(1)}, bf16[24,128,128]{2,1,0:T(8,128)(2,1)S(1)}, f32[8,128]{1,0:T(8,128)S(1)}, f32[128,128]{1,0:T(8,128)S(1)}, f32[128,128]{1,0:T(8,128)S(1)}) custom-call(f32[128,6400]{1,0:T(8,128)S(1)} %copy-done, f32[128,128]{1,0:T(8,128)S(1)} %copy-done.28, f32[8,3328]{1,0:T(8,128)S(1)} %collective-permute-done.halo_ref, ...), custom_call_target="tpu_custom_call" | custom-call | tf_op jit(solution)/shard_map/mixer_in/pallas_call | solution.py:1281
  134.0 36.4 %scan_forward.1 = (bf16[48,2,32,128]{3,2,1,0:T(8,128)(2,1)S(1)}, f32[32,8,128]{2,1,0:T(8,128)S(1)}, bf16[4,128,1536]{2,1,0:T(8,128)(2,1)S(1)}) custom-call(bf16[48,2,32,128]{3,2,1,0:T(8,128)(2,1)S(1)} %bitcast.144, f32[8,128]{1,0:T(8,128)S(1)} %get-tuple-element.63.totals_ref, bf16[128,1536]{1,0:T(8,128)(2,1)S(1)} %copy-done.18), custom_call_target="tpu_custom_call" | custom-call | tf_op jit(solution)/shard_map/scan_forward/pallas_call | solution.py:483
  170.5 5.1 mixer_out.1
  178.1 21.9 %gather_rows.1 = (bf16[4,128,1536]{2,1,0:T(8,128)(2,1)S(1)}, f32[4,8,128]{2,1,0:T(8,128)S(1)}) custom-call(bf16[128,1536]{1,0:T(8,128)(2,1)S(1)} %multiply_convert_fusion.4.refs_0_, f32[8,128]{1,0:T(8,128)S(1)} %fusion.21.refs_1_), custom_call_target="tpu_custom_call" | custom-call | tf_op jit(solution)/shard_map/gather_rows/pallas_call | solution.py:522
  201.1 2.8 slice-done.3
  203.8 3.4 convolution_bitcast_fusion.1
  207.3 2.6 multiply_convert_fusion.3
  209.9 3.5 fusion.1
  214.4 4.9 fusion.2
  222.4 2.0 copy.75
  226.4 2.0 copy.77
  230.3 2.6 copy.70
  238.1 46.1 %expert_sum.1 = (f32[2,48,1536]{2,1,0:T(8,128)S(1)}, f32[128,1536]{1,0:T(8,128)S(1)}, f32[4,8,128]{2,1,0:T(8,128)S(1)}) custom-call(bf16[2,1536,512]{2,1,0:T(8,128)(2,1)} %pad_maximum_fusion.rows_ref, bf16[2,512,1024]{2,1,0:T(8,128)(2,1)} %pad_maximum_fusion.1.acts_ref, bf16[2,512,512]{2,1,0:T(8,128)(2,1)} %pad_maximum_fusion.3.hidden_ref, ...), custom_call_target="tpu_custom_call" | custom-call | tf_op jit(solution)/shard_map/expert_sum/pallas_call | solution.py:751
  288.4 2.2 convolution_add_fusion.2
  292.2 7.1 %fusion.19.back_ref = f32[128,3072]{1,0:T(8,128)S(1)} fusion(bf16[3072,1536]{1,0:T(8,128)(2,1)} %get-tuple-element.66, f32[128,1536]{1,0:T(8,128)S(1)} %fusion.6.refs_7_), kind=kOutput, calls=%fused_computation.94 | convolution fusion | flops 1208156160 | bytes 11796480 | tf_op jit(solution)/shard_map/td,kd->tk/dot_general | solution.py:1559
  299.4 6.4 %gate_back.1 = (f32[128,3072]{1,0:T(8,128)S(1)}, bf16[128,3072]{1,0:T(8,128)(2,1)S(1)}, f32[8,3072]{1,0:T(8,128)S(1)}, bf16[24,128,128]{2,1,0:T(8,128)(2,1)S(1)}) custom-call(f32[128,6400]{1,0:T(8,128)S(1)} %copy-done, f32[128,3328]{1,0:T(8,128)S(1)} %copy-done.2, f32[128,3072]{1,0:T(8,128)S(1)} %copy-done.15, f32[128,3072]{1,0:T(8,128)S(1)} %fusion.19.back_ref, ...), custom_call_target="tpu_custom_call" | custom-call | tf_op jit(solution)/shard_map/gate_back/pallas_call | solution.py:1281
  305.9 33.8 %scan_backward.1 = (bf16[48,2,32,128]{3,2,1,0:T(8,128)(2,1)S(1)}, f32[128,1536]{1,0:T(8,128)S(1)}) custom-call(bf16[48,2,32,128]{3,2,1,0:T(8,128)(2,1)S(1)} %bitcast.143, f32[32,8,128]{2,1,0:T(8,128)S(1)} %copy-done.31, bf16[4,128,1536]{2,1,0:T(8,128)(2,1)S(1)} %bitcast.138), custom_call_target="tpu_custom_call" | custom-call | tf_op jit(solution)/shard_map/scan_backward/pallas_call | solution.py:483
  339.7 16.2 %mixer_back.1 = (f32[128,3328]{1,0:T(8,128)S(1)}, f32[8,3328]{1,0:T(8,128)S(1)}, f32[8,3328]{1,0:T(8,128)S(1)}, f32[128,128]{1,0:T(8,128)S(1)}, f32[8,128]{1,0:T(8,128)S(1)}) custom-call(f32[128,6400]{1,0:T(8,128)S(1)} %copy-done, f32[128,128]{1,0:T(8,128)S(1)} %copy-done.29, f32[8,3328]{1,0:T(8,128)S(1)} %collective-permute-done.halo_ref, ...), custom_call_target="tpu_custom_call" | custom-call | tf_op jit(solution)/shard_map/mixer_back/pallas_call | solution.py:1281
  365.2 3.4 fusion.5
  382.5 14.1 %project_back.1 = (f32[128,1536]{1,0:T(8,128)}, f32[1,1536]{1,0:T(1,128)}) custom-call(bf16[128,6400]{1,0:T(8,128)(2,1)} %pad_maximum_fusion.2.back_ref, bf16[128,128]{1,0:T(8,128)(2,1)} %get-tuple-element.98.tail_back_ref, bf16[4,6400,384]{2,1,0:T(8,128)(2,1)} %get-tuple-element.55.refs_0_.refs_1_.refs_2_.refs_3_, ...), custom_call_target="tpu_custom_call" | custom-call | tf_op jit(solution)/shard_map/project_back/pallas_call | solution.py:1374
  396.6 114.0 %grad_sum.1 = (f32[16,13824]{1,0:T(8,128)}, f32[8,4864]{1,0:T(8,128)}) custom-call(bf16[7,1536,128]{2,1,0:T(8,128)(2,1)} %constant_dynamic-update-slice_fusion.a_ref, bf16[128,13824]{1,0:T(8,128)(2,1)} %constant_dynamic-update-slice_fusion.7.b_ref, f32[8,3328]{1,0:T(8,128)} %copy-done.37, f32[8,3072]{1,0:T(8,128)} %copy-done.38, ...), custom_call_target="tpu_custom_call" | custom-call | flops 5435817984 | bytes 8388608 | tf_op jit(solution)/shard_map/grad_sum/pallas_call | solution.py:320
  (291 shorter events, 86.5 us)
Async XLA Ops:
  103.0 23.4 %collective-permute-start = (f32[8,3328]{1,0:T(8,128)}, f32[8,3328]{1,0:T(8,128)S(1)}, u32[]{:S(2)}, u32[]{:S(2)}) collective-permute-start(f32[8,3328]{1,0:T(8,128)} %slice.89), channel_id=1, source_target_pairs={{0,4},{4,8},{8,12},{12,16},{16,20},{20,24},{24,28},{28,32},{32,36}... | collective-permute-start | bytes 319496 | tf_op jit(solution)/shard_map/ppermute | solution.py:1400
  124.9 45.6 %copy-start.24 = (f32[2,3072]{1,0:T(2,128)S(1)}, f32[2,3072]{1,0:T(2,128)}, u32[]{:S(2)}) copy-start(f32[2,3072]{1,0:T(2,128)} %pad_maximum_fusion.5.wide_ref) | copy-start | bytes 73732
  126.4 44.0 %copy-start.35 = (f32[8,128]{1,0:T(8,128)}, f32[8,128]{1,0:T(8,128)S(1)}, u32[]{:S(2)}) copy-start(f32[8,128]{1,0:T(8,128)S(1)} %select_maximum_fusion.heads_ref) | copy-start | bytes 12292
  127.3 48.4 %copy-start.40 = (bf16[3072,1536]{1,0:T(8,128)(2,1)S(1)}, bf16[3072,1536]{1,0:T(8,128)(2,1)}, u32[]{:S(2)}) copy-start(bf16[3072,1536]{1,0:T(8,128)(2,1)} %get-tuple-element.66) | copy-start | bytes 28311556
  133.9 41.7 %copy-start.1 = (f32[128,3328]{1,0:T(8,128)}, f32[128,3328]{1,0:T(8,128)S(1)}, u32[]{:S(2)}) copy-start(f32[128,3328]{1,0:T(8,128)S(1)} %get-tuple-element.59.mixed_ref) | copy-start | bytes 5111812
  134.0 41.7 %copy-start.26 = (f32[128,128]{1,0:T(8,128)}, f32[128,128]{1,0:T(8,128)S(1)}, u32[]{:S(2)}) copy-start(f32[128,128]{1,0:T(8,128)S(1)} %get-tuple-element.61.step_ref) | copy-start | bytes 196612
  177.3 43.7 %copy-start.41 = (f32[128,1536]{1,0:T(8,128)}, f32[128,1536]{1,0:T(8,128)S(1)}, u32[]{:S(2)}) copy-start(f32[128,1536]{1,0:T(8,128)S(1)} %get-tuple-element.119) | copy-start | bytes 2359300
  177.3 43.7 %copy-start.75 = (f32[128]{0:T(128)}, f32[128]{0:T(128)S(1)}, u32[]{:S(2)}) copy-start(f32[128]{0:T(128)S(1)} %fusion.17) | copy-start | bytes 1540
  177.3 23.8 %slice-start.2 = ((s8[6291456]{0:T(1024)(128)(4,1)}), s8[2097152]{0:T(1024)(128)(4,1)S(1)}, s32[]{:S(2)}) async-start(s8[6291456]{0:T(1024)(128)(4,1)} %bitcast.179), calls=%async_computation.2 | async-start | bytes 4194304
  177.8 23.0 %copy-start.3 = (bf16[128,1536]{1,0:T(8,128)(2,1)}, bf16[128,1536]{1,0:T(8,128)(2,1)S(1)}, u32[]{:S(2)}) copy-start(bf16[128,1536]{1,0:T(8,128)(2,1)S(1)} %multiply_convert_fusion.4.refs_0_) | copy-start | bytes 1179652
  178.0 22.8 %copy-start.70 = (f32[128]{0:T(128)}, f32[128]{0:T(128)S(1)}, u32[]{:S(2)}) copy-start(f32[128]{0:T(128)S(1)} %get-tuple-element.120) | copy-start | bytes 1540
  236.1 48.1 %slice-start = ((s8[6291456]{0:T(1024)(128)(4,1)}), s8[4194304]{0:T(1024)(128)(4,1)S(1)}, s32[]{:S(2)}) async-start(s8[6291456]{0:T(1024)(128)(4,1)} %bitcast.145), calls=%async_computation | async-start | bytes 8388608
  238.0 46.2 %copy-start.64 = (f32[128,8]{0,1:T(8,128)S(1)}, f32[128,8]{0,1:T(8,128)}, u32[]{:S(2)}) copy-start(f32[128,8]{0,1:T(8,128)} %copy-done.63) | copy-start | bytes 12292
  238.1 46.2 %copy-start.71 = (f32[128]{0:T(128)S(1)}, f32[128]{0:T(128)}, u32[]{:S(2)}) copy-start(f32[128]{0:T(128)} %copy-done.70) | copy-start | bytes 1540
  238.1 46.2 %copy-start.74 = (f32[128]{0:T(128)S(1)}, f32[128]{0:T(128)}, u32[]{:S(2)}) copy-start(f32[128]{0:T(128)} %copy-done.73) | copy-start | bytes 1540
  238.1 46.2 %copy-start.4 = (bf16[128,1536]{1,0:T(8,128)(2,1)S(1)}, bf16[128,1536]{1,0:T(8,128)(2,1)}, u32[]{:S(2)}) copy-start(bf16[128,1536]{1,0:T(8,128)(2,1)} %copy-done.3) | copy-start | bytes 1179652
  238.1 46.2 %slice-start.1 = ((s8[6291456]{0:T(1024)(128)(4,1)}), s8[2097152]{0:T(1024)(128)(4,1)S(1)}, s32[]{:S(2)}) async-start(s8[6291456]{0:T(1024)(128)(4,1)} %bitcast.145), calls=%async_computation.1 | async-start | bytes 4194304
  299.4 40.3 %copy-start.11 = (bf16[48,2,32,128]{3,2,1,0:T(8,128)(2,1)S(1)}, bf16[48,2,32,128]{3,2,1,0:T(8,128)(2,1)}, u32[]{:S(2)}) copy-start(bf16[48,2,32,128]{3,2,1,0:T(8,128)(2,1)} %copy-done.10) | copy-start | bytes 2359300
  299.4 40.3 %copy-start.27 = (f32[128,128]{1,0:T(8,128)S(1)}, f32[128,128]{1,0:T(8,128)}, u32[]{:S(2)}) copy-start(f32[128,128]{1,0:T(8,128)} %copy-done.26) | copy-start | bytes 196612
  299.4 40.3 %copy-start.29 = (f32[128,128]{1,0:T(8,128)S(1)}, f32[128,128]{1,0:T(8,128)}, u32[]{:S(2)}) copy-start(f32[128,128]{1,0:T(8,128)} %get-tuple-element.58.tail_ref) | copy-start | bytes 196612
  299.4 40.3 %copy-start.36 = (f32[8,128]{1,0:T(8,128)S(1)}, f32[8,128]{1,0:T(8,128)}, u32[]{:S(2)}) copy-start(f32[8,128]{1,0:T(8,128)} %copy-done.35) | copy-start | bytes 12292
  305.8 50.1 %copy-start.38 = (f32[8,3072]{1,0:T(8,128)}, f32[8,3072]{1,0:T(8,128)S(1)}, u32[]{:S(2)}) copy-start(f32[8,3072]{1,0:T(8,128)S(1)} %get-tuple-element.87.gain_ref) | copy-start | bytes 294916
  305.8 53.3 %copy-start.8 = (bf16[128,3072]{1,0:T(8,128)(2,1)}, bf16[128,3072]{1,0:T(8,128)(2,1)S(1)}, u32[]{:S(2)}) copy-start(bf16[128,3072]{1,0:T(8,128)(2,1)S(1)} %get-tuple-element.78) | copy-start | bytes 2359300
  357.8 16.3 %collective-permute-start.1 = (bf16[8,3328]{1,0:T(8,128)(2,1)S(1)}, bf16[8,3328]{1,0:T(8,128)(2,1)S(1)}, u32[]{:S(2)}, u32[]{:S(2)}) collective-permute-start(bf16[8,3328]{1,0:T(8,128)(2,1)S(1)} %convert_element_type.89), channel_id=1, source_target_pairs={{4,0},{8,4},{12,8},{16,12},{20,16},{24,20},{28,24},{32,28},{36,32}... | collective-permute-start | bytes 159752 | tf_op jit(solution)/shard_map/ppermute | solution.py:1400
  (68 other events, 384.2 us)

commit v3 on v2

--- a/solution.py
+++ b/solution.py
@@ -32,8 +32,13 @@
 
 MESH_ID = pl.DeviceIdType.MESH
 RS_ORDERS = (("x", "y", "z"), ("y", "z", "x"), ("z", "x", "y"))
-RS_STEPS = 9
+RS_COUNTS = (5, 4, 4)
+RS_FIRST = (0, 5, 9)
+RS_SLOTS = 13
 RS_COLS = 512
+RS_LAGS = 6
+RS_TIMES = max(RS_COUNTS) + RS_LAGS - 1
+NEIGHBOURS = [("c", 1)] + [(axis, o) for axis in ("x", "y", "z") for o in (1, 2, 3)]
 
 
 def ring(axis, offset):
@@ -46,6 +51,10 @@
     for target in targets:
         pl.semaphore_signal(barrier, inc=1, device_id=target, device_id_type=MESH_ID)
     pl.semaphore_wait(barrier, len(targets))
+
+
+def greet_neighbours():
+    greet([{axis: ring(axis, o)} for axis, o in NEIGHBOURS])
 
 
 def remote(src, dst, send_sem, recv_sem, target):
@@ -63,25 +72,202 @@
     return jnp.dot(left, right, preferred_element_type=jnp.float32)
 
 
-def grad_sum_kernel(
-    a_ref, b_ref, taps_ref, gain_ref, norm_ref, post_ref, heads_ref, router_ref, out_ref, small_ref,
-    core_out, core_in, near, far, second_in, third_out, third_in, lines,
-    core_ss, core_rs, near_ss, near_rs, far_ss, far_rs, second_ss, second_rs, third_ss, third_rs,
-    pack, pack_in, pack_work, pack_others, pack_ss, pack_rs,
-):
+def grad_sum_scratch(rows):
+    half, block, low = rows // 2, rows // 8, jnp.bfloat16
+    sems = lambda *shape: [pltpu.SemaphoreType.DMA(shape)] * 2
+    return [
+        pltpu.VMEM((2, 3, half, RS_COLS), low),
+        pltpu.VMEM((RS_SLOTS, half, RS_COLS), low),
+        pltpu.VMEM((RS_SLOTS, 4, block // 2, RS_COLS), low),
+        pltpu.VMEM((RS_SLOTS, 2, block // 2, RS_COLS), low),
+        pltpu.VMEM((RS_SLOTS, 3, block // 4, RS_COLS), low),
+        pltpu.VMEM((RS_SLOTS, 4, 16, RS_COLS), low),
+        pltpu.VMEM((RS_SLOTS, 3, 16, RS_COLS), low),
+        pltpu.VMEM((3, block // 4 + 8, RS_COLS), jnp.float32),
+        *sems(RS_SLOTS), *sems(RS_SLOTS, 4), *sems(RS_SLOTS, 2), *sems(RS_SLOTS, 3), *sems(RS_SLOTS, 3),
+    ]
+
+
+def grad_sum_steps(scratch, left_of, right_of, store):
+    core_out, core_in, near, far, second_in, third_out, third_in, lines = scratch[:8]
+    core_ss, core_rs, near_ss, near_rs, far_ss, far_rs, second_ss, second_rs, third_ss, third_rs = scratch[8:]
     me_core = lax.axis_index("c")
     other = 1 - me_core
     half = core_out.shape[2]
     block = half // 4
     edge = block // 2
     small = block // 4
-    unit = out_ref.shape[0]
+    unit = third_out.shape[2]
     kept = small // 4
     lines[...] = jnp.zeros_like(lines)
-    greet(
-        [{"c": other}]
-        + [{axis: ring(axis, o)} for axis in ("x", "y", "z") for o in (1, 2, 3)]
-    )
+
+    def core_copy(part, k):
+        slot = RS_FIRST[part] + k
+        return remote(
+            core_out.at[lax.rem(k, 2), part], core_in.at[slot],
+            core_ss.at[slot], core_rs.at[slot], {"c": other},
+        )
+
+    def near_copies(part, k):
+        slot = RS_FIRST[part] + k
+        axis = RS_ORDERS[part][0]
+        after, before, across = ring(axis, 1), ring(axis, -1), ring(axis, 2)
+        plan = ((before, 0, before), (after, edge, after), (across, 0, after), (across, edge, before))
+        return [
+            remote(
+                core_in.at[slot, pl.ds(which * block + offset, edge)], near.at[slot, n],
+                near_ss.at[slot, n], near_rs.at[slot, n], {axis: target},
+            )
+            for n, (which, offset, target) in enumerate(plan)
+        ]
+
+    def far_copies(part, k):
+        slot = RS_FIRST[part] + k
+        axis = RS_ORDERS[part][0]
+        return [
+            remote(
+                near.at[slot, 2 + n], far.at[slot, n],
+                far_ss.at[slot, n], far_rs.at[slot, n], {axis: ring(axis, o)},
+            )
+            for n, o in enumerate((1, -1))
+        ]
+
+    def second_copies(part, k):
+        slot = RS_FIRST[part] + k
+        axis = RS_ORDERS[part][1]
+        copies = []
+        for o in (1, 2, 3):
+            target = ring(axis, o)
+            copies.append(
+                remote(
+                    near.at[slot, target // 2, pl.ds(lax.rem(target, 2) * small, small)],
+                    second_in.at[slot, o - 1],
+                    second_ss.at[slot, o - 1], second_rs.at[slot, o - 1], {axis: target},
+                )
+            )
+        return copies
+
+    def third_copies(part, k):
+        slot = RS_FIRST[part] + k
+        axis = RS_ORDERS[part][2]
+        return [
+            remote(
+                third_out.at[slot, ring(axis, o)], third_in.at[slot, o - 1],
+                third_ss.at[slot, o - 1], third_rs.at[slot, o - 1], {axis: ring(axis, o)},
+            )
+            for o in (1, 2, 3)
+        ]
+
+    def stage_product(part, k):
+        @pl.when(k >= 2)
+        def _():
+            core_copy(part, k - 2).wait_send()
+
+        left = left_of(part, k, other)
+        for col in range(0, RS_COLS, 256):
+            core_out[lax.rem(k, 2), part, :, col : col + 256] = dot32(left, right_of(part, k, col)).astype(jnp.bfloat16)
+        core_copy(part, k).start()
+
+    def stage_near(part, k):
+        slot = RS_FIRST[part] + k
+        core_copy(part, k).wait_recv()
+        left = left_of(part, k, me_core)
+        for col in range(0, RS_COLS, 256):
+            mine = dot32(left, right_of(part, k, col))
+            theirs = core_in[slot, :, col : col + 256].astype(jnp.float32)
+            core_in[slot, :, col : col + 256] = (mine + theirs).astype(jnp.bfloat16)
+        for copy in near_copies(part, k):
+            copy.start()
+
+    def load(ref, *where):
+        return ref[where].astype(jnp.float32)
+
+    def stage_far(part, k):
+        slot = RS_FIRST[part] + k
+        axis = RS_ORDERS[part][0]
+        copies = near_copies(part, k)
+        for n, (which, offset) in enumerate(((ring(axis, 1), 0), (ring(axis, -1), edge))):
+            copies[2 + n].wait_recv()
+            rows = pl.ds(pl.multiple_of(which * block + offset, edge), edge)
+            near[slot, 2 + n] = (load(near, slot, 2 + n) + load(core_in, slot, rows)).astype(jnp.bfloat16)
+        for copy in far_copies(part, k):
+            copy.start()
+
+    def stage_second(part, k):
+        slot = RS_FIRST[part] + k
+        me = lax.axis_index(RS_ORDERS[part][0])
+        copies, far_in = near_copies(part, k), far_copies(part, k)
+        for n in range(2):
+            copies[n].wait_recv()
+            far_in[n].wait_recv()
+            rows = pl.ds(pl.multiple_of(me * block + n * edge, edge), edge)
+            near[slot, n] = (
+                load(near, slot, n) + load(far, slot, n) + load(core_in, slot, rows)
+            ).astype(jnp.bfloat16)
+        for copy in second_copies(part, k):
+            copy.start()
+
+    def stage_third(part, k):
+        slot = RS_FIRST[part] + k
+        me = lax.axis_index(RS_ORDERS[part][1])
+        for copy in second_copies(part, k):
+            copy.wait_recv()
+        rows = pl.ds(pl.multiple_of(lax.rem(me, 2) * small, small), small)
+        lines[part, :small] = load(near, slot, me // 2, rows) + (
+            load(second_in, slot, 0) + load(second_in, slot, 1) + load(second_in, slot, 2)
+        )
+        for j in range(4):
+            third_out[slot, j] = lines[part, kept * j : kept * j + unit].astype(jnp.bfloat16)
+        for copy in third_copies(part, k):
+            copy.start()
+
+    def stage_last(part, k):
+        slot = RS_FIRST[part] + k
+        for copy in third_copies(part, k):
+            copy.wait_recv()
+        me = lax.axis_index(RS_ORDERS[part][2])
+        total = load(third_out, slot, me) + (
+            load(third_in, slot, 0) + load(third_in, slot, 1) + load(third_in, slot, 2)
+        )
+        store(part, k, total)
+
+    stages = (stage_product, stage_near, stage_far, stage_second, stage_third, stage_last)
+
+    def step(t):
+        for lag, stage in enumerate(stages):
+            k = t - lag
+            for count in sorted(set(RS_COUNTS)):
+                @pl.when((k >= 0) & (k < count))
+                def _():
+                    for part in range(3):
+                        if RS_COUNTS[part] == count:
+                            stage(part, k)
+
+    def finish():
+        for part in range(3):
+            def wait_sent(k, carry, part=part):
+                @pl.when(k >= RS_COUNTS[part] - 2)
+                def _():
+                    core_copy(part, k).wait_send()
+
+                for copies in (near_copies, far_copies, second_copies, third_copies):
+                    for copy in copies(part, k):
+                        copy.wait_send()
+                return carry
+
+            lax.fori_loop(0, RS_COUNTS[part], wait_sent, 0)
+
+    return step, finish
+
+
+def grad_sum_kernel(
+    lefts_ref, rights_ref, taps_ref, gain_ref, norm_ref, post_ref, heads_ref, router_ref, out_ref, small_ref, *scratch
+):
+    *sum_scratch, pack, pack_in, pack_work, pack_others, pack_ss, pack_rs = scratch
+    me_core = lax.axis_index("c")
+    other = 1 - me_core
+    half = lefts_ref.shape[1] // 2
+    greet_neighbours()
 
     taps_width, wide = taps_ref.shape[1], pack.shape[1] // 2
     pack[:, :taps_width] = taps_ref[...]
@@ -133,369 +319,299 @@
                 for copy in pack_copies(n):
                     copy.wait_send()
 
-    def left_of(part, k):
-        if part == 0:
-            return 0
-        if part == 1:
-            return 1 + k // 4
-        return 4 + k // 3
-
-    def core_copy(part, k):
-        slot = part * RS_STEPS + k
-        return remote(
-            core_out.at[lax.rem(k, 2), part], core_in.at[slot],
-            core_ss.at[slot], core_rs.at[slot], {"c": other},
-        )
-
-    def near_copies(part, k):
-        slot = part * RS_STEPS + k
-        axis = RS_ORDERS[part][0]
-        after, before, across = ring(axis, 1), ring(axis, -1), ring(axis, 2)
-        plan = ((before, 0, before), (after, edge, after), (across, 0, after), (across, edge, before))
-        return [
-            remote(
-                core_in.at[slot, pl.ds(which * block + offset, edge)], near.at[slot, n],
-                near_ss.at[slot, n], near_rs.at[slot, n], {axis: target},
-            )
-            for n, (which, offset, target) in enumerate(plan)
-        ]
-
-    def far_copies(part, k):
-        slot = part * RS_STEPS + k
-        axis = RS_ORDERS[part][0]
-        return [
-            remote(
-                near.at[slot, 2 + n], far.at[slot, n],
-                far_ss.at[slot, n], far_rs.at[slot, n], {axis: ring(axis, o)},
-            )
-            for n, o in enumerate((1, -1))
-        ]
-
-    def second_copies(part, k):
-        slot = part * RS_STEPS + k
-        axis = RS_ORDERS[part][1]
-        copies = []
-        for o in (1, 2, 3):
-            target = ring(axis, o)
-            copies.append(
-                remote(
-                    near.at[slot, target // 2, pl.ds(lax.rem(target, 2) * small, small)],
-                    second_in.at[slot, o - 1],
-                    second_ss.at[slot, o - 1], second_rs.at[slot, o - 1], {axis: target},
-                )
-            )
-        return copies
-
-    def third_copies(part, k):
-        slot = part * RS_STEPS + k
-        axis = RS_ORDERS[part][2]
-        return [
-            remote(
-                third_out.at[slot, ring(axis, o)], third_in.at[slot, o - 1],
-                third_ss.at[slot, o - 1], third_rs.at[slot, o - 1], {axis: ring(axis, o)},
-            )
-            for o in (1, 2, 3)
-        ]
-
-    def stage_product(part, k):
-        slot = part * RS_STEPS + k
-
-        @pl.when(k >= 2)
+    def left_of(part, k, which):
+        return lefts_ref[part, pl.ds(pl.multiple_of(which * half, half), half), :]
+
+    def right_of(part, k, col):
+        return rights_ref[:, pl.ds(pl.multiple_of((RS_FIRST[part] + k) * RS_COLS + col, 256), 256)]
+
+    whole = out_ref.shape[1] // RS_COLS
+    rows = out_ref.shape[0]
+
+    def store(part, k, total):
+        chunk = RS_FIRST[part] + k
+
+        @pl.when(chunk < whole)
         def _():
-            core_copy(part, k - 2).wait_send()
-
-        left = a_ref[left_of(part, k), pl.ds(pl.multiple_of(other * half, half), half), :]
-        for col in range(0, RS_COLS, 256):
-            core_out[lax.rem(k, 2), part, :, col : col + 256] = dot32(
-                left, b_ref[:, pl.ds(pl.multiple_of(slot * RS_COLS + col, 256), 256)]
-            ).astype(jnp.bfloat16)
-        core_copy(part, k).start()
-
-    def stage_near(part, k):
-        slot = part * RS_STEPS + k
-        core_copy(part, k).wait_recv()
-
-        left = a_ref[left_of(part, k), pl.ds(pl.multiple_of(me_core * half, half), half), :]
-        for col in range(0, RS_COLS, 256):
-            mine = dot32(left, b_ref[:, pl.ds(pl.multiple_of(slot * RS_COLS + col, 256), 256)])
-            theirs = core_in[slot, :, col : col + 256].astype(jnp.float32)
-            core_in[slot, :, col : col + 256] = (mine + theirs).astype(jnp.bfloat16)
-        for copy in near_copies(part, k):
-            copy.start()
-
-    def load(ref, *where):
-        return ref[where].astype(jnp.float32)
-
-    def stage_far(part, k):
-        slot = part * RS_STEPS + k
-        axis = RS_ORDERS[part][0]
-        copies = near_copies(part, k)
-        for n, (which, offset) in enumerate(((ring(axis, 1), 0), (ring(axis, -1), edge))):
-            copies[2 + n].wait_recv()
-            rows = pl.ds(pl.multiple_of(which * block + offset, edge), edge)
-            near[slot, 2 + n] = (load(near, slot, 2 + n) + load(core_in, slot, rows)).astype(jnp.bfloat16)
-        for copy in far_copies(part, k):
-            copy.start()
-
-    def stage_second(part, k):
-        slot = part * RS_STEPS + k
-        me = lax.axis_index(RS_ORDERS[part][0])
-        copies, far_in = near_copies(part, k), far_copies(part, k)
-        for n in range(2):
-            copies[n].wait_recv()
-            far_in[n].wait_recv()
-            rows = pl.ds(pl.multiple_of(me * block + n * edge, edge), edge)
-            near[slot, n] = (
-                load(near, slot, n) + load(far, slot, n) + load(core_in, slot, rows)
-            ).astype(jnp.bfloat16)
-        for copy in second_copies(part, k):
-            copy.start()
-
-    def stage_third(part, k):
-        slot = part * RS_STEPS + k
-        me = lax.axis_index(RS_ORDERS[part][1])
-        for copy in second_copies(part, k):
-            copy.wait_recv()
-        rows = pl.ds(pl.multiple_of(lax.rem(me, 2) * small, small), small)
-        lines[part, :small] = load(near, slot, me // 2, rows) + (
-            load(second_in, slot, 0) + load(second_in, slot, 1) + load(second_in, slot, 2)
-        )
-        for j in range(4):
-            third_out[slot, j] = lines[part, kept * j : kept * j + unit].astype(jnp.bfloat16)
-        for copy in third_copies(part, k):
-            copy.start()
-
-    def stage_last(part, k):
-        slot = part * RS_STEPS + k
-        for copy in third_copies(part, k):
-            copy.wait_recv()
-        me = lax.axis_index(RS_ORDERS[part][2])
-        out_ref[:, pl.ds(pl.multiple_of(slot * RS_COLS, RS_COLS), RS_COLS)] = load(
-            third_out, slot, me
-        ) + (load(third_in, slot, 0) + load(third_in, slot, 1) + load(third_in, slot, 2))
-
-    stages = (stage_product, stage_near, stage_far, stage_second, stage_third, stage_last)
-
-    def step(t, carry):
+            out_ref[:, pl.ds(pl.multiple_of(chunk * RS_COLS, RS_COLS), RS_COLS)] = total[:rows]
+
+        if part == 2:
+            @pl.when(chunk == whole)
+            def _():
+                out_ref[:, whole * RS_COLS :] = total[:rows, : out_ref.shape[1] - whole * RS_COLS]
+
+    step, finish = grad_sum_steps(sum_scratch, left_of, right_of, store)
+
+    def run(t, carry):
         for s in range(6):
             @pl.when(t == s)
             def _():
                 pack_step(s)
 
-        for lag, stage in enumerate(stages):
-            k = t - lag
-
-            @pl.when((k >= 0) & (k < RS_STEPS))
-            def _():
-                for part in range(3):
-                    stage(part, k)
-
+        step(t)
         return carry
 
-    lax.fori_loop(0, RS_STEPS + len(stages) - 1, step, 0)
-
-    def finish(k, carry):
-        for part in range(3):
-            @pl.when(k >= RS_STEPS - 2)
-            def _():
-                core_copy(part, k).wait_send()
-
-            for copies in (near_copies, far_copies, second_copies, third_copies):
-                for copy in copies(part, k):
-                    copy.wait_send()
-        return carry
-
-    lax.fori_loop(0, RS_STEPS, finish, 0)
-
-
-def grad_sum(lefts, rights, taps, gain, norm, post, heads, router):
-    cols, slots, depth = RS_COLS, rights.shape[1] // RS_COLS, rights.shape[0]
+    lax.fori_loop(0, RS_TIMES, run, 0)
+    finish()
+
+
+def grad_sum(lefts, rights, columns, taps, gain, norm, post, heads, router):
     rows = lefts.shape[1]
-    half = rows // 2
-    block = half // 4
-    low = jnp.bfloat16
     wide = taps.shape[1] + router.shape[1]
     space = pl.BlockSpec(memory_space=pltpu.VMEM)
-    sems = lambda *shape: pltpu.SemaphoreType.DMA(shape)
     return pl.pallas_call(
         grad_sum_kernel,
         out_shape=(
-            jax.ShapeDtypeStruct((16, slots * cols), jnp.float32),
+            jax.ShapeDtypeStruct((rows // 128, columns), jnp.float32),
             jax.ShapeDtypeStruct((8, wide), jnp.float32),
         ),
         in_specs=[space] * 8,
         out_specs=(space, space),
-        scratch_shapes=[
-            pltpu.VMEM((2, 3, half, cols), low),
-            pltpu.VMEM((slots, half, cols), low),
-            pltpu.VMEM((slots, 4, block // 2, cols), low),
-            pltpu.VMEM((slots, 2, block // 2, cols), low),
-            pltpu.VMEM((slots, 3, block // 4, cols), low),
-            pltpu.VMEM((slots, 4, 16, cols), low),
-            pltpu.VMEM((slots, 3, 16, cols), low),
-            pltpu.VMEM((3, block // 4 + 8, cols), jnp.float32),
-            sems(slots), sems(slots), sems(slots, 4), sems(slots, 4), sems(slots, 2), sems(slots, 2),
-            sems(slots, 3), sems(slots, 3), sems(slots, 3), sems(slots, 3),
+        scratch_shapes=grad_sum_scratch(rows)
+        + [
             pltpu.VMEM((8, wide), jnp.float32),
             pltpu.VMEM((8, wide // 2), jnp.float32),
             pltpu.VMEM((4, 8, wide // 2), jnp.float32),
             pltpu.VMEM((3, 3, 8, wide // 2), jnp.float32),
-            sems(5, 4), sems(5, 4),
+            pltpu.SemaphoreType.DMA((5, 4)),
+            pltpu.SemaphoreType.DMA((5, 4)),
         ],
         compiler_params=pltpu.CompilerParams(
-            collective_id=0, has_side_effects=True, vmem_limit_bytes=61 * 2**20
+            collective_id=0, has_side_effects=True, vmem_limit_bytes=58 * 2**20
         ),
-        cost_estimate=pl.CostEstimate(flops=2 * slots * rows * depth * cols, bytes_accessed=8 * 2**20, transcendentals=0),
         name="grad_sum",
     )(lefts, rights, taps, gain, norm, post, heads, router)
 
 
-def plane_spot(position):
-    return {"x": position // 8, "y": lax.rem(position // 2, 4), "c": lax.rem(position, 2)}
-
-
-def state_exchange(
-    reverse, state_ref, totals_ref, rows_ref, out_ref, decays_ref, all_rows, rows_sum, got, back, ss, rs, ts, tr, bs, br
-):
-    spots = 32
-    me = lax.axis_index("x") * 8 + lax.axis_index("y") * 2 + lax.axis_index("c")
-    heads = got.shape[1]
-    barrier = pltpu.get_barrier_semaphore()
-
-    def spot(o):
-        return lax.rem(me + o, spots)
-
-    def share(ref, position):
-        return ref.at[pl.ds(heads * (position // 2), heads), lax.rem(position, 2)]
-
-    def knock(o, carry):
-        pl.semaphore_signal(barrier, inc=1, device_id=plane_spot(spot(o)), device_id_type=MESH_ID)
-        return carry
-
-    lax.fori_loop(1, spots, knock, 0)
-    sides = (1, 3, 2)
-    for o in sides:
-        pl.semaphore_signal(barrier, inc=1, device_id={"z": ring("z", o)}, device_id_type=MESH_ID)
-    pl.semaphore_wait(barrier, spots - 1 + len(sides))
-    me_z = lax.axis_index("z")
+LEFT_SOURCES = (("shared", 0), ("hidden", 0), ("gated_0", 1), ("hidden", 1), ("gated_1", 2), ("hidden", 2))
+
+
+def owner_moves(order, stride, offset, rows):
+    moves = []
+    for to in range(128):
+        digits = {"c": to // 64}
+        for axis, at in zip(order, (to // 16 % 4, to // 4 % 4, to % 4)):
+            digits[axis] = at
+        owner = ((digits["x"] * 4 + digits["y"]) * 2 + digits["c"]) * 4 + digits["z"]
+        source, target = owner * stride + offset, to * 12
+        if moves and moves[-1][0] + moves[-1][2] == source and moves[-1][1] + moves[-1][2] == target:
+            moves[-1][2] += rows
+        else:
+            moves.append([source, target, rows])
+    return moves
+
+
+def lefts_kernel(first_ref, second_ref, gated_ref, hidden_ref, early_ref, late_ref, turned, sorted_rows):
+    def turn(ref):
+        for j in range(ref.shape[1] // TILE):
+            turned[j * TILE : (j + 1) * TILE] = ref[:, j * TILE : (j + 1) * TILE].astype(jnp.float32).T
+
+    def place(out_ref, at, order, stride, offset, rows):
+        if rows < 12:
+            sorted_rows[...] = jnp.zeros_like(sorted_rows)
+        for source, target, size in owner_moves(order, stride, offset, rows):
+            sorted_rows[target : target + size] = turned[source : source + size]
+        out_ref[at] = sorted_rows[...].astype(jnp.bfloat16)
+
+    turn(first_ref)
+    for part in range(3):
+        place(late_ref, part, RS_ORDERS[part], 12, 0, 12)
+    turn(second_ref)
+    place(early_ref, 0, RS_ORDERS[0], 12, 0, 12)
+    turn(hidden_ref)
+    for at, part in ((1, 0), (3, 1), (5, 2)):
+        place(early_ref, at, RS_ORDERS[part], 8, 0, 8)
+    turn(gated_ref)
+    place(early_ref, 2, RS_ORDERS[1], 24, 0, 12)
+    place(early_ref, 4, RS_ORDERS[2], 24, 12, 12)
+
+
+def state_exchange(reverse, state_ref, totals_ref, rows_ref, out_ref, *refs):
+    if reverse:
+        rows_sum, all_rows, *refs = refs
+    else:
+        all_rows, *refs = refs
+    pair_in, pair_totals, outgoing, got, back, mine, hand, ps, pr, ss, rs, bs, br, zs, zr = refs
+    x, y, c, z = (lax.axis_index(a) for a in ALL)
+    chip = x * 4 + y
+    half = pair_in.shape[0]
+    groups, size = back.shape[1:3]
+    others = [(dx, dy) for dx in range(4) for dy in range(4) if dx + dy]
+
+    def far(dx, dy):
+        tx, ty = lax.rem(x + dx, 4), lax.rem(y + dy, 4)
+        return tx * 4 + ty, {"x": tx, "y": ty}
+
+    greet([{"c": 1 - c}] + [{"z": ring("z", o)} for o in (1, 2, 3)] + [far(*d)[1] for d in others])
+    mine_at, theirs_at = c * half, (1 - c) * half
+
+    def pair_copies():
+        return [
+            remote(state_ref.at[pl.ds(theirs_at, half)], pair_in, ps.at[0], pr.at[0], {"c": 1 - c}),
+            remote(totals_ref, pair_totals, ps.at[1], pr.at[1], {"c": 1 - c}),
+        ]
+
+    def out_copy(dx, dy):
+        target, where = far(dx, dy)
+        at = dx * 4 + dy
+        return remote(outgoing.at[target], got.at[chip], ss.at[at], rs.at[at], where)
+
+    def back_copy(dx, dy):
+        target, where = far(dx, dy)
+        at = dx * 4 + dy
+        return remote(back.at[target], mine.at[pl.ds(groups * chip, groups)], bs.at[at], br.at[at], where)
+
+    def hand_copy():
+        return remote(hand, out_ref.at[pl.ds(mine_at, half)], ps.at[2], pr.at[2], {"c": 1 - c})
+
     row_copies = []
-    for o in sides:
+    for o in (1, 3, 2):
         source = rows_ref.at[ring("z", o)] if reverse else rows_ref
-        target = all_rows.at[o - 1] if reverse else all_rows.at[me_z]
-        row_copies.append(remote(source, target, ts.at[o + 32], tr.at[o + 32], {"z": ring("z", o)}))
-
-    def out_copy(o):
-        target = spot(o)
-        return remote(share(state_ref, target), got.at[me], ss.at[o], rs.at[o], plane_spot(target))
-
-    def total_copy(o):
-        return remote(totals_ref, decays_ref.at[me], ts.at[o], tr.at[o], plane_spot(spot(o)))
-
-    def back_copy(o):
-        target = spot(o)
-        return remote(back.at[target], share(out_ref, me), bs.at[o], br.at[o], plane_spot(target))
-
-    def send(o, carry):
-        if not reverse:
-            total_copy(o).start()
-        out_copy(o).start()
-        return carry
-
-    lax.fori_loop(1, spots, send, 0)
+        target = all_rows.at[o - 1] if reverse else all_rows.at[z]
+        row_copies.append(remote(source, target, zs.at[o], zr.at[o], {"z": ring("z", o)}))
+    for copy in pair_copies():
+        copy.start()
     for copy in row_copies:
         copy.start()
     if not reverse:
-        all_rows[me_z] = rows_ref[...]
-    mine = pl.ds(heads * (me // 2), heads)
-    got[me] = state_ref[mine, lax.rem(me, 2)]
-    if not reverse:
-        decays_ref[me] = totals_ref[...]
-
-    def arrive(o, carry):
-        if not reverse:
-            total_copy(o).wait_recv()
-        out_copy(o).wait_recv()
+        all_rows[z] = rows_ref[...]
+    for copy in pair_copies():
+        copy.wait_recv()
+    first = jnp.where(c == 0, totals_ref[...], pair_totals[...])
+    second = jnp.where(c == 0, pair_totals[...], totals_ref[...])
+    inner, outer = (first, second) if reverse else (second, first)
+    lanes = lax.broadcasted_iota(jnp.int32, (8, TILE), 1) - c * (half // 2)
+
+    def decay(logs, head):
+        return jnp.exp(jnp.sum(jnp.where(lanes[: logs.shape[0]] == head, logs, 0.0), 1, keepdims=True))[:1]
+
+    def states(g):
+        own, other = state_ref[mine_at + g].astype(jnp.float32), pair_in[g].astype(jnp.float32)
+        return jnp.where(c == 0, own, other), jnp.where(c == 0, other, own)
+
+    total = (first + second)[:1]
+    high = total.astype(jnp.bfloat16).astype(jnp.float32)
+    middle = (total - high).astype(jnp.bfloat16).astype(jnp.float32)
+    row = lax.broadcasted_iota(jnp.int32, (16, TILE), 0)
+    split = jnp.where(row == 0, high, jnp.where(row == 1, middle, jnp.where(row == 2, total - high - middle, 0.0)))
+    split = split.astype(jnp.bfloat16)
+
+    def combine(m, carry):
+        for i in range(groups):
+            g = groups * m + i
+            early, late = states(g)
+            rate = decay(inner, g // 2)
+            pair = early + rate * late if reverse else rate * early + late
+            outgoing[m, i * size : (i + 1) * size] = pair.astype(jnp.bfloat16)
+        outgoing[m, groups * size :] = split
         return carry
 
-    lax.fori_loop(1, spots, arrive, 0)
-    source = totals_ref if reverse else decays_ref
-    lanes = lax.broadcasted_iota(jnp.int32, (8, 128), 1) - heads * (me // 2)
+    lax.fori_loop(0, 16, combine, 0)
+    for d in others:
+        out_copy(*d).start()
+    got[chip] = outgoing[chip]
+    for d in others:
+        out_copy(*d).wait_recv()
 
     def advance(step, carried):
-        p = spots - 1 - step if reverse else step
-        logs = source[p]
+        p = 15 - step if reverse else step
+        logs = jnp.sum(got[p, groups * size :].astype(jnp.float32), 0, keepdims=True)
         new = []
-        for h in range(heads):
-            back[p, h] = carried[h].astype(back.dtype)
-            decay = jnp.exp(jnp.sum(jnp.where(lanes == h, logs, 0.0), 1, keepdims=True))[:1]
-            new.append(carried[h] * decay + got[p, h].astype(jnp.float32))
+        for i in range(groups):
+            back[p, i] = carried[i].astype(back.dtype)
+            here = got[p, i * size : (i + 1) * size].astype(jnp.float32)
+            new.append(carried[i] * decay(logs, (groups * chip + i) // 2) + here)
         return tuple(new)
 
-    zero = jnp.zeros(got.shape[2:], jnp.float32)
-    lax.fori_loop(0, spots, advance, (zero,) * heads)
-
-    def send_back(o, carry):
-        back_copy(o).start()
+    lax.fori_loop(0, 16, advance, (jnp.zeros((size, TILE), jnp.float32),) * groups)
+    for d in others:
+        back_copy(*d).start()
+    mine[pl.ds(groups * chip, groups)] = back[chip]
+    for d in others:
+        back_copy(*d).wait_recv()
+
+    def spread(h, carry):
+        rate = decay(outer, h)
+        for i in range(2):
+            g = 2 * h + i
+            early, late = states(g)
+            near = mine[g].astype(jnp.float32)
+            beyond = rate * near + (late if reverse else early)
+            swap = (c == 1) if reverse else (c == 0)
+            out_ref[mine_at + g] = jnp.where(swap, near, beyond).astype(out_ref.dtype)
+            hand[g] = jnp.where(swap, beyond, near).astype(hand.dtype)
         return carry
 
-    lax.fori_loop(1, spots, send_back, 0)
-    out_ref[mine, lax.rem(me, 2)] = back[me]
-
-    def finish(o, carry):
-        back_copy(o).wait_recv()
-        back_copy(o).wait_send()
-        out_copy(o).wait_send()
-        if not reverse:
-            total_copy(o).wait_send()
-        return carry
-
-    lax.fori_loop(1, spots, finish, 0)
+    lax.fori_loop(0, half // 2, spread, 0)
+    hand_copy().start()
     for copy in row_copies:
         copy.wait()
     if reverse:
-        add_parts(rows_ref, me_z, all_rows, rows_sum)
-
-
-def scan_forward_kernel(state_ref, totals_ref, rows_ref, out_ref, decays_ref, all_rows, *scratch):
-    state_exchange(False, state_ref, totals_ref, rows_ref, out_ref, decays_ref, all_rows, None, *scratch)
-
-
-def scan_backward_kernel(state_ref, decays_ref, parts_ref, out_ref, rows_sum, got_parts, *scratch):
-    state_exchange(True, state_ref, decays_ref, parts_ref, out_ref, None, got_parts, rows_sum, *scratch)
-
-
-def carried_states(state, logs, rows):
+        add_parts(rows_ref, z, all_rows, rows_sum)
+    hand_copy().wait()
+    for copy in pair_copies():
+        copy.wait_send()
+    for d in others:
+        out_copy(*d).wait_send()
+        back_copy(*d).wait_send()
+
+
+def add_parts(ref, me, got, out):
+    def rows_at(j, carry):
+        rows = pl.ds(pl.multiple_of(j * 32, 32), 32)
+        total = ref[me, rows].astype(jnp.float32)
+        for o in range(3):
+            total = total + got[o, rows].astype(jnp.float32)
+        out[rows] = total
+        return carry
+
+    lax.fori_loop(0, out.shape[0] // 32, rows_at, 0)
+
+
+def scan_forward_kernel(*refs):
+    state_exchange(False, *refs)
+
+
+def scan_backward_kernel(*refs):
+    state_exchange(True, *refs)
+
+
+def carried_states(state, totals, rows):
     reverse = rows.ndim == 3
-    heads, size, width = state.shape
-    share = (heads // 16, size // 2, width)
-    state = state.astype(jnp.bfloat16).reshape(heads, 2, size // 2, width)
-    sem = pltpu.SemaphoreType.DMA((32,))
-    out_shape = jax.ShapeDtypeStruct(state.shape, jnp.bfloat16)
+    low = jnp.bfloat16
+    pairs = state.shape
+    state = state.reshape(96, 32, TILE)
     space = pl.BlockSpec(memory_space=pltpu.VMEM)
-    kept = jax.ShapeDtypeStruct((32, 8, 128), jnp.float32)
-    args = (state, logs, rows)
+    outs = [jax.ShapeDtypeStruct(state.shape, low)]
+    extra = []
     if reverse:
-        outs = [out_shape, jax.ShapeDtypeStruct(rows.shape[1:], jnp.float32)]
-        extra = [pltpu.VMEM((3, *rows.shape[1:]), rows.dtype)]
+        outs.append(jax.ShapeDtypeStruct(rows.shape[1:], jnp.float32))
+        extra.append(pltpu.VMEM((3, *rows.shape[1:]), rows.dtype))
     else:
-        outs = [out_shape, kept, jax.ShapeDtypeStruct((4, *rows.shape), rows.dtype)]
-        extra = []
+        outs.append(jax.ShapeDtypeStruct((4, *rows.shape), rows.dtype))
+    sem = pltpu.SemaphoreType.DMA
     result = pl.pallas_call(
         scan_backward_kernel if reverse else scan_forward_kernel,
         out_shape=tuple(outs),
-        in_specs=[space] * len(args),
-        out_specs=(space,) * len(outs),
+        in_specs=[space] * 3,
+        out_specs=(space,) * 2,
         scratch_shapes=extra
-        + [pltpu.VMEM((32, *share), jnp.bfloat16)] * 2
-        + [sem] * 2
-        + [pltpu.SemaphoreType.DMA((36,))] * 2
-        + [sem] * 2,
+        + [
+            pltpu.VMEM((48, 32, TILE), low),
+            pltpu.VMEM((8, TILE), jnp.float32),
+            pltpu.VMEM((16, 112, TILE), low),
+            pltpu.VMEM((16, 112, TILE), low),
+            pltpu.VMEM((16, 3, 32, TILE), low),
+            pltpu.VMEM((48, 32, TILE), low),
+            pltpu.VMEM((48, 32, TILE), low),
+            sem((3,)), sem((3,)), sem((16,)), sem((16,)), sem((16,)), sem((16,)), sem((4,)), sem((4,)),
+        ],
         compiler_params=pltpu.CompilerParams(
             collective_id=2 if reverse else 1, has_side_effects=True, vmem_limit_bytes=32 * 2**20
         ),
         name="scan_backward" if reverse else "scan_forward",
-    )(*args)
-    return (result[0].reshape(heads, size, width), *result[1:])
+    )(state, totals, rows)
+    return result[0].reshape(pairs), result[1]
 
 
 def z_gather_kernel(count, *refs):
@@ -537,22 +653,10 @@
 EXPERT_COLS = 256
 
 
-def add_parts(ref, me, got, out):
-    def rows_at(j, carry):
-        rows = pl.ds(pl.multiple_of(j * 32, 32), 32)
-        total = ref[me, rows].astype(jnp.float32)
-        for o in range(3):
-            total = total + got[o, rows].astype(jnp.float32)
-        out[rows] = total
-        return carry
-
-    lax.fori_loop(0, out.shape[0] // 32, rows_at, 0)
-
-
 def expert_sum_kernel(
     rows_ref, acts_ref, hidden_ref, grads_ref, back_ref, picks_ref,
     out_ref, back_sum, picks_all,
-    core_out, core_in, near, far, second_in, got,
+    core_out, core_in, near, far, second_in, got, turned_rows, turned_hidden,
     core_ss, core_rs, near_ss, near_rs, far_ss, far_rs, second_ss, second_rs, zs, zr,
 ):
     me_core = lax.axis_index("c")
@@ -582,6 +686,19 @@
     for copy in sums:
         copy.start()
     picks_all[me_z] = picks_ref[me_z]
+    for j in range(rows_ref.shape[1] // TILE):
+        turned_rows[j * TILE : (j + 1) * TILE] = rows_ref[:, j * TILE : (j + 1) * TILE].T
+    for part in range(2):
+        for j in range(hidden_ref.shape[2] // TILE):
+            turned_hidden[part, j * TILE : (j + 1) * TILE] = hidden_ref[part, :, j * TILE : (j + 1) * TILE].T
+
+    def plane_rows(part, which, load, size):
+        blocks = []
+        for j in range(4):
+            for i in range(4):
+                spot = (j * 4 + i if part == 0 else i * 4 + j) * 2 + which
+                blocks.append(load(pl.ds(pl.multiple_of(spot * size, 16), size)))
+        return jnp.concatenate(blocks, 0)
 
     def core_copy(part, k):
         slot = part * EXPERT_STEPS + k
@@ -637,13 +754,12 @@
         def _():
             right = acts_ref[part, :, pl.ds(pl.multiple_of(k * cols, cols), cols)]
 
-            at = pl.multiple_of(which_half * half, half)
-            store(0, half, dot32(rows_ref[part, pl.ds(at, half), :], right))
+            left = plane_rows(part, which_half, lambda rows: turned_rows[rows], small)
+            store(0, half, dot32(left, right))
 
         @pl.when(k >= 4)
         def _():
-            at = pl.multiple_of(which_half * (half // 3), half // 3)
-            left = hidden_ref[part, pl.ds(at, half // 3), :]
+            left = plane_rows(part, which_half, lambda rows: turned_hidden[part, rows], third)
             for t in range(3):
                 right = grads_ref[part, :, pl.ds(pl.multiple_of(t * 2 * cols + (k - 4) * cols, cols), cols)]
                 product = dot32(left, right)
@@ -764,6 +880,8 @@
             pltpu.VMEM((slots, 2, block // 2, cols), low),
             pltpu.VMEM((slots, 3, block // 4, cols), low),
             pltpu.VMEM((1, 3, *back.shape[1:]), low),
+            pltpu.VMEM(rows.shape[::-1], low),
+            pltpu.VMEM((2, *hidden.shape[:0:-1]), low),
             sems(slots), sems(slots), sems(slots, 4), sems(slots, 4), sems(slots, 2), sems(slots, 2),
             sems(slots, 3), sems(slots, 3), sems(3, 4), sems(3, 4),
         ],
@@ -1155,10 +1273,43 @@
 
 def mixer_back_kernel(
     proj_ref, tail_ref, halo_ref, cw_ref, heads_ref, mixed_ref, run_ref, step_ref, wide_ref,
-    carried_ref, result_ref, leaving_ref,
-    conv_ref, rim_ref, taps_ref, step_back_ref, heads_back_ref,
-    rows, column_sums, row_sums, kernel_back, maps_back, mixed_back, ext, padded,
+    carried_ref, result_ref, leaving_ref, lefts_ref, acts_ref, mix_ref, up_ref,
+    conv_ref, rim_ref, taps_ref, step_back_ref, heads_back_ref, shared_in_ref, out_ref, shared_out_ref,
+    rows, column_sums, row_sums, kernel_back, maps_back, mixed_back, ext, padded, rights, *sum_scratch,
 ):
+    greet_neighbours()
+    model = mix_ref.shape[1]
+    rights[:, : 4 * RS_COLS] = acts_ref[...]
+    for part in range(3):
+        at = (RS_FIRST[part] + RS_COUNTS[part] - 1) * RS_COLS
+        rights[:, at : at + RS_COLS] = up_ref[:, part * RS_COLS : (part + 1) * RS_COLS]
+        if part:
+            rights[:, at - model : at] = mix_ref[...]
+    share = lefts_ref.shape[1] // 2
+
+    def left_of(part, k, which):
+        n = k // 4 if part == 0 else 2 * part + k // 3
+        return lefts_ref[n, pl.ds(pl.multiple_of(which * share, share), share), :]
+
+    def right_of(part, k, col):
+        return rights[:, pl.ds(pl.multiple_of((RS_FIRST[part] + k) * RS_COLS + col, 256), 256)]
+
+    def store(part, k, total):
+        plain = RS_COUNTS[part] - 1
+
+        @pl.when(k < plain)
+        def _():
+            lanes = pl.ds(pl.multiple_of(k * RS_COLS, RS_COLS), RS_COLS)
+            if part == 0:
+                shared_in_ref[:, lanes] = total[:12]
+            else:
+                out_ref[12 * part - 12 : 12 * part, lanes] = total[:12]
+
+        @pl.when(k == plain)
+        def _():
+            shared_out_ref[:, part * RS_COLS : (part + 1) * RS_COLS] = total[:8]
+
+    sum_step, sum_finish = grad_sum_steps(sum_scratch, left_of, right_of, store)
     run, step = run_ref[...], step_ref[...]
     rows[0] = run.T
     rows[1] = step.T
@@ -1179,6 +1330,10 @@
     maps_back[...] = jnp.zeros_like(maps_back)
 
     def pair(p, carry):
+        @pl.when(lax.rem(p, 3) == 0)
+        def _():
+            sum_step(p // 3)
+
         lanes = tile_at(p)
         values, back = mixed_ref[:, lanes], result_ref[:, lanes]
         values_low, back_low = short(values), short(back)
@@ -1255,6 +1410,10 @@
     padded[8 + TILE : 16 + TILE] = jnp.zeros((8, TILE), jnp.float32)
 
     def conv(j, carry):
+        @pl.when(lax.rem(j, 13) == 0)
+        def _():
+            sum_step(8 + j // 13)
+
         lanes = tile_at(j)
         fill_ext(ext, halo_ref, proj_ref, j)
         u = taps_of(ext, cw_ref, lanes)
@@ -1274,17 +1433,21 @@
         return carry
 
     lax.fori_loop(0, CONV // TILE, conv, 0)
-
-
-def tile_call(kernel, outs, scratch, name, *args):
+    sum_finish()
+
+
+def tile_call(kernel, outs, scratch, name, *args, collective=None):
     space = pl.BlockSpec(memory_space=pltpu.VMEM)
+    params = dict(vmem_limit_bytes=40 * 2**20)
+    if collective is not None:
+        params = dict(vmem_limit_bytes=58 * 2**20, collective_id=collective, has_side_effects=True)
     return pl.pallas_call(
         kernel,
         out_shape=tuple(jax.ShapeDtypeStruct(s, d) for s, d in outs),
         in_specs=[space] * len(args),
         out_specs=(space,) * len(outs),
-        scratch_shapes=[pltpu.VMEM(s, jnp.float32) for s in scratch],
-        compiler_params=pltpu.CompilerParams(vmem_limit_bytes=40 * 2**20),
+        scratch_shapes=[pltpu.VMEM(s, jnp.float32) if isinstance(s, tuple) else s for s in scratch],
+        compiler_params=pltpu.CompilerParams(**params),
         name=name,
     )(*args)
 
@@ -1343,18 +1506,28 @@
     )(tokens, gain, *[main] * parts, tail)
 
 
-def project_back_kernel(back_ref, tail_back_ref, *refs):
-    *mains, tail_ref, tokens_ref, gain_ref, middle_ref, tokens_back_ref, gain_back_ref, total = refs
+def project_back_kernel(gate_ref, conv_ref, tail_back_ref, rim_ref, *refs):
+    *mains, tail_ref, tokens_ref, gain_ref, middle_ref, tokens_back_ref, gain_back_ref, back_ref, total = refs
     parts, width = len(mains), mains[0].shape[2]
     step = pl.program_id(0)
 
     @pl.when(step == 0)
     def _():
         for i in range(parts):
-            total[:, i * width : (i + 1) * width] = dot32(tail_back_ref[...], tail_ref[i])
-
+            total[:, i * width : (i + 1) * width] = dot32(short(tail_back_ref[...]), tail_ref[i])
+        inner, conv = gate_ref.shape[1], conv_ref.shape[1]
+        back_ref[:, :inner] = gate_ref[...]
+        back_ref[:, inner : inner + conv] = short(conv_ref[...])
+        rim = jnp.concatenate([jnp.zeros((8, conv), jnp.float32), rim_ref[...]], 0)
+        back_ref[TILE - 16 :, inner : inner + conv] = short(conv_ref[TILE - 16 :] + rim)
+        back_ref[:, inner + conv : inner + conv + TILE] = short(tail_back_ref[...])
+        rest = back_ref.shape[1] - inner - conv - TILE
+        back_ref[:, inner + conv + TILE :] = jnp.zeros((TILE, rest), jnp.bfloat16)
+
+    block = mains[0].shape[1]
+    here = back_ref[:, pl.ds(pl.multiple_of(step * block, TILE), block)]
     for i in range(parts):
-        total[:, i * width : (i + 1) * width] += dot32(back_ref[...], mains[i][0])
+        total[:, i * width : (i + 1) * width] += dot32(here, mains[i][0])
 
     @pl.when(step == pl.num_programs(0) - 1)
     def _():
@@ -1367,7 +1540,7 @@
         tokens_back_ref[...] = middle_ref[...] + spread * scale - values * shift
 
 
-def project_back(back, tail_back, main, tail, tokens, gain, middle_back):
+def project_back(gate, conv, tail_back, rim, main, tail, tokens, gain, middle_back):
     parts, rows, width = main.shape
     slots, model = tokens.shape
     whole = lambda shape: pl.BlockSpec(shape, lambda j: (0,) * len(shape))
@@ -1377,49 +1550,30 @@
         out_shape=(
             jax.ShapeDtypeStruct((slots, model), jnp.float32),
             jax.ShapeDtypeStruct((1, model), jnp.float32),
+            jax.ShapeDtypeStruct((slots, RS_SLOTS * RS_COLS), jnp.bfloat16),
         ),
         in_specs=[
-            pl.BlockSpec((slots, PROJ_BLOCK), lambda j: (0, j)),
+            whole(gate.shape),
+            whole(conv.shape),
             whole(tail_back.shape),
+            whole(rim.shape),
             *[pl.BlockSpec((1, PROJ_BLOCK, width), lambda j, i=i: (i, j, 0)) for i in range(parts)],
             whole(tail.shape),
             whole((slots, model)),
             whole((1, model)),
             whole((slots, model)),
         ],
-        out_specs=(whole((slots, model)), whole((1, model))),
+        out_specs=(whole((slots, model)), whole((1, model)), whole((slots, RS_SLOTS * RS_COLS))),
         scratch_shapes=[pltpu.VMEM((slots, model), jnp.float32)],
         compiler_params=pltpu.CompilerParams(vmem_limit_bytes=56 * 2**20),
         name="project_back",
-    )(back, tail_back, *[main] * parts, tail, tokens, gain, middle_back)
+    )(gate, conv, tail_back, rim, *[main] * parts, tail, tokens, gain, middle_back)
 
 
 def from_behind(block, axis, distance):
     devices = range(lax.axis_size(axis))
     route = [(i - distance, i) for i in devices if i - distance in devices]
     return lax.ppermute(block, axis, route)
-
-
-def owner_rows(values, order, per_owner):
-    depth, columns = values.shape
-    grid = values.T.reshape(4, 4, 2, 4, per_owner, depth)
-    place = {"x": 0, "y": 1, "c": 2, "z": 3}
-    return jnp.transpose(grid, [place[a] for a in ("c", *order)] + [4, 5])
-
-
-def plane_rows(values, order):
-    depth, columns = values.shape
-    grid = values.T.reshape(4, 4, 2, columns // 32, depth)
-    place = {"x": 0, "y": 1, "c": 2}
-    return jnp.transpose(grid, [place[a] for a in ("c", *order)] + [3, 4]).reshape(columns, depth)
-
-
-def left_rows(values, order, per_owner=12):
-    grid = owner_rows(values, order, per_owner)
-    if per_owner == 24:
-        return [grid[..., :12, :].reshape(1536, -1), grid[..., 12:, :].reshape(1536, -1)]
-    grid = jnp.pad(grid, ((0, 0),) * 4 + ((0, 12 - per_owner), (0, 0)))
-    return [grid.reshape(1536, -1)]
 
 
 def local(
@@ -1485,9 +1639,7 @@
         "mixer_in",
         projected, tail_values, halo, taps, heads,
     )
-    states = (head_count, inner_width // head_count, TILE)
-    carried, decays, all_upstream = carried_states(leaving.reshape(states), totals, upstream_low)
-    carried = carried.reshape(pairs)
+    carried, all_upstream = carried_states(leaving, totals, upstream_low)
     normed_low, scanned = tile_call(
         mixer_out_kernel,
         [((TILE, inner_width), low), ((TILE, inner_width), jnp.float32)],
@@ -1525,9 +1677,9 @@
     picks = jnp.swapaxes(picks.reshape(owned, 4, slot_count), 0, 1)
     picks = jnp.pad(picks, ((0, 0), (0, 8 - owned), (0, 0)))
     expert_parts, back_sum, all_picks = expert_sum(
-        jnp.stack([plane_rows(rows, order) for order in EXPERT_ORDERS]),
+        rows,
         act_grad,
-        jnp.stack([plane_rows(hidden[e], EXPERT_ORDERS[e]) for e in range(owned)]),
+        hidden,
         out_grad,
         back.reshape(4, slot_count, model_width),
         picks,
@@ -1564,67 +1716,43 @@
         "gate_back",
         projected, mixed, scanned, normed_back, running, wide,
     )
+    early_lefts, late_lefts = tile_call(
+        lefts_kernel,
+        [((6, model_width, TILE), low), ((3, model_width, TILE), low)],
+        [(inner_width, TILE), (model_width, TILE)],
+        "lefts",
+        first_norm, second_norm, normed_low, shared_hidden,
+    )
     leaving_back, expert_total = carried_states(
-        incoming_back.reshape(states), decays, part.reshape(4, slot_count, model_width)
+        incoming_back, totals, part.reshape(4, slot_count, model_width)
     )
-    leaving_back = leaving_back.reshape(pairs)
     block_out = jnp.where(valid[:, None], middle + expert_total + shared_sum, 0.0).astype(low)
-    conv_part, rim_part, taps_back, steps_back, heads_back = tile_call(
+    conv_part, rim_part, taps_back, steps_back, heads_back, shared_in_part, w_out_part, shared_out_part = tile_call(
         mixer_back_kernel,
         [
             ((TILE, conv_width), jnp.float32), ((8, conv_width), jnp.float32), ((8, conv_width), jnp.float32),
-            (square, jnp.float32), ((8, TILE), jnp.float32),
+            (square, jnp.float32), ((8, TILE), jnp.float32), ((12, 2 * shared_width), jnp.float32),
+            ((24, model_width), jnp.float32), ((8, model_width), jnp.float32),
         ],
         [
             (2, *square), (2, *square), (4, *square), square, (2, *square),
             (TILE, conv_width), (TILE + 8, TILE), (TILE + 16, TILE),
-        ],
+            pltpu.VMEM((TILE, RS_SLOTS * RS_COLS), low),
+        ]
+        + grad_sum_scratch(model_width),
         "mixer_back",
         projected, tail_values, halo, taps, heads, mixed, running, steps, wide, carried, result_back, leaving_back,
+        early_lefts, shared_act_grad, mix_low, upstream_low,
+        collective=7,
     )
     rim_back = from_behind(rim_part.astype(low), SEQ, -1).astype(jnp.float32)
-    conv_back = conv_part + jnp.pad(rim_back, ((slot_count - 8, 0), (0, 0)))
-    proj_back = jnp.concatenate([gate_back, conv_back.astype(low)], 1)
-    tail_back = steps_back.astype(low)
-    grad_tokens, grad_norm_gain = project_back(
-        proj_back, tail_back, full_in, tails, tokens, norm_gain[None], middle_back
-    )
-
-    first, second, third = RS_ORDERS
-    lefts = jnp.stack(
-        left_rows(first_norm, first)
-        + left_rows(first_norm, second)
-        + left_rows(second_norm, second) * 2
-        + left_rows(normed_low, third, 24)
-        + left_rows(shared_hidden, third, 8)
-    )
-    zeros = lambda columns: jnp.zeros((slot_count, columns), low)
-    rights = jnp.concatenate(
-        [
-            proj_back,
-            tail_back,
-            zeros(13 * RS_COLS - main_rows - TILE),
-            shared_act_grad,
-            zeros(RS_COLS),
-            mix_low,
-            mix_low,
-            upstream_low,
-        ],
-        1,
+    grad_tokens, grad_norm_gain, proj_back = project_back(
+        gate_back, conv_part, steps_back, rim_back, full_in, tails, tokens, norm_gain[None], middle_back
     )
     router_back = jnp.einsum("te,td->ed", logit_grads, second_norm, preferred_element_type=jnp.float32)
-    summed, small = grad_sum(
-        lefts, rights, taps_back, gain_back, grad_norm_gain, grad_post_gain[None], heads_back, router_back
+    w_in_part, small = grad_sum(
+        late_lefts, proj_back, w_in.shape[1], taps_back, gain_back, grad_norm_gain, grad_post_gain[None], heads_back, router_back
     )
-    at = 13 * RS_COLS
-    w_in_part = summed[:12, : w_in.shape[1]]
-    shared_in_part = summed[:12, at : at + 2 * shared_width]
-    at = at + 5 * RS_COLS
-    w_out_part = jnp.concatenate(
-        [summed[:12, at : at + model_width], summed[:12, at + model_width : at + 2 * model_width]], 0
-    )
-    at = at + 2 * model_width
-    shared_out_part = summed[:8, at : at + model_width]
     owner = lax.axis_index(ALL)
 
     def owned_part(values):

time: 532 us -> 483 us (0.908)
  local copies, waits for them, and re-layouts: 69.1 us -> 27.8 us
  Pallas kernels: 398 us -> 391 us
  other arithmetic: 19.1 us -> 13.4 us
  matrix products: 33.5 us -> 39 us
    pallas_call x4 -> x5, Pallas kernels: 34.4 us -> 89.7 us  [tile_call(): pl.pallas_call(kernel, out_shape=tuple((jax.ShapeDtypeStruct(s, d) for s,...]
    pallas_call x1, Pallas kernels: 114 us -> 66 us  [grad_sum(): pl.pallas_call(grad_sum_kernel, out_shape=(jax.ShapeDtypeStruct((rows //...]
    transpose x14 -> x0, local copies, waits for them, and re-layouts: 17.7 us -> none  [the longest x4 5.57 us: plane_rows(): jnp.transpose(grid, [place[a] for a in ('c', *order)] + [3, 4])]
    pallas_call x2, Pallas kernels: 70.2 us -> 55.4 us  [carried_states(): pl.pallas_call(scan_backward_kernel if reverse else scan_forward_kernel,...]
    unnamed x193 -> x99, local copies, waits for them, and re-layouts: 18.8 us -> 10.3 us
    slice x7 -> x0, local copies, waits for them, and re-layouts: 6.1 us -> none  [the longest x1 1.79 us: local(): w_in_part = summed[:12, :w_in.shape[1]]]
  transfers between devices with their start and end apart: 2 -> 2, of which waited for: 0 -> 0; matrix products, arithmetic and copies ran while one was open for 7% -> 2% of each run, Pallas kernels for 0% -> 0%
where the time goes in v3:
time: 483 us; the launch traced here: 478 us
  Pallas kernels  391 us (81%)
  matrix products  39 us (8%)
  local copies, waits for them, and re-layouts  27.8 us (6%)
  other arithmetic  13.4 us (3%)
    pallas_call x5, Pallas kernels, tile_call(): pl.pallas_call(kernel, out_shape=tuple((jax.ShapeDtypeStruct(s, d) for s,...  89.7 us
    pallas_call x1, Pallas kernels, gather_weights(): pl.pallas_call(functools.partial(gather_kernel, count), out_shape=tuple((...  82.4 us
    pallas_call x1, Pallas kernels, grad_sum(): pl.pallas_call(grad_sum_kernel, out_shape=(jax.ShapeDtypeStruct((rows //...  66 us
    pallas_call x2, Pallas kernels, carried_states(): pl.pallas_call(scan_backward_kernel if reverse else scan_forward_kernel,...  55.4 us
    pallas_call x1, Pallas kernels, expert_sum(): pl.pallas_call(expert_sum_kernel, out_shape=(jax.ShapeDtypeStruct((2, blo...  45.1 us
    pallas_call x1, Pallas kernels, z_gather(): pl.pallas_call(functools.partial(z_gather_kernel, count), out_shape=tuple...  21.7 us
    pallas_call x1, Pallas kernels, project_back(): pl.pallas_call(project_back_kernel, grid=(rows // PROJ_BLOCK,), out_shape...  15.3 us
    pallas_call x1, Pallas kernels, project(): pl.pallas_call(project_kernel, grid=(rows // PROJ_BLOCK,), out_shape=(jax...  14.8 us
  transfers between devices with their start and end apart: 2, of which 0 were waited for; matrix products, arithmetic and copies ran while one was open for 2% of the time, Pallas kernels for 0%

profile of v3, /device:TPU:0, one launch (start us, length us, event | category | flops | bytes accessed | tf_op | source)
XLA Modules:
  0.0 477.7 jit_solution(7245741313087143319)
XLA Ops:
  4.4 82.4 %gather_weights.1 = (bf16[4,6400,384]{2,1,0:T(8,128)(2,1)}, bf16[3072,1536]{1,0:T(8,128)(2,1)}, bf16[1536,2048]{1,0:T(8,128)(2,1)}, bf16[1024,1536]{1,0:T(8,128)(2,1)}, bf16[4,128,384]{2,1,0:T(8,128)(2,1)}) custom-call(bf16[6448,384]{1,0:T(8,128)(2,1)} %bitcast.107, bf16[768,1536]{1,0:T(8,128)(2,1)} %refs_1_.1, bf16[384,2048]{1,0:T(8,128)(2,1)} %refs_2_.1, ...), custom_call_target="tpu_custom_call" | custom-call | tf_op jit(solution)/shard_map/gather_weights/pallas_call | solution.py:1094
  86.9 14.8 %project.1 = (bf16[128,1536]{1,0:T(8,128)(2,1)}, f32[128,6400]{1,0:T(8,128)}, f32[128,128]{1,0:T(8,128)}) custom-call(bf16[128,1536]{1,0:T(8,128)(2,1)} %bitcast.108, f32[1,1536]{1,0:T(1,128)} %broadcast_in_dim.64.gain_ref.refs_6_, bf16[4,6400,384]{2,1,0:T(8,128)(2,1)} %get-tuple-element.60.refs_0_.refs_1_.refs_2_.refs_3_, ...), custom_call_target="tpu_custom_call" | custom-call | tf_op jit(solution)/shard_map/project/pallas_call | solution.py:1484
  101.6 1.5 slice.62
  103.2 3.2 collective-permute-start
  115.0 1.9 copy-done.2
  117.8 7.4 %mixer_in.1 = (f32[128,3328]{1,0:T(8,128)S(1)}, bf16[24,128,128]{2,1,0:T(8,128)(2,1)S(1)}, f32[8,128]{1,0:T(8,128)S(1)}, f32[128,128]{1,0:T(8,128)S(1)}, f32[128,128]{1,0:T(8,128)S(1)}) custom-call(f32[128,6400]{1,0:T(8,128)S(1)} %copy-done.2, f32[128,128]{1,0:T(8,128)S(1)} %copy-done.21, f32[8,3328]{1,0:T(8,128)} %collective-permute-done.halo_ref, ...), custom_call_target="tpu_custom_call" | custom-call | tf_op jit(solution)/shard_map/mixer_in/pallas_call | solution.py:1444
  125.2 27.9 %scan_forward.1 = (bf16[96,32,128]{2,1,0:T(8,128)(2,1)S(1)}, bf16[4,128,1536]{2,1,0:T(8,128)(2,1)S(1)}) custom-call(bf16[96,32,128]{2,1,0:T(8,128)(2,1)S(1)} %bitcast.102, f32[8,128]{1,0:T(8,128)S(1)} %get-tuple-element.68.refs_1_, bf16[128,1536]{1,0:T(8,128)(2,1)S(1)} %bitcast_select_fusion.refs_2_.up_ref), custom_call_target="tpu_custom_call" | custom-call | tf_op jit(solution)/shard_map/scan_forward/pallas_call | solution.py:593
  153.2 5.1 %mixer_out.1 = (bf16[128,3072]{1,0:T(8,128)(2,1)S(1)}, f32[128,3072]{1,0:T(8,128)S(1)}) custom-call(f32[128,6400]{1,0:T(8,128)S(1)} %copy-done.2, f32[128,3328]{1,0:T(8,128)S(1)} %get-tuple-element.64.mixed_ref, f32[128,128]{1,0:T(8,128)S(1)} %get-tuple-element.65.run_ref, f32[128,128]{1,0:T(8,128)S(1)} %get-tuple-element.66.step_ref, ...), custom_call_target="tpu_custom_call" | custom-call | tf_op jit(solution)/shard_map/mixer_out/pallas_call | solution.py:1444
  158.4 5.3 %multiply_reduce_fusion.2 = (f32[128]{0:T(128)S(1)}, f32[128,1536]{1,0:T(8,128)S(1)}) fusion(bf16[128,3072]{1,0:T(8,128)(2,1)S(1)} %get-tuple-element.70.gated_ref, bf16[3072,1536]{1,0:T(8,128)(2,1)} %get-tuple-element.71, bf16[1,128,1536]{2,1,0:T(8,128)(2,1)S(1)} %copy-done.25), kind=kOutput, calls=%fused_computation.24 | convolution fusion | flops 1208745856 | bytes 11403776 | tf_op jit(solution)/shard_map/dot_general | solution.py:72
  164.2 21.7 %gather_rows.1 = (bf16[4,128,1536]{2,1,0:T(8,128)(2,1)S(1)}, f32[4,8,128]{2,1,0:T(8,128)S(1)}) custom-call(bf16[128,1536]{1,0:T(8,128)(2,1)S(1)} %multiply_convert_fusion.4.refs_0_.second_ref, f32[8,128]{1,0:T(8,128)S(1)} %fusion.13.refs_1_), custom_call_target="tpu_custom_call" | custom-call | tf_op jit(solution)/shard_map/gather_rows/pallas_call | solution.py:638
  186.4 3.4 convolution_bitcast_fusion.1
  190.2 2.5 multiply_convert_fusion.3
  192.8 1.7 pad_maximum_fusion.acts_ref
  194.5 8.2 %fusion.2 = bf16[512,1536]{1,0:T(8,128)(2,1)} fusion(bf16[2,1536,1024]{2,1,0:T(8,128)(2,1)} %param.36, bf16[2,512,512]{2,1,0:T(8,128)(2,1)S(1)} %get-tuple-element.110, bf16[2,512,512]{2,1,0:T(8,128)(2,1)S(1)} %get-tuple-element.109), kind=kOutput, calls=%fused_computation.7 | convolution fusion | flops 3226206208 | bytes 9961472 | tf_op jit(solution)/shard_map/etf,edf->td/dot_general | solution.py:1676
  206.6 3.3 fusion.1
  210.7 45.1 %expert_sum.1 = (f32[2,48,1536]{2,1,0:T(8,128)S(1)}, f32[128,1536]{1,0:T(8,128)S(1)}, f32[4,8,128]{2,1,0:T(8,128)S(1)}) custom-call(bf16[512,1536]{1,0:T(8,128)(2,1)} %bitcast.98, bf16[2,512,1024]{2,1,0:T(8,128)(2,1)} %pad_maximum_fusion.acts_ref, bf16[2,512,512]{2,1,0:T(8,128)(2,1)} %copy-done.29, bf16[2,512,1536]{2,1,0:T(8,128)(2,1)} %copy-done.24, ...), custom_call_target="tpu_custom_call" | custom-call | tf_op jit(solution)/shard_map/expert_sum/pallas_call | solution.py:867
  255.9 5.0 %convolution_add_fusion.1 = f32[128,1536]{1,0:T(8,128)S(1)} fusion(f32[128,1536]{1,0:T(8,128)S(1)} %get-tuple-element.78, bf16[1536,2048]{1,0:T(8,128)(2,1)} %get-tuple-element.74, bf16[128,1024]{1,0:T(8,128)(2,1)S(1)} %copy-done.31, bf16[128,1024]{1,0:T(8,128)(2,1)S(1)} %get-tuple-element.112), kind=kOutput, calls=%fused_computation.9 | convolution fusion | flops 806551552 | bytes 8388608 | tf_op jit(solution)/shard_map/tf,df->td/dot_general | solution.py:1700
  262.8 6.9 %fusion.19.back_ref = f32[128,3072]{1,0:T(8,128)S(1)} fusion(bf16[128,1536]{1,0:T(8,128)(2,1)S(1)} %get-tuple-element.107.mix_ref, bf16[3072,1536]{1,0:T(8,128)(2,1)} %get-tuple-element.71), kind=kOutput, calls=%fused_computation.70 | convolution fusion | flops 1207959552 | bytes 11403264 | tf_op jit(solution)/shard_map/td,kd->tk/dot_general | solution.py:1711
  271.2 6.4 %gate_back.1 = (f32[128,3072]{1,0:T(8,128)S(1)}, bf16[128,3072]{1,0:T(8,128)(2,1)S(1)}, f32[8,3072]{1,0:T(8,128)S(1)}, bf16[24,128,128]{2,1,0:T(8,128)(2,1)S(1)}) custom-call(f32[128,6400]{1,0:T(8,128)S(1)} %copy-done.3, f32[128,3328]{1,0:T(8,128)S(1)} %get-tuple-element.64.mixed_ref, f32[128,3072]{1,0:T(8,128)S(1)} %get-tuple-element.72.scanned_ref, ...), custom_call_target="tpu_custom_call" | custom-call | tf_op jit(solution)/shard_map/gate_back/pallas_call | solution.py:1444
  278.8 27.5 %scan_backward.1 = (bf16[96,32,128]{2,1,0:T(8,128)(2,1)S(1)}, f32[128,1536]{1,0:T(8,128)S(1)}) custom-call(bf16[96,32,128]{2,1,0:T(8,128)(2,1)S(1)} %bitcast.103, f32[8,128]{1,0:T(8,128)S(1)} %get-tuple-element.68.refs_1_, bf16[4,128,1536]{2,1,0:T(8,128)(2,1)S(1)} %bitcast.99), custom_call_target="tpu_custom_call" | custom-call | tf_op jit(solution)/shard_map/scan_backward/pallas_call | solution.py:593
  307.2 69.5 %mixer_back.1 = (f32[128,3328]{1,0:T(8,128)}, f32[8,3328]{1,0:T(8,128)}, f32[8,3328]{1,0:T(8,128)}, f32[128,128]{1,0:T(8,128)}, f32[8,128]{1,0:T(8,128)}, /*inde...) custom-call(f32[128,6400]{1,0:T(8,128)} %get-tuple-element.62.proj_ref, ...), custom_call_target="tpu_custom_call" | custom-call | tf_op jit(solution)/shard_map/mixer_back/pallas_call | solution.py:1444
  383.7 15.3 %project_back.1 = (f32[128,1536]{1,0:T(8,128)}, f32[1,1536]{1,0:T(1,128)}, bf16[128,6656]{1,0:T(8,128)(2,1)}) custom-call(bf16[128,3072]{1,0:T(8,128)(2,1)} %copy-done.14, f32[128,3328]{1,0:T(8,128)} %get-tuple-element.87.conv_ref, f32[128,128]{1,0:T(8,128)} %get-tuple-element.88.tail_back_ref, f32[8,3328]{1,0:T(8,128)} %convert_element_type.82.rim_ref, ...), custom_call_target="tpu_custom_call" | custom-call | tf_op jit(solution)/shard_map/project_back/pallas_call | solution.py:1547
  399.0 66.0 %grad_sum.1 = (f32[12,6448]{1,0:T(8,128)}, f32[8,4864]{1,0:T(8,128)}) custom-call(bf16[3,1536,128]{2,1,0:T(8,128)(2,1)} %copy-done.12, bf16[128,6656]{1,0:T(8,128)(2,1)} %get-tuple-element.92.rights_ref, f32[8,3328]{1,0:T(8,128)} %get-tuple-element.93.taps_ref, f32[8,3072]{1,0:T(8,128)} %copy-done.22, f32[1,1536]{1,0:T(1,128)} %get-tuple-element.95.norm_ref, ...), custom_call_target="tpu_custom_call" | custom-call | tf_op jit(solution)/shard_map/grad_sum/pallas_call | solution.py:362
  473.7 1.8 copy.58
  (159 shorter events, 41.2 us)
Async XLA Ops:
  0.7 189.5 %copy-start = (bf16[2,512,1536]{2,1,0:T(8,128)(2,1)S(1)}, bf16[2,512,1536]{2,1,0:T(8,128)(2,1)}, u32[]{:S(2)}) copy-start(bf16[2,512,1536]{2,1,0:T(8,128)(2,1)} %param.37) | copy-start | bytes 9437188
  86.8 20.9 %copy-start.37 = (f32[3328]{0:T(1024)S(1)}, f32[3328]{0:T(1024)}, u32[]{:S(2)}) copy-start(f32[3328]{0:T(1024)} %param.26) | copy-start | bytes 39940
  86.8 21.6 %copy-start.42 = (f32[48]{0:T(128)S(1)}, f32[48]{0:T(128)}, u32[]{:S(2)}) copy-start(f32[48]{0:T(128)} %param.29) | copy-start | bytes 580
  86.8 22.3 %copy-start.41 = (s32[1,128,6]{1,0,2:T(1,128)S(1)}, s32[1,128,6]{1,0,2:T(1,128)}, u32[]{:S(2)}) copy-start(s32[1,128,6]{1,0,2:T(1,128)} %param.22) | copy-start | bytes 9220
  103.2 11.8 %collective-permute-start = (f32[8,3328]{1,0:T(8,128)}, f32[8,3328]{1,0:T(8,128)}, u32[]{:S(2)}, u32[]{:S(2)}) collective-permute-start(f32[8,3328]{1,0:T(8,128)} %slice.62), channel_id=1, source_target_pairs={{0,4},{4,8},{8,12},{12,16},{16,20},{20,24},{24,28},{28,32},{32,36}... | collective-permute-start | bytes 319496 | tf_op jit(solution)/shard_map/ppermute | solution.py:1576
  111.9 46.3 %copy-start.5 = (bf16[128,1536]{1,0:T(8,128)(2,1)}, bf16[128,1536]{1,0:T(8,128)(2,1)S(1)}, u32[]{:S(2)}) copy-start(bf16[128,1536]{1,0:T(8,128)(2,1)S(1)} %bitcast_select_fusion.refs_2_.up_ref) | copy-start | bytes 1179652
  113.4 39.8 %copy-start.18 = (f32[2,3072]{1,0:T(2,128)S(1)}, f32[2,3072]{1,0:T(2,128)}, u32[]{:S(2)}) copy-start(f32[2,3072]{1,0:T(2,128)} %pad_maximum_fusion.2.wide_ref) | copy-start | bytes 73732
  114.3 11.0 %copy-start.13 = (f32[8,3328]{1,0:T(8,128)}, f32[8,3328]{1,0:T(8,128)S(1)}, u32[]{:S(2)}) copy-start(f32[8,3328]{1,0:T(8,128)S(1)} %maximum_maximum_fusion.cw_ref) | copy-start | bytes 319492
  115.0 43.3 %copy-start.23 = (f32[8,128]{1,0:T(8,128)}, f32[8,128]{1,0:T(8,128)S(1)}, u32[]{:S(2)}) copy-start(f32[8,128]{1,0:T(8,128)S(1)} %select_maximum_fusion.heads_ref) | copy-start | bytes 12292
  125.2 33.1 %copy-start.16 = (f32[128,128]{1,0:T(8,128)}, f32[128,128]{1,0:T(8,128)S(1)}, u32[]{:S(2)}) copy-start(f32[128,128]{1,0:T(8,128)S(1)} %get-tuple-element.65.run_ref) | copy-start | bytes 196612
  125.2 33.1 %copy-start.20 = (f32[128,128]{1,0:T(8,128)}, f32[128,128]{1,0:T(8,128)S(1)}, u32[]{:S(2)}) copy-start(f32[128,128]{1,0:T(8,128)S(1)} %get-tuple-element.66.step_ref) | copy-start | bytes 196612
  125.2 145.9 %copy-start.4 = (f32[128,3328]{1,0:T(8,128)}, f32[128,3328]{1,0:T(8,128)S(1)}, u32[]{:S(2)}) copy-start(f32[128,3328]{1,0:T(8,128)S(1)} %get-tuple-element.64.mixed_ref) | copy-start | bytes 5111812
  153.1 10.6 %copy-start.7 = (bf16[96,32,128]{2,1,0:T(8,128)(2,1)}, bf16[96,32,128]{2,1,0:T(8,128)(2,1)S(1)}, u32[]{:S(2)}) copy-start(bf16[96,32,128]{2,1,0:T(8,128)(2,1)S(1)} %get-tuple-element.69) | copy-start | bytes 2359300
  158.3 28.0 %slice-start.2 = ((s8[6291456]{0:T(1024)(128)(4,1)}), s8[4194304]{0:T(1024)(128)(4,1)S(1)}, s32[]{:S(2)}) async-start(s8[6291456]{0:T(1024)(128)(4,1)} %bitcast.123), calls=%async_computation.2 | async-start | bytes 8388608
  158.4 28.0 %slice-start.3 = ((s8[6291456]{0:T(1024)(128)(4,1)}), s8[2097152]{0:T(1024)(128)(4,1)S(1)}, s32[]{:S(2)}) async-start(s8[6291456]{0:T(1024)(128)(4,1)} %bitcast.123), calls=%async_computation.3 | async-start | bytes 4194304
  192.8 13.8 %copy-start.29 = (bf16[2,512,512]{2,1,0:T(8,128)(2,1)}, bf16[2,512,512]{2,1,0:T(8,128)(2,1)S(1)}, u32[]{:S(2)}) copy-start(bf16[2,512,512]{2,1,0:T(8,128)(2,1)S(1)} %get-tuple-element.111.hidden_ref) | copy-start | bytes 3145732
  210.7 45.1 %copy-start.31 = (bf16[128,1024]{1,0:T(8,128)(2,1)S(1)}, bf16[128,1024]{1,0:T(8,128)(2,1)}, u32[]{:S(2)}) copy-start(bf16[128,1024]{1,0:T(8,128)(2,1)} %copy-done.30) | copy-start | bytes 786436
  278.8 27.6 %copy-start.14 = (bf16[128,3072]{1,0:T(8,128)(2,1)}, bf16[128,3072]{1,0:T(8,128)(2,1)S(1)}, u32[]{:S(2)}) copy-start(bf16[128,3072]{1,0:T(8,128)(2,1)S(1)} %get-tuple-element.82.gate_ref) | copy-start | bytes 2359300
  278.8 28.5 %copy-start.22 = (f32[8,3072]{1,0:T(8,128)}, f32[8,3072]{1,0:T(8,128)S(1)}, u32[]{:S(2)}) copy-start(f32[8,3072]{1,0:T(8,128)S(1)} %get-tuple-element.94.gain_ref) | copy-start | bytes 294916
  377.7 5.4 %collective-permute-start.1 = (bf16[8,3328]{1,0:T(8,128)(2,1)S(1)}, bf16[8,3328]{1,0:T(8,128)(2,1)S(1)}, u32[]{:S(2)}, u32[]{:S(2)}) collective-permute-start(bf16[8,3328]{1,0:T(8,128)(2,1)S(1)} %convert_element_type.81), channel_id=1, source_target_pairs={{4,0},{8,4},{12,8},{16,12},{20,16},{24,20},{28,24},{32,28},{36,32}... | collective-permute-start | bytes 159752 | tf_op jit(solution)/shard_map/ppermute | solution.py:1576
  383.7 93.7 %copy-start.1 = (bf16[2,512,1536]{2,1,0:T(8,128)(2,1)S(1)}, bf16[2,512,1536]{2,1,0:T(8,128)(2,1)}, u32[]{:S(2)}) copy-start(bf16[2,512,1536]{2,1,0:T(8,128)(2,1)} %param.37) | copy-start | bytes 9437188
  399.0 76.5 %copy-start.33 = (f32[24,1536]{1,0:T(8,128)S(1)}, f32[24,1536]{1,0:T(8,128)}, u32[]{:S(2)}) copy-start(f32[24,1536]{1,0:T(8,128)} %get-tuple-element.154) | copy-start | bytes 442372
  399.0 77.1 %copy-start.34 = (f32[12,2048]{1,0:T(8,128)S(1)}, f32[12,2048]{1,0:T(8,128)}, u32[]{:S(2)}) copy-start(f32[12,2048]{1,0:T(8,128)} %get-tuple-element.157) | copy-start | bytes 294916
  399.0 77.8 %copy-start.36 = (f32[8,1536]{1,0:T(8,128)S(1)}, f32[8,1536]{1,0:T(8,128)}, u32[]{:S(2)}) copy-start(f32[8,1536]{1,0:T(8,128)} %get-tuple-element.158) | copy-start | bytes 147460
  (25 other events, 121.1 us)

commit v4 on v3

--- a/solution.py
+++ b/solution.py
@@ -32,10 +32,10 @@
 
 MESH_ID = pl.DeviceIdType.MESH
 RS_ORDERS = (("x", "y", "z"), ("y", "z", "x"), ("z", "x", "y"))
-RS_COUNTS = (5, 4, 4)
-RS_FIRST = (0, 5, 9)
-RS_SLOTS = 13
-RS_COLS = 512
+RS_COUNTS = (9, 9, 8)
+RS_FIRST = (0, 9, 18)
+RS_SLOTS = 26
+RS_COLS = 256
 RS_LAGS = 6
 RS_TIMES = max(RS_COUNTS) + RS_LAGS - 1
 NEIGHBOURS = [("c", 1)] + [(axis, o) for axis in ("x", "y", "z") for o in (1, 2, 3)]
@@ -261,22 +261,87 @@
 
 
 def grad_sum_kernel(
-    lefts_ref, rights_ref, taps_ref, gain_ref, norm_ref, post_ref, heads_ref, router_ref, out_ref, small_ref, *scratch
+    tail_back_ref, rim_ref, gain_ref, tail_ref, taps_ref, gated_gain_ref, post_ref, heads_ref, router_ref,
+    main_ref, gate_far, conv_far, lefts_far, tokens_far, middle_far,
+    out_ref, small_ref, tokens_back_far, *scratch
 ):
-    *sum_scratch, pack, pack_in, pack_work, pack_others, pack_ss, pack_rs = scratch
+    gate_ref, conv_ref, lefts_ref, tokens_ref, middle_ref, load_sem, tokens_back_ref, save_sem, *scratch = scratch
+    save = pltpu.make_async_copy(tokens_back_ref, tokens_back_far, save_sem.at[0])
+    loads = [
+        pltpu.make_async_copy(far, near, load_sem.at[i])
+        for i, (far, near) in enumerate(
+            zip((gate_far, conv_far, lefts_far, tokens_far, middle_far), (gate_ref, conv_ref, lefts_ref, tokens_ref, middle_ref))
+        )
+    ]
+    for copy in loads:
+        copy.start()
+    *sum_scratch, back_ref, total, weights, weight_sem, pack, pack_in, pack_work, pack_others, pack_ss, pack_rs = scratch
     me_core = lax.axis_index("c")
     other = 1 - me_core
     half = lefts_ref.shape[1] // 2
+    blocks = main_ref.shape[1] // weights.shape[2]
+
+    def fetch(j):
+        rows = weights.shape[2]
+        return [
+            pltpu.make_async_copy(
+                main_ref.at[i, pl.ds(pl.multiple_of(j * rows, 16), rows)],
+                weights.at[lax.rem(j, 2), i],
+                weight_sem.at[lax.rem(j, 2), i],
+            )
+            for i in range(4)
+        ]
+
+    for copy in fetch(0) + fetch(1):
+        copy.start()
     greet_neighbours()
-
+    inner, conv = gate_ref.shape[1], conv_ref.shape[1]
+    for copy in loads[:3]:
+        copy.wait()
+    back_ref[:, :inner] = gate_ref[...]
+    back_ref[:, inner : inner + conv] = short(conv_ref[...])
+    rim = jnp.concatenate([jnp.zeros((8, conv), jnp.float32), rim_ref[...]], 0)
+    back_ref[TILE - 16 :, inner : inner + conv] = short(conv_ref[TILE - 16 :] + rim)
+    back_ref[:, inner + conv : inner + conv + TILE] = short(tail_back_ref[...])
+    rest = back_ref.shape[1] - inner - conv - TILE
+    back_ref[:, inner + conv + TILE :] = jnp.zeros((TILE, rest), jnp.bfloat16)
     taps_width, wide = taps_ref.shape[1], pack.shape[1] // 2
-    pack[:, :taps_width] = taps_ref[...]
-    pack[5:6, : gain_ref.shape[1]] = gain_ref[0:1]
-    pack[6:7, : norm_ref.shape[1]] = norm_ref[...]
-    pack[6:7, norm_ref.shape[1] : 2 * norm_ref.shape[1]] = post_ref[...]
-    for i in range(3):
-        pack[7:8, TILE * i : TILE * (i + 1)] = heads_ref[i : i + 1]
-    pack[:, taps_width:] = router_ref[...]
+
+    def project_step(j):
+        for copy in fetch(j):
+            copy.wait()
+        rows, width = weights.shape[2:]
+        here = back_ref[:, pl.ds(pl.multiple_of(j * rows, TILE), rows)]
+        for i in range(4):
+            total[:, i * width : (i + 1) * width] += dot32(here, weights[lax.rem(j, 2), i])
+
+        @pl.when(j + 2 < blocks)
+        def _():
+            for copy in fetch(j + 2):
+                copy.start()
+
+    def project_end():
+        for copy in loads[3:]:
+            copy.wait()
+        values = tokens_ref[...].astype(jnp.float32)
+        scale = lax.rsqrt(jnp.mean(values * values, 1, keepdims=True) + NORM_EPS)
+        back = total[...]
+        spread = back * gain_ref[...]
+        shift = jnp.mean(spread * values, 1, keepdims=True) * scale * scale * scale
+        tokens_back_ref[...] = middle_ref[...] + spread * scale - values * shift
+        save.start()
+        model = tokens_ref.shape[1]
+        pack[:, :taps_width] = taps_ref[...]
+        pack[5:6, : gated_gain_ref.shape[1]] = gated_gain_ref[0:1]
+        pack[6:7, :model] = jnp.sum(back * values * scale, 0, keepdims=True)
+        pack[6:7, model : 2 * model] = post_ref[...]
+        for i in range(3):
+            pack[7:8, TILE * i : TILE * (i + 1)] = heads_ref[i : i + 1]
+        pack[:, taps_width:] = router_ref[...]
+
+    width = weights.shape[3]
+    for i in range(4):
+        total[:, i * width : (i + 1) * width] = dot32(short(tail_back_ref[...]), tail_ref[i])
 
     def pack_half(ref, which):
         return ref.at[:, pl.ds(pl.multiple_of(which * wide, 128), wide)]
@@ -295,6 +360,7 @@
 
     def pack_step(s):
         if s == 0:
+            project_end()
             pack_core(False).start()
         if s == 1:
             pack_core(False).wait_recv()
@@ -323,7 +389,7 @@
         return lefts_ref[part, pl.ds(pl.multiple_of(which * half, half), half), :]
 
     def right_of(part, k, col):
-        return rights_ref[:, pl.ds(pl.multiple_of((RS_FIRST[part] + k) * RS_COLS + col, 256), 256)]
+        return back_ref[:, pl.ds(pl.multiple_of((RS_FIRST[part] + k) * RS_COLS + col, 256), 256)]
 
     whole = out_ref.shape[1] // RS_COLS
     rows = out_ref.shape[0]
@@ -343,32 +409,47 @@
     step, finish = grad_sum_steps(sum_scratch, left_of, right_of, store)
 
     def run(t, carry):
+        step(t)
+
+        @pl.when(t < blocks)
+        def _():
+            project_step(t)
+
         for s in range(6):
-            @pl.when(t == s)
+            @pl.when(t == blocks + s)
             def _():
                 pack_step(s)
 
-        step(t)
         return carry
 
     lax.fori_loop(0, RS_TIMES, run, 0)
     finish()
-
-
-def grad_sum(lefts, rights, columns, taps, gain, norm, post, heads, router):
+    save.wait()
+
+
+def grad_sum(lefts, gate, conv, tail_back, rim, tokens, gain, middle, tails, taps, gated_gain, post, heads, router, main, columns):
     rows = lefts.shape[1]
     wide = taps.shape[1] + router.shape[1]
+    slots, model = tokens.shape
     space = pl.BlockSpec(memory_space=pltpu.VMEM)
+    block = main.shape[1] // 5
     return pl.pallas_call(
         grad_sum_kernel,
         out_shape=(
             jax.ShapeDtypeStruct((rows // 128, columns), jnp.float32),
             jax.ShapeDtypeStruct((8, wide), jnp.float32),
+            jax.ShapeDtypeStruct((slots, model), jnp.float32),
         ),
-        in_specs=[space] * 8,
-        out_specs=(space, space),
-        scratch_shapes=grad_sum_scratch(rows)
+        in_specs=[space] * 9 + [pl.BlockSpec(memory_space=pl.ANY)] * 6,
+        out_specs=(space, space, pl.BlockSpec(memory_space=pl.ANY)),
+        scratch_shapes=[pltpu.VMEM(a.shape, a.dtype) for a in (gate, conv, lefts, tokens, middle)]
+        + [pltpu.SemaphoreType.DMA((5,)), pltpu.VMEM((slots, model), jnp.float32), pltpu.SemaphoreType.DMA((1,))]
+        + grad_sum_scratch(rows)
         + [
+            pltpu.VMEM((slots, RS_SLOTS * RS_COLS), jnp.bfloat16),
+            pltpu.VMEM((slots, model), jnp.float32),
+            pltpu.VMEM((2, 4, block, main.shape[2]), jnp.bfloat16),
+            pltpu.SemaphoreType.DMA((2, 4)),
             pltpu.VMEM((8, wide), jnp.float32),
             pltpu.VMEM((8, wide // 2), jnp.float32),
             pltpu.VMEM((4, 8, wide // 2), jnp.float32),
@@ -377,13 +458,10 @@
             pltpu.SemaphoreType.DMA((5, 4)),
         ],
         compiler_params=pltpu.CompilerParams(
-            collective_id=0, has_side_effects=True, vmem_limit_bytes=58 * 2**20
+            collective_id=0, has_side_effects=True, vmem_limit_bytes=60 * 2**20
         ),
         name="grad_sum",
-    )(lefts, rights, taps, gain, norm, post, heads, router)
-
-
-LEFT_SOURCES = (("shared", 0), ("hidden", 0), ("gated_0", 1), ("hidden", 1), ("gated_1", 2), ("hidden", 2))
+    )(tail_back, rim, gain, tails, taps, gated_gain, post, heads, router, main, gate, conv, lefts, tokens, middle)
 
 
 def owner_moves(order, stride, offset, rows):
@@ -426,23 +504,40 @@
     place(early_ref, 4, RS_ORDERS[2], 24, 12, 12)
 
 
-def state_exchange(reverse, state_ref, totals_ref, rows_ref, out_ref, *refs):
-    if reverse:
-        rows_sum, all_rows, *refs = refs
-    else:
-        all_rows, *refs = refs
+def plane_others():
+    x, y = lax.axis_index("x"), lax.axis_index("y")
+    found = []
+    for dx in range(4):
+        for dy in range(4):
+            if dx + dy:
+                tx, ty = lax.rem(x + dx, 4), lax.rem(y + dy, 4)
+                found.append((dx * 4 + dy, tx * 4 + ty, {"x": tx, "y": ty}))
+    return found
+
+
+def line_neighbour(ahead):
+    x, y, c = lax.axis_index("x"), lax.axis_index("y"), lax.axis_index("c")
+    chip = lax.rem(x * 4 + y + (c if ahead else c + 15), 16)
+    return {"x": chip // 4, "y": lax.rem(chip, 4), "c": 1 - c}
+
+
+def greet_plane():
+    c = lax.axis_index("c")
+    chip = lax.rem(lax.axis_index("x") * 4 + lax.axis_index("y") + 2 * c + 15, 16)
+    greet(
+        [{"c": 1 - c}, {"x": chip // 4, "y": lax.rem(chip, 4), "c": 1 - c}]
+        + [{"z": ring("z", o)} for o in (1, 2, 3)]
+        + [where for unused, unused_too, where in plane_others()]
+    )
+
+
+def state_exchange(reverse, state_ref, totals_ref, rows_ref, out_ref, all_rows, rows_sum, tick, *refs):
     pair_in, pair_totals, outgoing, got, back, mine, hand, ps, pr, ss, rs, bs, br, zs, zr = refs
     x, y, c, z = (lax.axis_index(a) for a in ALL)
     chip = x * 4 + y
     half = pair_in.shape[0]
     groups, size = back.shape[1:3]
-    others = [(dx, dy) for dx in range(4) for dy in range(4) if dx + dy]
-
-    def far(dx, dy):
-        tx, ty = lax.rem(x + dx, 4), lax.rem(y + dy, 4)
-        return tx * 4 + ty, {"x": tx, "y": ty}
-
-    greet([{"c": 1 - c}] + [{"z": ring("z", o)} for o in (1, 2, 3)] + [far(*d)[1] for d in others])
+    others = plane_others()
     mine_at, theirs_at = c * half, (1 - c) * half
 
     def pair_copies():
@@ -451,14 +546,10 @@
             remote(totals_ref, pair_totals, ps.at[1], pr.at[1], {"c": 1 - c}),
         ]
 
-    def out_copy(dx, dy):
-        target, where = far(dx, dy)
-        at = dx * 4 + dy
+    def out_copy(at, target, where):
         return remote(outgoing.at[target], got.at[chip], ss.at[at], rs.at[at], where)
 
-    def back_copy(dx, dy):
-        target, where = far(dx, dy)
-        at = dx * 4 + dy
+    def back_copy(at, target, where):
         return remote(back.at[target], mine.at[pl.ds(groups * chip, groups)], bs.at[at], br.at[at], where)
 
     def hand_copy():
@@ -473,8 +564,10 @@
         copy.start()
     for copy in row_copies:
         copy.start()
+    own_rows = None if reverse else pltpu.make_async_copy(rows_ref, all_rows.at[z], zs.at[0])
     if not reverse:
-        all_rows[z] = rows_ref[...]
+        own_rows.start()
+    tick(0)
     for copy in pair_copies():
         copy.wait_recv()
     first = jnp.where(c == 0, totals_ref[...], pair_totals[...])
@@ -510,6 +603,7 @@
     for d in others:
         out_copy(*d).start()
     got[chip] = outgoing[chip]
+    tick(1)
     for d in others:
         out_copy(*d).wait_recv()
 
@@ -527,6 +621,7 @@
     for d in others:
         back_copy(*d).start()
     mine[pl.ds(groups * chip, groups)] = back[chip]
+    tick(2)
     for d in others:
         back_copy(*d).wait_recv()
 
@@ -544,8 +639,11 @@
 
     lax.fori_loop(0, half // 2, spread, 0)
     hand_copy().start()
+    tick(3)
     for copy in row_copies:
         copy.wait()
+    if not reverse:
+        own_rows.wait()
     if reverse:
         add_parts(rows_ref, z, all_rows, rows_sum)
     hand_copy().wait()
@@ -568,84 +666,129 @@
     lax.fori_loop(0, out.shape[0] // 32, rows_at, 0)
 
 
-def scan_forward_kernel(*refs):
-    state_exchange(False, *refs)
-
-
-def scan_backward_kernel(*refs):
-    state_exchange(True, *refs)
-
-
-def carried_states(state, totals, rows):
-    reverse = rows.ndim == 3
-    low = jnp.bfloat16
-    pairs = state.shape
-    state = state.reshape(96, 32, TILE)
-    space = pl.BlockSpec(memory_space=pltpu.VMEM)
-    outs = [jax.ShapeDtypeStruct(state.shape, low)]
-    extra = []
-    if reverse:
-        outs.append(jax.ShapeDtypeStruct(rows.shape[1:], jnp.float32))
-        extra.append(pltpu.VMEM((3, *rows.shape[1:]), rows.dtype))
-    else:
-        outs.append(jax.ShapeDtypeStruct((4, *rows.shape), rows.dtype))
-    sem = pltpu.SemaphoreType.DMA
-    result = pl.pallas_call(
-        scan_backward_kernel if reverse else scan_forward_kernel,
-        out_shape=tuple(outs),
-        in_specs=[space] * 3,
-        out_specs=(space,) * 2,
-        scratch_shapes=extra
-        + [
-            pltpu.VMEM((48, 32, TILE), low),
-            pltpu.VMEM((8, TILE), jnp.float32),
-            pltpu.VMEM((16, 112, TILE), low),
-            pltpu.VMEM((16, 112, TILE), low),
-            pltpu.VMEM((16, 3, 32, TILE), low),
-            pltpu.VMEM((48, 32, TILE), low),
-            pltpu.VMEM((48, 32, TILE), low),
-            sem((3,)), sem((3,)), sem((16,)), sem((16,)), sem((16,)), sem((16,)), sem((4,)), sem((4,)),
-        ],
+def scan_scratch():
+    low, sem = jnp.bfloat16, pltpu.SemaphoreType.DMA
+    return [
+        pltpu.VMEM((48, 32, TILE), low),
+        pltpu.VMEM((8, TILE), jnp.float32),
+        pltpu.VMEM((16, 112, TILE), low),
+        pltpu.VMEM((16, 112, TILE), low),
+        pltpu.VMEM((16, 3, 32, TILE), low),
+        pltpu.VMEM((48, 32, TILE), low),
+        pltpu.VMEM((48, 32, TILE), low),
+        sem((3,)), sem((3,)), sem((16,)), sem((16,)), sem((16,)), sem((16,)), sem((4,)), sem((4,)),
+    ]
+
+
+def middle_kernel(
+    normed_ref, tokens_ref, gain_ref, router_ref, chosen_ref, up_ref, out_far, in_far, down_far,
+    *refs
+):
+    outs, refs = refs[:6], refs[6:]
+    all_rows, all_gates, out_w, in_w, down_w, *refs = refs
+    inside, refs = refs[:6], refs[6:]
+    middle_ref, second_ref, base_ref, back_ref, hidden_ref, acts_ref = inside
+    save_sem, load_sem, row_ss, row_rs, gate_ss, gate_rs = refs
+    saves = [pltpu.make_async_copy(near, far, save_sem.at[i]) for i, (near, far) in enumerate(zip(inside, outs))]
+    z = lax.axis_index("z")
+    own_rows = pltpu.make_async_copy(second_ref, all_rows.at[z], save_sem.at[6])
+    loads = []
+    for far, near, parts in ((out_far, out_w, 4), (in_far, in_w, 3), (down_far, down_w, 2)):
+        rows = near.shape[0] // parts
+        for i in range(parts):
+            here = pl.ds(i * rows, rows)
+            loads.append(pltpu.make_async_copy(far.at[here], near.at[here], load_sem.at[len(loads)]))
+    for copy in loads:
+        copy.start()
+    greet([{"z": ring("z", o)} for o in (1, 2, 3)])
+    depth = normed_ref.shape[1] // 4
+    middle = tokens_ref[...].astype(jnp.float32)
+    for i in range(4):
+        loads[i].wait()
+        here = slice(i * depth, (i + 1) * depth)
+        middle = middle + dot32(normed_ref[:, here], out_w[here])
+    middle_ref[...] = middle
+    saves[0].start()
+    scale = lax.rsqrt(jnp.mean(middle * middle, 1, keepdims=True) + NORM_EPS)
+    second_ref[...] = short(middle * scale * gain_ref[...])
+    saves[1].start()
+    own_rows.start()
+
+    def row_copy(o):
+        return remote(second_ref, all_rows.at[z], row_ss.at[o], row_rs.at[o], {"z": ring("z", o)})
+
+    def row_forward(o):
+        half = all_rows.shape[1] // 2
+        block = all_rows.at[lax.rem(z + 4 - o, 4), pl.ds(0 if o == 1 else half, half)]
+        return remote(block, block, row_ss.at[3 + o], row_rs.at[3 + o], {"z": ring("z", o)})
+
+    def gate_copy(o):
+        return remote(all_gates.at[z], all_gates.at[z], gate_ss.at[o], gate_rs.at[o], {"z": ring("z", o)})
+
+    for o in (1, 3):
+        row_copy(o).start()
+    logits = dot_nt(router_ref[...], second_ref[...])
+    masked = jnp.where(chosen_ref[...] > 0.0, logits, -jnp.inf)
+    powers = jnp.exp(masked - jnp.max(masked, 0, keepdims=True))
+    all_gates[z] = powers / jnp.sum(powers, 0, keepdims=True)
+    for o in (1, 3, 2):
+        gate_copy(o).start()
+    width = hidden_ref.shape[1]
+    block = 256
+    for copy in loads[4:]:
+        copy.wait()
+    second = second_ref[...]
+    for j in range(0, width, block):
+        gate = dot32(second, in_w[:, j : j + block])
+        up = dot32(second, in_w[:, width + j : width + j + block])
+        sig = jax.nn.sigmoid(gate)
+        hidden_ref[:, j : j + block] = short(gate * sig * up)
+        back = dot_nt(up_ref[...], down_w[j : j + block])
+        acts_ref[:, j : j + block] = short(back * up * sig * (1.0 + gate * (1.0 - sig)))
+        acts_ref[:, width + j : width + j + block] = short(back * gate * sig)
+    saves[4].start()
+    saves[5].start()
+    for o in (1, 3):
+        row_copy(o).wait_recv()
+        row_forward(o).start()
+    model = middle_ref.shape[1]
+    for j in range(0, model, 2 * block):
+        here = slice(j, j + 2 * block)
+        base_ref[:, here] = middle_ref[:, here] + dot32(hidden_ref[...], down_w[:, here])
+        back_ref[:, here] = dot_nt(acts_ref[...], in_w[here])
+    saves[2].start()
+    saves[3].start()
+    for o in (1, 3):
+        row_copy(o).wait_send()
+        row_forward(o).wait()
+    for o in (1, 3, 2):
+        gate_copy(o).wait()
+    for copy in saves:
+        copy.wait()
+    own_rows.wait()
+
+
+def middle_part(normed, tokens, gain, router, chosen, upstream, out_w, in_w, down_w):
+    space, away = pl.BlockSpec(memory_space=pltpu.VMEM), pl.BlockSpec(memory_space=pl.ANY)
+    slots, model = tokens.shape
+    f32, low, sem = jnp.float32, jnp.bfloat16, pltpu.SemaphoreType.DMA
+    outs = [
+        ((slots, model), f32), ((slots, model), low), ((slots, model), f32), ((slots, model), f32),
+        ((slots, down_w.shape[0]), low), ((slots, in_w.shape[1]), low), ((4, slots, model), low), ((4, *chosen.shape), f32),
+    ]
+    return pl.pallas_call(
+        middle_kernel,
+        out_shape=tuple(jax.ShapeDtypeStruct(s, d) for s, d in outs),
+        in_specs=[space] * 6 + [away] * 3,
+        out_specs=(away,) * 7 + (space,),
+        scratch_shapes=[pltpu.VMEM(w.shape, w.dtype) for w in (out_w, in_w, down_w)]
+        + [pltpu.VMEM(s, d) for s, d in outs[:6]]
+        + [sem((7,)), sem((9,)), sem((7,)), sem((7,)), sem((4,)), sem((4,))],
         compiler_params=pltpu.CompilerParams(
-            collective_id=2 if reverse else 1, has_side_effects=True, vmem_limit_bytes=32 * 2**20
+            collective_id=5, has_side_effects=True, vmem_limit_bytes=60 * 2**20
         ),
-        name="scan_backward" if reverse else "scan_forward",
-    )(state, totals, rows)
-    return result[0].reshape(pairs), result[1]
-
-
-def z_gather_kernel(count, *refs):
-    ins, outs, (ss, rs) = refs[:count], refs[count : 2 * count], refs[2 * count :]
-    me = lax.axis_index("z")
-    greet([{"z": ring("z", o)} for o in (1, 2, 3)])
-    copies = []
-    for n in range(count):
-        for o in (1, 3, 2):
-            copies.append(
-                remote(ins[n], outs[n].at[me], ss.at[n, o], rs.at[n, o], {"z": ring("z", o)})
-            )
-            copies[-1].start()
-    for n in range(count):
-        outs[n][me] = ins[n][...]
-    for copy in copies:
-        copy.wait()
-
-
-def z_gather(arrays, cid, name):
-    count = len(arrays)
-    space = pl.BlockSpec(memory_space=pltpu.VMEM)
-    sem = pltpu.SemaphoreType.DMA((count, 4))
-    return pl.pallas_call(
-        functools.partial(z_gather_kernel, count),
-        out_shape=tuple(jax.ShapeDtypeStruct((4, *a.shape), a.dtype) for a in arrays),
-        in_specs=[space] * count,
-        out_specs=(space,) * count,
-        scratch_shapes=[sem, sem],
-        compiler_params=pltpu.CompilerParams(
-            collective_id=cid, has_side_effects=True, vmem_limit_bytes=32 * 2**20
-        ),
-        name=name,
-    )(*arrays)
+        name="middle",
+    )(normed, tokens, gain, router, chosen, upstream, out_w, in_w, down_w)
 
 
 EXPERT_ORDERS = (("x", "y"), ("y", "x"))
@@ -654,8 +797,27 @@
 
 
 def expert_sum_kernel(
+    picks_ref, gates_ref, gain_ref, back_far, *refs
+):
+    far, refs = refs[:9], refs[9:]
+    weights_far, out_ref, middle_out, mix_out, post_back, router_back, normed_out, *refs = refs
+    (middle_back, mix_ref, normed_back, back_ref), refs = refs[:4], refs[4:]
+    near_refs, refs = refs[:9], refs[9:]
+    rows_ref, acts_ref, hidden_ref, grads_ref, middle_ref, shared_ref, up_ref, second_ref, router_ref = near_refs
+    expert_sum_body(
+        list(zip(far, near_refs)),
+        rows_ref, acts_ref, hidden_ref, grads_ref, back_ref, picks_ref,
+        middle_ref, shared_ref, up_ref, second_ref, gates_ref, router_ref, gain_ref, weights_far,
+        out_ref, middle_back, mix_ref, post_back, router_back, normed_back, back_far, middle_out, mix_out, normed_out, *refs,
+    )
+
+
+def expert_sum_body(
+    far_near,
     rows_ref, acts_ref, hidden_ref, grads_ref, back_ref, picks_ref,
-    out_ref, back_sum, picks_all,
+    middle_ref, shared_ref, up_ref, second_ref, gates_ref, router_ref, gain_ref, weights_far,
+    out_ref, middle_back, mix_ref, post_back, router_back, normed_back, back_far, middle_out, mix_out, normed_out,
+    stage_sem, save_sem, weights, load_sem, back_sum, picks_all,
     core_out, core_in, near, far, second_in, got, turned_rows, turned_hidden,
     core_ss, core_rs, near_ss, near_rs, far_ss, far_rs, second_ss, second_rs, zs, zr,
 ):
@@ -668,13 +830,23 @@
     small = block // 4
     third = small // 3
     cols = EXPERT_COLS
-    greet(
-        [{"c": other}]
-        + [{axis: ring(axis, o)} for axis in ("x", "y", "z") for o in (1, 2, 3)]
-    )
+    quarter = weights.shape[0] // 4
+    loads = [
+        pltpu.make_async_copy(weights_far.at[pl.ds(i * quarter, quarter)], weights.at[pl.ds(i * quarter, quarter)], load_sem.at[i])
+        for i in range(4)
+    ]
+    staged = [pltpu.make_async_copy(far, here, stage_sem.at[i]) for i, (far, here) in enumerate(far_near)]
+    staged.append(pltpu.make_async_copy(back_far, back_ref, stage_sem.at[9]))
+    saves = [
+        pltpu.make_async_copy(here, far, save_sem.at[i])
+        for i, (here, far) in enumerate(((middle_back, middle_out), (mix_ref, mix_out), (normed_back, normed_out)))
+    ]
+    for copy in staged + loads:
+        copy.start()
+    greet_neighbours()
 
     sums = []
-    for n, ref in enumerate((back_ref,)):
+    for n, ref in enumerate((back_far,)):
         for o in (1, 3, 2):
             sums.append(
                 remote(ref.at[ring("z", o)], got.at[n, o - 1], zs.at[n, o], zr.at[n, o], {"z": ring("z", o)})
@@ -686,6 +858,8 @@
     for copy in sums:
         copy.start()
     picks_all[me_z] = picks_ref[me_z]
+    for copy in staged[:4]:
+        copy.wait()
     for j in range(rows_ref.shape[1] // TILE):
         turned_rows[j * TILE : (j + 1) * TILE] = rows_ref[:, j * TILE : (j + 1) * TILE].T
     for part in range(2):
@@ -826,7 +1000,38 @@
 
     stages = (stage_product, stage_near, stage_far, stage_second, stage_last)
 
+    def way_back():
+        for copy in sums + staged[4:]:
+            copy.wait()
+        add_parts(back_ref, me_z, got.at[0], back_sum)
+        gates = gates_ref[me_z]
+        picked = jnp.concatenate([picks_all[i, 0:2] for i in range(4)], 0)
+        logits_back = gates * (picked - jnp.sum(gates * picked, 0, keepdims=True))
+        padded = jnp.concatenate([logits_back, jnp.zeros((TILE - 8, TILE), jnp.float32)], 0)
+        router_back[...] = dot32(short(padded), second_ref[...])[:8]
+        middle = middle_ref[...]
+        scale = lax.rsqrt(jnp.mean(middle * middle, 1, keepdims=True) + NORM_EPS)
+        back = shared_ref[...] + back_sum[...] + dot32(short(padded.T), router_ref[...])
+        post_back[...] = jnp.sum(back * middle * scale, 0, keepdims=True)
+        spread = back * gain_ref[...]
+        shift = jnp.mean(spread * middle, 1, keepdims=True) * scale * scale * scale
+        total = spread * scale - middle * shift + up_ref[...].astype(jnp.float32)
+        middle_back[...] = total
+        mix_ref[...] = short(total)
+        saves[0].start()
+        saves[1].start()
+        turned = short(total.T)
+        for i in range(4):
+            loads[i].wait()
+            here = slice(i * quarter, (i + 1) * quarter)
+            normed_back[:, here] = dot32(weights[here], turned).T
+        saves[2].start()
+
     def step(t, carry):
+        @pl.when(t == 5)
+        def _():
+            way_back()
+
         for lag, stage in enumerate(stages):
             k = t - lag
 
@@ -838,10 +1043,6 @@
         return carry
 
     lax.fori_loop(0, EXPERT_STEPS + len(stages) - 1, step, 0)
-
-    for copy in sums:
-        copy.wait()
-    add_parts(back_ref, me_z, got.at[0], back_sum)
 
     def finish(k, carry):
         for part in range(2):
@@ -855,25 +1056,38 @@
         return carry
 
     lax.fori_loop(0, EXPERT_STEPS, finish, 0)
-
-
-def expert_sum(rows, acts, hidden, grads, back, picks):
+    for copy in saves:
+        copy.wait()
+
+
+def expert_sum(rows, acts, hidden, grads, back, picks, middle, shared, upstream, second, gates, router, gain, weights):
     slots, cols, half = 2 * EXPERT_STEPS, EXPERT_COLS, rows.shape[1] // 2
     block = half // 4
-    low = jnp.bfloat16
-    sems = lambda *shape: pltpu.SemaphoreType.DMA(shape)
-    space = pl.BlockSpec(memory_space=pltpu.VMEM)
-    total = jax.ShapeDtypeStruct(back.shape[1:], jnp.float32)
+    low, f32 = jnp.bfloat16, jnp.float32
+    sem = pltpu.SemaphoreType.DMA
+    sems = lambda *shape: [sem(shape)] * 2
+    space, away = pl.BlockSpec(memory_space=pltpu.VMEM), pl.BlockSpec(memory_space=pl.ANY)
+    depth, model = middle.shape
+    staged = [rows, acts, hidden, grads, middle, shared, upstream, second, router]
+    outs = [
+        ((2, block // 4, EXPERT_STEPS * cols), f32), ((depth, model), f32), ((depth, model), low),
+        ((1, model), f32), ((8, model), f32), ((depth, weights.shape[0]), f32),
+    ]
     return pl.pallas_call(
         expert_sum_kernel,
-        out_shape=(
-            jax.ShapeDtypeStruct((2, block // 4, EXPERT_STEPS * cols), jnp.float32),
-            total,
-            jax.ShapeDtypeStruct(picks.shape, picks.dtype),
-        ),
-        in_specs=[space] * 6,
-        out_specs=(space,) * 3,
+        out_shape=tuple(jax.ShapeDtypeStruct(s, d) for s, d in outs),
+        in_specs=[space] * 3 + [away] * 11,
+        out_specs=(space, away, away, space, space, away),
         scratch_shapes=[
+            *[pltpu.VMEM(*outs[i]) for i in (1, 2, 5)],
+            pltpu.VMEM(back.shape, back.dtype),
+            *[pltpu.VMEM(a.shape, a.dtype) for a in staged],
+            sem((10,)),
+            sem((3,)),
+            pltpu.VMEM(weights.shape, low),
+            sem((4,)),
+            pltpu.VMEM((depth, model), f32),
+            pltpu.VMEM(picks.shape, f32),
             pltpu.VMEM((2, 2, half, cols), low),
             pltpu.VMEM((slots, half, cols), low),
             pltpu.VMEM((slots, 4, block // 2, cols), low),
@@ -882,20 +1096,22 @@
             pltpu.VMEM((1, 3, *back.shape[1:]), low),
             pltpu.VMEM(rows.shape[::-1], low),
             pltpu.VMEM((2, *hidden.shape[:0:-1]), low),
-            sems(slots), sems(slots), sems(slots, 4), sems(slots, 4), sems(slots, 2), sems(slots, 2),
-            sems(slots, 3), sems(slots, 3), sems(3, 4), sems(3, 4),
+            *sems(slots), *sems(slots, 4), *sems(slots, 2), *sems(slots, 3), *sems(3, 4),
         ],
         compiler_params=pltpu.CompilerParams(
-            collective_id=4, has_side_effects=True, vmem_limit_bytes=52 * 2**20
+            collective_id=4, has_side_effects=True, vmem_limit_bytes=60 * 2**20
         ),
         name="expert_sum",
-    )(rows, acts, hidden, grads, back, picks)
-
-
-def gather_kernel(count, *refs):
-    shards, plain_in = refs[:count], refs[count : count + 1]
-    fulls, plain_out = refs[count + 1 : 2 * count + 1], refs[2 * count + 1 : 2 * count + 2]
-    load_sem, own_sem, unit_ss, unit_rs, deep_ss, deep_rs, first_ss, first_rs, second_ss, second_rs, core_ss, core_rs, row_ss, row_rs, *staged = refs[2 * count + 2 :]
+    )(picks, gates, gain, back, *staged, weights)
+
+
+def gather_sems(count):
+    sem = lambda *shape: [pltpu.SemaphoreType.DMA(shape)] * 2
+    return sem(count, 4) + sem(count, 8) + sem(count, 4, 4) + sem(count, 4, 8) + sem(count, 4, 5)
+
+
+def gather_steps(shards, fulls, by_rows, main, sems):
+    unit_ss, unit_rs, deep_ss, deep_rs, first_ss, first_rs, second_ss, second_rs, core_ss, core_rs = sems
     x, y, c, z = (lax.axis_index(a) for a in ALL)
     first_at = (1 - c) * x + c * y
     second_at = c * x + (1 - c) * y
@@ -906,15 +1122,8 @@
     def along_second(o):
         return {"x": lax.rem(x + c * o, 4), "y": lax.rem(y + (1 - c) * o, 4)}
 
-    greet(
-        [{"c": 1 - c}]
-        + [{axis: ring(axis, o)} for axis in ("x", "y", "z") for o in (1, 2, 3)]
-    )
-
-    by_rows = (0, 1)
-
     def sizes(n):
-        if n == 0:
+        if main and n == 0:
             total = fulls[0].shape[1]
             spread = total * 16 // 25
             return total // 2, spread // 2, spread // 32
@@ -933,7 +1142,7 @@
     def window(n, shard, deep, offset, length):
         rows, width = shards[n].shape
         at = place(n, deep, offset)
-        if n == 0:
+        if main and n == 0:
             return fulls[0].at[shard, pl.ds(pl.multiple_of(at, 16), length)]
         rows = pl.ds(pl.multiple_of(at + shard * rows, 16), length)
         if n in by_rows:
@@ -947,20 +1156,6 @@
             return shards[n].at[rows]
         return shards[n].at[rows, pl.ds(pl.multiple_of(c * (width // 2), 128), width // 2)]
 
-    def own_rows(n):
-        return fulls[0].shape[1] if n == 0 else shards[n].shape[0]
-
-    def own_load(n):
-        return pltpu.make_async_copy(shards[n].at[pl.ds(0, own_rows(n))], staged[n], load_sem.at[n])
-
-    def own_copy(n):
-        if n == 0:
-            return pltpu.make_async_copy(staged[0], fulls[0].at[z], own_sem.at[0])
-        total = shards[n].shape[0]
-        return pltpu.make_async_copy(
-            staged[n], fulls[n].at[pl.ds(pl.multiple_of(z * total, 16), total)], own_sem.at[n]
-        )
-
     def came_from(o):
         return lax.rem(z - o + 4, 4)
 
@@ -1001,116 +1196,213 @@
         block = window(n, came_from(o), False, at, 2 * unit)
         return remote(block, block, second_ss.at[n, o, 4 + step], second_rs.at[n, o, 4 + step], along_second(step))
 
-    def core_copies(n, o):
+    def core_copy(n, o, which):
         total, spread, unit = sizes(n)
         shard = came_from(o)
-        blocks = [window(n, shard, False, 0, spread)]
-        if spread < total:
-            blocks.append(window(n, shard, True, 0, total - spread))
-        return [
-            remote(block, block, core_ss.at[n, o, i], core_rs.at[n, o, i], {"c": 1 - c})
-            for i, block in enumerate(blocks)
-        ]
-
-    def plain_copy(i, o):
-        return remote(plain_in[i], plain_out[i].at[z], row_ss.at[i, o], row_rs.at[i, o], {"z": ring("z", o)})
-
-    arrays = range(count)
+        if which == 4:
+            block = window(n, shard, True, 0, total - spread)
+        else:
+            block = window(n, shard, False, lax.rem(second_at + 4 - which, 4) * 4 * unit, 4 * unit)
+        return remote(block, block, core_ss.at[n, o, which], core_rs.at[n, o, which], {"c": 1 - c})
+
+    def core_copies(n, o):
+        return [core_copy(n, o, which) for which in ((0, 1, 3, 2, 4) if n in deep else (0, 1, 3, 2))]
+
+    arrays = range(len(shards))
     deep = [n for n in arrays if sizes(n)[0] > sizes(n)[1]]
     sides, offsets = (1, 3), (1, 3, 2)
-    for n in arrays:
-        for o in offsets:
-            unit_copy(n, o).start()
-    for n in deep:
-        for o in sides:
-            deep_copy(n, o).start()
-    for i in range(1):
-        for o in offsets:
-            plain_copy(i, o).start()
-    for n in arrays:
-        own_load(n).start()
-    own_plain = [pltpu.make_async_copy(plain_in[i], plain_out[i].at[z], own_sem.at[count + i]) for i in range(1)]
-    for copy in own_plain:
-        copy.start()
-    for n in arrays:
-        for o in offsets:
-            unit_copy(n, o).wait_recv()
-            for step in offsets:
-                first_copy(n, o, step).start()
-    for n in arrays:
-        own_load(n).wait()
-        own_copy(n).start()
-    for n in arrays:
-        for o in offsets:
-            for step in offsets:
-                first_copy(n, o, step).wait_recv()
-            for step in sides:
-                second_copy(n, o, step).start()
-    for n in arrays:
-        if n in deep:
+
+    def begin():
+        for n in arrays:
+            for o in offsets:
+                unit_copy(n, o).start()
+        for n in deep:
+            for o in sides:
+                deep_copy(n, o).start()
+
+    def go_first():
+        for n in arrays:
+            for o in offsets:
+                unit_copy(n, o).wait_recv()
+                for step in offsets:
+                    first_copy(n, o, step).start()
+
+    def go_second():
+        for n in arrays:
+            for o in offsets:
+                for step in offsets:
+                    first_copy(n, o, step).wait_recv()
+                for step in sides:
+                    second_copy(n, o, step).start()
+                core_copy(n, o, 0).start()
+
+    def go_deep():
+        for n in deep:
             for o in sides:
                 deep_copy(n, o).wait_recv()
                 deep_forward(n, o).start()
-                core_copies(n, o)[1].start()
-        for o in offsets:
-            for step in sides:
-                second_copy(n, o, step).wait_recv()
-                second_forward(n, o, step).start()
-    for n in arrays:
-        for o in offsets:
-            for step in sides:
-                second_forward(n, o, step).wait_recv()
-            core_copies(n, o)[0].start()
-        if n in deep:
-            for o in sides:
-                deep_forward(n, o).wait_recv()
-            core_copies(n, 2)[1].start()
-    for i in range(1):
-        for o in offsets:
-            plain_copy(i, o).wait()
-        own_plain[i].wait()
-    for n in arrays:
-        own_copy(n).wait()
-        for o in offsets:
-            for copy in core_copies(n, o):
-                copy.wait()
-            unit_copy(n, o).wait_send()
-            for step in offsets:
-                first_copy(n, o, step).wait_send()
-            for step in sides:
-                second_copy(n, o, step).wait_send()
-                second_forward(n, o, step).wait_send()
-        if n in deep:
-            for o in sides:
-                deep_copy(n, o).wait_send()
-                deep_forward(n, o).wait_send()
-
-
-def gather_weights(shards, plain, main_rows):
-    count = len(shards)
-    space = pl.BlockSpec(memory_space=pl.ANY)
-    sem = lambda *shape: pltpu.SemaphoreType.DMA(shape)
-    fulls = [(4, main_rows, shards[0].shape[1])] + [(4 * s.shape[0], s.shape[1]) for s in shards[1:]]
+                core_copy(n, o, 4).start()
+
+    def go_forward():
+        for n in arrays:
+            for o in offsets:
+                for step in sides:
+                    second_copy(n, o, step).wait_recv()
+                    second_forward(n, o, step).start()
+                    core_copy(n, o, step).start()
+
+    def go_core():
+        for n in arrays:
+            for o in offsets:
+                for step in sides:
+                    second_forward(n, o, step).wait_recv()
+                core_copy(n, o, 2).start()
+            if n in deep:
+                for o in sides:
+                    deep_forward(n, o).wait_recv()
+                core_copy(n, 2, 4).start()
+
+    def arrived(n, o):
+        for copy in core_copies(n, o):
+            copy.wait_recv()
+
+    def finish():
+        for n in arrays:
+            for o in offsets:
+                for copy in core_copies(n, o):
+                    copy.wait_send()
+                unit_copy(n, o).wait_send()
+                for step in offsets:
+                    first_copy(n, o, step).wait_send()
+                for step in sides:
+                    second_copy(n, o, step).wait_send()
+                    second_forward(n, o, step).wait_send()
+            if n in deep:
+                for o in sides:
+                    deep_copy(n, o).wait_send()
+                    deep_forward(n, o).wait_send()
+
+    return dict(
+        begin=begin, first=go_first, second=go_second, deep=go_deep, forward=go_forward, core=go_core,
+        arrived=arrived, finish=finish, came_from=came_from,
+    )
+
+
+def project_kernel(
+    tokens_ref, gain_ref, tail_ref, shard_ref, main_out, norm_far, proj_far, tail_out, tails_ref,
+    kept, main, turned, norm_ref, proj_ref, out_sem, save_sem, load_sem, tail_ss, tail_rs, *sems
+):
+    z = lax.axis_index("z")
+    rows, width = main.shape[1:]
+    load = pltpu.make_async_copy(shard_ref.at[pl.ds(0, rows)], main.at[z], load_sem.at[0])
+    load.start()
+    greet_neighbours()
+    steps = gather_steps([shard_ref], [main], (0,), True, sems)
+    steps["begin"]()
+    tails = [
+        remote(tail_ref, tails_ref.at[z], tail_ss.at[o], tail_rs.at[o], {"z": ring("z", o)}) for o in (1, 3, 2)
+    ]
+    for copy in tails:
+        copy.start()
+    tails_ref[z] = tail_ref[...]
+
+    def save(shard):
+        return pltpu.make_async_copy(main.at[shard], main_out.at[shard], save_sem.at[shard])
+
+    values = tokens_ref[...].astype(jnp.float32)
+    scale = lax.rsqrt(jnp.mean(values * values, 1, keepdims=True) + NORM_EPS)
+    normed = values * scale * gain_ref[...]
+    norm_ref[...] = short(normed)
+    save_norm = pltpu.make_async_copy(norm_ref, norm_far, out_sem.at[0])
+    save_norm.start()
+    kept[...] = short(normed.T)
+    steps["first"]()
+    block = PROJ_BLOCK
+
+    def add(shard, fresh):
+        right = kept[pl.ds(pl.multiple_of(shard * width, TILE), width)]
+
+        def rows_at(j, carry):
+            here = pl.ds(pl.multiple_of(j * block, block), block)
+            product = dot32(main[shard, here], right)
+            turned[here] = product if fresh else turned[here] + product
+            return carry
+
+        lax.fori_loop(0, rows // block, rows_at, 0)
+
+    load.wait()
+    add(z, True)
+    save(z).start()
+    steps["second"]()
+    steps["deep"]()
+    for copy in tails:
+        copy.wait()
+    total = dot32(tails_ref[0], kept[:width])
+    for i in range(1, 4):
+        total = total + dot32(tails_ref[i], kept[i * width : (i + 1) * width])
+    tail_out[...] = total.T
+    steps["forward"]()
+    steps["core"]()
+    for o in (1, 3):
+        steps["arrived"](0, o)
+        shard = steps["came_from"](o)
+        save(shard).start()
+        add(shard, False)
+    steps["arrived"](0, 2)
+    shard = steps["came_from"](2)
+    save(shard).start()
+    right = kept[pl.ds(pl.multiple_of(shard * width, TILE), width)]
+
+    def save_block(j):
+        here = pl.ds(pl.multiple_of(j * block, block), block)
+        return pltpu.make_async_copy(proj_ref.at[:, here], proj_far.at[:, here], out_sem.at[1 + j])
+
+    def last(j, carry):
+        here = pl.ds(pl.multiple_of(j * block, block), block)
+        proj_ref[:, here] = (turned[here] + dot32(main[shard, here], right)).T
+        save_block(j).start()
+        return carry
+
+    lax.fori_loop(0, rows // block, last, 0)
+    save_norm.wait()
+    for j in range(rows // block):
+        save_block(j).wait()
+    steps["finish"]()
+    for i in range(4):
+        save(i).wait()
+
+
+def project(tokens, gain, tail, shard, main_rows):
+    slots, model = tokens.shape
+    width = shard.shape[1]
+    space, away = pl.BlockSpec(memory_space=pltpu.VMEM), pl.BlockSpec(memory_space=pl.ANY)
+    sem = pltpu.SemaphoreType.DMA
     return pl.pallas_call(
-        functools.partial(gather_kernel, count),
-        out_shape=tuple(jax.ShapeDtypeStruct(f, jnp.bfloat16) for f in fulls)
-        + tuple(jax.ShapeDtypeStruct((4, *p.shape), p.dtype) for p in plain),
-        in_specs=[space] * (count + 1),
-        out_specs=(space,) * (count + 1),
+        project_kernel,
+        out_shape=(
+            jax.ShapeDtypeStruct((4, main_rows, width), jnp.bfloat16),
+            jax.ShapeDtypeStruct((slots, model), jnp.bfloat16),
+            jax.ShapeDtypeStruct((slots, main_rows), jnp.float32),
+            jax.ShapeDtypeStruct((slots, tail.shape[0]), jnp.float32),
+            jax.ShapeDtypeStruct((4, *tail.shape), jnp.bfloat16),
+        ),
+        in_specs=[space, space, space, away],
+        out_specs=(away, away, away, space, space),
         scratch_shapes=[
-            sem(count),
-            sem(count + 1),
-            sem(count, 4), sem(count, 4), sem(count, 8), sem(count, 8),
-            sem(count, 4, 4), sem(count, 4, 4), sem(count, 4, 8), sem(count, 4, 8),
-            sem(count, 4, 2), sem(count, 4, 2), sem(1, 4), sem(1, 4),
-            pltpu.VMEM((main_rows, shards[0].shape[1]), jnp.bfloat16),
+            pltpu.VMEM((model, slots), jnp.bfloat16),
+            pltpu.VMEM((4, main_rows, width), jnp.bfloat16),
+            pltpu.VMEM((main_rows, slots), jnp.float32),
+            pltpu.VMEM((slots, model), jnp.bfloat16),
+            pltpu.VMEM((slots, main_rows), jnp.float32),
+            sem((1 + main_rows // PROJ_BLOCK,)),
+            sem((4,)), sem((1,)), sem((4,)), sem((4,)),
         ]
-        + [pltpu.VMEM(s.shape, s.dtype) for s in shards[1:]],
+        + gather_sems(1),
         compiler_params=pltpu.CompilerParams(
             collective_id=6, has_side_effects=True, vmem_limit_bytes=60 * 2**20
         ),
-        name="gather_weights",
-    )(*shards, *plain)
+        name="project",
+    )(tokens, gain, tail, shard)
 
 
 TILE = 128
@@ -1168,7 +1460,7 @@
     ext[8 : 8 + TILE] = proj_ref[:, pl.ds(pl.multiple_of(INNER + j * TILE, TILE), TILE)]
 
 
-def mixer_in_kernel(proj_ref, tail_ref, halo_ref, cw_ref, heads_ref, mixed_ref, state_ref, totals_ref, run_ref, step_ref, ext):
+def mixer_in_part(tick, halo_copy, proj_ref, tail_ref, halo_ref, cw_ref, heads_ref, mixed_ref, state_ref, totals_ref, run_ref, step_ref, ext):
     unused_raw, step, log_decay = head_steps(tail_ref, heads_ref)
     lower = (row_ids() >= lane_ids()).astype(jnp.float32)
     run = jnp.dot(lower, log_decay, precision=HIGH, preferred_element_type=jnp.float32)
@@ -1178,6 +1470,13 @@
     totals_ref[...] = jnp.broadcast_to(last, totals_ref.shape)
     weight = jnp.exp(last - run) * step
 
+    halo_copy.wait()
+    spot = lax.axis_index("x") * 8 + lax.axis_index("y") * 2 + lax.axis_index("c")
+
+    @pl.when(spot == 0)
+    def _():
+        halo_ref[...] = jnp.zeros_like(halo_ref)
+
     def conv(j, carry):
         fill_ext(ext, halo_ref, proj_ref, j)
         u = taps_of(ext, cw_ref, tile_at(j))
@@ -1185,11 +1484,12 @@
         return carry
 
     lax.fori_loop(0, CONV // TILE, conv, 0)
+    tick()
     in_map = short(mixed_ref[:, INNER : INNER + TILE])
 
     def state(p, carry):
         scaled = mixed_ref[:, tile_at(p)] * both_heads(head_columns(weight, p))
-        state_ref[p] = short(dot32(short(scaled.T), in_map))
+        state_ref[pl.ds(4 * p, 4)] = short(dot32(short(scaled.T), in_map)).reshape(4, 32, TILE)
         return carry
 
     lax.fori_loop(0, HEADS // 2, state, 0, unroll=2)
@@ -1199,7 +1499,7 @@
     return jnp.where(lower, jnp.exp(jnp.minimum(column - row, 0.0)), 0.0)
 
 
-def mixer_out_kernel(proj_ref, mixed_ref, run_ref, step_ref, carried_ref, wide_ref, normed_ref, scanned_ref, gated, rows, ):
+def mixer_out_part(proj_ref, mixed_ref, run_ref, step_ref, carried_ref, wide_ref, normed_ref, scanned_ref, gated, rows):
     run = run_ref[...]
     rows[0] = run.T
     rows[1] = step_ref[...].T
@@ -1219,7 +1519,7 @@
             weights = kernel * decays * rows[1, pl.ds(2 * p + h, 1)]
             parts.append(dot32(short(weights), values_low))
         result = jnp.where(lane_ids() < TILE // 2, parts[0], parts[1])
-        result = result + jnp.exp(both_heads(columns)) * dot_nt(out_low, carried_ref[p])
+        result = result + jnp.exp(both_heads(columns)) * dot_nt(out_low, carried_ref[pl.ds(4 * p, 4)].reshape(TILE, TILE))
         result = result + wide_ref[0:1, tile_at(p)] * values
         scanned_ref[:, tile_at(p)] = result
         gate = proj_ref[:, tile_at(p)]
@@ -1237,7 +1537,113 @@
     lax.fori_loop(0, HEADS // 2, norm, 0, unroll=2)
 
 
-def gate_back_kernel(proj_ref, mixed_ref, scanned_ref, back_ref, run_ref, wide_ref, result_ref, gate_ref, gain_ref, state_ref, gated):
+def mixer_kernel(
+    tail_ref, cw_ref, heads_ref, wide_ref, rows_ref, proj_far, *refs
+):
+    shards, refs = refs[:3], refs[3:]
+    (mixed_far, totals_ref, run_ref, step_ref, halo_ref, carried_far, normed_ref, scanned_far, all_rows), refs = refs[:9], refs[9:]
+    fulls, refs = refs[:3], refs[3:]
+    edge, state_ref, ext, gated, rows, mixed_ref, scanned_ref, carried_ref, proj_ref, proj_sem, halo_ss, halo_rs, load_sem, save_sem, out_sem, *refs = refs
+    staged, refs = refs[:3], refs[3:]
+    scan_refs, sems = refs[: len(scan_scratch())], refs[len(scan_scratch()) :]
+    z = lax.axis_index("z")
+    loads = [pltpu.make_async_copy(shards[n], staged[n], load_sem.at[n]) for n in range(3)]
+    views = [
+        ref.at[at : at + 64, columns]
+        for columns in (slice(INNER, INNER + CONV), slice(0, INNER))
+        for at in (0, 64)
+        for ref in (proj_far, proj_ref)
+    ]
+    proj_loads = [pltpu.make_async_copy(views[2 * i], views[2 * i + 1], proj_sem.at[i]) for i in range(4)]
+    for copy in proj_loads + loads:
+        copy.start()
+    greet_plane()
+    proj_loads[0].wait()
+    proj_loads[1].wait()
+    edge[...] = proj_ref[TILE - 8 :, INNER : INNER + CONV]
+    halo_copy = remote(edge, halo_ref, halo_ss.at[0], halo_rs.at[0], line_neighbour(True))
+    halo_copy.start()
+    steps = gather_steps(shards, fulls, (0,), False, sems)
+    steps["begin"]()
+    mixer_in_part(steps["first"], halo_copy, proj_ref, tail_ref, halo_ref, cw_ref, heads_ref, mixed_ref, state_ref, totals_ref, run_ref, step_ref, ext)
+    save_mixed = pltpu.make_async_copy(mixed_ref, mixed_far, out_sem.at[0])
+    save_mixed.start()
+    steps["second"]()
+    saves = []
+    for n in range(3):
+        loads[n].wait()
+        total = shards[n].shape[0]
+        saves.append(
+            pltpu.make_async_copy(
+                staged[n], fulls[n].at[pl.ds(pl.multiple_of(z * total, 16), total)], save_sem.at[n]
+            )
+        )
+        saves[-1].start()
+
+    def tick(n):
+        if n == 0:
+            steps["deep"]()
+        if n == 2:
+            steps["forward"]()
+        if n == 3:
+            steps["core"]()
+
+    state_exchange(False, state_ref, totals_ref, rows_ref, carried_ref, all_rows, None, tick, *scan_refs)
+    save_carried = pltpu.make_async_copy(carried_ref, carried_far, out_sem.at[2])
+    save_carried.start()
+    proj_loads[2].wait()
+    proj_loads[3].wait()
+    mixer_out_part(proj_ref, mixed_ref, run_ref, step_ref, carried_ref, wide_ref, normed_ref, scanned_ref, gated, rows)
+    save_scanned = pltpu.make_async_copy(scanned_ref, scanned_far, out_sem.at[1])
+    save_scanned.start()
+    for n in range(3):
+        saves[n].wait()
+        for o in (1, 3, 2):
+            steps["arrived"](n, o)
+    steps["finish"]()
+    save_mixed.wait()
+    save_scanned.wait()
+    save_carried.wait()
+
+
+def mixer(projected, tail_values, taps, heads, wide, rows, shards):
+    space, away = pl.BlockSpec(memory_space=pltpu.VMEM), pl.BlockSpec(memory_space=pl.ANY)
+    f32, low, sem = jnp.float32, jnp.bfloat16, pltpu.SemaphoreType.DMA
+    square = (TILE, TILE)
+    outs = [
+        ((TILE, CONV), f32), ((8, TILE), f32), (square, f32), (square, f32), ((8, CONV), f32),
+        ((96, 32, TILE), low), ((TILE, INNER), low), ((TILE, INNER), f32), ((4, *rows.shape), low),
+    ]
+    fulls = [((4 * s.shape[0], s.shape[1]), low) for s in shards]
+    return pl.pallas_call(
+        mixer_kernel,
+        out_shape=tuple(jax.ShapeDtypeStruct(s, d) for s, d in outs + fulls),
+        in_specs=[space] * 5 + [away] * 4,
+        out_specs=tuple(away if i in (0, 5, 7, 8) else space for i in range(len(outs))) + (away,) * 3,
+        scratch_shapes=[
+            pltpu.VMEM((8, CONV), f32),
+            pltpu.VMEM((96, 32, TILE), low),
+            pltpu.VMEM((TILE + 8, TILE), f32),
+            pltpu.VMEM((TILE, INNER), f32),
+            pltpu.VMEM((2, *square), f32),
+            pltpu.VMEM((TILE, CONV), f32),
+            pltpu.VMEM((TILE, INNER), f32),
+            pltpu.VMEM((96, 32, TILE), low),
+            pltpu.VMEM(projected.shape, f32),
+            sem((4,)),
+            sem((1,)), sem((1,)), sem((3,)), sem((3,)), sem((3,)),
+            *[pltpu.VMEM(s.shape, s.dtype) for s in shards],
+        ]
+        + scan_scratch()
+        + gather_sems(3),
+        compiler_params=pltpu.CompilerParams(
+            collective_id=1, has_side_effects=True, vmem_limit_bytes=60 * 2**20
+        ),
+        name="mixer",
+    )(tail_values, taps, heads, wide, rows, projected, *shards)
+
+
+def gate_back_part(tick, proj_ref, mixed_ref, scanned_ref, back_ref, run_ref, wide_ref, result_ref, gate_ref, gain_ref, state_ref, gated):
     run = run_ref[...]
     out_map = short(mixed_ref[:, INNER + TILE : INNER + 2 * TILE])
 
@@ -1252,6 +1658,8 @@
     squares, products = lax.fori_loop(0, HEADS // 2, first, (zero, zero), unroll=2)
     scale = lax.rsqrt(jnp.sum(squares, 1, keepdims=True) / INNER + NORM_EPS)
     shift = jnp.sum(products, 1, keepdims=True) * scale * scale * scale / INNER
+
+    tick()
 
     def second(p, carry):
         lanes = tile_at(p)
@@ -1265,39 +1673,48 @@
         result_ref[:, lanes] = result_back
         gate_ref[:, lanes] = short(g_back * scanned_ref[:, lanes] * sig * (1.0 + gate * (1.0 - sig)))
         moved = result_back * jnp.exp(both_heads(head_columns(run, p)))
-        state_ref[p] = short(dot32(short(moved.T), out_map))
+        state_ref[pl.ds(4 * p, 4)] = short(dot32(short(moved.T), out_map)).reshape(4, 32, TILE)
         return carry
 
     lax.fori_loop(0, HEADS // 2, second, 0, unroll=2)
 
 
 def mixer_back_kernel(
-    proj_ref, tail_ref, halo_ref, cw_ref, heads_ref, mixed_ref, run_ref, step_ref, wide_ref,
-    carried_ref, result_ref, leaving_ref, lefts_ref, acts_ref, mix_ref, up_ref,
-    conv_ref, rim_ref, taps_ref, step_back_ref, heads_back_ref, shared_in_ref, out_ref, shared_out_ref,
-    rows, column_sums, row_sums, kernel_back, maps_back, mixed_back, ext, padded, rights, *sum_scratch,
+    tail_ref, halo_ref, cw_ref, heads_ref, run_ref, step_ref, wide_ref, totals_ref, valid_ref, *refs
 ):
-    greet_neighbours()
+    away, refs = refs[:11], refs[11:]
+    (rim_in_ref, taps_ref, step_back_ref, heads_back_ref, shared_in_ref, out_ref, shared_out_ref,
+    gate_far, gain_ref, block_ref, conv_far,
+    gate_ref, parts_sum, save_sem, result_ref, gated, rim_ref, rows, column_sums, row_sums, kernel_back, maps_back, mixed_back, ext, padded, rights,
+    state_ref, leaving_ref, parts_in, rim_ss, rim_rs, load_sem, conv_ref), refs = refs[:33], refs[33:]
+    here, refs = refs[:11], refs[11:]
+    scan_refs, sum_scratch = refs[: len(scan_scratch())], refs[len(scan_scratch()) :]
+    loads = [pltpu.make_async_copy(far, near, load_sem.at[i]) for i, (far, near) in enumerate(zip(away, here))]
+    for copy in loads:
+        copy.start()
+    lefts_ref, acts_ref, mix_ref, up_ref, proj_ref, scanned_ref, back_ref, mixed_ref, parts_ref, carried_ref, base_ref = here
+    greet_plane()
+    for copy in loads[:4]:
+        copy.wait()
     model = mix_ref.shape[1]
-    rights[:, : 4 * RS_COLS] = acts_ref[...]
-    for part in range(3):
-        at = (RS_FIRST[part] + RS_COUNTS[part] - 1) * RS_COLS
-        rights[:, at : at + RS_COLS] = up_ref[:, part * RS_COLS : (part + 1) * RS_COLS]
-        if part:
-            rights[:, at - model : at] = mix_ref[...]
+    plain = [acts_ref.shape[1] // RS_COLS, model // RS_COLS, model // RS_COLS]
+    up_at = [0, RS_COUNTS[0] - plain[0], RS_COUNTS[0] + RS_COUNTS[1] - plain[0] - plain[1]]
+    for part, ref in enumerate((acts_ref, mix_ref, mix_ref)):
+        at, end = RS_FIRST[part] * RS_COLS, (RS_FIRST[part] + RS_COUNTS[part]) * RS_COLS
+        rights[:, at : at + ref.shape[1]] = ref[...]
+        at = at + ref.shape[1]
+        rights[:, at:end] = up_ref[:, up_at[part] * RS_COLS : up_at[part] * RS_COLS + end - at]
     share = lefts_ref.shape[1] // 2
 
     def left_of(part, k, which):
-        n = k // 4 if part == 0 else 2 * part + k // 3
+        n = 2 * part + k // plain[part]
         return lefts_ref[n, pl.ds(pl.multiple_of(which * share, share), share), :]
 
     def right_of(part, k, col):
         return rights[:, pl.ds(pl.multiple_of((RS_FIRST[part] + k) * RS_COLS + col, 256), 256)]
 
     def store(part, k, total):
-        plain = RS_COUNTS[part] - 1
-
-        @pl.when(k < plain)
+        @pl.when(k < plain[part])
         def _():
             lanes = pl.ds(pl.multiple_of(k * RS_COLS, RS_COLS), RS_COLS)
             if part == 0:
@@ -1305,11 +1722,27 @@
             else:
                 out_ref[12 * part - 12 : 12 * part, lanes] = total[:12]
 
-        @pl.when(k == plain)
+        @pl.when(k >= plain[part])
         def _():
-            shared_out_ref[:, part * RS_COLS : (part + 1) * RS_COLS] = total[:8]
+            lanes = pl.ds(pl.multiple_of((k - plain[part] + up_at[part]) * RS_COLS, RS_COLS), RS_COLS)
+            shared_out_ref[:, lanes] = total[:8]
 
     sum_step, sum_finish = grad_sum_steps(sum_scratch, left_of, right_of, store)
+
+    sum_step(0)
+    for copy in loads[4:8]:
+        copy.wait()
+    gate_back_part(
+        lambda: sum_step(1), proj_ref, mixed_ref, scanned_ref, back_ref, run_ref, wide_ref, result_ref, gate_ref, gain_ref,
+        state_ref, gated,
+    )
+    save_gate = pltpu.make_async_copy(gate_ref, gate_far, save_sem.at[0])
+    save_gate.start()
+    sum_step(2)
+    loads[8].wait()
+    state_exchange(
+        True, state_ref, totals_ref, parts_ref, leaving_ref, parts_in, parts_sum, lambda n: sum_step(3 + n), *scan_refs
+    )
     run, step = run_ref[...], step_ref[...]
     rows[0] = run.T
     rows[1] = step.T
@@ -1329,10 +1762,14 @@
     kernel_back[...] = jnp.zeros_like(kernel_back)
     maps_back[...] = jnp.zeros_like(maps_back)
 
+    loads[9].wait()
+    loads[10].wait()
+    block_ref[...] = short(jnp.where(valid_ref[...] > 0.0, base_ref[...] + parts_sum[...], 0.0))
+
     def pair(p, carry):
-        @pl.when(lax.rem(p, 3) == 0)
+        @pl.when(lax.rem(p, 4) == 0)
         def _():
-            sum_step(p // 3)
+            sum_step(7 + p // 4)
 
         lanes = tile_at(p)
         values, back = mixed_ref[:, lanes], result_ref[:, lanes]
@@ -1357,7 +1794,8 @@
             row_sums[1, at] = jnp.sum(loose, 0, keepdims=True)
             parts.append(dot32(short(weights.T), back_low))
         values_back = jnp.where(left_half, parts[0], parts[1]) + wide_ref[0:1, lanes] * back
-        carried, leaving = carried_ref[p], leaving_ref[p]
+        carried = carried_ref[pl.ds(4 * p, 4)].reshape(TILE, TILE)
+        leaving = leaving_ref[pl.ds(4 * p, 4)].reshape(TILE, TILE)
         moved = back * jnp.exp(both_heads(columns))
         moved_low = short(moved)
         seen = dot_nt(out_low, carried)
@@ -1407,13 +1845,10 @@
     mixed_back[:, INNER : INNER + TILE] = maps_back[0] + dot32(short(both.T), out_low)
     mixed_back[:, INNER + TILE : INNER + 2 * TILE] = maps_back[1] + dot32(short(both), in_low)
     padded[0:8] = jnp.zeros((8, TILE), jnp.float32)
+    sum_step(13)
     padded[8 + TILE : 16 + TILE] = jnp.zeros((8, TILE), jnp.float32)
 
     def conv(j, carry):
-        @pl.when(lax.rem(j, 13) == 0)
-        def _():
-            sum_step(8 + j // 13)
-
         lanes = tile_at(j)
         fill_ext(ext, halo_ref, proj_ref, j)
         u = taps_of(ext, cw_ref, lanes)
@@ -1433,19 +1868,32 @@
         return carry
 
     lax.fori_loop(0, CONV // TILE, conv, 0)
+    rim_copy = remote(rim_ref, rim_in_ref, rim_ss.at[0], rim_rs.at[0], line_neighbour(False))
+    rim_copy.start()
+    save_conv = pltpu.make_async_copy(conv_ref, conv_far, save_sem.at[1])
+    save_conv.start()
     sum_finish()
-
-
-def tile_call(kernel, outs, scratch, name, *args, collective=None):
+    rim_copy.wait()
+    save_gate.wait()
+    save_conv.wait()
+    spot = lax.axis_index("x") * 8 + lax.axis_index("y") * 2 + lax.axis_index("c")
+
+    @pl.when(spot == 31)
+    def _():
+        rim_in_ref[...] = jnp.zeros_like(rim_in_ref)
+
+
+def tile_call(kernel, outs, scratch, name, *args, collective=None, away=0, away_outs=()):
     space = pl.BlockSpec(memory_space=pltpu.VMEM)
+    far = pl.BlockSpec(memory_space=pl.ANY)
     params = dict(vmem_limit_bytes=40 * 2**20)
     if collective is not None:
-        params = dict(vmem_limit_bytes=58 * 2**20, collective_id=collective, has_side_effects=True)
+        params = dict(vmem_limit_bytes=60 * 2**20, collective_id=collective, has_side_effects=True)
     return pl.pallas_call(
         kernel,
         out_shape=tuple(jax.ShapeDtypeStruct(s, d) for s, d in outs),
-        in_specs=[space] * len(args),
-        out_specs=(space,) * len(outs),
+        in_specs=[space] * (len(args) - away) + [far] * away,
+        out_specs=tuple(far if i in away_outs else space for i in range(len(outs))),
         scratch_shapes=[pltpu.VMEM(s, jnp.float32) if isinstance(s, tuple) else s for s in scratch],
         compiler_params=pltpu.CompilerParams(**params),
         name=name,
@@ -1453,127 +1901,6 @@
 
 
 PROJ_BLOCK = 640
-
-
-def project_kernel(tokens_ref, gain_ref, *refs):
-    *mains, tail_ref, norm_ref, proj_ref, tail_out, kept = refs
-    width = mains[0].shape[2]
-
-    def product(weights):
-        total = dot32(weights[0], kept[:width])
-        for i in range(1, len(weights)):
-            total = total + dot32(weights[i], kept[i * width : (i + 1) * width])
-        return total.T
-
-    @pl.when(pl.program_id(0) == 0)
-    def _():
-        values = tokens_ref[...].astype(jnp.float32)
-        scale = lax.rsqrt(jnp.mean(values * values, 1, keepdims=True) + NORM_EPS)
-        normed = values * scale * gain_ref[...]
-        norm_ref[...] = short(normed)
-        kept[...] = short(normed.T)
-        tail_out[...] = product([tail_ref[i] for i in range(len(mains))])
-
-    proj_ref[...] = product([m[0] for m in mains])
-
-
-def project(tokens, gain, main, tail):
-    parts, rows, width = main.shape
-    slots, model = tokens.shape
-    whole = lambda shape: pl.BlockSpec(shape, lambda j: (0,) * len(shape))
-    return pl.pallas_call(
-        project_kernel,
-        grid=(rows // PROJ_BLOCK,),
-        out_shape=(
-            jax.ShapeDtypeStruct((slots, model), jnp.bfloat16),
-            jax.ShapeDtypeStruct((slots, rows), jnp.float32),
-            jax.ShapeDtypeStruct((slots, tail.shape[1]), jnp.float32),
-        ),
-        in_specs=[
-            whole((slots, model)),
-            whole((1, model)),
-            *[pl.BlockSpec((1, PROJ_BLOCK, width), lambda j, i=i: (i, j, 0)) for i in range(parts)],
-            whole(tail.shape),
-        ],
-        out_specs=(
-            whole((slots, model)),
-            pl.BlockSpec((slots, PROJ_BLOCK), lambda j: (0, j)),
-            whole((slots, tail.shape[1])),
-        ),
-        scratch_shapes=[pltpu.VMEM((model, slots), jnp.bfloat16)],
-        compiler_params=pltpu.CompilerParams(vmem_limit_bytes=56 * 2**20),
-        name="project",
-    )(tokens, gain, *[main] * parts, tail)
-
-
-def project_back_kernel(gate_ref, conv_ref, tail_back_ref, rim_ref, *refs):
-    *mains, tail_ref, tokens_ref, gain_ref, middle_ref, tokens_back_ref, gain_back_ref, back_ref, total = refs
-    parts, width = len(mains), mains[0].shape[2]
-    step = pl.program_id(0)
-
-    @pl.when(step == 0)
-    def _():
-        for i in range(parts):
-            total[:, i * width : (i + 1) * width] = dot32(short(tail_back_ref[...]), tail_ref[i])
-        inner, conv = gate_ref.shape[1], conv_ref.shape[1]
-        back_ref[:, :inner] = gate_ref[...]
-        back_ref[:, inner : inner + conv] = short(conv_ref[...])
-        rim = jnp.concatenate([jnp.zeros((8, conv), jnp.float32), rim_ref[...]], 0)
-        back_ref[TILE - 16 :, inner : inner + conv] = short(conv_ref[TILE - 16 :] + rim)
-        back_ref[:, inner + conv : inner + conv + TILE] = short(tail_back_ref[...])
-        rest = back_ref.shape[1] - inner - conv - TILE
-        back_ref[:, inner + conv + TILE :] = jnp.zeros((TILE, rest), jnp.bfloat16)
-
-    block = mains[0].shape[1]
-    here = back_ref[:, pl.ds(pl.multiple_of(step * block, TILE), block)]
-    for i in range(parts):
-        total[:, i * width : (i + 1) * width] += dot32(here, mains[i][0])
-
-    @pl.when(step == pl.num_programs(0) - 1)
-    def _():
-        values = tokens_ref[...].astype(jnp.float32)
-        scale = lax.rsqrt(jnp.mean(values * values, 1, keepdims=True) + NORM_EPS)
-        back = total[...]
-        gain_back_ref[...] = jnp.sum(back * values * scale, 0, keepdims=True)
-        spread = back * gain_ref[...]
-        shift = jnp.mean(spread * values, 1, keepdims=True) * scale * scale * scale
-        tokens_back_ref[...] = middle_ref[...] + spread * scale - values * shift
-
-
-def project_back(gate, conv, tail_back, rim, main, tail, tokens, gain, middle_back):
-    parts, rows, width = main.shape
-    slots, model = tokens.shape
-    whole = lambda shape: pl.BlockSpec(shape, lambda j: (0,) * len(shape))
-    return pl.pallas_call(
-        project_back_kernel,
-        grid=(rows // PROJ_BLOCK,),
-        out_shape=(
-            jax.ShapeDtypeStruct((slots, model), jnp.float32),
-            jax.ShapeDtypeStruct((1, model), jnp.float32),
-            jax.ShapeDtypeStruct((slots, RS_SLOTS * RS_COLS), jnp.bfloat16),
-        ),
-        in_specs=[
-            whole(gate.shape),
-            whole(conv.shape),
-            whole(tail_back.shape),
-            whole(rim.shape),
-            *[pl.BlockSpec((1, PROJ_BLOCK, width), lambda j, i=i: (i, j, 0)) for i in range(parts)],
-            whole(tail.shape),
-            whole((slots, model)),
-            whole((1, model)),
-            whole((slots, model)),
-        ],
-        out_specs=(whole((slots, model)), whole((1, model)), whole((slots, RS_SLOTS * RS_COLS))),
-        scratch_shapes=[pltpu.VMEM((slots, model), jnp.float32)],
-        compiler_params=pltpu.CompilerParams(vmem_limit_bytes=56 * 2**20),
-        name="project_back",
-    )(gate, conv, tail_back, rim, *[main] * parts, tail, tokens, gain, middle_back)
-
-
-def from_behind(block, axis, distance):
-    devices = range(lax.axis_size(axis))
-    route = [(i - distance, i) for i in devices if i - distance in devices]
-    return lax.ppermute(block, axis, route)
 
 
 def local(
@@ -1620,42 +1947,24 @@
         ],
         0,
     )
-    full_in, full_out, full_shared_in, full_shared_out, tails = gather_weights(
-        [turned, w_out, shared_in, shared_out], [tail_shard], main_rows
+    full_in, first_norm, projected, tail_values, tails = project(
+        tokens, norm_gain[None], tail_shard, turned, main_rows
     )
     full_router = jnp.swapaxes(tails[:, head_count : head_count + expert_count], 0, 1)
     full_router = full_router.reshape(expert_count, model_width)
 
-    first_norm, projected, tail_values = project(tokens, norm_gain[None], full_in, tails)
-    halo = from_behind(projected[slot_count - 8 :, inner_width:], SEQ, 1)
     taps = jnp.concatenate([conv_weight, conv_bias[None], jnp.zeros((3, conv_width), jnp.float32)], 0)
     heads = jnp.pad(jnp.stack([a_log, dt_bias]), ((0, 6), (0, TILE - head_count)))
     wide = jnp.stack([jnp.repeat(skip_scale, inner_width // head_count), gated_gain])
-    square, pairs = (TILE, TILE), (head_count // 2, TILE, TILE)
-    mixed, leaving, totals, running, steps = tile_call(
-        mixer_in_kernel,
-        [((TILE, conv_width), jnp.float32), (pairs, low), ((8, TILE), jnp.float32), (square, jnp.float32), (square, jnp.float32)],
-        [(TILE + 8, TILE)],
-        "mixer_in",
-        projected, tail_values, halo, taps, heads,
+    square = (TILE, TILE)
+    mixed, totals, running, steps, halo, carried, normed_low, scanned, all_upstream, full_out, full_shared_in, full_shared_out = mixer(
+        projected, tail_values, taps, heads, wide, upstream_low, [w_out, shared_in, shared_out]
     )
-    carried, all_upstream = carried_states(leaving, totals, upstream_low)
-    normed_low, scanned = tile_call(
-        mixer_out_kernel,
-        [((TILE, inner_width), low), ((TILE, inner_width), jnp.float32)],
-        [(TILE, inner_width), (2, *square)],
-        "mixer_out",
-        projected, mixed, running, steps, carried, wide,
+    chosen = jnp.any(routes[:, :, None] == jnp.arange(expert_count)[None, None, :], 1)
+    middle, second_norm, base_out, shared_second, shared_hidden, shared_act_grad, all_rows, all_gates = middle_part(
+        normed_low, tokens, post_gain[None], full_router, chosen.T.astype(jnp.float32), upstream_low,
+        full_out, full_shared_in, full_shared_out,
     )
-    middle = residual + dot32(normed_low, full_out)
-    second_norm = scaled_rows(middle, post_gain).astype(low)
-    logits = dot_nt(second_norm, full_router)
-    chosen = jnp.any(routes[:, :, None] == jnp.arange(expert_count)[None, None, :], 1)
-    masked = jnp.where(chosen, logits, -jnp.inf)
-    powers = jnp.exp(masked - jnp.max(masked, -1, keepdims=True))
-    gate_dense = powers / jnp.sum(powers, -1, keepdims=True)
-
-    all_rows, all_gates = z_gather((second_norm, gate_dense.T), 5, "gather_rows")
     rows = all_rows.reshape(-1, model_width)
     back_rows = all_upstream.reshape(-1, model_width)
     owned = expert_in.shape[0]
@@ -1676,13 +1985,21 @@
     back = jnp.einsum("etf,edf->td", act_grad, expert_in, preferred_element_type=jnp.float32).astype(low)
     picks = jnp.swapaxes(picks.reshape(owned, 4, slot_count), 0, 1)
     picks = jnp.pad(picks, ((0, 0), (0, 8 - owned), (0, 0)))
-    expert_parts, back_sum, all_picks = expert_sum(
+    expert_parts, middle_back, mix_low, grad_post_gain, router_back, normed_back = expert_sum(
         rows,
         act_grad,
         hidden,
         out_grad,
         back.reshape(4, slot_count, model_width),
         picks,
+        middle,
+        shared_second,
+        upstream_low,
+        second_norm,
+        all_gates,
+        jnp.pad(full_router, ((0, TILE - expert_count), (0, 0))),
+        post_gain[None],
+        full_out,
     )
     act_width = act_grad.shape[2]
     grad_expert_in = expert_parts[:, :, :act_width]
@@ -1690,32 +2007,6 @@
     grad_expert_out = jnp.swapaxes(grad_expert_out, 1, 2).reshape(owned, -1, model_width)
 
     shared_width = full_shared_out.shape[0]
-    shared_acts = dot32(second_norm, full_shared_in)
-    shared_hidden = (
-        jax.nn.silu(shared_acts[:, :shared_width]) * shared_acts[:, shared_width:]
-    ).astype(low)
-    shared_sum = dot32(shared_hidden, full_shared_out)
-    shared_back = jnp.einsum("td,hd->th", upstream_low, full_shared_out, preferred_element_type=jnp.float32)
-    shared_act_grad = glu_back(shared_acts, shared_back)
-    second_back = jnp.einsum("tf,df->td", shared_act_grad, full_shared_in, preferred_element_type=jnp.float32)
-    gate_grads = all_picks[:, :owned].reshape(expert_count, slot_count).T
-    pick_grads = gate_dense * (gate_grads - jnp.sum(gate_dense * gate_grads, -1, keepdims=True))
-    logit_grads = pick_grads.astype(low)
-    second_back = second_back + back_sum + jnp.einsum(
-        "te,ed->td", logit_grads, full_router, preferred_element_type=jnp.float32
-    )
-    unused_second, second_pull = jax.vjp(scaled_rows, middle, post_gain)
-    middle_back, grad_post_gain = second_pull(second_back)
-    middle_back = middle_back + upstream
-    mix_low = middle_back.astype(low)
-    normed_back = jnp.einsum("td,kd->tk", mix_low, full_out, preferred_element_type=jnp.float32)
-    result_back, gate_back, gain_back, incoming_back = tile_call(
-        gate_back_kernel,
-        [((TILE, inner_width), jnp.float32), ((TILE, inner_width), low), ((8, inner_width), jnp.float32), (pairs, low)],
-        [(TILE, inner_width)],
-        "gate_back",
-        projected, mixed, scanned, normed_back, running, wide,
-    )
     early_lefts, late_lefts = tile_call(
         lefts_kernel,
         [((6, model_width, TILE), low), ((3, model_width, TILE), low)],
@@ -1723,35 +2014,49 @@
         "lefts",
         first_norm, second_norm, normed_low, shared_hidden,
     )
-    leaving_back, expert_total = carried_states(
-        incoming_back, totals, part.reshape(4, slot_count, model_width)
-    )
-    block_out = jnp.where(valid[:, None], middle + expert_total + shared_sum, 0.0).astype(low)
-    conv_part, rim_part, taps_back, steps_back, heads_back, shared_in_part, w_out_part, shared_out_part = tile_call(
+    large = [
+        early_lefts, shared_act_grad, mix_low, upstream_low, projected, scanned, normed_back, mixed,
+        part.reshape(4, slot_count, model_width), carried, base_out,
+    ]
+    (
+        rim_back, taps_back, steps_back, heads_back, shared_in_part, w_out_part, shared_out_part,
+        gate_back, gain_back, block_out, conv_part,
+    ) = tile_call(
         mixer_back_kernel,
         [
-            ((TILE, conv_width), jnp.float32), ((8, conv_width), jnp.float32), ((8, conv_width), jnp.float32),
+            ((8, conv_width), jnp.float32), ((8, conv_width), jnp.float32),
             (square, jnp.float32), ((8, TILE), jnp.float32), ((12, 2 * shared_width), jnp.float32),
             ((24, model_width), jnp.float32), ((8, model_width), jnp.float32),
+            ((TILE, inner_width), low), ((8, inner_width), jnp.float32), ((TILE, model_width), low),
+            ((TILE, conv_width), jnp.float32),
         ],
         [
+            pltpu.VMEM((TILE, inner_width), low), (TILE, model_width), pltpu.SemaphoreType.DMA((2,)),
+            (TILE, inner_width), (TILE, inner_width), (8, conv_width),
             (2, *square), (2, *square), (4, *square), square, (2, *square),
             (TILE, conv_width), (TILE + 8, TILE), (TILE + 16, TILE),
             pltpu.VMEM((TILE, RS_SLOTS * RS_COLS), low),
+            pltpu.VMEM((96, 32, TILE), low),
+            pltpu.VMEM((96, 32, TILE), low),
+            pltpu.VMEM((3, TILE, model_width), low),
+            pltpu.SemaphoreType.DMA((1,)),
+            pltpu.SemaphoreType.DMA((1,)),
+            pltpu.SemaphoreType.DMA((11,)),
+            (TILE, conv_width),
         ]
+        + [pltpu.VMEM(a.shape, a.dtype) for a in large]
+        + scan_scratch()
         + grad_sum_scratch(model_width),
         "mixer_back",
-        projected, tail_values, halo, taps, heads, mixed, running, steps, wide, carried, result_back, leaving_back,
-        early_lefts, shared_act_grad, mix_low, upstream_low,
+        tail_values, halo, taps, heads, running, steps, wide, totals,
+        valid[:, None].astype(jnp.float32), *large,
         collective=7,
+        away=len(large),
+        away_outs=(7, 10),
     )
-    rim_back = from_behind(rim_part.astype(low), SEQ, -1).astype(jnp.float32)
-    grad_tokens, grad_norm_gain, proj_back = project_back(
-        gate_back, conv_part, steps_back, rim_back, full_in, tails, tokens, norm_gain[None], middle_back
-    )
-    router_back = jnp.einsum("te,td->ed", logit_grads, second_norm, preferred_element_type=jnp.float32)
-    w_in_part, small = grad_sum(
-        late_lefts, proj_back, w_in.shape[1], taps_back, gain_back, grad_norm_gain, grad_post_gain[None], heads_back, router_back
+    w_in_part, small, grad_tokens = grad_sum(
+        late_lefts, gate_back, conv_part, steps_back, rim_back, tokens, norm_gain[None], middle_back, tails,
+        taps_back, gain_back, grad_post_gain, heads_back, router_back, full_in, w_in.shape[1]
     )
     owner = lax.axis_index(ALL)
 

time: 483 us -> 447 us (0.925)
  matrix products: 39 us -> 16.8 us
  Pallas kernels: 391 us -> 383 us
    pallas_call x7 -> x4, Pallas kernels: 235 us -> 202 us  [the longest x1 67.2 us: mixer(): pl.pallas_call(mixer_kernel, out_shape=tuple((jax.ShapeDtypeStruct(s, d)...]
    dot_general x9 -> x0, matrix products: 21.6 us -> none  [the longest x1 6.95 us: local(): jnp.einsum('td,kd->tk', mix_low, full_out, preferred_element_type=jnp.flo...]
    pallas_call x5 -> x2, Pallas kernels: 89.7 us -> 105 us  [tile_call(): pl.pallas_call(kernel, out_shape=tuple((jax.ShapeDtypeStruct(s, d) for s,...]
    pallas_call x1, Pallas kernels: 66 us -> 75.4 us  [grad_sum(): pl.pallas_call(grad_sum_kernel, out_shape=(jax.ShapeDtypeStruct((rows //...]
    unnamed x99 -> x57, local copies, waits for them, and re-layouts: 10.3 us -> 12.2 us
  transfers between devices with their start and end apart: 2 -> 0, of which waited for: 0 -> 0; matrix products, arithmetic and copies ran while one was open for 2% -> 0% of each run, Pallas kernels for 0% -> 0%
where the time goes in v4:
time: 447 us; the launch traced here: 443 us
  Pallas kernels  383 us (86%)
  local copies, waits for them, and re-layouts  31.1 us (7%)
  matrix products  16.8 us (4%)
  other arithmetic  10.4 us (2%)
    pallas_call x2, Pallas kernels, tile_call(): pl.pallas_call(kernel, out_shape=tuple((jax.ShapeDtypeStruct(s, d) for s,...  105 us
    pallas_call x1, Pallas kernels, grad_sum(): pl.pallas_call(grad_sum_kernel, out_shape=(jax.ShapeDtypeStruct((rows //...  75.4 us
    pallas_call x1, Pallas kernels, mixer(): pl.pallas_call(mixer_kernel, out_shape=tuple((jax.ShapeDtypeStruct(s, d)...  67.2 us
    pallas_call x1, Pallas kernels, project(): pl.pallas_call(project_kernel, out_shape=(jax.ShapeDtypeStruct((4, main_r...  61.3 us
    pallas_call x1, Pallas kernels, expert_sum(): pl.pallas_call(expert_sum_kernel, out_shape=tuple((jax.ShapeDtypeStruct(s...  51.9 us
    pallas_call x1, Pallas kernels, middle_part(): pl.pallas_call(middle_kernel, out_shape=tuple((jax.ShapeDtypeStruct(s, d)...  21.8 us
    unnamed x57, local copies, waits for them, and re-layouts  12.2 us

profile of v4, /device:TPU:0, one launch (start us, length us, event | category | flops | bytes accessed | tf_op | source)
XLA Modules:
  0.0 443.0 jit_solution(1577504115366184837)
XLA Ops:
  1.5 1.9 bitcast_select_fusion.rows_ref.up_ref.refs_6_.refs_3_
  4.4 1.4 maximum_maximum_fusion.1.tail_ref
  5.8 1.3 broadcast_in_dim.42.gain_ref
  7.1 61.3 %project.1 = (bf16[4,6400,384]{2,1,0:T(8,128)(2,1)}, bf16[128,1536]{1,0:T(8,128)(2,1)}, f32[128,6400]{1,0:T(8,128)}, f32[128,128]{1,0:T(8,128)}, bf16[4,128,384]{2,1,0:T(8,128)(2,1)}) custom-call(bf16[128,1536]{1,0:T(8,128)(2,1)} %bitcast.70, f32[1,1536]{1,0:T(1,128)} %broadcast_in_dim.42.gain_ref, bf16[128,384]{1,0:T(8,128)(2,1)} %maximum_maximum_fusion.1.tail_ref, ...), custom_call_target="tpu_custom_call" | custom-call | tf_op jit(solution)/shard_map/project/pallas_call | solution.py:1380
  70.7 67.2 %mixer.1 = (f32[128,3328]{1,0:T(8,128)}, f32[8,128]{1,0:T(8,128)}, f32[128,128]{1,0:T(8,128)}, f32[128,128]{1,0:T(8,128)}, f32[8,3328]{1,0:T(8,128)}, /*index=5*...) custom-call(f32[128,128]{1,0:T(8,128)} %get-tuple-element.64.tail_re, ...), custom_call_target="tpu_custom_call" | custom-call | tf_op jit(solution)/shard_map/mixer/pallas_call | solution.py:1618
  137.9 1.3 slice.48
  140.5 21.8 %middle.1 = (f32[128,1536]{1,0:T(8,128)}, bf16[128,1536]{1,0:T(8,128)(2,1)}, f32[128,1536]{1,0:T(8,128)}, f32[128,1536]{1,0:T(8,128)}, bf16[128,1024]{1,0:T(8,12...) custom-call(bf16[128,3072]{1,0:T(8,128)(2,1)} %get-tuple-element.71.normed_ref.gated_ref, ...), custom_call_target="tpu_custom_call" | custom-call | tf_op jit(solution)/shard_map/middle/pallas_call | solution.py:779
  163.0 1.8 convert.10
  165.2 1.1 copy-done.8
  166.3 6.2 %convolution_bitcast_fusion.1 = f32[2,512,1024]{2,1,0:T(8,128)S(1)} fusion(bf16[512,1536,1]{1,0,2:T(8,128)(2,1)S(1)} %bitcast.75, bf16[2,1536,1024]{2,1,0:T(8,128)(2,1)} %param.36), kind=kOutput, calls=%fused_computation.8 | convolution fusion | flops 3221225472 | bytes 12058624 | tf_op jit(solution)/shard_map/td,edf->etf/dot_general | solution.py:1975
  172.5 2.6 multiply_convert_fusion.2
  175.2 1.7 pad_maximum_fusion.refs_1_
  176.8 4.7 %fusion.2 = bf16[512,1536]{1,0:T(8,128)(2,1)} fusion(bf16[2,1536,1024]{2,1,0:T(8,128)(2,1)S(1)} %bitcast.91, bf16[2,512,512]{2,1,0:T(8,128)(2,1)S(1)} %get-tuple-element.114, bf16[2,512,512]{2,1,0:T(8,128)(2,1)S(1)} %get-tuple-element.113), kind=kOutput, calls=%fused_computation.7 | convolution fusion | flops 3226206208 | bytes 9961472 | tf_op jit(solution)/shard_map/etf,edf->td/dot_general | solution.py:1985
  181.5 3.3 fusion.1
  186.3 51.9 %expert_sum.1 = (f32[2,48,1536]{2,1,0:T(8,128)}, f32[128,1536]{1,0:T(8,128)}, bf16[128,1536]{1,0:T(8,128)(2,1)}, f32[1,1536]{1,0:T(1,128)}, f32[8,1536]{1,0:T(8,128)}, /*index=5*/f32[128,3072]{1,0:T(8,128)}) custom-call(f32[4,8,128]{2,1,0:T(8,128)} %pad.13.picks_ref, f32[4,8,128]{2,1,0:T(8,128)} %get-tuple-element.82.gates_ref, ...), custom_call_target="tpu_custom_call" | custom-call | tf_op jit(solution)/shard_map/expert_sum/pallas_call | solution.py:1076
  238.2 1.1 copy-done.1
  240.2 1.4 lefts.1
  241.6 1.4 copy-done.2
  244.7 103.6 %mixer_back.1 = (f32[8,3328]{1,0:T(8,128)}, f32[8,3328]{1,0:T(8,128)}, f32[128,128]{1,0:T(8,128)}, f32[8,128]{1,0:T(8,128)}, f32[12,2048]{1,0:T(8,128)}, /*index...) custom-call(f32[128,128]{1,0:T(8,128)} %get-tuple-element.64.tail_re, ...), custom_call_target="tpu_custom_call" | custom-call | tf_op jit(solution)/shard_map/mixer_back/pallas_call | solution.py:1892
  348.3 75.4 %grad_sum.1 = (f32[12,6448]{1,0:T(8,128)}, f32[8,4864]{1,0:T(8,128)}, f32[128,1536]{1,0:T(8,128)}) custom-call(f32[128,128]{1,0:T(8,128)} %get-tuple-element.92.tail_back_ref, f32[8,3328]{1,0:T(8,128)} %get-tuple-element.93.rim_ref, f32[1,1536]{1,0:T(1,128)} %broadcast_in_dim.42.gain_ref, bf16[4,128,384]{2,1,0:T(8,128)(2,1)} %get-tuple-element.72.tail_ref, ...), custom_call_target="tpu_custom_call" | custom-call | tf_op jit(solution)/shard_map/grad_sum/pallas_call | solution.py:436
  431.2 1.2 slice_bitcast_fusion
  434.4 1.8 slice.60
  436.2 1.8 copy.64
  437.9 2.1 copy.65
  (86 shorter events, 21.7 us)
Async XLA Ops:
  0.7 171.9 %copy-start = (bf16[2,512,1536]{2,1,0:T(8,128)(2,1)S(1)}, bf16[2,512,1536]{2,1,0:T(8,128)(2,1)}, u32[]{:S(2)}) copy-start(bf16[2,512,1536]{2,1,0:T(8,128)(2,1)} %param.37) | copy-start | bytes 9437188
  1.5 66.9 %copy-start.16 = (f32[3328]{0:T(1024)S(1)}, f32[3328]{0:T(1024)}, u32[]{:S(2)}) copy-start(f32[3328]{0:T(1024)} %param.26) | copy-start | bytes 39940
  1.5 67.0 %copy-start.14 = (f32[4,3328]{1,0:T(4,128)S(1)}, f32[4,3328]{1,0:T(4,128)}, u32[]{:S(2)}) copy-start(f32[4,3328]{1,0:T(4,128)} %param.25) | copy-start | bytes 159748
  3.5 65.8 %copy-start.20 = (f32[48]{0:T(128)S(1)}, f32[48]{0:T(128)}, u32[]{:S(2)}) copy-start(f32[48]{0:T(128)} %param.29) | copy-start | bytes 580
  3.5 66.0 %copy-start.17 = (f32[3072]{0:T(1024)S(1)}, f32[3072]{0:T(1024)}, u32[]{:S(2)}) copy-start(f32[3072]{0:T(1024)} %param.30) | copy-start | bytes 36868
  3.5 66.6 %copy-start.21 = (f32[48]{0:T(128)S(1)}, f32[48]{0:T(128)}, u32[]{:S(2)}) copy-start(f32[48]{0:T(128)} %param.28) | copy-start | bytes 580
  3.5 66.6 %copy-start.22 = (f32[48]{0:T(128)S(1)}, f32[48]{0:T(128)}, u32[]{:S(2)}) copy-start(f32[48]{0:T(128)} %param.27) | copy-start | bytes 580
  70.7 68.6 %copy-start.18 = (f32[1536]{0:T(1024)S(1)}, f32[1536]{0:T(1024)}, u32[]{:S(2)}) copy-start(f32[1536]{0:T(1024)} %param.32) | copy-start | bytes 18436
  70.7 69.2 %copy-start.19 = (s32[1,128,6]{1,0,2:T(1,128)S(1)}, s32[1,128,6]{1,0,2:T(1,128)}, u32[]{:S(2)}) copy-start(s32[1,128,6]{1,0,2:T(1,128)} %param.22) | copy-start | bytes 9220
  164.8 1.5 copy-start.8
  165.2 7.3 %copy-start.7 = (bf16[2,512,1536]{2,1,0:T(8,128)(2,1)}, bf16[2,512,1536]{2,1,0:T(8,128)(2,1)S(1)}, u32[]{:S(2)}) copy-start(bf16[2,512,1536]{2,1,0:T(8,128)(2,1)S(1)} %multiply_convert_fusion.refs_3_) | copy-start | bytes 9437188
  166.3 10.5 %slice-start = ((s8[6291456]{0:T(1024)(128)(4,1)}), s8[4194304]{0:T(1024)(128)(4,1)S(1)}, s32[]{:S(2)}) async-start(s8[6291456]{0:T(1024)(128)(4,1)} %bitcast.90), calls=%async_computation | async-start | bytes 8388608
  172.5 4.3 slice-start.1
  175.1 6.4 %copy-start.9 = (bf16[2,512,512]{2,1,0:T(8,128)(2,1)}, bf16[2,512,512]{2,1,0:T(8,128)(2,1)S(1)}, u32[]{:S(2)}) copy-start(bf16[2,512,512]{2,1,0:T(8,128)(2,1)S(1)} %get-tuple-element.115.refs_2_) | copy-start | bytes 3145732
  181.5 3.9 copy-start.11
  186.3 51.9 %copy-start.3 = (bf16[128,1536]{1,0:T(8,128)(2,1)S(1)}, bf16[128,1536]{1,0:T(8,128)(2,1)}, u32[]{:S(2)}) copy-start(bf16[128,1536]{1,0:T(8,128)(2,1)} %get-tuple-element.76.second_ref.refs_7_) | copy-start | bytes 1179652
  186.3 51.9 %copy-start.5 = (bf16[128,1536]{1,0:T(8,128)(2,1)S(1)}, bf16[128,1536]{1,0:T(8,128)(2,1)}, u32[]{:S(2)}) copy-start(bf16[128,1536]{1,0:T(8,128)(2,1)} %get-tuple-element.70.first_ref) | copy-start | bytes 1179652
  238.2 1.1 copy-start.1
  241.6 1.4 copy-start.2
  243.0 1.1 copy-start.4
  423.7 17.1 %copy-start.12 = (f32[24,1536]{1,0:T(8,128)S(1)}, f32[24,1536]{1,0:T(8,128)}, u32[]{:S(2)}) copy-start(f32[24,1536]{1,0:T(8,128)} %get-tuple-element.150) | copy-start | bytes 442372
  434.4 5.7 %copy-start.10 = (f32[12,6448]{1,0:T(8,128)S(1)}, f32[12,6448]{1,0:T(8,128)}, u32[]{:S(2)}) copy-start(f32[12,6448]{1,0:T(8,128)} %get-tuple-element.143) | copy-start | bytes 928516
  434.4 7.1 %copy-start.13 = (f32[12,2048]{1,0:T(8,128)S(1)}, f32[12,2048]{1,0:T(8,128)}, u32[]{:S(2)}) copy-start(f32[12,2048]{1,0:T(8,128)} %get-tuple-element.153) | copy-start | bytes 294916
  434.4 7.7 %copy-start.15 = (f32[8,1536]{1,0:T(8,128)S(1)}, f32[8,1536]{1,0:T(8,128)}, u32[]{:S(2)}) copy-start(f32[8,1536]{1,0:T(8,128)} %get-tuple-element.154) | copy-start | bytes 147460
  (1 other events, 0.9 us)

commit v5 on v4

--- a/solution.py
+++ b/solution.py
@@ -36,8 +36,8 @@
 RS_FIRST = (0, 9, 18)
 RS_SLOTS = 26
 RS_COLS = 256
-RS_LAGS = 6
-RS_TIMES = max(RS_COUNTS) + RS_LAGS - 1
+RS_LAGS = (0, 2, 4, 6, 8)
+RS_TIMES = max(RS_COUNTS) + RS_LAGS[-1]
 NEIGHBOURS = [("c", 1)] + [(axis, o) for axis in ("x", "y", "z") for o in (1, 2, 3)]
 
 
@@ -76,7 +76,6 @@
     half, block, low = rows // 2, rows // 8, jnp.bfloat16
     sems = lambda *shape: [pltpu.SemaphoreType.DMA(shape)] * 2
     return [
-        pltpu.VMEM((2, 3, half, RS_COLS), low),
         pltpu.VMEM((RS_SLOTS, half, RS_COLS), low),
         pltpu.VMEM((RS_SLOTS, 4, block // 2, RS_COLS), low),
         pltpu.VMEM((RS_SLOTS, 2, block // 2, RS_COLS), low),
@@ -84,29 +83,51 @@
         pltpu.VMEM((RS_SLOTS, 4, 16, RS_COLS), low),
         pltpu.VMEM((RS_SLOTS, 3, 16, RS_COLS), low),
         pltpu.VMEM((3, block // 4 + 8, RS_COLS), jnp.float32),
-        *sems(RS_SLOTS), *sems(RS_SLOTS, 4), *sems(RS_SLOTS, 2), *sems(RS_SLOTS, 3), *sems(RS_SLOTS, 3),
+        *sems(RS_SLOTS, 4), *sems(RS_SLOTS, 2), *sems(RS_SLOTS, 3), *sems(RS_SLOTS, 3),
     ]
 
 
-def grad_sum_steps(scratch, left_of, right_of, store):
-    core_out, core_in, near, far, second_in, third_out, third_in, lines = scratch[:8]
-    core_ss, core_rs, near_ss, near_rs, far_ss, far_rs, second_ss, second_rs, third_ss, third_rs = scratch[8:]
-    me_core = lax.axis_index("c")
-    other = 1 - me_core
-    half = core_out.shape[2]
+def share_factors(lefts_ref, left_in, left_both, rights, sems):
+    me, half = lax.axis_index("c"), left_in.shape[1]
+    copies = [
+        remote(
+            lefts_ref.at[:, pl.ds(pl.multiple_of((1 - me) * half, half), half)], left_in, sems[0].at[0], sems[1].at[0], {"c": 1 - me}
+        ),
+        remote(rights.at[:TILE], rights.at[TILE:], sems[0].at[1], sems[1].at[1], {"c": 1 - me}),
+    ]
+    for copy in copies:
+        copy.start()
+
+    def receive():
+        left_both[:, :, :TILE] = lefts_ref[:, pl.ds(pl.multiple_of(me * half, half), half), :]
+        for copy in copies:
+            copy.wait()
+        left_both[:, :, TILE:] = left_in[...]
+
+    return receive
+
+
+def share_scratch(lefts):
+    count, rows, depth = lefts.shape
+    return [
+        pltpu.VMEM((count, rows // 2, depth), lefts.dtype),
+        pltpu.VMEM((count, rows // 2, 2 * depth), lefts.dtype),
+        pltpu.VMEM((2 * depth, RS_SLOTS * RS_COLS), lefts.dtype),
+        pltpu.SemaphoreType.DMA((2,)),
+        pltpu.SemaphoreType.DMA((2,)),
+    ]
+
+
+def grad_sum_steps(scratch, product, store):
+    core_in, near, far, second_in, third_out, third_in, lines = scratch[:7]
+    near_ss, near_rs, far_ss, far_rs, second_ss, second_rs, third_ss, third_rs = scratch[7:]
+    half = core_in.shape[1]
     block = half // 4
     edge = block // 2
     small = block // 4
     unit = third_out.shape[2]
     kept = small // 4
     lines[...] = jnp.zeros_like(lines)
-
-    def core_copy(part, k):
-        slot = RS_FIRST[part] + k
-        return remote(
-            core_out.at[lax.rem(k, 2), part], core_in.at[slot],
-            core_ss.at[slot], core_rs.at[slot], {"c": other},
-        )
 
     def near_copies(part, k):
         slot = RS_FIRST[part] + k
@@ -158,24 +179,8 @@
             for o in (1, 2, 3)
         ]
 
-    def stage_product(part, k):
-        @pl.when(k >= 2)
-        def _():
-            core_copy(part, k - 2).wait_send()
-
-        left = left_of(part, k, other)
-        for col in range(0, RS_COLS, 256):
-            core_out[lax.rem(k, 2), part, :, col : col + 256] = dot32(left, right_of(part, k, col)).astype(jnp.bfloat16)
-        core_copy(part, k).start()
-
     def stage_near(part, k):
-        slot = RS_FIRST[part] + k
-        core_copy(part, k).wait_recv()
-        left = left_of(part, k, me_core)
-        for col in range(0, RS_COLS, 256):
-            mine = dot32(left, right_of(part, k, col))
-            theirs = core_in[slot, :, col : col + 256].astype(jnp.float32)
-            core_in[slot, :, col : col + 256] = (mine + theirs).astype(jnp.bfloat16)
+        core_in[RS_FIRST[part] + k] = product(part, k).astype(jnp.bfloat16)
         for copy in near_copies(part, k):
             copy.start()
 
@@ -231,10 +236,10 @@
         )
         store(part, k, total)
 
-    stages = (stage_product, stage_near, stage_far, stage_second, stage_third, stage_last)
+    stages = (stage_near, stage_far, stage_second, stage_third, stage_last)
 
     def step(t):
-        for lag, stage in enumerate(stages):
+        for lag, stage in zip(RS_LAGS, stages):
             k = t - lag
             for count in sorted(set(RS_COUNTS)):
                 @pl.when((k >= 0) & (k < count))
@@ -246,10 +251,6 @@
     def finish():
         for part in range(3):
             def wait_sent(k, carry, part=part):
-                @pl.when(k >= RS_COUNTS[part] - 2)
-                def _():
-                    core_copy(part, k).wait_send()
-
                 for copies in (near_copies, far_copies, second_copies, third_copies):
                     for copy in copies(part, k):
                         copy.wait_send()
@@ -275,10 +276,9 @@
     ]
     for copy in loads:
         copy.start()
-    *sum_scratch, back_ref, total, weights, weight_sem, pack, pack_in, pack_work, pack_others, pack_ss, pack_rs = scratch
+    *sum_scratch, left_in, left_both, back_ref, share_ss, share_rs, total, weights, weight_sem, pack, pack_in, pack_work, pack_others, pack_ss, pack_rs = scratch
     me_core = lax.axis_index("c")
     other = 1 - me_core
-    half = lefts_ref.shape[1] // 2
     blocks = main_ref.shape[1] // weights.shape[2]
 
     def fetch(j):
@@ -298,20 +298,21 @@
     inner, conv = gate_ref.shape[1], conv_ref.shape[1]
     for copy in loads[:3]:
         copy.wait()
-    back_ref[:, :inner] = gate_ref[...]
-    back_ref[:, inner : inner + conv] = short(conv_ref[...])
+    back_ref[:TILE, :inner] = gate_ref[...]
+    back_ref[:TILE, inner : inner + conv] = short(conv_ref[...])
     rim = jnp.concatenate([jnp.zeros((8, conv), jnp.float32), rim_ref[...]], 0)
-    back_ref[TILE - 16 :, inner : inner + conv] = short(conv_ref[TILE - 16 :] + rim)
-    back_ref[:, inner + conv : inner + conv + TILE] = short(tail_back_ref[...])
+    back_ref[TILE - 16 : TILE, inner : inner + conv] = short(conv_ref[TILE - 16 :] + rim)
+    back_ref[:TILE, inner + conv : inner + conv + TILE] = short(tail_back_ref[...])
     rest = back_ref.shape[1] - inner - conv - TILE
-    back_ref[:, inner + conv + TILE :] = jnp.zeros((TILE, rest), jnp.bfloat16)
+    back_ref[:TILE, inner + conv + TILE :] = jnp.zeros((TILE, rest), jnp.bfloat16)
+    receive = share_factors(lefts_ref, left_in, left_both, back_ref, (share_ss, share_rs))
     taps_width, wide = taps_ref.shape[1], pack.shape[1] // 2
 
     def project_step(j):
         for copy in fetch(j):
             copy.wait()
         rows, width = weights.shape[2:]
-        here = back_ref[:, pl.ds(pl.multiple_of(j * rows, TILE), rows)]
+        here = back_ref[:TILE, pl.ds(pl.multiple_of(j * rows, TILE), rows)]
         for i in range(4):
             total[:, i * width : (i + 1) * width] += dot32(here, weights[lax.rem(j, 2), i])
 
@@ -385,11 +386,9 @@
                 for copy in pack_copies(n):
                     copy.wait_send()
 
-    def left_of(part, k, which):
-        return lefts_ref[part, pl.ds(pl.multiple_of(which * half, half), half), :]
-
-    def right_of(part, k, col):
-        return back_ref[:, pl.ds(pl.multiple_of((RS_FIRST[part] + k) * RS_COLS + col, 256), 256)]
+    def product(part, k):
+        chunk = pl.ds(pl.multiple_of((RS_FIRST[part] + k) * RS_COLS, RS_COLS), RS_COLS)
+        return dot32(left_both[part], back_ref[:, chunk])
 
     whole = out_ref.shape[1] // RS_COLS
     rows = out_ref.shape[0]
@@ -406,7 +405,8 @@
             def _():
                 out_ref[:, whole * RS_COLS :] = total[:rows, : out_ref.shape[1] - whole * RS_COLS]
 
-    step, finish = grad_sum_steps(sum_scratch, left_of, right_of, store)
+    step, finish = grad_sum_steps(sum_scratch, product, store)
+    receive()
 
     def run(t, carry):
         step(t)
@@ -446,7 +446,7 @@
         + [pltpu.SemaphoreType.DMA((5,)), pltpu.VMEM((slots, model), jnp.float32), pltpu.SemaphoreType.DMA((1,))]
         + grad_sum_scratch(rows)
         + [
-            pltpu.VMEM((slots, RS_SLOTS * RS_COLS), jnp.bfloat16),
+            *share_scratch(lefts),
             pltpu.VMEM((slots, model), jnp.float32),
             pltpu.VMEM((2, 4, block, main.shape[2]), jnp.bfloat16),
             pltpu.SemaphoreType.DMA((2, 4)),
@@ -1330,10 +1330,10 @@
 
         lax.fori_loop(0, rows // block, rows_at, 0)
 
+    steps["second"]()
     load.wait()
     add(z, True)
     save(z).start()
-    steps["second"]()
     steps["deep"]()
     for copy in tails:
         copy.wait()
@@ -1460,7 +1460,7 @@
     ext[8 : 8 + TILE] = proj_ref[:, pl.ds(pl.multiple_of(INNER + j * TILE, TILE), TILE)]
 
 
-def mixer_in_part(tick, halo_copy, proj_ref, tail_ref, halo_ref, cw_ref, heads_ref, mixed_ref, state_ref, totals_ref, run_ref, step_ref, ext):
+def mixer_in_part(ticks, halo_copy, proj_ref, tail_ref, halo_ref, cw_ref, heads_ref, mixed_ref, state_ref, totals_ref, run_ref, step_ref, ext):
     unused_raw, step, log_decay = head_steps(tail_ref, heads_ref)
     lower = (row_ids() >= lane_ids()).astype(jnp.float32)
     run = jnp.dot(lower, log_decay, precision=HIGH, preferred_element_type=jnp.float32)
@@ -1471,6 +1471,7 @@
     weight = jnp.exp(last - run) * step
 
     halo_copy.wait()
+    ticks[0]()
     spot = lax.axis_index("x") * 8 + lax.axis_index("y") * 2 + lax.axis_index("c")
 
     @pl.when(spot == 0)
@@ -1484,7 +1485,7 @@
         return carry
 
     lax.fori_loop(0, CONV // TILE, conv, 0)
-    tick()
+    ticks[1]()
     in_map = short(mixed_ref[:, INNER : INNER + TILE])
 
     def state(p, carry):
@@ -1565,10 +1566,9 @@
     halo_copy.start()
     steps = gather_steps(shards, fulls, (0,), False, sems)
     steps["begin"]()
-    mixer_in_part(steps["first"], halo_copy, proj_ref, tail_ref, halo_ref, cw_ref, heads_ref, mixed_ref, state_ref, totals_ref, run_ref, step_ref, ext)
+    mixer_in_part((steps["first"], steps["second"]), halo_copy, proj_ref, tail_ref, halo_ref, cw_ref, heads_ref, mixed_ref, state_ref, totals_ref, run_ref, step_ref, ext)
     save_mixed = pltpu.make_async_copy(mixed_ref, mixed_far, out_sem.at[0])
     save_mixed.start()
-    steps["second"]()
     saves = []
     for n in range(3):
         loads[n].wait()
@@ -1685,8 +1685,8 @@
     away, refs = refs[:11], refs[11:]
     (rim_in_ref, taps_ref, step_back_ref, heads_back_ref, shared_in_ref, out_ref, shared_out_ref,
     gate_far, gain_ref, block_ref, conv_far,
-    gate_ref, parts_sum, save_sem, result_ref, gated, rim_ref, rows, column_sums, row_sums, kernel_back, maps_back, mixed_back, ext, padded, rights,
-    state_ref, leaving_ref, parts_in, rim_ss, rim_rs, load_sem, conv_ref), refs = refs[:33], refs[33:]
+    gate_ref, parts_sum, save_sem, result_ref, gated, rim_ref, rows, column_sums, row_sums, kernel_back, maps_back, mixed_back, ext, padded, left_in, left_both, rights, share_ss, share_rs,
+    state_ref, leaving_ref, parts_in, rim_ss, rim_rs, load_sem, conv_ref), refs = refs[:37], refs[37:]
     here, refs = refs[:11], refs[11:]
     scan_refs, sum_scratch = refs[: len(scan_scratch())], refs[len(scan_scratch()) :]
     loads = [pltpu.make_async_copy(far, near, load_sem.at[i]) for i, (far, near) in enumerate(zip(away, here))]
@@ -1701,17 +1701,14 @@
     up_at = [0, RS_COUNTS[0] - plain[0], RS_COUNTS[0] + RS_COUNTS[1] - plain[0] - plain[1]]
     for part, ref in enumerate((acts_ref, mix_ref, mix_ref)):
         at, end = RS_FIRST[part] * RS_COLS, (RS_FIRST[part] + RS_COUNTS[part]) * RS_COLS
-        rights[:, at : at + ref.shape[1]] = ref[...]
+        rights[:TILE, at : at + ref.shape[1]] = ref[...]
         at = at + ref.shape[1]
-        rights[:, at:end] = up_ref[:, up_at[part] * RS_COLS : up_at[part] * RS_COLS + end - at]
-    share = lefts_ref.shape[1] // 2
-
-    def left_of(part, k, which):
-        n = 2 * part + k // plain[part]
-        return lefts_ref[n, pl.ds(pl.multiple_of(which * share, share), share), :]
-
-    def right_of(part, k, col):
-        return rights[:, pl.ds(pl.multiple_of((RS_FIRST[part] + k) * RS_COLS + col, 256), 256)]
+        rights[:TILE, at:end] = up_ref[:, up_at[part] * RS_COLS : up_at[part] * RS_COLS + end - at]
+    receive = share_factors(lefts_ref, left_in, left_both, rights, (share_ss, share_rs))
+
+    def product(part, k):
+        chunk = pl.ds(pl.multiple_of((RS_FIRST[part] + k) * RS_COLS, RS_COLS), RS_COLS)
+        return dot32(left_both[2 * part + k // plain[part]], rights[:, chunk])
 
     def store(part, k, total):
         @pl.when(k < plain[part])
@@ -1727,11 +1724,12 @@
             lanes = pl.ds(pl.multiple_of((k - plain[part] + up_at[part]) * RS_COLS, RS_COLS), RS_COLS)
             shared_out_ref[:, lanes] = total[:8]
 
-    sum_step, sum_finish = grad_sum_steps(sum_scratch, left_of, right_of, store)
-
-    sum_step(0)
+    sum_step, sum_finish = grad_sum_steps(sum_scratch, product, store)
+
     for copy in loads[4:8]:
         copy.wait()
+    receive()
+    sum_step(0)
     gate_back_part(
         lambda: sum_step(1), proj_ref, mixed_ref, scanned_ref, back_ref, run_ref, wide_ref, result_ref, gate_ref, gain_ref,
         state_ref, gated,
@@ -1740,8 +1738,11 @@
     save_gate.start()
     sum_step(2)
     loads[8].wait()
+    def tick_scan(n):
+        sum_step(3 + n)
+
     state_exchange(
-        True, state_ref, totals_ref, parts_ref, leaving_ref, parts_in, parts_sum, lambda n: sum_step(3 + n), *scan_refs
+        True, state_ref, totals_ref, parts_ref, leaving_ref, parts_in, parts_sum, tick_scan, *scan_refs
     )
     run, step = run_ref[...], step_ref[...]
     rows[0] = run.T
@@ -1767,9 +1768,9 @@
     block_ref[...] = short(jnp.where(valid_ref[...] > 0.0, base_ref[...] + parts_sum[...], 0.0))
 
     def pair(p, carry):
-        @pl.when(lax.rem(p, 4) == 0)
+        @pl.when((lax.rem(p, 2) == 0) & (p < 20))
         def _():
-            sum_step(7 + p // 4)
+            sum_step(7 + p // 2)
 
         lanes = tile_at(p)
         values, back = mixed_ref[:, lanes], result_ref[:, lanes]
@@ -1845,7 +1846,6 @@
     mixed_back[:, INNER : INNER + TILE] = maps_back[0] + dot32(short(both.T), out_low)
     mixed_back[:, INNER + TILE : INNER + 2 * TILE] = maps_back[1] + dot32(short(both), in_low)
     padded[0:8] = jnp.zeros((8, TILE), jnp.float32)
-    sum_step(13)
     padded[8 + TILE : 16 + TILE] = jnp.zeros((8, TILE), jnp.float32)
 
     def conv(j, carry):
@@ -2035,7 +2035,7 @@
             (TILE, inner_width), (TILE, inner_width), (8, conv_width),
             (2, *square), (2, *square), (4, *square), square, (2, *square),
             (TILE, conv_width), (TILE + 8, TILE), (TILE + 16, TILE),
-            pltpu.VMEM((TILE, RS_SLOTS * RS_COLS), low),
+            *share_scratch(early_lefts),
             pltpu.VMEM((96, 32, TILE), low),
             pltpu.VMEM((96, 32, TILE), low),
             pltpu.VMEM((3, TILE, model_width), low),
@@ -2060,24 +2060,24 @@
     )
     owner = lax.axis_index(ALL)
 
-    def owned_part(values):
-        size = values.shape[-1] // 128
-        return lax.dynamic_slice_in_dim(values, owner * size, size, values.ndim - 1)
+    def owned_part(row, rows, start, width):
+        size = width // 128
+        return lax.dynamic_slice(small, (row, start + owner * size), (rows, size))
 
     return (
         block_out[None],
         grad_tokens[None],
-        owned_part(small[6, :model_width]),
+        owned_part(6, 1, 0, model_width)[0],
         w_in_part,
-        owned_part(small[:4, :conv_width]),
-        owned_part(small[4, :conv_width]),
+        owned_part(0, 4, 0, conv_width),
+        owned_part(4, 1, 0, conv_width)[0],
         small[7, :head_count],
         small[7, TILE : TILE + head_count],
         small[7, 2 * TILE : 2 * TILE + head_count],
-        owned_part(small[5, :inner_width]),
+        owned_part(5, 1, 0, inner_width)[0],
         w_out_part,
-        owned_part(small[6, model_width : 2 * model_width]),
-        owned_part(small[:, conv_width:]).T,
+        owned_part(6, 1, model_width, model_width)[0],
+        owned_part(0, 8, conv_width, model_width).T,
         shared_in_part,
         shared_out_part,
         grad_expert_in,

time: 447 us -> 437 us (0.978)
  Pallas kernels: 383 us -> 373 us
    pallas_call x2, Pallas kernels: 105 us -> 94.1 us  [tile_call(): pl.pallas_call(kernel, out_shape=tuple((jax.ShapeDtypeStruct(s, d) for s,...]
where the time goes in v5:
time: 437 us; the launch traced here: 432 us
  Pallas kernels  373 us (85%)
  local copies, waits for them, and re-layouts  30.3 us (7%)
  matrix products  16.5 us (4%)
  other arithmetic  10.4 us (2%)
    pallas_call x2, Pallas kernels, tile_call(): pl.pallas_call(kernel, out_shape=tuple((jax.ShapeDtypeStruct(s, d) for s,...  94.1 us
    pallas_call x1, Pallas kernels, grad_sum(): pl.pallas_call(grad_sum_kernel, out_shape=(jax.ShapeDtypeStruct((rows //...  73.6 us
    pallas_call x1, Pallas kernels, mixer(): pl.pallas_call(mixer_kernel, out_shape=tuple((jax.ShapeDtypeStruct(s, d)...  69.1 us
    pallas_call x1, Pallas kernels, project(): pl.pallas_call(project_kernel, out_shape=(jax.ShapeDtypeStruct((4, main_r...  61.4 us
    pallas_call x1, Pallas kernels, expert_sum(): pl.pallas_call(expert_sum_kernel, out_shape=tuple((jax.ShapeDtypeStruct(s...  51 us
    pallas_call x1, Pallas kernels, middle_part(): pl.pallas_call(middle_kernel, out_shape=tuple((jax.ShapeDtypeStruct(s, d)...  23.8 us
    unnamed x57, local copies, waits for them, and re-layouts  12.3 us

profile of v5, /device:TPU:0, one launch (start us, length us, event | category | flops | bytes accessed | tf_op | source)
XLA Modules:
  0.0 432.0 jit_solution(13256919514459440944)
XLA Ops:
  1.5 1.9 bitcast_select_fusion.rows_ref.up_ref.refs_6_.refs_3_
  4.4 1.4 maximum_maximum_fusion.1.tail_ref
  5.8 1.3 broadcast_in_dim.42.gain_ref
  7.1 61.4 %project.1 = (bf16[4,6400,384]{2,1,0:T(8,128)(2,1)}, bf16[128,1536]{1,0:T(8,128)(2,1)}, f32[128,6400]{1,0:T(8,128)}, f32[128,128]{1,0:T(8,128)}, bf16[4,128,384]{2,1,0:T(8,128)(2,1)}) custom-call(bf16[128,1536]{1,0:T(8,128)(2,1)} %bitcast.70, f32[1,1536]{1,0:T(1,128)} %broadcast_in_dim.42.gain_ref, bf16[128,384]{1,0:T(8,128)(2,1)} %maximum_maximum_fusion.1.tail_ref, ...), custom_call_target="tpu_custom_call" | custom-call | tf_op jit(solution)/shard_map/project/pallas_call | solution.py:1380
  70.7 69.1 %mixer.1 = (f32[128,3328]{1,0:T(8,128)}, f32[8,128]{1,0:T(8,128)}, f32[128,128]{1,0:T(8,128)}, f32[128,128]{1,0:T(8,128)}, f32[8,3328]{1,0:T(8,128)}, /*index=5*...) custom-call(f32[128,128]{1,0:T(8,128)} %get-tuple-element.64.tail_re, ...), custom_call_target="tpu_custom_call" | custom-call | tf_op jit(solution)/shard_map/mixer/pallas_call | solution.py:1618
  139.8 1.3 slice.30
  142.3 23.8 %middle.1 = (f32[128,1536]{1,0:T(8,128)}, bf16[128,1536]{1,0:T(8,128)(2,1)}, f32[128,1536]{1,0:T(8,128)}, f32[128,1536]{1,0:T(8,128)}, bf16[128,1024]{1,0:T(8,12...) custom-call(bf16[128,3072]{1,0:T(8,128)(2,1)} %get-tuple-element.71.normed_ref.gated_ref, ...), custom_call_target="tpu_custom_call" | custom-call | tf_op jit(solution)/shard_map/middle/pallas_call | solution.py:779
  166.8 1.8 convert.10
  170.2 5.9 %convolution_bitcast_fusion.1 = f32[2,512,1024]{2,1,0:T(8,128)S(1)} fusion(bf16[512,1536,1]{1,0,2:T(8,128)(2,1)S(1)} %bitcast.75, bf16[2,1536,1024]{2,1,0:T(8,128)(2,1)} %param.36), kind=kOutput, calls=%fused_computation.8 | convolution fusion | flops 3221225472 | bytes 12058624 | tf_op jit(solution)/shard_map/td,edf->etf/dot_general | solution.py:1975
  176.1 2.6 multiply_convert_fusion.2
  178.7 1.6 pad_maximum_fusion.refs_1_
  180.4 4.7 %fusion.2 = bf16[512,1536]{1,0:T(8,128)(2,1)} fusion(bf16[2,1536,1024]{2,1,0:T(8,128)(2,1)S(1)} %bitcast.91, bf16[2,512,512]{2,1,0:T(8,128)(2,1)S(1)} %get-tuple-element.114, bf16[2,512,512]{2,1,0:T(8,128)(2,1)S(1)} %get-tuple-element.113), kind=kOutput, calls=%fused_computation.7 | convolution fusion | flops 3226206208 | bytes 9961472 | tf_op jit(solution)/shard_map/etf,edf->td/dot_general | solution.py:1985
  185.1 3.3 fusion.1
  189.8 51.0 %expert_sum.1 = (f32[2,48,1536]{2,1,0:T(8,128)}, f32[128,1536]{1,0:T(8,128)}, bf16[128,1536]{1,0:T(8,128)(2,1)}, f32[1,1536]{1,0:T(1,128)}, f32[8,1536]{1,0:T(8,128)}, /*index=5*/f32[128,3072]{1,0:T(8,128)}) custom-call(f32[4,8,128]{2,1,0:T(8,128)} %pad.13.picks_ref, f32[4,8,128]{2,1,0:T(8,128)} %get-tuple-element.82.gates_ref, ...), custom_call_target="tpu_custom_call" | custom-call | tf_op jit(solution)/shard_map/expert_sum/pallas_call | solution.py:1076
  242.9 1.4 lefts.1
  244.3 1.4 copy-done.2
  247.3 92.7 %mixer_back.1 = (f32[8,3328]{1,0:T(8,128)}, f32[8,3328]{1,0:T(8,128)}, f32[128,128]{1,0:T(8,128)}, f32[8,128]{1,0:T(8,128)}, f32[12,2048]{1,0:T(8,128)}, /*index...) custom-call(f32[128,128]{1,0:T(8,128)} %get-tuple-element.64.tail_re, ...), custom_call_target="tpu_custom_call" | custom-call | tf_op jit(solution)/shard_map/mixer_back/pallas_call | solution.py:1892
  340.1 73.6 %grad_sum.1 = (f32[12,6448]{1,0:T(8,128)}, f32[8,4864]{1,0:T(8,128)}, f32[128,1536]{1,0:T(8,128)}) custom-call(f32[128,128]{1,0:T(8,128)} %get-tuple-element.92.tail_back_ref, f32[8,3328]{1,0:T(8,128)} %get-tuple-element.93.rim_ref, f32[1,1536]{1,0:T(1,128)} %broadcast_in_dim.42.gain_ref, bf16[4,128,384]{2,1,0:T(8,128)(2,1)} %get-tuple-element.72.tail_ref, ...), custom_call_target="tpu_custom_call" | custom-call | tf_op jit(solution)/shard_map/grad_sum/pallas_call | solution.py:436
  413.7 1.3 fusion.6
  415.0 1.4 dynamic-slice_bitcast_fusion
  416.4 1.3 constant_dynamic-slice_fusion.2
  423.4 1.8 slice.36
  425.3 1.8 copy.64
  427.0 2.1 copy.65
  (81 shorter events, 20.2 us)
Async XLA Ops:
  0.7 175.4 %copy-start = (bf16[2,512,1536]{2,1,0:T(8,128)(2,1)S(1)}, bf16[2,512,1536]{2,1,0:T(8,128)(2,1)}, u32[]{:S(2)}) copy-start(bf16[2,512,1536]{2,1,0:T(8,128)(2,1)} %param.37) | copy-start | bytes 9437188
  1.5 67.0 %copy-start.16 = (f32[3328]{0:T(1024)S(1)}, f32[3328]{0:T(1024)}, u32[]{:S(2)}) copy-start(f32[3328]{0:T(1024)} %param.26) | copy-start | bytes 39940
  1.5 67.1 %copy-start.14 = (f32[4,3328]{1,0:T(4,128)S(1)}, f32[4,3328]{1,0:T(4,128)}, u32[]{:S(2)}) copy-start(f32[4,3328]{1,0:T(4,128)} %param.25) | copy-start | bytes 159748
  3.5 65.8 %copy-start.20 = (f32[48]{0:T(128)S(1)}, f32[48]{0:T(128)}, u32[]{:S(2)}) copy-start(f32[48]{0:T(128)} %param.29) | copy-start | bytes 580
  3.5 66.0 %copy-start.17 = (f32[3072]{0:T(1024)S(1)}, f32[3072]{0:T(1024)}, u32[]{:S(2)}) copy-start(f32[3072]{0:T(1024)} %param.30) | copy-start | bytes 36868
  3.5 66.6 %copy-start.21 = (f32[48]{0:T(128)S(1)}, f32[48]{0:T(128)}, u32[]{:S(2)}) copy-start(f32[48]{0:T(128)} %param.28) | copy-start | bytes 580
  3.5 66.6 %copy-start.22 = (f32[48]{0:T(128)S(1)}, f32[48]{0:T(128)}, u32[]{:S(2)}) copy-start(f32[48]{0:T(128)} %param.27) | copy-start | bytes 580
  70.7 70.4 %copy-start.18 = (f32[1536]{0:T(1024)S(1)}, f32[1536]{0:T(1024)}, u32[]{:S(2)}) copy-start(f32[1536]{0:T(1024)} %param.32) | copy-start | bytes 18436
  70.7 71.0 %copy-start.19 = (s32[1,128,6]{1,0,2:T(1,128)S(1)}, s32[1,128,6]{1,0,2:T(1,128)}, u32[]{:S(2)}) copy-start(s32[1,128,6]{1,0,2:T(1,128)} %param.22) | copy-start | bytes 9220
  168.7 1.5 copy-start.8
  169.1 7.0 %copy-start.7 = (bf16[2,512,1536]{2,1,0:T(8,128)(2,1)}, bf16[2,512,1536]{2,1,0:T(8,128)(2,1)S(1)}, u32[]{:S(2)}) copy-start(bf16[2,512,1536]{2,1,0:T(8,128)(2,1)S(1)} %multiply_convert_fusion.refs_3_) | copy-start | bytes 9437188
  170.2 10.2 %slice-start = ((s8[6291456]{0:T(1024)(128)(4,1)}), s8[4194304]{0:T(1024)(128)(4,1)S(1)}, s32[]{:S(2)}) async-start(s8[6291456]{0:T(1024)(128)(4,1)} %bitcast.90), calls=%async_computation | async-start | bytes 8388608
  176.1 4.3 slice-start.1
  178.7 6.4 %copy-start.9 = (bf16[2,512,512]{2,1,0:T(8,128)(2,1)}, bf16[2,512,512]{2,1,0:T(8,128)(2,1)S(1)}, u32[]{:S(2)}) copy-start(bf16[2,512,512]{2,1,0:T(8,128)(2,1)S(1)} %get-tuple-element.115.refs_2_) | copy-start | bytes 3145732
  185.1 3.9 copy-start.11
  189.8 51.0 %copy-start.3 = (bf16[128,1536]{1,0:T(8,128)(2,1)S(1)}, bf16[128,1536]{1,0:T(8,128)(2,1)}, u32[]{:S(2)}) copy-start(bf16[128,1536]{1,0:T(8,128)(2,1)} %get-tuple-element.76.second_ref.refs_7_) | copy-start | bytes 1179652
  189.8 51.0 %copy-start.5 = (bf16[128,1536]{1,0:T(8,128)(2,1)S(1)}, bf16[128,1536]{1,0:T(8,128)(2,1)}, u32[]{:S(2)}) copy-start(bf16[128,1536]{1,0:T(8,128)(2,1)} %get-tuple-element.70.first_ref) | copy-start | bytes 1179652
  240.8 1.1 copy-start.1
  244.2 1.4 copy-start.2
  245.6 1.1 copy-start.4
  413.7 16.2 %copy-start.12 = (f32[24,1536]{1,0:T(8,128)S(1)}, f32[24,1536]{1,0:T(8,128)}, u32[]{:S(2)}) copy-start(f32[24,1536]{1,0:T(8,128)} %get-tuple-element.148) | copy-start | bytes 442372
  423.4 5.7 %copy-start.10 = (f32[12,6448]{1,0:T(8,128)S(1)}, f32[12,6448]{1,0:T(8,128)}, u32[]{:S(2)}) copy-start(f32[12,6448]{1,0:T(8,128)} %get-tuple-element.141) | copy-start | bytes 928516
  423.4 7.1 %copy-start.13 = (f32[12,2048]{1,0:T(8,128)S(1)}, f32[12,2048]{1,0:T(8,128)}, u32[]{:S(2)}) copy-start(f32[12,2048]{1,0:T(8,128)} %get-tuple-element.151) | copy-start | bytes 294916
  423.4 7.7 %copy-start.15 = (f32[8,1536]{1,0:T(8,128)S(1)}, f32[8,1536]{1,0:T(8,128)}, u32[]{:S(2)}) copy-start(f32[8,1536]{1,0:T(8,128)} %get-tuple-element.152) | copy-start | bytes 147460
  (1 other events, 0.9 us)

commit v6 on v5

--- a/solution.py
+++ b/solution.py
@@ -817,7 +817,7 @@
     rows_ref, acts_ref, hidden_ref, grads_ref, back_ref, picks_ref,
     middle_ref, shared_ref, up_ref, second_ref, gates_ref, router_ref, gain_ref, weights_far,
     out_ref, middle_back, mix_ref, post_back, router_back, normed_back, back_far, middle_out, mix_out, normed_out,
-    stage_sem, save_sem, weights, load_sem, back_sum, picks_all,
+    stage_sem, save_sem, turned_mix, weights, load_sem, back_sum, picks_all,
     core_out, core_in, near, far, second_in, got, turned_rows, turned_hidden,
     core_ss, core_rs, near_ss, near_rs, far_ss, far_rs, second_ss, second_rs, zs, zr,
 ):
@@ -1020,17 +1020,24 @@
         mix_ref[...] = short(total)
         saves[0].start()
         saves[1].start()
-        turned = short(total.T)
-        for i in range(4):
-            loads[i].wait()
-            here = slice(i * quarter, (i + 1) * quarter)
-            normed_back[:, here] = dot32(weights[here], turned).T
-        saves[2].start()
+        turned_mix[...] = short(total.T)
+
+    def way_back_rows(i):
+        loads[i].wait()
+        here = slice(i * quarter, (i + 1) * quarter)
+        normed_back[:, here] = dot32(weights[here], turned_mix[...]).T
+        if i == 3:
+            saves[2].start()
 
     def step(t, carry):
-        @pl.when(t == 5)
+        @pl.when(t == 4)
         def _():
             way_back()
+
+        for i in range(4):
+            @pl.when(t == 5 + i)
+            def _():
+                way_back_rows(i)
 
         for lag, stage in enumerate(stages):
             k = t - lag
@@ -1084,6 +1091,7 @@
             *[pltpu.VMEM(a.shape, a.dtype) for a in staged],
             sem((10,)),
             sem((3,)),
+            pltpu.VMEM((model, depth), low),
             pltpu.VMEM(weights.shape, low),
             sem((4,)),
             pltpu.VMEM((depth, model), f32),

time: 437 us -> 436 us (level)
  no operation moved by 1% of the time
where the time goes in v6:
time: 436 us; the launch traced here: 432 us
  Pallas kernels  373 us (86%)
  local copies, waits for them, and re-layouts  30.3 us (7%)
  matrix products  16.5 us (4%)
  other arithmetic  10.4 us (2%)
    pallas_call x2, Pallas kernels, tile_call(): pl.pallas_call(kernel, out_shape=tuple((jax.ShapeDtypeStruct(s, d) for s,...  93.7 us
    pallas_call x1, Pallas kernels, grad_sum(): pl.pallas_call(grad_sum_kernel, out_shape=(jax.ShapeDtypeStruct((rows //...  73.9 us
    pallas_call x1, Pallas kernels, mixer(): pl.pallas_call(mixer_kernel, out_shape=tuple((jax.ShapeDtypeStruct(s, d)...  69.1 us
    pallas_call x1, Pallas kernels, project(): pl.pallas_call(project_kernel, out_shape=(jax.ShapeDtypeStruct((4, main_r...  61.4 us
    pallas_call x1, Pallas kernels, expert_sum(): pl.pallas_call(expert_sum_kernel, out_shape=tuple((jax.ShapeDtypeStruct(s...  51 us
    pallas_call x1, Pallas kernels, middle_part(): pl.pallas_call(middle_kernel, out_shape=tuple((jax.ShapeDtypeStruct(s, d)...  23.8 us
    unnamed x57, local copies, waits for them, and re-layouts  12.3 us

profile of v6, /device:TPU:0, one launch (start us, length us, event | category | flops | bytes accessed | tf_op | source)
XLA Modules:
  0.0 431.9 jit_solution(18304863961435192765)
XLA Ops:
  1.5 1.9 bitcast_select_fusion.rows_ref.up_ref.refs_6_.refs_3_
  4.4 1.4 maximum_maximum_fusion.1.tail_ref
  5.8 1.3 broadcast_in_dim.42.gain_ref
  7.1 61.4 %project.1 = (bf16[4,6400,384]{2,1,0:T(8,128)(2,1)}, bf16[128,1536]{1,0:T(8,128)(2,1)}, f32[128,6400]{1,0:T(8,128)}, f32[128,128]{1,0:T(8,128)}, bf16[4,128,384]{2,1,0:T(8,128)(2,1)}) custom-call(bf16[128,1536]{1,0:T(8,128)(2,1)} %bitcast.70, f32[1,1536]{1,0:T(1,128)} %broadcast_in_dim.42.gain_ref, bf16[128,384]{1,0:T(8,128)(2,1)} %maximum_maximum_fusion.1.tail_ref, ...), custom_call_target="tpu_custom_call" | custom-call | tf_op jit(solution)/shard_map/project/pallas_call | solution.py:1388
  70.7 69.1 %mixer.1 = (f32[128,3328]{1,0:T(8,128)}, f32[8,128]{1,0:T(8,128)}, f32[128,128]{1,0:T(8,128)}, f32[128,128]{1,0:T(8,128)}, f32[8,3328]{1,0:T(8,128)}, /*index=5*...) custom-call(f32[128,128]{1,0:T(8,128)} %get-tuple-element.64.tail_re, ...), custom_call_target="tpu_custom_call" | custom-call | tf_op jit(solution)/shard_map/mixer/pallas_call | solution.py:1626
  139.8 1.3 slice.30
  142.3 23.8 %middle.1 = (f32[128,1536]{1,0:T(8,128)}, bf16[128,1536]{1,0:T(8,128)(2,1)}, f32[128,1536]{1,0:T(8,128)}, f32[128,1536]{1,0:T(8,128)}, bf16[128,1024]{1,0:T(8,12...) custom-call(bf16[128,3072]{1,0:T(8,128)(2,1)} %get-tuple-element.71.normed_ref.gated_ref, ...), custom_call_target="tpu_custom_call" | custom-call | tf_op jit(solution)/shard_map/middle/pallas_call | solution.py:779
  166.8 1.8 convert.10
  170.2 5.9 %convolution_bitcast_fusion.1 = f32[2,512,1024]{2,1,0:T(8,128)S(1)} fusion(bf16[512,1536,1]{1,0,2:T(8,128)(2,1)S(1)} %bitcast.75, bf16[2,1536,1024]{2,1,0:T(8,128)(2,1)} %param.36), kind=kOutput, calls=%fused_computation.8 | convolution fusion | flops 3221225472 | bytes 12058624 | tf_op jit(solution)/shard_map/td,edf->etf/dot_general | solution.py:1983
  176.1 2.6 multiply_convert_fusion.2
  178.7 1.6 pad_maximum_fusion.refs_1_
  180.4 4.7 %fusion.2 = bf16[512,1536]{1,0:T(8,128)(2,1)} fusion(bf16[2,1536,1024]{2,1,0:T(8,128)(2,1)S(1)} %bitcast.91, bf16[2,512,512]{2,1,0:T(8,128)(2,1)S(1)} %get-tuple-element.114, bf16[2,512,512]{2,1,0:T(8,128)(2,1)S(1)} %get-tuple-element.113), kind=kOutput, calls=%fused_computation.7 | convolution fusion | flops 3226206208 | bytes 9961472 | tf_op jit(solution)/shard_map/etf,edf->td/dot_general | solution.py:1993
  185.1 3.3 fusion.1
  189.8 51.0 %expert_sum.1 = (f32[2,48,1536]{2,1,0:T(8,128)}, f32[128,1536]{1,0:T(8,128)}, bf16[128,1536]{1,0:T(8,128)(2,1)}, f32[1,1536]{1,0:T(1,128)}, f32[8,1536]{1,0:T(8,128)}, /*index=5*/f32[128,3072]{1,0:T(8,128)}) custom-call(f32[4,8,128]{2,1,0:T(8,128)} %pad.13.picks_ref, f32[4,8,128]{2,1,0:T(8,128)} %get-tuple-element.82.gates_ref, ...), custom_call_target="tpu_custom_call" | custom-call | tf_op jit(solution)/shard_map/expert_sum/pallas_call | solution.py:1083
  242.9 1.4 lefts.1
  244.3 1.4 copy-done.2
  247.4 92.3 %mixer_back.1 = (f32[8,3328]{1,0:T(8,128)}, f32[8,3328]{1,0:T(8,128)}, f32[128,128]{1,0:T(8,128)}, f32[8,128]{1,0:T(8,128)}, f32[12,2048]{1,0:T(8,128)}, /*index...) custom-call(f32[128,128]{1,0:T(8,128)} %get-tuple-element.64.tail_re, ...), custom_call_target="tpu_custom_call" | custom-call | tf_op jit(solution)/shard_map/mixer_back/pallas_call | solution.py:1900
  339.7 73.9 %grad_sum.1 = (f32[12,6448]{1,0:T(8,128)}, f32[8,4864]{1,0:T(8,128)}, f32[128,1536]{1,0:T(8,128)}) custom-call(f32[128,128]{1,0:T(8,128)} %get-tuple-element.92.tail_back_ref, f32[8,3328]{1,0:T(8,128)} %get-tuple-element.93.rim_ref, f32[1,1536]{1,0:T(1,128)} %broadcast_in_dim.42.gain_ref, bf16[4,128,384]{2,1,0:T(8,128)(2,1)} %get-tuple-element.72.tail_ref, ...), custom_call_target="tpu_custom_call" | custom-call | tf_op jit(solution)/shard_map/grad_sum/pallas_call | solution.py:436
  413.6 1.3 fusion.6
  415.0 1.4 dynamic-slice_bitcast_fusion
  416.3 1.3 constant_dynamic-slice_fusion.2
  423.3 1.8 slice.36
  425.2 1.8 copy.64
  426.9 2.1 copy.65
  (81 shorter events, 20.2 us)
Async XLA Ops:
  0.7 175.4 %copy-start = (bf16[2,512,1536]{2,1,0:T(8,128)(2,1)S(1)}, bf16[2,512,1536]{2,1,0:T(8,128)(2,1)}, u32[]{:S(2)}) copy-start(bf16[2,512,1536]{2,1,0:T(8,128)(2,1)} %param.37) | copy-start | bytes 9437188
  1.5 67.0 %copy-start.16 = (f32[3328]{0:T(1024)S(1)}, f32[3328]{0:T(1024)}, u32[]{:S(2)}) copy-start(f32[3328]{0:T(1024)} %param.26) | copy-start | bytes 39940
  1.5 67.1 %copy-start.14 = (f32[4,3328]{1,0:T(4,128)S(1)}, f32[4,3328]{1,0:T(4,128)}, u32[]{:S(2)}) copy-start(f32[4,3328]{1,0:T(4,128)} %param.25) | copy-start | bytes 159748
  3.5 65.8 %copy-start.20 = (f32[48]{0:T(128)S(1)}, f32[48]{0:T(128)}, u32[]{:S(2)}) copy-start(f32[48]{0:T(128)} %param.29) | copy-start | bytes 580
  3.5 66.0 %copy-start.17 = (f32[3072]{0:T(1024)S(1)}, f32[3072]{0:T(1024)}, u32[]{:S(2)}) copy-start(f32[3072]{0:T(1024)} %param.30) | copy-start | bytes 36868
  3.5 66.6 %copy-start.21 = (f32[48]{0:T(128)S(1)}, f32[48]{0:T(128)}, u32[]{:S(2)}) copy-start(f32[48]{0:T(128)} %param.28) | copy-start | bytes 580
  3.5 66.6 %copy-start.22 = (f32[48]{0:T(128)S(1)}, f32[48]{0:T(128)}, u32[]{:S(2)}) copy-start(f32[48]{0:T(128)} %param.27) | copy-start | bytes 580
  70.7 70.4 %copy-start.18 = (f32[1536]{0:T(1024)S(1)}, f32[1536]{0:T(1024)}, u32[]{:S(2)}) copy-start(f32[1536]{0:T(1024)} %param.32) | copy-start | bytes 18436
  70.7 71.0 %copy-start.19 = (s32[1,128,6]{1,0,2:T(1,128)S(1)}, s32[1,128,6]{1,0,2:T(1,128)}, u32[]{:S(2)}) copy-start(s32[1,128,6]{1,0,2:T(1,128)} %param.22) | copy-start | bytes 9220
  168.7 1.5 copy-start.8
  169.1 7.0 %copy-start.7 = (bf16[2,512,1536]{2,1,0:T(8,128)(2,1)}, bf16[2,512,1536]{2,1,0:T(8,128)(2,1)S(1)}, u32[]{:S(2)}) copy-start(bf16[2,512,1536]{2,1,0:T(8,128)(2,1)S(1)} %multiply_convert_fusion.refs_3_) | copy-start | bytes 9437188
  170.2 10.2 %slice-start = ((s8[6291456]{0:T(1024)(128)(4,1)}), s8[4194304]{0:T(1024)(128)(4,1)S(1)}, s32[]{:S(2)}) async-start(s8[6291456]{0:T(1024)(128)(4,1)} %bitcast.90), calls=%async_computation | async-start | bytes 8388608
  176.1 4.3 slice-start.1
  178.7 6.4 %copy-start.9 = (bf16[2,512,512]{2,1,0:T(8,128)(2,1)}, bf16[2,512,512]{2,1,0:T(8,128)(2,1)S(1)}, u32[]{:S(2)}) copy-start(bf16[2,512,512]{2,1,0:T(8,128)(2,1)S(1)} %get-tuple-element.115.refs_2_) | copy-start | bytes 3145732
  185.1 3.9 copy-start.11
  189.8 51.0 %copy-start.3 = (bf16[128,1536]{1,0:T(8,128)(2,1)S(1)}, bf16[128,1536]{1,0:T(8,128)(2,1)}, u32[]{:S(2)}) copy-start(bf16[128,1536]{1,0:T(8,128)(2,1)} %get-tuple-element.76.second_ref.refs_7_) | copy-start | bytes 1179652
  189.8 51.1 %copy-start.5 = (bf16[128,1536]{1,0:T(8,128)(2,1)S(1)}, bf16[128,1536]{1,0:T(8,128)(2,1)}, u32[]{:S(2)}) copy-start(bf16[128,1536]{1,0:T(8,128)(2,1)} %get-tuple-element.70.first_ref) | copy-start | bytes 1179652
  240.8 1.1 copy-start.1
  244.3 1.4 copy-start.2
  245.6 1.1 copy-start.4
  413.6 16.2 %copy-start.12 = (f32[24,1536]{1,0:T(8,128)S(1)}, f32[24,1536]{1,0:T(8,128)}, u32[]{:S(2)}) copy-start(f32[24,1536]{1,0:T(8,128)} %get-tuple-element.148) | copy-start | bytes 442372
  423.3 5.7 %copy-start.10 = (f32[12,6448]{1,0:T(8,128)S(1)}, f32[12,6448]{1,0:T(8,128)}, u32[]{:S(2)}) copy-start(f32[12,6448]{1,0:T(8,128)} %get-tuple-element.141) | copy-start | bytes 928516
  423.3 7.1 %copy-start.13 = (f32[12,2048]{1,0:T(8,128)S(1)}, f32[12,2048]{1,0:T(8,128)}, u32[]{:S(2)}) copy-start(f32[12,2048]{1,0:T(8,128)} %get-tuple-element.151) | copy-start | bytes 294916
  423.3 7.7 %copy-start.15 = (f32[8,1536]{1,0:T(8,128)S(1)}, f32[8,1536]{1,0:T(8,128)}, u32[]{:S(2)}) copy-start(f32[8,1536]{1,0:T(8,128)} %get-tuple-element.152) | copy-start | bytes 147460
  (1 other events, 0.9 us)
